TPU v7x, 256 devices: a whole 4x4x8 slice. The times are simulated.
256 devices in a mesh: batch: 8 (over z_lo, x), expert: 32 (over y, z_hi, core).
Axes of the slice: x: 4, y: 4, z: 8 (z_hi: 4, z_lo: 2; z = z_hi * 2 + z_lo), core: 2. Of those that a mesh axis runs over, the one named last changes fastest.
Arguments:
- tokens: bfloat16 [256, 256, 1280], P(('batch', 'expert')), may hold values from -18 to 18
- slot_params: bfloat16 [1280, 64], replicated, as said below
- weight_in: bfloat16 [64, 1280, 4096], P('expert', None, 'batch'), may hold values from -0.15625 to 0.15625
- weight_out: bfloat16 [64, 4096, 1280], P('expert', 'batch'), may hold values from -0.09375 to 0.09375
- output_grad: bfloat16 [256, 256, 1280], P(('batch', 'expert')), may hold values from -6 to 6
Outputs:
- tokens_grad: bfloat16 [256, 256, 1280], P(('batch', 'expert'))
- params_grad: float32 [1280, 64], replicated
- weight_in_grad: bfloat16 [64, 1280, 4096], P('expert', None, 'batch')
- weight_out_grad: bfloat16 [64, 4096, 1280], P('expert', 'batch')
Inputs may be any that keep to these rules, and one draw needn't show every extreme that they name: Every entry of slot_params is plus or minus one common magnitude, the bfloat16 value nearest to 1280 ** -0.5.
All inputs are finite; a program needn't handle non-finite values.
Results may differ from a plain program's by a relative error of at most 0.023.
Values may be sent and summed in bfloat16 or wider, within the bound.
No kernel may reach another device: no remote copies, remote signals or barrier semaphores. Data moves between devices by JAX's collectives and lax.ppermute only.
A program may use at most 64 MiB of HBM per device.

v0:
```python
import math

import jax
import jax.numpy as jnp
from jax import lax
from jax.sharding import PartitionSpec as P

GELU_CUBIC = 0.044715
GELU_ROOT = math.sqrt(2.0 / math.pi)


def gelu_pair(pre_act):
    tanh_arg = GELU_ROOT * (pre_act + GELU_CUBIC * pre_act * pre_act * pre_act)
    tanh_value = jnp.tanh(tanh_arg)
    gelu_value = 0.5 * pre_act * (1.0 + tanh_value)
    gelu_slope = 0.5 * (1.0 + tanh_value) + 0.5 * pre_act * (
        1.0 - tanh_value * tanh_value
    ) * GELU_ROOT * (1.0 + 3.0 * GELU_CUBIC * pre_act * pre_act)
    return (gelu_value, gelu_slope)


def body(tokens, slot_params, weight_in, weight_out, output_grad):
    images = tokens.shape[0]
    width = tokens.shape[2]
    logits = jnp.einsum("bmd,ds->bsm", tokens, slot_params, preferred_element_type=jnp.float32)
    dispatch = jax.nn.softmax(logits, axis=2)
    combine = jax.nn.softmax(logits, axis=1)
    dispatch_half = dispatch.astype(jnp.bfloat16)
    combine_half = combine.astype(jnp.bfloat16)
    slot_in = jnp.einsum(
        "bsm,bmd->bsd", dispatch_half, tokens, preferred_element_type=jnp.float32
    ).astype(jnp.bfloat16)
    slot_cot = jnp.einsum(
        "bsm,bmd->bsd", combine_half, output_grad, preferred_element_type=jnp.float32
    ).astype(jnp.bfloat16)
    routed_in, routed_cot = (
        lax.all_to_all(slot_in, "expert", split_axis=1, concat_axis=1, tiled=True),
        lax.all_to_all(slot_cot, "expert", split_axis=1, concat_axis=1, tiled=True),
    )
    rows_in, rows_cot = (
        lax.all_gather(routed_in, "batch", axis=0, tiled=True),
        lax.all_gather(routed_cot, "batch", axis=0, tiled=True),
    )
    experts_here = weight_in.shape[0]
    lead_rows = rows_in.shape[0]
    blocks = rows_in.shape[1] // experts_here
    shaped_in = rows_in.reshape(lead_rows, blocks, experts_here, width)
    shaped_cot = rows_cot.reshape(lead_rows, blocks, experts_here, width)
    pre_act = jnp.einsum("rjed,edf->rjef", shaped_in, weight_in, preferred_element_type=jnp.float32)
    gelu_value, gelu_slope = gelu_pair(pre_act)
    activation = gelu_value.astype(jnp.bfloat16)
    piece_rows = activation
    product = jnp.einsum(
        "rjef,efd->rjed", piece_rows, weight_out, preferred_element_type=jnp.float32
    )
    output_share = lax.psum_scatter(
        product.reshape(lax.axis_size("batch") * images, blocks * experts_here, width).astype(
            jnp.bfloat16
        ),
        "batch",
        scatter_dimension=0,
        tiled=True,
    )
    slot_out = lax.all_to_all(output_share, "expert", split_axis=1, concat_axis=1, tiled=True)
    act_grad = jnp.einsum(
        "rjed,efd->rjef", shaped_cot, weight_out, preferred_element_type=jnp.float32
    )
    pre_grad = (act_grad * gelu_slope).astype(jnp.bfloat16)
    weight_out_grad = jnp.einsum(
        "rjef,rjed->efd", activation, shaped_cot, preferred_element_type=jnp.float32
    ).astype(jnp.bfloat16)
    weight_in_grad = jnp.einsum(
        "rjed,rjef->edf", shaped_in, pre_grad, preferred_element_type=jnp.float32
    ).astype(jnp.bfloat16)
    piece_rows = pre_grad
    product = jnp.einsum(
        "rjef,edf->rjed", piece_rows, weight_in, preferred_element_type=jnp.float32
    )
    input_share = lax.psum_scatter(
        product.reshape(lax.axis_size("batch") * images, blocks * experts_here, width).astype(
            jnp.bfloat16
        ),
        "batch",
        scatter_dimension=0,
        tiled=True,
    )
    slot_in_grad = lax.all_to_all(input_share, "expert", split_axis=1, concat_axis=1, tiled=True)
    combine_grad = jnp.einsum(
        "bmd,bsd->bsm", output_grad, slot_out, preferred_element_type=jnp.float32
    )
    dispatch_grad = jnp.einsum(
        "bmd,bsd->bsm", tokens, slot_in_grad, preferred_element_type=jnp.float32
    )
    combine_part = combine * (combine_grad - jnp.sum(combine * combine_grad, axis=1, keepdims=True))
    dispatch_part = dispatch * (
        dispatch_grad - jnp.sum(dispatch * dispatch_grad, axis=2, keepdims=True)
    )
    logits_grad = (combine_part + dispatch_part).astype(jnp.bfloat16)
    direct = jnp.einsum(
        "bsm,bsd->bmd", dispatch_half, slot_in_grad, preferred_element_type=jnp.float32
    )
    through = jnp.einsum(
        "bsm,ds->bmd", logits_grad, slot_params, preferred_element_type=jnp.float32
    )
    tokens_grad = (direct + through).astype(jnp.bfloat16)
    local_params = jnp.einsum(
        "bmd,bsm->ds", tokens, logits_grad, preferred_element_type=jnp.float32
    )
    total_images = images * lax.axis_size("batch") * lax.axis_size("expert")
    params_grad = lax.psum(local_params, ("batch", "expert")) / total_images
    return (tokens_grad, params_grad, weight_in_grad, weight_out_grad)


def solution(mesh):
    in_specs = (
        P(("batch", "expert"), None, None),
        P(),
        P("expert", None, "batch"),
        P("expert", "batch", None),
        P(("batch", "expert"), None, None),
    )
    out_specs = (
        P(("batch", "expert"), None, None),
        P(),
        P("expert", None, "batch"),
        P("expert", "batch", None),
    )
    return jax.shard_map(body, mesh=mesh, in_specs=in_specs, out_specs=out_specs, check_vma=False)
```

profile of v0, /device:TPU:1, one launch (start us, length us, event | category | flops | bytes accessed | tf_op | source)
XLA Modules:
  0.0 496.6 jit_solution(13365088074514332280)
XLA Ops:
  7.2 1.8 fusion.59
  9.2 1.4 fusion.11
  11.4 1.5 reduce.13
  13.0 24.1 %all_to_all.20 = bf16[32,2,1280]{2,1,0:T(2,128)(2,1)S(1)} all-to-all(bf16[32,2,1280]{2,1,0:T(2,128)(2,1)S(1)} %reshape.115), channel_id=1, replica_groups=mesh['batch'=8,'expert'=32] {'expert'}, dimensions={0} | all-to-all | bytes 327680 | tf_op jit(solution)/shard_map/all_to_all | solution.py:37
  38.0 1.3 fusion.10
  39.5 1.5 reduce.12
  41.2 15.9 %all_to_all.21 = bf16[32,2,1280]{2,1,0:T(2,128)(2,1)S(1)} all-to-all(bf16[32,2,1280]{2,1,0:T(2,128)(2,1)S(1)} %reshape.113), channel_id=1, replica_groups=mesh['batch'=8,'expert'=32] {'expert'}, dimensions={0} | all-to-all | bytes 327680 | tf_op jit(solution)/shard_map/all_to_all | solution.py:38
  57.9 14.1 %all-gather.5.cloned.1.call-done = bf16[8,64,1280]{2,1,0:T(8,128)(2,1)} async-done(((bf16[1,64,1280]{2,1,0:T(8,128)(2,1)}), bf16[8,64,1280]{2,1,0:T(8,128)(2,1)}) %all-gather.5.cloned.1.call-update) | async-done | bytes 1310736 | tf_op jit(solution)/shard_map/all_gather | solution.py:41
  72.0 2.0 copy.53
  75.2 1.9 fusion.18
  77.0 38.6 %all-gather.3.cloned.1.call-done = bf16[8,64,1280]{2,1,0:T(8,128)(2,1)} async-done(((bf16[1,64,1280]{2,1,0:T(8,128)(2,1)}), bf16[8,64,1280]{2,1,0:T(8,128)(2,1)}) %all-gather.3.cloned.1.call-update) | async-done | bytes 1310736 | tf_op jit(solution)/shard_map/all_gather | solution.py:42
  115.6 2.2 copy.49
  117.8 3.1 fusion.22
  124.1 3.0 fusion.1
  129.1 3.8 bitcast_convert_fusion.1
  132.9 33.0 %reduce-scatter.3.cloned.1.call-done = bf16[1,64,1280]{2,1,0:T(8,128)(2,1)} async-done(((bf16[8,64,1280]{2,1,0:T(8,128)(2,1)}), bf16[1,64,1280]{2,1,0:T(8,128)(2,1)}) %reduce-scatter.3.cloned.1.call-update) | async-done | bytes 163856 | tf_op jit(solution)/shard_map/reduce_scatter | solution.py:79
  167.1 1.5 reduce.14
  169.3 14.3 %all-to-all-start.2 = ((bf16[32,2,1280]{2,1,0:T(2,128)(2,1)}), bf16[32,2,1280]{2,1,0:T(2,128)(2,1)}, u32[]{:S(2)}, u32[]{:S(2)}) async-start(bf16[32,2,1280]{2,1,0:T(2,128)(2,1)} %reshape.117), calls=%async_computation.3 | async-start | bytes 327680 | tf_op jit(solution)/shard_map/all_to_all | solution.py:87
  183.6 4.3 bitcast_convert_fusion
  187.9 24.1 %reduce-scatter.5.cloned.1.call-done = bf16[1,64,1280]{2,1,0:T(8,128)(2,1)} async-done(((bf16[8,64,1280]{2,1,0:T(8,128)(2,1)}), bf16[1,64,1280]{2,1,0:T(8,128)(2,1)}) %reduce-scatter.5.cloned.1.call-update) | async-done | bytes 163856 | tf_op jit(solution)/shard_map/reduce_scatter | solution.py:56
  212.0 1.9 copy.94
  213.9 2.5 reduce.15
  217.1 13.7 %all-to-all-start.3 = ((bf16[32,2,1280]{2,1,0:T(2,128)(2,1)}), bf16[32,2,1280]{2,1,0:T(2,128)(2,1)S(1)}, u32[]{:S(2)}, u32[]{:S(2)}) async-start(bf16[32,2,1280]{2,1,0:T(2,128)(2,1)} %reshape.119), calls=%async_computation.5 | async-start | bytes 327680 | tf_op jit(solution)/shard_map/all_to_all | solution.py:64
  230.9 2.1 reshape.118
  233.0 1.9 fusion.36
  234.9 2.5 fusion.45
  237.4 5.1 %all-to-all-done.3 = bf16[32,2,1280]{2,1,0:T(2,128)(2,1)S(1)} async-done(((bf16[32,2,1280]{2,1,0:T(2,128)(2,1)}), bf16[32,2,1280]{2,1,0:T(2,128)(2,1)S(1)}, u32[]{:S(2)}, u32[]{:S(2)}) %all-to-all-start.3) | async-done | bytes 163872 | tf_op jit(solution)/shard_map/all_to_all | solution.py:64
  243.3 1.7 multiply_reduce_fusion.1
  245.6 1.9 convolution_bitcast_fusion
  247.5 2.7 fusion.9
  250.2 238.2 %all-reduce.2.cloned.1.call-done = f32[1280,64]{0,1:T(8,128)} async-done(((f32[1280,64]{0,1:T(8,128)}), f32[1280,64]{0,1:T(8,128)}) %all-reduce.2.cloned.1.call-update) | async-done | bytes 327696 | tf_op jit(solution)/shard_map/psum | solution.py:110
  488.4 1.7 broadcast_multiply_fusion
  (44 shorter events, 13.6 us)
Async XLA Ops:
  7.2 68.0 %copy-start = (bf16[2,1280,512]{2,1,0:T(8,128)(2,1)S(1)}, bf16[2,1280,512]{2,1,0:T(8,128)(2,1)}, u32[]{:S(2)}) copy-start(bf16[2,1280,512]{2,1,0:T(8,128)(2,1)} %param.7) | copy-start | bytes 7864324
  7.2 64.9 %all-gather.5.cloned.1.call-start = ((), (), s32[]{:S(2)}) async-start(), calls=%async_computation.7 | async-start | bytes 1474560 | tf_op jit(solution)/shard_map/all_gather | solution.py:41
  37.9 77.7 %all-gather.3.cloned.1.call-start = ((), (), s32[]{:S(2)}) async-start(), calls=%async_computation.6 | async-start | bytes 1474560 | tf_op jit(solution)/shard_map/all_gather | solution.py:42
  57.9 108.0 %reduce-scatter.3.cloned.1.call-start = ((), (), s32[]{:S(2)}) async-start(), calls=%async_computation.8 | async-start | bytes 1474560 | tf_op jit(solution)/shard_map/reduce_scatter | solution.py:79
  74.1 1.1 copy-start.3
  115.6 2.2 copy-start.6
  117.8 3.1 copy-start.2
  123.9 88.1 %reduce-scatter.5.cloned.1.call-start = ((), (), s32[]{:S(2)}) async-start(), calls=%async_computation.9 | async-start | bytes 1474560 | tf_op jit(solution)/shard_map/reduce_scatter | solution.py:56
  169.3 47.7 %all-to-all-start.2 = ((bf16[32,2,1280]{2,1,0:T(2,128)(2,1)}), bf16[32,2,1280]{2,1,0:T(2,128)(2,1)}, u32[]{:S(2)}, u32[]{:S(2)}) async-start(bf16[32,2,1280]{2,1,0:T(2,128)(2,1)} %reshape.117), calls=%async_computation.3 | async-start | bytes 327680 | tf_op jit(solution)/shard_map/all_to_all | solution.py:87
  187.9 45.0 %copy-start.1 = (bf16[1,256,1280]{2,1,0:T(8,128)(2,1)S(1)}, bf16[1,256,1280]{2,1,0:T(8,128)(2,1)}, u32[]{:S(2)}) copy-start(bf16[1,256,1280]{2,1,0:T(8,128)(2,1)} %param.5) | copy-start | bytes 1966084
  217.1 25.4 %all-to-all-start.3 = ((bf16[32,2,1280]{2,1,0:T(2,128)(2,1)}), bf16[32,2,1280]{2,1,0:T(2,128)(2,1)S(1)}, u32[]{:S(2)}, u32[]{:S(2)}) async-start(bf16[32,2,1280]{2,1,0:T(2,128)(2,1)} %reshape.119), calls=%async_computation.5 | async-start | bytes 327680 | tf_op jit(solution)/shard_map/all_to_all | solution.py:64
  230.8 257.6 %all-reduce.2.cloned.1.call-start = ((), (), s32[]{:S(2)}) async-start(), calls=%async_computation.10 | async-start | bytes 655360 | tf_op jit(solution)/shard_map/psum | solution.py:110
  243.3 4.2 copy-start.4
  245.0 0.6 copy-start.5
Sparse Core Ops, SparseCore 0:
  38.0 33.9 all-gather.4
  74.4 41.1 all-gather.2
  124.0 41.8 reduce-scatter.2
  168.3 43.6 reduce-scatter.4
  247.6 240.7 all-reduce.1
where the time goes:
time: 498 us; the launch traced here: 497 us
  waiting for transfers between devices  353 us (71%)
  blocking collectives  39.9 us (8%)
  matrix products  31.9 us (6%)
  starting transfers between devices  28.4 us (6%)
  local copies, waits for them, and re-layouts  20.2 us (4%)
  between operations  14 us (3%)
  other arithmetic  9.03 us (2%)
    psum x1, waiting for transfers between devices, body(): params_grad = lax.psum(local_params, ('batch', 'expert')) / total_images  238 us
    reduce_scatter x2, waiting for transfers between devices, body(): lax.psum_scatter(product.reshape(lax.axis_size('batch') * images, blocks...  57.1 us
    all_gather x1, waiting for transfers between devices, body(): lax.all_gather(routed_cot, 'batch', axis=0, tiled=True)  38.6 us
    all_to_all x1, blocking collectives, body(): lax.all_to_all(slot_in, 'expert', split_axis=1, concat_axis=1, tiled=True)  24.1 us
    all_to_all x1, blocking collectives, body(): lax.all_to_all(slot_cot, 'expert', split_axis=1, concat_axis=1, tiled=True)  15.9 us
    all_to_all x1, starting transfers between devices, body(): lax.all_to_all(input_share, 'expert', split_axis=1, concat_axis=1, tiled=...  14.3 us
    all_gather x1, waiting for transfers between devices, body(): lax.all_gather(routed_in, 'batch', axis=0, tiled=True)  14.1 us
    all_to_all x1, starting transfers between devices, body(): lax.all_to_all(output_share, 'expert', split_axis=1, concat_axis=1, tiled...  13.7 us
  transfers between devices with their start and end apart: 7, of which 6 were waited for; matrix products, arithmetic and copies ran while one was open for 8% of the time, Pallas kernels for 0%

commit v1 on v0

v1 whole, which is shorter than its diff:
```python
import math

import jax
import jax.numpy as jnp
from jax import lax
from jax.sharding import PartitionSpec as P

GELU_CUBIC = 0.044715
GELU_ROOT = math.sqrt(2.0 / math.pi)
BF16 = jnp.bfloat16
F32 = jnp.float32

X, ZL, Y, ZH, CORE = 4, 2, 4, 4, 2
OFFSETS = [(dz, dx) for dz in range(ZL) for dx in range(X)]


def gelu_pair(pre_act):
    tanh_arg = GELU_ROOT * (pre_act + GELU_CUBIC * pre_act * pre_act * pre_act)
    tanh_value = jnp.tanh(tanh_arg)
    gelu_value = 0.5 * pre_act * (1.0 + tanh_value)
    gelu_slope = 0.5 * (1.0 + tanh_value) + 0.5 * pre_act * (
        1.0 - tanh_value * tanh_value
    ) * GELU_ROOT * (1.0 + 3.0 * GELU_CUBIC * pre_act * pre_act)
    return (gelu_value, gelu_slope)


def batch_send(value, dz, dx):
    pairs = [
        (z * X + x, ((z + dz) % ZL) * X + (x + dx) % X) for z in range(ZL) for x in range(X)
    ]
    return lax.ppermute(value, "batch", pairs)


def batch_fetch(value, dz, dx):
    return batch_send(value, -dz, -dx)


def expert_send(value, dy, dh, dc):
    pairs = []
    for y in range(Y):
        for h in range(ZH):
            for c in range(CORE):
                to = (((y + dy) % Y) * ZH + (h + dh) % ZH) * CORE + (c + dc) % CORE
                pairs.append(((y * ZH + h) * CORE + c, to))
    return lax.ppermute(value, "expert", pairs)


def thirds(width):
    tiles = width // 128
    first = -(-tiles // 3) * 128
    second = first + (tiles - first // 128 + 1) // 2 * 128
    return (slice(0, first), slice(first, second), slice(second, width))


def gather_blocks(mine):
    blocks = {(0, 0): mine}
    blocks[0, 1] = batch_fetch(mine, 0, 1)
    blocks[0, 3] = batch_fetch(mine, 0, 3)
    blocks[1, 0] = batch_fetch(mine, 1, 0)
    blocks[0, 2] = batch_fetch(blocks[0, 1], 0, 1)
    blocks[1, 3] = batch_fetch(blocks[1, 0], 0, 3)
    blocks[1, 1] = batch_fetch(blocks[0, 1], 1, 0)
    a, b, c = thirds(mine.shape[1])
    blocks[1, 2] = jnp.concatenate(
        [
            batch_fetch(blocks[1, 1][:, a], 0, 1),
            batch_fetch(blocks[1, 3][:, b], 0, 3),
            batch_fetch(blocks[0, 2][:, c], 1, 0),
        ],
        axis=1,
    )
    return blocks


def add(*terms):
    total = terms[0].astype(F32)
    for term in terms[1:]:
        total = total + term.astype(F32)
    return total.astype(BF16)


def scatter_blocks(parts):
    a, b, c = thirds(parts[0, 0].shape[1])
    far = parts[1, 2]
    got_a = batch_send(far[:, a], 0, 1)
    got_b = batch_send(far[:, b], 0, 3)
    got_c = batch_send(far[:, c], 1, 0)

    def add_cols(part, got, cols):
        return jnp.concatenate(
            [part[:, : cols.start], add(part[:, cols], got), part[:, cols.stop :]], axis=1
        )

    got_11 = batch_send(add_cols(parts[1, 1], got_a, a), 1, 0)
    got_13 = batch_send(add_cols(parts[1, 3], got_b, b), 0, 3)
    got_02 = batch_send(add_cols(parts[0, 2], got_c, c), 0, 1)
    got_01 = batch_send(add(parts[0, 1], got_11, got_02), 0, 1)
    got_03 = batch_send(parts[0, 3], 0, 3)
    got_10 = batch_send(add(parts[1, 0], got_13), 1, 0)
    return add(parts[0, 0], got_01, got_03, got_10)


def sum_all(partial):
    core = lax.axis_index("expert") % CORE
    halves = partial.reshape(CORE, partial.shape[0] // CORE, partial.shape[1])
    keep = lax.dynamic_index_in_dim(halves, core, 0, False)
    give = lax.dynamic_index_in_dim(halves, 1 - core, 0, False)
    total = add(keep, expert_send(give, 0, 0, 1))
    total = add(total, *[batch_send(total, 0, k) for k in (1, 2, 3)])
    total = add(total, *[expert_send(total, k, 0, 0) for k in (1, 2, 3)])
    total = add(total, batch_send(total, 1, 0))
    total = add(total, *[expert_send(total, 0, k, 0) for k in (1, 2, 3)])
    other = expert_send(total, 0, 0, 1)
    first = jnp.where(core == 0, total, other)
    second = jnp.where(core == 0, other, total)
    return jnp.concatenate([first, second], axis=0).astype(F32)


def body(tokens, slot_params, weight_in, weight_out, output_grad):
    tokens, output_grad = tokens[0], output_grad[0]
    width = tokens.shape[1]
    slots = slot_params.shape[1]
    groups = lax.axis_size("expert")
    each = slots // groups
    params = slot_params.reshape(width, groups, each).swapaxes(1, 2).reshape(width, slots)
    logits = jnp.einsum("md,ds->sm", tokens, params, preferred_element_type=F32)
    dispatch = jax.nn.softmax(logits, axis=1)
    combine = jax.nn.softmax(logits, axis=0)
    dispatch_half = dispatch.astype(BF16)
    combine_half = combine.astype(BF16)
    slot_in = jnp.dot(dispatch_half, tokens, preferred_element_type=F32).astype(BF16)
    slot_cot = jnp.dot(combine_half, output_grad, preferred_element_type=F32).astype(BF16)
    rows = jnp.concatenate(
        [slot_in[j * groups : (j + 1) * groups] for j in range(each)]
        + [slot_cot[j * groups : (j + 1) * groups] for j in range(each)],
        axis=1,
    )
    routed = lax.all_to_all(rows, "expert", split_axis=0, concat_axis=0, tiled=True)
    blocks = gather_blocks(routed)
    gathered = jnp.concatenate([blocks[o] for o in OFFSETS], axis=0)
    out_cols, in_cols, in_grads, out_grads = [], [], [], []
    for j in range(each):
        rows_in = gathered[:, j * width : (j + 1) * width]
        rows_cot = gathered[:, (each + j) * width : (each + j + 1) * width]
        pre_act = jnp.dot(rows_in, weight_in[j], preferred_element_type=F32)
        gelu_value, gelu_slope = gelu_pair(pre_act)
        activation = gelu_value.astype(BF16)
        out_cols.append(jnp.dot(activation, weight_out[j], preferred_element_type=F32).astype(BF16))
        act_grad = lax.dot_general(
            rows_cot, weight_out[j], (((1,), (1,)), ((), ())), preferred_element_type=F32
        )
        pre_grad = (act_grad * gelu_slope).astype(BF16)
        in_cols.append(
            lax.dot_general(
                pre_grad, weight_in[j], (((1,), (1,)), ((), ())), preferred_element_type=F32
            ).astype(BF16)
        )
        out_grads.append(
            lax.dot_general(
                activation, rows_cot, (((0,), (0,)), ((), ())), preferred_element_type=F32
            ).astype(BF16)
        )
        in_grads.append(
            lax.dot_general(
                rows_in, pre_grad, (((0,), (0,)), ((), ())), preferred_element_type=F32
            ).astype(BF16)
        )
    partial = jnp.concatenate(out_cols + in_cols, axis=1)
    parts = {o: partial[i * groups : (i + 1) * groups] for i, o in enumerate(OFFSETS)}
    share = scatter_blocks(parts)
    back = lax.all_to_all(share, "expert", split_axis=0, concat_axis=0, tiled=True)
    slot_out = jnp.concatenate([back[:, j * width : (j + 1) * width] for j in range(each)], axis=0)
    slot_in_grad = jnp.concatenate(
        [back[:, (each + j) * width : (each + j + 1) * width] for j in range(each)], axis=0
    )
    combine_grad = jnp.einsum("md,sd->sm", output_grad, slot_out, preferred_element_type=F32)
    dispatch_grad = jnp.einsum("md,sd->sm", tokens, slot_in_grad, preferred_element_type=F32)
    combine_part = combine * (combine_grad - jnp.sum(combine * combine_grad, axis=0, keepdims=True))
    dispatch_part = dispatch * (
        dispatch_grad - jnp.sum(dispatch * dispatch_grad, axis=1, keepdims=True)
    )
    logits_grad = (combine_part + dispatch_part).astype(BF16)
    tokens_grad = (
        jnp.einsum("sm,sd->md", dispatch_half, slot_in_grad, preferred_element_type=F32)
        + jnp.einsum("sm,ds->md", logits_grad, params, preferred_element_type=F32)
    ).astype(BF16)
    local_params = jnp.einsum("md,sm->ds", tokens, logits_grad, preferred_element_type=F32)
    total_images = lax.axis_size("batch") * groups
    params_grad = sum_all(local_params.astype(BF16)) / total_images
    params_grad = params_grad.reshape(width, each, groups).swapaxes(1, 2).reshape(width, slots)
    return (tokens_grad[None], params_grad, jnp.stack(in_grads), jnp.stack(out_grads))


def solution(mesh):
    in_specs = (
        P(("batch", "expert"), None, None),
        P(),
        P("expert", None, "batch"),
        P("expert", "batch", None),
        P(("batch", "expert"), None, None),
    )
    out_specs = (
        P(("batch", "expert"), None, None),
        P(),
        P("expert", None, "batch"),
        P("expert", "batch", None),
    )
    return jax.shard_map(body, mesh=mesh, in_specs=in_specs, out_specs=out_specs, check_vma=False)
```

time: 498 us -> 176 us (0.35)
  waiting for transfers between devices: 353 us -> 59.2 us
  starting transfers between devices: 28.4 us -> 51.4 us
  matrix products: 31.9 us -> 14.9 us
  between operations: 14 us -> 1.25 us
  blocking collectives: 39.9 us -> 27.3 us
  local copies, waits for them, and re-layouts: 20.2 us -> 15.2 us
    psum x1 -> x0, waiting for transfers between devices: 238 us -> none  [body(): params_grad = lax.psum(local_params, ('batch', 'expert')) / total_images]
    reduce_scatter x2 -> x0, waiting for transfers between devices: 57.1 us -> none  [body(): lax.psum_scatter(product.reshape(lax.axis_size('batch') * images, blocks...]
    all_gather x2 -> x0, waiting for transfers between devices: 52.7 us -> none  [the longest x1 38.6 us: body(): lax.all_gather(routed_cot, 'batch', axis=0, tiled=True)]
    ppermute x0 -> x30, waiting for transfers between devices: none -> 48.4 us  [the longest x22 39.1 us: batch_send(): return lax.ppermute(value, 'batch', pairs)]
    ppermute x0 -> x30, starting transfers between devices: none -> 37.9 us  [the longest x22 24.1 us: batch_send(): return lax.ppermute(value, 'batch', pairs)]
    dot_general x14 -> x20, matrix products: 31.9 us -> 14.9 us  [the longest x2 3.3 us: body(): lax.dot_general(rows_in, pre_grad, (((0,), (0,)), ((), ())), preferred_el...]
    all_to_all x2 -> x1, starting transfers between devices: 28 us -> 13.5 us  [body(): lax.all_to_all(share, 'expert', split_axis=0, concat_axis=0, tiled=True)]
    all_to_all x2 -> x1, blocking collectives: 39.9 us -> 27.3 us  [body(): lax.all_to_all(rows, 'expert', split_axis=0, concat_axis=0, tiled=True)]
  transfers between devices with their start and end apart: 7 -> 31, of which waited for: 6 -> 21; matrix products, arithmetic and copies ran while one was open for 8% -> 6% of each run, Pallas kernels for 0% -> 0%
where the time goes in v1:
time: 176 us; the launch traced here: 175 us
  waiting for transfers between devices  59.2 us (34%)
  starting transfers between devices  51.4 us (29%)
  blocking collectives  27.3 us (16%)
  local copies, waits for them, and re-layouts  15.2 us (9%)
  matrix products  14.9 us (8%)
  other arithmetic  6.19 us (4%)
    ppermute x22, waiting for transfers between devices, batch_send(): return lax.ppermute(value, 'batch', pairs)  39.1 us
    all_to_all x1, blocking collectives, body(): lax.all_to_all(rows, 'expert', split_axis=0, concat_axis=0, tiled=True)  27.3 us
    ppermute x22, starting transfers between devices, batch_send(): return lax.ppermute(value, 'batch', pairs)  24.1 us
    ppermute x8, starting transfers between devices, expert_send(): return lax.ppermute(value, 'expert', pairs)  13.7 us
    all_to_all x1, starting transfers between devices, body(): lax.all_to_all(share, 'expert', split_axis=0, concat_axis=0, tiled=True)  13.5 us
    all_to_all x1, waiting for transfers between devices, body(): lax.all_to_all(share, 'expert', split_axis=0, concat_axis=0, tiled=True)  10.7 us
    ppermute x8, waiting for transfers between devices, expert_send(): return lax.ppermute(value, 'expert', pairs)  9.39 us
    unnamed x50, local copies, waits for them, and re-layouts  9.29 us
  transfers between devices with their start and end apart: 31, of which 21 were waited for; matrix products, arithmetic and copies ran while one was open for 6% of the time, Pallas kernels for 0%

profile of v1, /device:TPU:1, one launch (start us, length us, event | category | flops | bytes accessed | tf_op | source)
XLA Modules:
  0.0 175.4 jit_solution(3482733657889823907)
XLA Ops:
  4.6 27.3 %all_to_all.24 = bf16[32,2,2560]{2,1,0:T(2,128)(2,1)S(1)} all-to-all(bf16[32,2,2560]{2,1,0:T(2,128)(2,1)S(1)} %reshape.40), channel_id=1, replica_groups=mesh['batch'=8,'expert'=32] {'expert'}, dimensions={0} | all-to-all | bytes 655360 | tf_op jit(solution)/shard_map/all_to_all | solution.py:138
  32.3 2.6 %collective-permute-start = (bf16[32,5120]{1,0:T(8,128)(2,1)S(1)}, bf16[32,5120]{1,0:T(8,128)(2,1)S(1)}, u32[]{:S(2)}, u32[]{:S(2)}) collective-permute-start(bf16[32,5120]{1,0:T(8,128)(2,1)S(1)} %get-tuple-element.11), channel_id=1, source_target_pairs={{0,96},{32,0},{64,32},{96,64},{128,224},{160,128},{192,160},{224,1... | collective-permute-start | bytes 983048 | tf_op jit(solution)/shard_map/ppermute | solution.py:31
  35.9 5.6 %collective-permute-done = bf16[32,5120]{1,0:T(8,128)(2,1)S(1)} collective-permute-done((bf16[32,5120]{1,0:T(8,128)(2,1)S(1)}, bf16[32,5120]{1,0:T(8,128)(2,1)S(1)}, u32[]{:S(2)}, u32[]{:S(2)}) %collective-permute-start) | collective-permute-done | bytes 327712 | tf_op jit(solution)/shard_map/ppermute | solution.py:31
  41.5 3.4 %collective-permute-start.1 = (bf16[32,5120]{1,0:T(8,128)(2,1)S(1)}, bf16[32,5120]{1,0:T(8,128)(2,1)S(1)}, u32[]{:S(2)}, u32[]{:S(2)}) collective-permute-start(bf16[32,5120]{1,0:T(8,128)(2,1)S(1)} %collective-permute-done), channel_id=1, source_target_pairs={{0,96},{32,0},{64,32},{96,64},{128,224},{160,128},{192,160},{224,1... | collective-permute-start | bytes 983048 | tf_op jit(solution)/shard_map/ppermute | solution.py:31
  46.1 4.5 %collective-permute-done.1 = bf16[32,5120]{1,0:T(8,128)(2,1)S(1)} collective-permute-done((bf16[32,5120]{1,0:T(8,128)(2,1)S(1)}, bf16[32,5120]{1,0:T(8,128)(2,1)S(1)}, u32[]{:S(2)}, u32[]{:S(2)}) %collective-permute-start.1) | collective-permute-done | bytes 327712 | tf_op jit(solution)/shard_map/ppermute | solution.py:31
  52.0 2.8 %collective-permute-done.6 = bf16[32,5120]{1,0:T(8,128)(2,1)S(1)} collective-permute-done((bf16[32,5120]{1,0:T(8,128)(2,1)S(1)}, bf16[32,5120]{1,0:T(8,128)(2,1)S(1)}, u32[]{:S(2)}, u32[]{:S(2)}) %collective-permute-start.6) | collective-permute-done | bytes 327712 | tf_op jit(solution)/shard_map/ppermute | solution.py:31
  54.9 2.7 %collective-permute-start.5 = (bf16[32,1792]{1,0:T(8,128)(2,1)S(1)}, bf16[32,1792]{1,0:T(8,128)(2,1)S(1)}, u32[]{:S(2)}, u32[]{:S(2)}) collective-permute-start(bf16[32,1792]{1,0:T(8,128)(2,1)S(1)} %slice.164), channel_id=1, source_target_pairs={{0,96},{32,0},{64,32},{96,64},{128,224},{160,128},{192,160},{224,1... | collective-permute-start | bytes 344072 | tf_op jit(solution)/shard_map/ppermute | solution.py:31
  57.8 1.9 %collective-permute-done.7 = bf16[32,1664]{1,0:T(8,128)(2,1)S(1)} collective-permute-done((bf16[32,1664]{1,0:T(8,128)(2,1)S(1)}, bf16[32,1664]{1,0:T(8,128)(2,1)S(1)}, u32[]{:S(2)}, u32[]{:S(2)}) %collective-permute-start.7) | collective-permute-done | bytes 106528 | tf_op jit(solution)/shard_map/ppermute | solution.py:31
  60.8 1.8 %copy-done.13 = bf16[2,512,1280]{2,1,0:T(8,128)(2,1)S(1)} copy-done((bf16[2,512,1280]{2,1,0:T(8,128)(2,1)S(1)}, bf16[2,512,1280]{2,1,0:T(8,128)(2,1)}, u32[]{:S(2)}) %copy-start.13) | copy-done | bytes 2621464
  66.9 2.9 %collective-permute-start.15 = (bf16[32,1664]{1,0:T(8,128)(2,1)S(1)}, bf16[32,1664]{1,0:T(8,128)(2,1)S(1)}, u32[]{:S(2)}, u32[]{:S(2)}) collective-permute-start(bf16[32,1664]{1,0:T(8,128)(2,1)S(1)} %get-tuple-element.21), channel_id=1, source_target_pairs={{0,96},{32,0},{64,32},{96,64},{128,224},{160,128},{192,160},{224,1... | collective-permute-start | bytes 319496 | tf_op jit(solution)/shard_map/ppermute | solution.py:31
  71.5 3.2 %collective-permute-done.9 = bf16[32,1792]{1,0:T(8,128)(2,1)S(1)} collective-permute-done((bf16[32,1792]{1,0:T(8,128)(2,1)S(1)}, bf16[32,1792]{1,0:T(8,128)(2,1)S(1)}, u32[]{:S(2)}, u32[]{:S(2)}) %collective-permute-start.9) | collective-permute-done | bytes 114720 | tf_op jit(solution)/shard_map/ppermute | solution.py:31
  76.4 2.6 %collective-permute-start.16 = (bf16[32,5120]{1,0:T(8,128)(2,1)S(1)}, bf16[32,5120]{1,0:T(8,128)(2,1)S(1)}, u32[]{:S(2)}, u32[]{:S(2)}) collective-permute-start(bf16[32,5120]{1,0:T(8,128)(2,1)S(1)} %get-tuple-element.15), channel_id=1, source_target_pairs={{0,96},{32,0},{64,32},{96,64},{128,224},{160,128},{192,160},{224,1... | collective-permute-start | bytes 983048 | tf_op jit(solution)/shard_map/ppermute | solution.py:31
  79.0 4.3 %collective-permute-done.12 = bf16[32,5120]{1,0:T(8,128)(2,1)S(1)} collective-permute-done((bf16[32,5120]{1,0:T(8,128)(2,1)S(1)}, bf16[32,5120]{1,0:T(8,128)(2,1)S(1)}, u32[]{:S(2)}, u32[]{:S(2)}) %collective-permute-start.12) | collective-permute-done | bytes 327712 | tf_op jit(solution)/shard_map/ppermute | solution.py:31
  84.9 1.6 collective-permute-done.14
  86.5 5.9 %collective-permute-done.17 = bf16[32,5120]{1,0:T(8,128)(2,1)S(1)} collective-permute-done((bf16[32,5120]{1,0:T(8,128)(2,1)S(1)}, bf16[32,5120]{1,0:T(8,128)(2,1)S(1)}, u32[]{:S(2)}, u32[]{:S(2)}) %collective-permute-start.17) | collective-permute-done | bytes 327712 | tf_op jit(solution)/shard_map/ppermute | solution.py:31
  95.1 13.5 %all-to-all-start.1 = ((bf16[32,2,2560]{2,1,0:T(2,128)(2,1)}), bf16[32,2,2560]{2,1,0:T(2,128)(2,1)}, u32[]{:S(2)}, u32[]{:S(2)}) async-start(bf16[32,2,2560]{2,1,0:T(2,128)(2,1)} %reshape.42), calls=%async_computation.1 | async-start | bytes 655360 | tf_op jit(solution)/shard_map/all_to_all | solution.py:171
  108.7 1.6 fusion.1
  110.3 1.7 fusion
  112.0 10.7 %all-to-all-done.1 = bf16[32,2,2560]{2,1,0:T(2,128)(2,1)} async-done(((bf16[32,2,2560]{2,1,0:T(2,128)(2,1)}), bf16[32,2,2560]{2,1,0:T(2,128)(2,1)}, u32[]{:S(2)}, u32[]{:S(2)}) %all-to-all-start.1) | async-done | bytes 327712 | tf_op jit(solution)/shard_map/all_to_all | solution.py:171
  122.7 3.2 %reshape.43 = bf16[32,1,5120]{2,1,0:T(2,128)(2,1)} reshape(bf16[32,2,2560]{2,1,0:T(2,128)(2,1)} %all-to-all-done.1) | data formatting | bytes 655360
  128.2 1.6 multiply_reduce_fusion.1
  131.4 1.6 reshape.37
  135.0 1.7 pad_maximum_fusion
  136.7 1.8 %collective-permute-start.21 = (bf16[640,64]{0,1:T(8,128)(2,1)S(1)}, bf16[640,64]{0,1:T(8,128)(2,1)S(1)}, u32[]{:S(2)}, u32[]{:S(2)}) collective-permute-start(bf16[640,64]{0,1:T(8,128)(2,1)S(1)} %fusion.83), channel_id=1, source_target_pairs={{0,96},{32,0},{64,32},{96,64},{128,224},{160,128},{192,160},{224,1... | collective-permute-start | bytes 245768 | tf_op jit(solution)/shard_map/ppermute | solution.py:31
  140.9 3.0 %collective-permute-done.20 = bf16[640,64]{0,1:T(8,128)(2,1)S(1)} collective-permute-done((bf16[640,64]{0,1:T(8,128)(2,1)S(1)}, bf16[640,64]{0,1:T(8,128)(2,1)S(1)}, u32[]{:S(2)}, u32[]{:S(2)}) %collective-permute-start.20) | collective-permute-done | bytes 81952 | tf_op jit(solution)/shard_map/ppermute | solution.py:31
  143.8 1.8 %collective-permute-done.19 = bf16[640,64]{0,1:T(8,128)(2,1)S(1)} collective-permute-done((bf16[640,64]{0,1:T(8,128)(2,1)S(1)}, bf16[640,64]{0,1:T(8,128)(2,1)S(1)}, u32[]{:S(2)}, u32[]{:S(2)}) %collective-permute-start.19) | collective-permute-done | bytes 81952 | tf_op jit(solution)/shard_map/ppermute | solution.py:31
  149.0 2.0 %collective-permute-done.23 = bf16[640,64]{0,1:T(8,128)(2,1)S(1)} collective-permute-done((bf16[640,64]{0,1:T(8,128)(2,1)S(1)}, bf16[640,64]{0,1:T(8,128)(2,1)S(1)}, u32[]{:S(2)}, u32[]{:S(2)}) %collective-permute-start.23) | collective-permute-done | bytes 81952 | tf_op jit(solution)/shard_map/ppermute | solution.py:45
  153.0 1.7 pad_maximum_fusion.1
  156.9 4.7 %collective-permute-start.27 = (bf16[640,64]{0,1:T(8,128)(2,1)S(1)}, bf16[640,64]{0,1:T(8,128)(2,1)S(1)}, u32[]{:S(2)}, u32[]{:S(2)}) collective-permute-start(bf16[640,64]{0,1:T(8,128)(2,1)S(1)} %add_convert_fusion.7), channel_id=1, source_target_pairs={{0,4},{1,5},{2,6},{3,7},{4,0},{5,1},{6,2},{7,3},{8,12},{9,13},{10,... | collective-permute-start | bytes 245768 | tf_op jit(solution)/shard_map/ppermute | solution.py:45
  162.0 2.2 %collective-permute-done.27 = bf16[640,64]{0,1:T(8,128)(2,1)S(1)} collective-permute-done((bf16[640,64]{0,1:T(8,128)(2,1)S(1)}, bf16[640,64]{0,1:T(8,128)(2,1)S(1)}, u32[]{:S(2)}, u32[]{:S(2)}) %collective-permute-start.27) | collective-permute-done | bytes 81952 | tf_op jit(solution)/shard_map/ppermute | solution.py:45
  164.2 2.8 %collective-permute-done.26 = bf16[640,64]{0,1:T(8,128)(2,1)S(1)} collective-permute-done((bf16[640,64]{0,1:T(8,128)(2,1)S(1)}, bf16[640,64]{0,1:T(8,128)(2,1)S(1)}, u32[]{:S(2)}, u32[]{:S(2)}) %collective-permute-start.26) | collective-permute-done | bytes 81952 | tf_op jit(solution)/shard_map/ppermute | solution.py:45
  167.0 5.8 %collective-permute-start.29 = (bf16[640,64]{0,1:T(8,128)(2,1)S(1)}, bf16[640,64]{0,1:T(8,128)(2,1)S(1)}, u32[]{:S(2)}, u32[]{:S(2)}) collective-permute-start(bf16[640,64]{0,1:T(8,128)(2,1)S(1)} %add_convert_fusion.6), channel_id=1, source_target_pairs={{0,1},{1,0},{2,3},{3,2},{4,5},{5,4},{6,7},{7,6},{8,9},{9,8},{10,11... | collective-permute-start | bytes 245768 | tf_op jit(solution)/shard_map/ppermute | solution.py:45
  (135 shorter events, 39.8 us)
Async XLA Ops:
  32.3 9.2 %collective-permute-start = (bf16[32,5120]{1,0:T(8,128)(2,1)S(1)}, bf16[32,5120]{1,0:T(8,128)(2,1)S(1)}, u32[]{:S(2)}, u32[]{:S(2)}) collective-permute-start(bf16[32,5120]{1,0:T(8,128)(2,1)S(1)} %get-tuple-element.11), channel_id=1, source_target_pairs={{0,96},{32,0},{64,32},{96,64},{128,224},{160,128},{192,160},{224,1... | collective-permute-start | bytes 983048 | tf_op jit(solution)/shard_map/ppermute | solution.py:31
  34.9 11.2 %collective-permute-start.3 = (bf16[32,5120]{1,0:T(8,128)(2,1)S(1)}, bf16[32,5120]{1,0:T(8,128)(2,1)S(1)}, u32[]{:S(2)}, u32[]{:S(2)}) collective-permute-start(bf16[32,5120]{1,0:T(8,128)(2,1)S(1)} %get-tuple-element.11), channel_id=1, source_target_pairs={{0,128},{32,160},{64,192},{96,224},{128,0},{160,32},{192,64},{224,... | collective-permute-start | bytes 983048 | tf_op jit(solution)/shard_map/ppermute | solution.py:31
  35.9 21.8 %collective-permute-start.2 = (bf16[32,5120]{1,0:T(8,128)(2,1)S(1)}, bf16[32,5120]{1,0:T(8,128)(2,1)S(1)}, u32[]{:S(2)}, u32[]{:S(2)}) collective-permute-start(bf16[32,5120]{1,0:T(8,128)(2,1)S(1)} %get-tuple-element.11), channel_id=1, source_target_pairs={{0,32},{32,64},{64,96},{96,0},{128,160},{160,192},{192,224},{224,1... | collective-permute-start | bytes 983048 | tf_op jit(solution)/shard_map/ppermute | solution.py:31
  41.5 9.1 %collective-permute-start.1 = (bf16[32,5120]{1,0:T(8,128)(2,1)S(1)}, bf16[32,5120]{1,0:T(8,128)(2,1)S(1)}, u32[]{:S(2)}, u32[]{:S(2)}) collective-permute-start(bf16[32,5120]{1,0:T(8,128)(2,1)S(1)} %collective-permute-done), channel_id=1, source_target_pairs={{0,96},{32,0},{64,32},{96,64},{128,224},{160,128},{192,160},{224,1... | collective-permute-start | bytes 983048 | tf_op jit(solution)/shard_map/ppermute | solution.py:31
  44.9 10.0 %collective-permute-start.4 = (bf16[32,5120]{1,0:T(8,128)(2,1)S(1)}, bf16[32,5120]{1,0:T(8,128)(2,1)S(1)}, u32[]{:S(2)}, u32[]{:S(2)}) collective-permute-start(bf16[32,5120]{1,0:T(8,128)(2,1)S(1)} %collective-permute-done), channel_id=1, source_target_pairs={{0,128},{32,160},{64,192},{96,224},{128,0},{160,32},{192,64},{224,... | collective-permute-start | bytes 983048 | tf_op jit(solution)/shard_map/ppermute | solution.py:31
  46.1 8.7 %collective-permute-start.6 = (bf16[32,5120]{1,0:T(8,128)(2,1)S(1)}, bf16[32,5120]{1,0:T(8,128)(2,1)S(1)}, u32[]{:S(2)}, u32[]{:S(2)}) collective-permute-start(bf16[32,5120]{1,0:T(8,128)(2,1)S(1)} %collective-permute-done.3), channel_id=1, source_target_pairs={{0,32},{32,64},{64,96},{96,0},{128,160},{160,192},{192,224},{224,1... | collective-permute-start | bytes 983048 | tf_op jit(solution)/shard_map/ppermute | solution.py:31
  50.6 7.2 %collective-permute-start.8 = (bf16[32,1664]{1,0:T(8,128)(2,1)S(1)}, bf16[32,1664]{1,0:T(8,128)(2,1)S(1)}, u32[]{:S(2)}, u32[]{:S(2)}) collective-permute-start(bf16[32,1664]{1,0:T(8,128)(2,1)S(1)} %slice.166), channel_id=1, source_target_pairs={{0,128},{32,160},{64,192},{96,224},{128,0},{160,32},{192,64},{224,... | collective-permute-start | bytes 319496 | tf_op jit(solution)/shard_map/ppermute | solution.py:31
  54.8 4.8 %collective-permute-start.7 = (bf16[32,1664]{1,0:T(8,128)(2,1)S(1)}, bf16[32,1664]{1,0:T(8,128)(2,1)S(1)}, u32[]{:S(2)}, u32[]{:S(2)}) collective-permute-start(bf16[32,1664]{1,0:T(8,128)(2,1)S(1)} %slice.165), channel_id=1, source_target_pairs={{0,32},{32,64},{64,96},{96,0},{128,160},{160,192},{192,224},{224,1... | collective-permute-start | bytes 319496 | tf_op jit(solution)/shard_map/ppermute | solution.py:31
  54.9 4.7 %collective-permute-start.5 = (bf16[32,1792]{1,0:T(8,128)(2,1)S(1)}, bf16[32,1792]{1,0:T(8,128)(2,1)S(1)}, u32[]{:S(2)}, u32[]{:S(2)}) collective-permute-start(bf16[32,1792]{1,0:T(8,128)(2,1)S(1)} %slice.164), channel_id=1, source_target_pairs={{0,96},{32,0},{64,32},{96,64},{128,224},{160,128},{192,160},{224,1... | collective-permute-start | bytes 344072 | tf_op jit(solution)/shard_map/ppermute | solution.py:31
  66.5 3.8 %collective-permute-start.11 = (bf16[32,1664]{1,0:T(8,128)(2,1)S(1)}, bf16[32,1664]{1,0:T(8,128)(2,1)S(1)}, u32[]{:S(2)}, u32[]{:S(2)}) collective-permute-start(bf16[32,1664]{1,0:T(8,128)(2,1)S(1)} %get-tuple-element.20), channel_id=1, source_target_pairs={{0,128},{32,160},{64,192},{96,224},{128,0},{160,32},{192,64},{224,... | collective-permute-start | bytes 319496 | tf_op jit(solution)/shard_map/ppermute | solution.py:31
  66.9 4.6 %collective-permute-start.15 = (bf16[32,1664]{1,0:T(8,128)(2,1)S(1)}, bf16[32,1664]{1,0:T(8,128)(2,1)S(1)}, u32[]{:S(2)}, u32[]{:S(2)}) collective-permute-start(bf16[32,1664]{1,0:T(8,128)(2,1)S(1)} %get-tuple-element.21), channel_id=1, source_target_pairs={{0,96},{32,0},{64,32},{96,64},{128,224},{160,128},{192,160},{224,1... | collective-permute-start | bytes 319496 | tf_op jit(solution)/shard_map/ppermute | solution.py:31
  69.7 4.9 %collective-permute-start.9 = (bf16[32,1792]{1,0:T(8,128)(2,1)S(1)}, bf16[32,1792]{1,0:T(8,128)(2,1)S(1)}, u32[]{:S(2)}, u32[]{:S(2)}) collective-permute-start(bf16[32,1792]{1,0:T(8,128)(2,1)S(1)} %pad_maximum_fusion.8), channel_id=1, source_target_pairs={{0,32},{32,64},{64,96},{96,0},{128,160},{160,192},{192,224},{224,1... | collective-permute-start | bytes 344072 | tf_op jit(solution)/shard_map/ppermute | solution.py:31
  74.8 8.4 %collective-permute-start.12 = (bf16[32,5120]{1,0:T(8,128)(2,1)S(1)}, bf16[32,5120]{1,0:T(8,128)(2,1)S(1)}, u32[]{:S(2)}, u32[]{:S(2)}) collective-permute-start(bf16[32,5120]{1,0:T(8,128)(2,1)S(1)} %get-tuple-element.17), channel_id=1, source_target_pairs={{0,32},{32,64},{64,96},{96,0},{128,160},{160,192},{192,224},{224,1... | collective-permute-start | bytes 983048 | tf_op jit(solution)/shard_map/ppermute | solution.py:31
  74.9 8.4 %collective-permute-start.10 = (bf16[32,5120]{1,0:T(8,128)(2,1)S(1)}, bf16[32,5120]{1,0:T(8,128)(2,1)S(1)}, u32[]{:S(2)}, u32[]{:S(2)}) collective-permute-start(bf16[32,5120]{1,0:T(8,128)(2,1)S(1)} %get-tuple-element.16), channel_id=1, source_target_pairs={{0,128},{32,160},{64,192},{96,224},{128,0},{160,32},{192,64},{224,... | collective-permute-start | bytes 983048 | tf_op jit(solution)/shard_map/ppermute | solution.py:31
  76.4 6.9 %collective-permute-start.16 = (bf16[32,5120]{1,0:T(8,128)(2,1)S(1)}, bf16[32,5120]{1,0:T(8,128)(2,1)S(1)}, u32[]{:S(2)}, u32[]{:S(2)}) collective-permute-start(bf16[32,5120]{1,0:T(8,128)(2,1)S(1)} %get-tuple-element.15), channel_id=1, source_target_pairs={{0,96},{32,0},{64,32},{96,64},{128,224},{160,128},{192,160},{224,1... | collective-permute-start | bytes 983048 | tf_op jit(solution)/shard_map/ppermute | solution.py:31
  78.9 7.5 %collective-permute-start.14 = (bf16[32,5120]{1,0:T(8,128)(2,1)S(1)}, bf16[32,5120]{1,0:T(8,128)(2,1)S(1)}, u32[]{:S(2)}, u32[]{:S(2)}) collective-permute-start(bf16[32,5120]{1,0:T(8,128)(2,1)S(1)} %get-tuple-element.14), channel_id=1, source_target_pairs={{0,96},{32,0},{64,32},{96,64},{128,224},{160,128},{192,160},{224,1... | collective-permute-start | bytes 983048 | tf_op jit(solution)/shard_map/ppermute | solution.py:31
  83.5 8.9 %collective-permute-start.17 = (bf16[32,5120]{1,0:T(8,128)(2,1)S(1)}, bf16[32,5120]{1,0:T(8,128)(2,1)S(1)}, u32[]{:S(2)}, u32[]{:S(2)}) collective-permute-start(bf16[32,5120]{1,0:T(8,128)(2,1)S(1)} %get-tuple-element.13), channel_id=1, source_target_pairs={{0,128},{32,160},{64,192},{96,224},{128,0},{160,32},{192,64},{224,... | collective-permute-start | bytes 983048 | tf_op jit(solution)/shard_map/ppermute | solution.py:31
  84.9 8.3 %collective-permute-start.13 = (bf16[32,5120]{1,0:T(8,128)(2,1)S(1)}, bf16[32,5120]{1,0:T(8,128)(2,1)S(1)}, u32[]{:S(2)}, u32[]{:S(2)}) collective-permute-start(bf16[32,5120]{1,0:T(8,128)(2,1)S(1)} %get-tuple-element.12), channel_id=1, source_target_pairs={{0,32},{32,64},{64,96},{96,0},{128,160},{160,192},{192,224},{224,1... | collective-permute-start | bytes 983048 | tf_op jit(solution)/shard_map/ppermute | solution.py:31
  95.1 27.6 %all-to-all-start.1 = ((bf16[32,2,2560]{2,1,0:T(2,128)(2,1)}), bf16[32,2,2560]{2,1,0:T(2,128)(2,1)}, u32[]{:S(2)}, u32[]{:S(2)}) async-start(bf16[32,2,2560]{2,1,0:T(2,128)(2,1)} %reshape.42), calls=%async_computation.1 | async-start | bytes 655360 | tf_op jit(solution)/shard_map/all_to_all | solution.py:171
  134.4 2.3 %collective-permute-start.18 = (bf16[640,64]{0,1:T(8,128)(2,1)S(1)}, bf16[640,64]{0,1:T(8,128)(2,1)S(1)}, u32[]{:S(2)}, u32[]{:S(2)}) collective-permute-start(bf16[640,64]{0,1:T(8,128)(2,1)S(1)} %bitcast.100), channel_id=1, source_target_pairs={{0,1},{1,0},{2,3},{3,2},{4,5},{5,4},{6,7},{7,6},{8,9},{9,8},{10,11... | collective-permute-start | bytes 245768 | tf_op jit(solution)/shard_map/ppermute | solution.py:45
  136.7 4.1 %collective-permute-start.21 = (bf16[640,64]{0,1:T(8,128)(2,1)S(1)}, bf16[640,64]{0,1:T(8,128)(2,1)S(1)}, u32[]{:S(2)}, u32[]{:S(2)}) collective-permute-start(bf16[640,64]{0,1:T(8,128)(2,1)S(1)} %fusion.83), channel_id=1, source_target_pairs={{0,96},{32,0},{64,32},{96,64},{128,224},{160,128},{192,160},{224,1... | collective-permute-start | bytes 245768 | tf_op jit(solution)/shard_map/ppermute | solution.py:31
  138.5 5.3 %collective-permute-start.20 = (bf16[640,64]{0,1:T(8,128)(2,1)S(1)}, bf16[640,64]{0,1:T(8,128)(2,1)S(1)}, u32[]{:S(2)}, u32[]{:S(2)}) collective-permute-start(bf16[640,64]{0,1:T(8,128)(2,1)S(1)} %fusion.83), channel_id=1, source_target_pairs={{0,64},{32,96},{64,0},{96,32},{128,192},{160,224},{192,128},{224,1... | collective-permute-start | bytes 245768 | tf_op jit(solution)/shard_map/ppermute | solution.py:31
  138.5 7.1 %collective-permute-start.19 = (bf16[640,64]{0,1:T(8,128)(2,1)S(1)}, bf16[640,64]{0,1:T(8,128)(2,1)S(1)}, u32[]{:S(2)}, u32[]{:S(2)}) collective-permute-start(bf16[640,64]{0,1:T(8,128)(2,1)S(1)} %fusion.83), channel_id=1, source_target_pairs={{0,32},{32,64},{64,96},{96,0},{128,160},{160,192},{192,224},{224,1... | collective-permute-start | bytes 245768 | tf_op jit(solution)/shard_map/ppermute | solution.py:31
  145.7 3.4 %collective-permute-start.24 = (bf16[640,64]{0,1:T(8,128)(2,1)S(1)}, bf16[640,64]{0,1:T(8,128)(2,1)S(1)}, u32[]{:S(2)}, u32[]{:S(2)}) collective-permute-start(bf16[640,64]{0,1:T(8,128)(2,1)S(1)} %add_convert_fusion.9), channel_id=1, source_target_pairs={{0,24},{1,25},{2,26},{3,27},{4,28},{5,29},{6,30},{7,31},{8,0},{9,1... | collective-permute-start | bytes 245768 | tf_op jit(solution)/shard_map/ppermute | solution.py:45
  146.2 4.8 %collective-permute-start.23 = (bf16[640,64]{0,1:T(8,128)(2,1)S(1)}, bf16[640,64]{0,1:T(8,128)(2,1)S(1)}, u32[]{:S(2)}, u32[]{:S(2)}) collective-permute-start(bf16[640,64]{0,1:T(8,128)(2,1)S(1)} %add_convert_fusion.9), channel_id=1, source_target_pairs={{0,16},{1,17},{2,18},{3,19},{4,20},{5,21},{6,22},{7,23},{8,24},{9,... | collective-permute-start | bytes 245768 | tf_op jit(solution)/shard_map/ppermute | solution.py:45
  147.3 5.2 %collective-permute-start.22 = (bf16[640,64]{0,1:T(8,128)(2,1)S(1)}, bf16[640,64]{0,1:T(8,128)(2,1)S(1)}, u32[]{:S(2)}, u32[]{:S(2)}) collective-permute-start(bf16[640,64]{0,1:T(8,128)(2,1)S(1)} %add_convert_fusion.9), channel_id=1, source_target_pairs={{0,8},{1,9},{2,10},{3,11},{4,12},{5,13},{6,14},{7,15},{8,16},{9,17... | collective-permute-start | bytes 245768 | tf_op jit(solution)/shard_map/ppermute | solution.py:45
  152.5 20.3 %copy-start.10 = (f32[64,256]{1,0:T(8,128)S(1)}, f32[64,256]{1,0:T(8,128)}, u32[]{:S(2)}) copy-start(f32[64,256]{1,0:T(8,128)} %copy-done.9) | copy-start | bytes 196612
  152.6 3.4 %collective-permute-start.25 = (bf16[640,64]{0,1:T(8,128)(2,1)S(1)}, bf16[640,64]{0,1:T(8,128)(2,1)S(1)}, u32[]{:S(2)}, u32[]{:S(2)}) collective-permute-start(bf16[640,64]{0,1:T(8,128)(2,1)S(1)} %add_convert_fusion.8), channel_id=1, source_target_pairs={{0,128},{32,160},{64,192},{96,224},{128,0},{160,32},{192,64},{224,... | collective-permute-start | bytes 245768 | tf_op jit(solution)/shard_map/ppermute | solution.py:31
  156.0 6.0 %collective-permute-start.28 = (bf16[640,64]{0,1:T(8,128)(2,1)S(1)}, bf16[640,64]{0,1:T(8,128)(2,1)S(1)}, u32[]{:S(2)}, u32[]{:S(2)}) collective-permute-start(bf16[640,64]{0,1:T(8,128)(2,1)S(1)} %add_convert_fusion.7), channel_id=1, source_target_pairs={{0,6},{1,7},{2,0},{3,1},{4,2},{5,3},{6,4},{7,5},{8,14},{9,15},{10,... | collective-permute-start | bytes 245768 | tf_op jit(solution)/shard_map/ppermute | solution.py:45
  156.9 7.3 %collective-permute-start.27 = (bf16[640,64]{0,1:T(8,128)(2,1)S(1)}, bf16[640,64]{0,1:T(8,128)(2,1)S(1)}, u32[]{:S(2)}, u32[]{:S(2)}) collective-permute-start(bf16[640,64]{0,1:T(8,128)(2,1)S(1)} %add_convert_fusion.7), channel_id=1, source_target_pairs={{0,4},{1,5},{2,6},{3,7},{4,0},{5,1},{6,2},{7,3},{8,12},{9,13},{10,... | collective-permute-start | bytes 245768 | tf_op jit(solution)/shard_map/ppermute | solution.py:45
  161.6 5.4 %collective-permute-start.26 = (bf16[640,64]{0,1:T(8,128)(2,1)S(1)}, bf16[640,64]{0,1:T(8,128)(2,1)S(1)}, u32[]{:S(2)}, u32[]{:S(2)}) collective-permute-start(bf16[640,64]{0,1:T(8,128)(2,1)S(1)} %add_convert_fusion.7), channel_id=1, source_target_pairs={{0,2},{1,3},{2,4},{3,5},{4,6},{5,7},{6,0},{7,1},{8,10},{9,11},{10,... | collective-permute-start | bytes 245768 | tf_op jit(solution)/shard_map/ppermute | solution.py:45
  167.0 7.1 %collective-permute-start.29 = (bf16[640,64]{0,1:T(8,128)(2,1)S(1)}, bf16[640,64]{0,1:T(8,128)(2,1)S(1)}, u32[]{:S(2)}, u32[]{:S(2)}) collective-permute-start(bf16[640,64]{0,1:T(8,128)(2,1)S(1)} %add_convert_fusion.6), channel_id=1, source_target_pairs={{0,1},{1,0},{2,3},{3,2},{4,5},{5,4},{6,7},{7,6},{8,9},{9,8},{10,11... | collective-permute-start | bytes 245768 | tf_op jit(solution)/shard_map/ppermute | solution.py:45
  (18 other events, 93.0 us)

commit v2 on v1

--- a/solution.py
+++ b/solution.py
@@ -1,8 +1,11 @@
+import functools
 import math
 
 import jax
 import jax.numpy as jnp
 from jax import lax
+from jax.experimental import pallas as pl
+from jax.experimental.pallas import tpu as pltpu
 from jax.sharding import PartitionSpec as P
 
 GELU_CUBIC = 0.044715
@@ -79,6 +82,99 @@
     return total.astype(BF16)
 
 
+LANES = 128
+
+
+def local_kernel(kernel, outs, scratch, flops, moved, name):
+    return pl.pallas_call(
+        kernel,
+        out_shape=outs,
+        scratch_shapes=scratch,
+        compiler_params=pltpu.CompilerParams(vmem_limit_bytes=32 * 1024 * 1024),
+        cost_estimate=pl.CostEstimate(flops=flops, bytes_accessed=moved, transcendentals=0),
+        name=name,
+    )
+
+
+def nt(a, b):
+    return lax.dot_general(a, b, (((1,), (1,)), ((), ())), preferred_element_type=F32)
+
+
+def front_kernel(each, tok_ref, cot_ref, par_ref, rows_ref, disp_ref, comb_ref, slots_ref, flat_ref):
+    tiles = slots_ref.shape[0]
+    groups = slots_ref.shape[1] // each
+    stride = 2 * each * tiles
+    logits = nt(par_ref[...], tok_ref[...])
+    raised = jnp.exp(logits - jnp.max(logits, axis=1, keepdims=True))
+    dispatch = raised / jnp.sum(raised, axis=1, keepdims=True)
+    raised = jnp.exp(logits - jnp.max(logits, axis=0, keepdims=True))
+    combine = raised / jnp.sum(raised, axis=0, keepdims=True)
+    disp_ref[...] = dispatch
+    comb_ref[...] = combine
+    for kind, (weights, values) in enumerate(((dispatch, tok_ref), (combine, cot_ref))):
+        mixed = jnp.dot(weights.astype(BF16), values[...], preferred_element_type=F32)
+        for k in range(tiles):
+            slots_ref[k] = mixed[:, k * LANES : (k + 1) * LANES]
+            for j in range(each):
+                row = (kind * each + j) * tiles + k
+                flat_ref[pl.ds(row, groups, stride=stride), :] = slots_ref[
+                    k, pl.ds(j, groups, stride=each), :
+                ]
+    rows_ref[...] = flat_ref[...].astype(BF16)
+
+
+def unpack_kernel(flat_in_ref, out_ref, flat_ref):
+    groups = out_ref.shape[0]
+    stride = out_ref.shape[1] // LANES
+    flat_ref[...] = flat_in_ref[...].astype(F32)
+    for c in range(stride):
+        out_ref[:, c * LANES : (c + 1) * LANES] = flat_ref[
+            pl.ds(c, groups, stride=stride), :
+        ].astype(BF16)
+
+
+def pack_sum_kernel(a_ref, b_ref, c_ref, d_ref, out_ref, flat_ref):
+    groups = a_ref.shape[0]
+    stride = a_ref.shape[1] // LANES
+    for c in range(stride):
+        cols = slice(c * LANES, (c + 1) * LANES)
+        total = a_ref[:, cols].astype(F32) + b_ref[:, cols].astype(F32)
+        total = total + c_ref[:, cols].astype(F32) + d_ref[:, cols].astype(F32)
+        flat_ref[pl.ds(c, groups, stride=stride), :] = total
+    out_ref[...] = flat_ref[...].astype(BF16)
+
+
+def final_kernel(
+    each, flat_in_ref, tok_ref, cot_ref, disp_ref, comb_ref, sig_ref, grad_ref, par_ref,
+    flat_ref, out_f_ref, sig_f_ref,
+):
+    groups = sig_ref.shape[0] // each
+    tiles = sig_ref.shape[1] // LANES
+    stride = 2 * each * tiles
+    flat_ref[...] = flat_in_ref[...].astype(F32)
+    for kind, ref in enumerate((out_f_ref, sig_f_ref)):
+        for j in range(each):
+            for k in range(tiles):
+                row = (kind * each + j) * tiles + k
+                ref[k, pl.ds(j, groups, stride=each), :] = flat_ref[
+                    pl.ds(row, groups, stride=stride), :
+                ]
+    slot_out = jnp.concatenate([out_f_ref[k].astype(BF16) for k in range(tiles)], axis=1)
+    sig = jnp.concatenate([sig_f_ref[k].astype(BF16) for k in range(tiles)], axis=1)
+    sig_ref[...] = sig
+    combine_grad = nt(slot_out, cot_ref[...])
+    dispatch_grad = nt(sig, tok_ref[...])
+    combine = comb_ref[...]
+    dispatch = disp_ref[...]
+    combine_part = combine * (combine_grad - jnp.sum(combine * combine_grad, axis=0, keepdims=True))
+    dispatch_part = dispatch * (
+        dispatch_grad - jnp.sum(dispatch * dispatch_grad, axis=1, keepdims=True)
+    )
+    logits_grad = (combine_part + dispatch_part).astype(BF16)
+    grad_ref[...] = logits_grad
+    par_ref[...] = jnp.dot(logits_grad, tok_ref[...], preferred_element_type=F32).astype(BF16)
+
+
 def scatter_blocks(parts):
     a, b, c = thirds(parts[0, 0].shape[1])
     far = parts[1, 2]
@@ -97,19 +193,25 @@
     got_01 = batch_send(add(parts[0, 1], got_11, got_02), 0, 1)
     got_03 = batch_send(parts[0, 3], 0, 3)
     got_10 = batch_send(add(parts[1, 0], got_13), 1, 0)
-    return add(parts[0, 0], got_01, got_03, got_10)
+    return parts[0, 0], got_01, got_03, got_10
 
 
 def sum_all(partial):
     core = lax.axis_index("expert") % CORE
-    halves = partial.reshape(CORE, partial.shape[0] // CORE, partial.shape[1])
-    keep = lax.dynamic_index_in_dim(halves, core, 0, False)
-    give = lax.dynamic_index_in_dim(halves, 1 - core, 0, False)
+    x = lax.axis_index("batch") % X
+    half = partial.shape[0] // CORE
+    rows = half // X
+    keep = lax.dynamic_slice_in_dim(partial, core * half, half)
+    give = lax.dynamic_slice_in_dim(partial, (1 - core) * half, half)
     total = add(keep, expert_send(give, 0, 0, 1))
-    total = add(total, *[batch_send(total, 0, k) for k in (1, 2, 3)])
-    total = add(total, *[expert_send(total, k, 0, 0) for k in (1, 2, 3)])
+    chunks = [lax.dynamic_slice_in_dim(total, (x + k) % X * rows, rows) for k in range(X)]
+    total = add(chunks[0], *[batch_send(chunks[k], 0, k) for k in range(1, X)])
+    total = add(total, *[expert_send(total, k, 0, 0) for k in range(1, Y)])
     total = add(total, batch_send(total, 1, 0))
-    total = add(total, *[expert_send(total, 0, k, 0) for k in (1, 2, 3)])
+    total = add(total, *[expert_send(total, 0, k, 0) for k in range(1, ZH)])
+    around = [batch_send(total, 0, k) for k in range(X - 1, 0, -1)] + [total]
+    ring = jnp.concatenate(around + around, axis=0)
+    total = lax.dynamic_slice_in_dim(ring, (X - 1 - x) * rows, half)
     other = expert_send(total, 0, 0, 1)
     first = jnp.where(core == 0, total, other)
     second = jnp.where(core == 0, other, total)
@@ -118,25 +220,37 @@
 
 def body(tokens, slot_params, weight_in, weight_out, output_grad):
     tokens, output_grad = tokens[0], output_grad[0]
-    width = tokens.shape[1]
+    patches, width = tokens.shape
     slots = slot_params.shape[1]
     groups = lax.axis_size("expert")
     each = slots // groups
-    params = slot_params.reshape(width, groups, each).swapaxes(1, 2).reshape(width, slots)
-    logits = jnp.einsum("md,ds->sm", tokens, params, preferred_element_type=F32)
-    dispatch = jax.nn.softmax(logits, axis=1)
-    combine = jax.nn.softmax(logits, axis=0)
-    dispatch_half = dispatch.astype(BF16)
-    combine_half = combine.astype(BF16)
-    slot_in = jnp.dot(dispatch_half, tokens, preferred_element_type=F32).astype(BF16)
-    slot_cot = jnp.dot(combine_half, output_grad, preferred_element_type=F32).astype(BF16)
-    rows = jnp.concatenate(
-        [slot_in[j * groups : (j + 1) * groups] for j in range(each)]
-        + [slot_cot[j * groups : (j + 1) * groups] for j in range(each)],
-        axis=1,
-    )
-    routed = lax.all_to_all(rows, "expert", split_axis=0, concat_axis=0, tiled=True)
-    blocks = gather_blocks(routed)
+    tiles = width // LANES
+    flat = groups * 2 * each * tiles
+    params = slot_params.T
+    flat_shape = jax.ShapeDtypeStruct((flat, LANES), BF16)
+    square = jax.ShapeDtypeStruct((slots, patches), F32)
+    dot_flops = 2 * slots * patches * width
+    rows, dispatch, combine = local_kernel(
+        functools.partial(front_kernel, each),
+        (flat_shape, square, square),
+        [pltpu.VMEM((tiles, slots, LANES), F32), pltpu.VMEM((flat, LANES), F32)],
+        3 * dot_flops,
+        4 * patches * width + 2 * flat * LANES,
+        "front",
+    )(tokens, output_grad, params)
+    routed = lax.all_to_all(
+        rows.reshape(groups, 2 * each * tiles, LANES), "expert", split_axis=0, concat_axis=0,
+        tiled=True,
+    ).reshape(flat, LANES)
+    mine = local_kernel(
+        unpack_kernel,
+        jax.ShapeDtypeStruct((groups, 2 * each * width), BF16),
+        [pltpu.VMEM((flat, LANES), F32)],
+        0,
+        4 * flat * LANES,
+        "unpack",
+    )(routed)
+    blocks = gather_blocks(mine)
     gathered = jnp.concatenate([blocks[o] for o in OFFSETS], axis=0)
     out_cols, in_cols, in_grads, out_grads = [], [], [], []
     for j in range(each):
@@ -168,26 +282,37 @@
     partial = jnp.concatenate(out_cols + in_cols, axis=1)
     parts = {o: partial[i * groups : (i + 1) * groups] for i, o in enumerate(OFFSETS)}
     share = scatter_blocks(parts)
-    back = lax.all_to_all(share, "expert", split_axis=0, concat_axis=0, tiled=True)
-    slot_out = jnp.concatenate([back[:, j * width : (j + 1) * width] for j in range(each)], axis=0)
-    slot_in_grad = jnp.concatenate(
-        [back[:, (each + j) * width : (each + j + 1) * width] for j in range(each)], axis=0
-    )
-    combine_grad = jnp.einsum("md,sd->sm", output_grad, slot_out, preferred_element_type=F32)
-    dispatch_grad = jnp.einsum("md,sd->sm", tokens, slot_in_grad, preferred_element_type=F32)
-    combine_part = combine * (combine_grad - jnp.sum(combine * combine_grad, axis=0, keepdims=True))
-    dispatch_part = dispatch * (
-        dispatch_grad - jnp.sum(dispatch * dispatch_grad, axis=1, keepdims=True)
-    )
-    logits_grad = (combine_part + dispatch_part).astype(BF16)
+    packed = local_kernel(
+        pack_sum_kernel,
+        flat_shape,
+        [pltpu.VMEM((flat, LANES), F32)],
+        0,
+        10 * flat * LANES,
+        "pack_sum",
+    )(*share)
+    back = lax.all_to_all(
+        packed.reshape(groups, 2 * each * tiles, LANES), "expert", split_axis=0, concat_axis=0,
+        tiled=True,
+    ).reshape(flat, LANES)
+    row_shape = jax.ShapeDtypeStruct((slots, width), BF16)
+    slot_in_grad, logits_grad, local_params = local_kernel(
+        functools.partial(final_kernel, each),
+        (row_shape, jax.ShapeDtypeStruct((slots, patches), BF16), row_shape),
+        [
+            pltpu.VMEM((flat, LANES), F32),
+            pltpu.VMEM((tiles, slots, LANES), F32),
+            pltpu.VMEM((tiles, slots, LANES), F32),
+        ],
+        3 * dot_flops,
+        4 * patches * width + 2 * flat * LANES,
+        "final",
+    )(back, tokens, output_grad, dispatch, combine)
     tokens_grad = (
-        jnp.einsum("sm,sd->md", dispatch_half, slot_in_grad, preferred_element_type=F32)
-        + jnp.einsum("sm,ds->md", logits_grad, params, preferred_element_type=F32)
+        jnp.einsum("sm,sd->md", dispatch.astype(BF16), slot_in_grad, preferred_element_type=F32)
+        + jnp.einsum("sm,sd->md", logits_grad, params, preferred_element_type=F32)
     ).astype(BF16)
-    local_params = jnp.einsum("md,sm->ds", tokens, logits_grad, preferred_element_type=F32)
     total_images = lax.axis_size("batch") * groups
-    params_grad = sum_all(local_params.astype(BF16)) / total_images
-    params_grad = params_grad.reshape(width, each, groups).swapaxes(1, 2).reshape(width, slots)
+    params_grad = (sum_all(local_params) / total_images).T
     return (tokens_grad[None], params_grad, jnp.stack(in_grads), jnp.stack(out_grads))
 
 

time: 176 us -> 162 us (0.920)
  local copies, waits for them, and re-layouts: 15.2 us -> 5.21 us
  matrix products: 14.9 us -> 10.9 us
  Pallas kernels: 0 us -> 3.08 us
  waiting for transfers between devices: 59.2 us -> 56.4 us
    unnamed x50 -> x43, local copies, waits for them, and re-layouts: 9.29 us -> 5.11 us
    dot_general x8 -> x2, matrix products: 5.53 us -> 1.55 us  [the longest x1 1.2 us: body(): jnp.einsum('sm,sd->md', logits_grad, params, preferred_element_type=F32)]
    ppermute x8, waiting for transfers between devices: 9.39 us -> 5.61 us  [expert_send(): return lax.ppermute(value, 'expert', pairs)]
    reshape x3 -> x0, local copies, waits for them, and re-layouts: 3.65 us -> none  [the longest x1 1.62 us: sum_all(): halves = partial.reshape(CORE, partial.shape[0] // CORE, partial.shape[1])]
    pallas_call x0 -> x4, Pallas kernels: none -> 3.08 us  [the longest x1 1.15 us: body(): local_kernel(functools.partial(front_kernel, each), (flat_shape, square,...]
    ppermute x22 -> x25, starting transfers between devices: 24.1 us -> 26.2 us  [batch_send(): return lax.ppermute(value, 'batch', pairs)]
    all_to_all x4 -> x0, other arithmetic: 1.86 us -> none  [the longest x2 1.01 us: body(): lax.all_to_all(share, 'expert', split_axis=0, concat_axis=0, tiled=True)]
    ppermute x22 -> x25, waiting for transfers between devices: 39.1 us -> 38.4 us  [batch_send(): return lax.ppermute(value, 'batch', pairs)]
  transfers between devices with their start and end apart: 31 -> 34, of which waited for: 21 -> 18; matrix products, arithmetic and copies ran while one was open for 6% -> 6% of each run, Pallas kernels for 0% -> 0%
where the time goes in v2:
time: 162 us; the launch traced here: 161 us
  waiting for transfers between devices  56.4 us (35%)
  starting transfers between devices  52.2 us (32%)
  blocking collectives  27.3 us (17%)
  matrix products  10.9 us (7%)
  local copies, waits for them, and re-layouts  5.21 us (3%)
  other arithmetic  4.77 us (3%)
  Pallas kernels  3.08 us (2%)
    ppermute x25, waiting for transfers between devices, batch_send(): return lax.ppermute(value, 'batch', pairs)  38.4 us
    all_to_all x1, blocking collectives, body(): lax.all_to_all(rows.reshape(groups, 2 * each * tiles, LANES), 'expert', s...  27.3 us
    ppermute x25, starting transfers between devices, batch_send(): return lax.ppermute(value, 'batch', pairs)  26.2 us
    ppermute x8, starting transfers between devices, expert_send(): return lax.ppermute(value, 'expert', pairs)  13.7 us
    all_to_all x1, waiting for transfers between devices, body(): lax.all_to_all(packed.reshape(groups, 2 * each * tiles, LANES), 'expert',...  12.5 us
    all_to_all x1, starting transfers between devices, body(): lax.all_to_all(packed.reshape(groups, 2 * each * tiles, LANES), 'expert',...  12.4 us
    ppermute x8, waiting for transfers between devices, expert_send(): return lax.ppermute(value, 'expert', pairs)  5.61 us
    unnamed x43, local copies, waits for them, and re-layouts  5.11 us
  transfers between devices with their start and end apart: 34, of which 18 were waited for; matrix products, arithmetic and copies ran while one was open for 6% of the time, Pallas kernels for 0%

profile of v2, /device:TPU:1, one launch (start us, length us, event | category | flops | bytes accessed | tf_op | source)
XLA Modules:
  0.0 161.2 jit_solution(7856342336385119379)
XLA Ops:
  4.9 27.3 %all_to_all.10 = bf16[32,40,128]{2,1,0:T(8,128)(2,1)S(1)} all-to-all(bf16[32,40,128]{2,1,0:T(8,128)(2,1)S(1)} %bitcast.61), channel_id=1, replica_groups=mesh['batch'=8,'expert'=32] {'expert'}, dimensions={0} | all-to-all | bytes 655360 | tf_op jit(solution)/shard_map/all_to_all | solution.py:241
  32.4 2.6 %collective-permute-start = (bf16[32,5120]{1,0:T(8,128)(2,1)S(1)}, bf16[32,5120]{1,0:T(8,128)(2,1)S(1)}, u32[]{:S(2)}, u32[]{:S(2)}) collective-permute-start(bf16[32,5120]{1,0:T(8,128)(2,1)S(1)} %unpack.1), channel_id=1, source_target_pairs={{0,96},{32,0},{64,32},{96,64},{128,224},{160,128},{192,160},{224,1... | collective-permute-start | bytes 983048 | tf_op jit(solution)/shard_map/ppermute | solution.py:34
  36.0 5.6 %collective-permute-done = bf16[32,5120]{1,0:T(8,128)(2,1)S(1)} collective-permute-done((bf16[32,5120]{1,0:T(8,128)(2,1)S(1)}, bf16[32,5120]{1,0:T(8,128)(2,1)S(1)}, u32[]{:S(2)}, u32[]{:S(2)}) %collective-permute-start) | collective-permute-done | bytes 327712 | tf_op jit(solution)/shard_map/ppermute | solution.py:34
  41.5 3.4 %collective-permute-start.1 = (bf16[32,5120]{1,0:T(8,128)(2,1)S(1)}, bf16[32,5120]{1,0:T(8,128)(2,1)S(1)}, u32[]{:S(2)}, u32[]{:S(2)}) collective-permute-start(bf16[32,5120]{1,0:T(8,128)(2,1)S(1)} %collective-permute-done), channel_id=1, source_target_pairs={{0,96},{32,0},{64,32},{96,64},{128,224},{160,128},{192,160},{224,1... | collective-permute-start | bytes 983048 | tf_op jit(solution)/shard_map/ppermute | solution.py:34
  46.2 4.4 %collective-permute-done.1 = bf16[32,5120]{1,0:T(8,128)(2,1)S(1)} collective-permute-done((bf16[32,5120]{1,0:T(8,128)(2,1)S(1)}, bf16[32,5120]{1,0:T(8,128)(2,1)S(1)}, u32[]{:S(2)}, u32[]{:S(2)}) %collective-permute-start.1) | collective-permute-done | bytes 327712 | tf_op jit(solution)/shard_map/ppermute | solution.py:34
  50.6 1.5 collective-permute-start.8
  52.2 2.8 %collective-permute-done.6 = bf16[32,5120]{1,0:T(8,128)(2,1)S(1)} collective-permute-done((bf16[32,5120]{1,0:T(8,128)(2,1)S(1)}, bf16[32,5120]{1,0:T(8,128)(2,1)S(1)}, u32[]{:S(2)}, u32[]{:S(2)}) %collective-permute-start.6) | collective-permute-done | bytes 327712 | tf_op jit(solution)/shard_map/ppermute | solution.py:34
  55.1 2.7 %collective-permute-start.5 = (bf16[32,1792]{1,0:T(8,128)(2,1)S(1)}, bf16[32,1792]{1,0:T(8,128)(2,1)S(1)}, u32[]{:S(2)}, u32[]{:S(2)}) collective-permute-start(bf16[32,1792]{1,0:T(8,128)(2,1)S(1)} %slice.128), channel_id=1, source_target_pairs={{0,96},{32,0},{64,32},{96,64},{128,224},{160,128},{192,160},{224,1... | collective-permute-start | bytes 344072 | tf_op jit(solution)/shard_map/ppermute | solution.py:34
  57.9 1.9 %collective-permute-done.7 = bf16[32,1664]{1,0:T(8,128)(2,1)S(1)} collective-permute-done((bf16[32,1664]{1,0:T(8,128)(2,1)S(1)}, bf16[32,1664]{1,0:T(8,128)(2,1)S(1)}, u32[]{:S(2)}, u32[]{:S(2)}) %collective-permute-start.7) | collective-permute-done | bytes 106528 | tf_op jit(solution)/shard_map/ppermute | solution.py:34
  61.0 1.8 %copy-done.9 = bf16[2,512,1280]{2,1,0:T(8,128)(2,1)S(1)} copy-done((bf16[2,512,1280]{2,1,0:T(8,128)(2,1)S(1)}, bf16[2,512,1280]{2,1,0:T(8,128)(2,1)}, u32[]{:S(2)}) %copy-start.9) | copy-done | bytes 2621464
  66.6 3.1 %collective-permute-start.15 = (bf16[32,1664]{1,0:T(8,128)(2,1)S(1)}, bf16[32,1664]{1,0:T(8,128)(2,1)S(1)}, u32[]{:S(2)}, u32[]{:S(2)}) collective-permute-start(bf16[32,1664]{1,0:T(8,128)(2,1)S(1)} %get-tuple-element.24), channel_id=1, source_target_pairs={{0,96},{32,0},{64,32},{96,64},{128,224},{160,128},{192,160},{224,1... | collective-permute-start | bytes 319496 | tf_op jit(solution)/shard_map/ppermute | solution.py:34
  69.8 1.6 collective-permute-done.15
  71.5 1.8 %collective-permute-done.11 = bf16[32,1664]{1,0:T(8,128)(2,1)S(1)} collective-permute-done((bf16[32,1664]{1,0:T(8,128)(2,1)S(1)}, bf16[32,1664]{1,0:T(8,128)(2,1)S(1)}, u32[]{:S(2)}, u32[]{:S(2)}) %collective-permute-start.11) | collective-permute-done | bytes 106528 | tf_op jit(solution)/shard_map/ppermute | solution.py:34
  76.3 1.4 collective-permute-start.14
  77.7 2.1 %collective-permute-done.16 = bf16[32,5120]{1,0:T(8,128)(2,1)S(1)} collective-permute-done((bf16[32,5120]{1,0:T(8,128)(2,1)S(1)}, bf16[32,5120]{1,0:T(8,128)(2,1)S(1)}, u32[]{:S(2)}, u32[]{:S(2)}) %collective-permute-start.16) | collective-permute-done | bytes 327712 | tf_op jit(solution)/shard_map/ppermute | solution.py:34
  79.8 3.4 %collective-permute-done.12 = bf16[32,5120]{1,0:T(8,128)(2,1)S(1)} collective-permute-done((bf16[32,5120]{1,0:T(8,128)(2,1)S(1)}, bf16[32,5120]{1,0:T(8,128)(2,1)S(1)}, u32[]{:S(2)}, u32[]{:S(2)}) %collective-permute-start.12) | collective-permute-done | bytes 327712 | tf_op jit(solution)/shard_map/ppermute | solution.py:34
  84.2 7.8 %collective-permute-done.13.b_ref = bf16[32,5120]{1,0:T(8,128)(2,1)S(1)} collective-permute-done((bf16[32,5120]{1,0:T(8,128)(2,1)S(1)}, bf16[32,5120]{1,0:T(8,128)(2,1)S(1)}, u32[]{:S(2)}, u32[]{:S(2)}) %collective-permute-start.13) | collective-permute-done | bytes 327712 | tf_op jit(solution)/shard_map/ppermute | solution.py:34
  92.8 12.4 %all-to-all-start.1 = ((bf16[32,40,128]{2,1,0:T(8,128)(2,1)}), bf16[32,40,128]{2,1,0:T(8,128)(2,1)S(1)}, u32[]{:S(2)}, u32[]{:S(2)}) async-start(bf16[32,40,128]{2,1,0:T(8,128)(2,1)} %bitcast.9), calls=%async_computation.1 | async-start | bytes 655360 | tf_op jit(solution)/shard_map/all_to_all | solution.py:293
  105.3 1.7 %fusion.1 = bf16[1,1280,512]{2,1,0:T(8,128)(2,1)S(1)} fusion(bf16[256,512]{1,0:T(8,128)(2,1)} %copy-done.8, bf16[256,5120]{1,0:T(8,128)(2,1)} %copy-done.6), kind=kOutput, calls=%fused_computation.6 | convolution fusion | flops 336199680 | bytes 2228224 | tf_op jit(solution)/shard_map/dot_general | solution.py:278
  107.0 12.5 %all-to-all-done.1 = bf16[32,40,128]{2,1,0:T(8,128)(2,1)S(1)} async-done(((bf16[32,40,128]{2,1,0:T(8,128)(2,1)}), bf16[32,40,128]{2,1,0:T(8,128)(2,1)S(1)}, u32[]{:S(2)}, u32[]{:S(2)}) %all-to-all-start.1) | async-done | bytes 327712 | tf_op jit(solution)/shard_map/all_to_all | solution.py:293
  120.8 1.6 %fusion = bf16[1,1280,512]{2,1,0:T(8,128)(2,1)S(1)} fusion(bf16[256,512]{1,0:T(8,128)(2,1)S(1)} %fusion.27, bf16[256,5120]{1,0:T(8,128)(2,1)} %copy-done.6), kind=kOutput, calls=%fused_computation.5 | convolution fusion | flops 336199680 | bytes 2228224 | tf_op jit(solution)/shard_map/dot_general | solution.py:278
  122.5 1.9 %collective-permute-start.21 = (bf16[8,1280]{1,0:T(8,128)(2,1)S(1)}, bf16[8,1280]{1,0:T(8,128)(2,1)S(1)}, u32[]{:S(2)}, u32[]{:S(2)}) collective-permute-start(bf16[8,1280]{1,0:T(8,128)(2,1)S(1)} %get-tuple-element.29), channel_id=1, source_target_pairs={{0,96},{32,0},{64,32},{96,64},{128,224},{160,128},{192,160},{224,1... | collective-permute-start | bytes 61448 | tf_op jit(solution)/shard_map/ppermute | solution.py:34
  125.1 1.7 %pad_maximum_fusion = bf16[2,1280,512]{2,1,0:T(8,128)(2,1)} fusion(bf16[1,1280,512]{2,1,0:T(8,128)(2,1)S(1)} %fusion.1, bf16[1,1280,512]{2,1,0:T(8,128)(2,1)S(1)} %fusion), kind=kLoop, calls=%fused_computation.9 | loop fusion | flops 1310720 | bytes 5242880 | tf_op jit(solution)/shard_map/stack | solution.py:316
  126.8 1.7 %collective-permute-done.20 = bf16[8,1280]{1,0:T(8,128)(2,1)S(1)} collective-permute-done((bf16[8,1280]{1,0:T(8,128)(2,1)S(1)}, bf16[8,1280]{1,0:T(8,128)(2,1)S(1)}, u32[]{:S(2)}, u32[]{:S(2)}) %collective-permute-start.20) | collective-permute-done | bytes 20512 | tf_op jit(solution)/shard_map/ppermute | solution.py:34
  129.6 1.5 collective-permute-start.23
  132.1 1.6 %collective-permute-done.23 = bf16[8,1280]{1,0:T(8,128)(2,1)S(1)} collective-permute-done((bf16[8,1280]{1,0:T(8,128)(2,1)S(1)}, bf16[8,1280]{1,0:T(8,128)(2,1)S(1)}, u32[]{:S(2)}, u32[]{:S(2)}) %collective-permute-start.23) | collective-permute-done | bytes 20512 | tf_op jit(solution)/shard_map/ppermute | solution.py:48
  136.6 1.3 collective-permute-done.25
  139.0 1.7 %collective-permute-start.27 = (bf16[8,1280]{1,0:T(8,128)(2,1)S(1)}, bf16[8,1280]{1,0:T(8,128)(2,1)S(1)}, u32[]{:S(2)}, u32[]{:S(2)}) collective-permute-start(bf16[8,1280]{1,0:T(8,128)(2,1)S(1)} %add_convert_fusion.7), channel_id=1, source_target_pairs={{0,4},{1,5},{2,6},{3,7},{4,0},{5,1},{6,2},{7,3},{8,12},{9,13},{10,... | collective-permute-start | bytes 61448 | tf_op jit(solution)/shard_map/ppermute | solution.py:48
  141.2 1.7 %pad_maximum_fusion.1 = bf16[2,512,1280]{2,1,0:T(8,128)(2,1)} fusion(bf16[1,512,1280]{2,1,0:T(8,128)(2,1)S(1)} %fusion.3, bf16[1,512,1280]{2,1,0:T(8,128)(2,1)S(1)} %fusion.2), kind=kLoop, calls=%fused_computation.10 | loop fusion | flops 1310720 | bytes 5242880 | tf_op jit(solution)/shard_map/stack | solution.py:316
  142.9 2.8 %collective-permute-done.27 = bf16[8,1280]{1,0:T(8,128)(2,1)S(1)} collective-permute-done((bf16[8,1280]{1,0:T(8,128)(2,1)S(1)}, bf16[8,1280]{1,0:T(8,128)(2,1)S(1)}, u32[]{:S(2)}, u32[]{:S(2)}) %collective-permute-start.27) | collective-permute-done | bytes 20512 | tf_op jit(solution)/shard_map/ppermute | solution.py:48
  148.5 2.7 %collective-permute-done.30 = bf16[8,1280]{1,0:T(8,128)(2,1)S(1)} collective-permute-done((bf16[8,1280]{1,0:T(8,128)(2,1)S(1)}, bf16[8,1280]{1,0:T(8,128)(2,1)S(1)}, u32[]{:S(2)}, u32[]{:S(2)}) %collective-permute-start.30) | collective-permute-done | bytes 20512 | tf_op jit(solution)/shard_map/ppermute | solution.py:34
  152.1 7.2 %collective-permute-start.32 = (bf16[32,1280]{1,0:T(8,128)(2,1)S(1)}, bf16[32,1280]{1,0:T(8,128)(2,1)S(1)}, u32[]{:S(2)}, u32[]{:S(2)}) collective-permute-start(bf16[32,1280]{1,0:T(8,128)(2,1)S(1)} %constant_dynamic-slice_fusion), channel_id=1, source_target_pairs={{0,1},{1,0},{2,3},{3,2},{4,5},{5,4},{6,7},{7,6},{8,9},{9,8},{10,11... | collective-permute-start | bytes 245768 | tf_op jit(solution)/shard_map/ppermute | solution.py:48
  (123 shorter events, 31.0 us)
Async XLA Ops:
  32.4 9.2 %collective-permute-start = (bf16[32,5120]{1,0:T(8,128)(2,1)S(1)}, bf16[32,5120]{1,0:T(8,128)(2,1)S(1)}, u32[]{:S(2)}, u32[]{:S(2)}) collective-permute-start(bf16[32,5120]{1,0:T(8,128)(2,1)S(1)} %unpack.1), channel_id=1, source_target_pairs={{0,96},{32,0},{64,32},{96,64},{128,224},{160,128},{192,160},{224,1... | collective-permute-start | bytes 983048 | tf_op jit(solution)/shard_map/ppermute | solution.py:34
  34.9 22.9 %collective-permute-start.2 = (bf16[32,5120]{1,0:T(8,128)(2,1)S(1)}, bf16[32,5120]{1,0:T(8,128)(2,1)S(1)}, u32[]{:S(2)}, u32[]{:S(2)}) collective-permute-start(bf16[32,5120]{1,0:T(8,128)(2,1)S(1)} %unpack.1), channel_id=1, source_target_pairs={{0,32},{32,64},{64,96},{96,0},{128,160},{160,192},{192,224},{224,1... | collective-permute-start | bytes 983048 | tf_op jit(solution)/shard_map/ppermute | solution.py:34
  34.9 11.2 %collective-permute-start.3 = (bf16[32,5120]{1,0:T(8,128)(2,1)S(1)}, bf16[32,5120]{1,0:T(8,128)(2,1)S(1)}, u32[]{:S(2)}, u32[]{:S(2)}) collective-permute-start(bf16[32,5120]{1,0:T(8,128)(2,1)S(1)} %unpack.1), channel_id=1, source_target_pairs={{0,128},{32,160},{64,192},{96,224},{128,0},{160,32},{192,64},{224,... | collective-permute-start | bytes 983048 | tf_op jit(solution)/shard_map/ppermute | solution.py:34
  41.5 9.1 %collective-permute-start.1 = (bf16[32,5120]{1,0:T(8,128)(2,1)S(1)}, bf16[32,5120]{1,0:T(8,128)(2,1)S(1)}, u32[]{:S(2)}, u32[]{:S(2)}) collective-permute-start(bf16[32,5120]{1,0:T(8,128)(2,1)S(1)} %collective-permute-done), channel_id=1, source_target_pairs={{0,96},{32,0},{64,32},{96,64},{128,224},{160,128},{192,160},{224,1... | collective-permute-start | bytes 983048 | tf_op jit(solution)/shard_map/ppermute | solution.py:34
  44.9 10.1 %collective-permute-start.4 = (bf16[32,5120]{1,0:T(8,128)(2,1)S(1)}, bf16[32,5120]{1,0:T(8,128)(2,1)S(1)}, u32[]{:S(2)}, u32[]{:S(2)}) collective-permute-start(bf16[32,5120]{1,0:T(8,128)(2,1)S(1)} %collective-permute-done), channel_id=1, source_target_pairs={{0,128},{32,160},{64,192},{96,224},{128,0},{160,32},{192,64},{224,... | collective-permute-start | bytes 983048 | tf_op jit(solution)/shard_map/ppermute | solution.py:34
  46.2 8.8 %collective-permute-start.6 = (bf16[32,5120]{1,0:T(8,128)(2,1)S(1)}, bf16[32,5120]{1,0:T(8,128)(2,1)S(1)}, u32[]{:S(2)}, u32[]{:S(2)}) collective-permute-start(bf16[32,5120]{1,0:T(8,128)(2,1)S(1)} %collective-permute-done.3), channel_id=1, source_target_pairs={{0,32},{32,64},{64,96},{96,0},{128,160},{160,192},{192,224},{224,1... | collective-permute-start | bytes 983048 | tf_op jit(solution)/shard_map/ppermute | solution.py:34
  50.6 7.3 %collective-permute-start.8 = (bf16[32,1664]{1,0:T(8,128)(2,1)S(1)}, bf16[32,1664]{1,0:T(8,128)(2,1)S(1)}, u32[]{:S(2)}, u32[]{:S(2)}) collective-permute-start(bf16[32,1664]{1,0:T(8,128)(2,1)S(1)} %slice.130), channel_id=1, source_target_pairs={{0,128},{32,160},{64,192},{96,224},{128,0},{160,32},{192,64},{224,... | collective-permute-start | bytes 319496 | tf_op jit(solution)/shard_map/ppermute | solution.py:34
  54.9 4.8 %collective-permute-start.7 = (bf16[32,1664]{1,0:T(8,128)(2,1)S(1)}, bf16[32,1664]{1,0:T(8,128)(2,1)S(1)}, u32[]{:S(2)}, u32[]{:S(2)}) collective-permute-start(bf16[32,1664]{1,0:T(8,128)(2,1)S(1)} %slice.129), channel_id=1, source_target_pairs={{0,32},{32,64},{64,96},{96,0},{128,160},{160,192},{192,224},{224,1... | collective-permute-start | bytes 319496 | tf_op jit(solution)/shard_map/ppermute | solution.py:34
  55.1 4.7 %collective-permute-start.5 = (bf16[32,1792]{1,0:T(8,128)(2,1)S(1)}, bf16[32,1792]{1,0:T(8,128)(2,1)S(1)}, u32[]{:S(2)}, u32[]{:S(2)}) collective-permute-start(bf16[32,1792]{1,0:T(8,128)(2,1)S(1)} %slice.128), channel_id=1, source_target_pairs={{0,96},{32,0},{64,32},{96,64},{128,224},{160,128},{192,160},{224,1... | collective-permute-start | bytes 344072 | tf_op jit(solution)/shard_map/ppermute | solution.py:34
  66.6 4.8 %collective-permute-start.15 = (bf16[32,1664]{1,0:T(8,128)(2,1)S(1)}, bf16[32,1664]{1,0:T(8,128)(2,1)S(1)}, u32[]{:S(2)}, u32[]{:S(2)}) collective-permute-start(bf16[32,1664]{1,0:T(8,128)(2,1)S(1)} %get-tuple-element.24), channel_id=1, source_target_pairs={{0,96},{32,0},{64,32},{96,64},{128,224},{160,128},{192,160},{224,1... | collective-permute-start | bytes 319496 | tf_op jit(solution)/shard_map/ppermute | solution.py:34
  69.7 3.6 %collective-permute-start.11 = (bf16[32,1664]{1,0:T(8,128)(2,1)S(1)}, bf16[32,1664]{1,0:T(8,128)(2,1)S(1)}, u32[]{:S(2)}, u32[]{:S(2)}) collective-permute-start(bf16[32,1664]{1,0:T(8,128)(2,1)S(1)} %get-tuple-element.25), channel_id=1, source_target_pairs={{0,128},{32,160},{64,192},{96,224},{128,0},{160,32},{192,64},{224,... | collective-permute-start | bytes 319496 | tf_op jit(solution)/shard_map/ppermute | solution.py:34
  69.7 5.3 %collective-permute-start.9 = (bf16[32,1792]{1,0:T(8,128)(2,1)S(1)}, bf16[32,1792]{1,0:T(8,128)(2,1)S(1)}, u32[]{:S(2)}, u32[]{:S(2)}) collective-permute-start(bf16[32,1792]{1,0:T(8,128)(2,1)S(1)} %pad_maximum_fusion.8), channel_id=1, source_target_pairs={{0,32},{32,64},{64,96},{96,0},{128,160},{160,192},{192,224},{224,1... | collective-permute-start | bytes 344072 | tf_op jit(solution)/shard_map/ppermute | solution.py:34
  73.5 6.3 %collective-permute-start.16 = (bf16[32,5120]{1,0:T(8,128)(2,1)S(1)}, bf16[32,5120]{1,0:T(8,128)(2,1)S(1)}, u32[]{:S(2)}, u32[]{:S(2)}) collective-permute-start(bf16[32,5120]{1,0:T(8,128)(2,1)S(1)} %get-tuple-element.18), channel_id=1, source_target_pairs={{0,96},{32,0},{64,32},{96,64},{128,224},{160,128},{192,160},{224,1... | collective-permute-start | bytes 983048 | tf_op jit(solution)/shard_map/ppermute | solution.py:34
  74.8 8.4 %collective-permute-start.12 = (bf16[32,5120]{1,0:T(8,128)(2,1)S(1)}, bf16[32,5120]{1,0:T(8,128)(2,1)S(1)}, u32[]{:S(2)}, u32[]{:S(2)}) collective-permute-start(bf16[32,5120]{1,0:T(8,128)(2,1)S(1)} %get-tuple-element.21), channel_id=1, source_target_pairs={{0,32},{32,64},{64,96},{96,0},{128,160},{160,192},{192,224},{224,1... | collective-permute-start | bytes 983048 | tf_op jit(solution)/shard_map/ppermute | solution.py:34
  75.1 8.0 %collective-permute-start.10 = (bf16[32,5120]{1,0:T(8,128)(2,1)S(1)}, bf16[32,5120]{1,0:T(8,128)(2,1)S(1)}, u32[]{:S(2)}, u32[]{:S(2)}) collective-permute-start(bf16[32,5120]{1,0:T(8,128)(2,1)S(1)} %fusion.68), channel_id=1, source_target_pairs={{0,128},{32,160},{64,192},{96,224},{128,0},{160,32},{192,64},{224,... | collective-permute-start | bytes 983048 | tf_op jit(solution)/shard_map/ppermute | solution.py:34
  76.3 7.9 %collective-permute-start.14 = (bf16[32,5120]{1,0:T(8,128)(2,1)S(1)}, bf16[32,5120]{1,0:T(8,128)(2,1)S(1)}, u32[]{:S(2)}, u32[]{:S(2)}) collective-permute-start(bf16[32,5120]{1,0:T(8,128)(2,1)S(1)} %get-tuple-element.20), channel_id=1, source_target_pairs={{0,96},{32,0},{64,32},{96,64},{128,224},{160,128},{192,160},{224,1... | collective-permute-start | bytes 983048 | tf_op jit(solution)/shard_map/ppermute | solution.py:34
  83.4 8.6 %collective-permute-start.13 = (bf16[32,5120]{1,0:T(8,128)(2,1)S(1)}, bf16[32,5120]{1,0:T(8,128)(2,1)S(1)}, u32[]{:S(2)}, u32[]{:S(2)}) collective-permute-start(bf16[32,5120]{1,0:T(8,128)(2,1)S(1)} %get-tuple-element.17), channel_id=1, source_target_pairs={{0,32},{32,64},{64,96},{96,0},{128,160},{160,192},{192,224},{224,1... | collective-permute-start | bytes 983048 | tf_op jit(solution)/shard_map/ppermute | solution.py:34
  83.5 8.5 %collective-permute-start.17 = (bf16[32,5120]{1,0:T(8,128)(2,1)S(1)}, bf16[32,5120]{1,0:T(8,128)(2,1)S(1)}, u32[]{:S(2)}, u32[]{:S(2)}) collective-permute-start(bf16[32,5120]{1,0:T(8,128)(2,1)S(1)} %get-tuple-element.16), channel_id=1, source_target_pairs={{0,128},{32,160},{64,192},{96,224},{128,0},{160,32},{192,64},{224,... | collective-permute-start | bytes 983048 | tf_op jit(solution)/shard_map/ppermute | solution.py:34
  92.8 26.6 %all-to-all-start.1 = ((bf16[32,40,128]{2,1,0:T(8,128)(2,1)}), bf16[32,40,128]{2,1,0:T(8,128)(2,1)S(1)}, u32[]{:S(2)}, u32[]{:S(2)}) async-start(bf16[32,40,128]{2,1,0:T(8,128)(2,1)} %bitcast.9), calls=%async_computation.1 | async-start | bytes 655360 | tf_op jit(solution)/shard_map/all_to_all | solution.py:293
  122.5 4.3 %collective-permute-start.21 = (bf16[8,1280]{1,0:T(8,128)(2,1)S(1)}, bf16[8,1280]{1,0:T(8,128)(2,1)S(1)}, u32[]{:S(2)}, u32[]{:S(2)}) collective-permute-start(bf16[8,1280]{1,0:T(8,128)(2,1)S(1)} %get-tuple-element.29), channel_id=1, source_target_pairs={{0,96},{32,0},{64,32},{96,64},{128,224},{160,128},{192,160},{224,1... | collective-permute-start | bytes 61448 | tf_op jit(solution)/shard_map/ppermute | solution.py:34
  124.4 4.1 %collective-permute-start.20 = (bf16[8,1280]{1,0:T(8,128)(2,1)S(1)}, bf16[8,1280]{1,0:T(8,128)(2,1)S(1)}, u32[]{:S(2)}, u32[]{:S(2)}) collective-permute-start(bf16[8,1280]{1,0:T(8,128)(2,1)S(1)} %get-tuple-element.30), channel_id=1, source_target_pairs={{0,64},{32,96},{64,0},{96,32},{128,192},{160,224},{192,128},{224,1... | collective-permute-start | bytes 61448 | tf_op jit(solution)/shard_map/ppermute | solution.py:34
  124.4 4.1 %collective-permute-start.19 = (bf16[8,1280]{1,0:T(8,128)(2,1)S(1)}, bf16[8,1280]{1,0:T(8,128)(2,1)S(1)}, u32[]{:S(2)}, u32[]{:S(2)}) collective-permute-start(bf16[8,1280]{1,0:T(8,128)(2,1)S(1)} %get-tuple-element.28), channel_id=1, source_target_pairs={{0,32},{32,64},{64,96},{96,0},{128,160},{160,192},{192,224},{224,1... | collective-permute-start | bytes 61448 | tf_op jit(solution)/shard_map/ppermute | solution.py:34
  128.5 3.5 %collective-permute-start.24 = (bf16[8,1280]{1,0:T(8,128)(2,1)S(1)}, bf16[8,1280]{1,0:T(8,128)(2,1)S(1)}, u32[]{:S(2)}, u32[]{:S(2)}) collective-permute-start(bf16[8,1280]{1,0:T(8,128)(2,1)S(1)} %add_convert_fusion.9), channel_id=1, source_target_pairs={{0,24},{1,25},{2,26},{3,27},{4,28},{5,29},{6,30},{7,31},{8,0},{9,1... | collective-permute-start | bytes 61448 | tf_op jit(solution)/shard_map/ppermute | solution.py:48
  129.6 4.1 %collective-permute-start.23 = (bf16[8,1280]{1,0:T(8,128)(2,1)S(1)}, bf16[8,1280]{1,0:T(8,128)(2,1)S(1)}, u32[]{:S(2)}, u32[]{:S(2)}) collective-permute-start(bf16[8,1280]{1,0:T(8,128)(2,1)S(1)} %add_convert_fusion.9), channel_id=1, source_target_pairs={{0,16},{1,17},{2,18},{3,19},{4,20},{5,21},{6,22},{7,23},{8,24},{9,... | collective-permute-start | bytes 61448 | tf_op jit(solution)/shard_map/ppermute | solution.py:48
  131.1 3.8 %collective-permute-start.22 = (bf16[8,1280]{1,0:T(8,128)(2,1)S(1)}, bf16[8,1280]{1,0:T(8,128)(2,1)S(1)}, u32[]{:S(2)}, u32[]{:S(2)}) collective-permute-start(bf16[8,1280]{1,0:T(8,128)(2,1)S(1)} %add_convert_fusion.9), channel_id=1, source_target_pairs={{0,8},{1,9},{2,10},{3,11},{4,12},{5,13},{6,14},{7,15},{8,16},{9,17... | collective-permute-start | bytes 61448 | tf_op jit(solution)/shard_map/ppermute | solution.py:48
  134.9 3.0 %collective-permute-start.25 = (bf16[8,1280]{1,0:T(8,128)(2,1)S(1)}, bf16[8,1280]{1,0:T(8,128)(2,1)S(1)}, u32[]{:S(2)}, u32[]{:S(2)}) collective-permute-start(bf16[8,1280]{1,0:T(8,128)(2,1)S(1)} %add_convert_fusion.8), channel_id=1, source_target_pairs={{0,128},{32,160},{64,192},{96,224},{128,0},{160,32},{192,64},{224,... | collective-permute-start | bytes 61448 | tf_op jit(solution)/shard_map/ppermute | solution.py:34
  138.0 4.9 %collective-permute-start.28 = (bf16[8,1280]{1,0:T(8,128)(2,1)S(1)}, bf16[8,1280]{1,0:T(8,128)(2,1)S(1)}, u32[]{:S(2)}, u32[]{:S(2)}) collective-permute-start(bf16[8,1280]{1,0:T(8,128)(2,1)S(1)} %add_convert_fusion.7), channel_id=1, source_target_pairs={{0,6},{1,7},{2,0},{3,1},{4,2},{5,3},{6,4},{7,5},{8,14},{9,15},{10,... | collective-permute-start | bytes 61448 | tf_op jit(solution)/shard_map/ppermute | solution.py:48
  139.0 6.7 %collective-permute-start.27 = (bf16[8,1280]{1,0:T(8,128)(2,1)S(1)}, bf16[8,1280]{1,0:T(8,128)(2,1)S(1)}, u32[]{:S(2)}, u32[]{:S(2)}) collective-permute-start(bf16[8,1280]{1,0:T(8,128)(2,1)S(1)} %add_convert_fusion.7), channel_id=1, source_target_pairs={{0,4},{1,5},{2,6},{3,7},{4,0},{5,1},{6,2},{7,3},{8,12},{9,13},{10,... | collective-permute-start | bytes 61448 | tf_op jit(solution)/shard_map/ppermute | solution.py:48
  140.7 5.0 %collective-permute-start.26 = (bf16[8,1280]{1,0:T(8,128)(2,1)S(1)}, bf16[8,1280]{1,0:T(8,128)(2,1)S(1)}, u32[]{:S(2)}, u32[]{:S(2)}) collective-permute-start(bf16[8,1280]{1,0:T(8,128)(2,1)S(1)} %add_convert_fusion.7), channel_id=1, source_target_pairs={{0,2},{1,3},{2,4},{3,5},{4,6},{5,7},{6,0},{7,1},{8,10},{9,11},{10,... | collective-permute-start | bytes 61448 | tf_op jit(solution)/shard_map/ppermute | solution.py:48
  147.0 4.2 %collective-permute-start.30 = (bf16[8,1280]{1,0:T(8,128)(2,1)S(1)}, bf16[8,1280]{1,0:T(8,128)(2,1)S(1)}, u32[]{:S(2)}, u32[]{:S(2)}) collective-permute-start(bf16[8,1280]{1,0:T(8,128)(2,1)S(1)} %add_convert_fusion.6), channel_id=1, source_target_pairs={{0,64},{32,96},{64,0},{96,32},{128,192},{160,224},{192,128},{224,1... | collective-permute-start | bytes 61448 | tf_op jit(solution)/shard_map/ppermute | solution.py:34
  148.2 3.8 %collective-permute-start.31 = (bf16[8,1280]{1,0:T(8,128)(2,1)S(1)}, bf16[8,1280]{1,0:T(8,128)(2,1)S(1)}, u32[]{:S(2)}, u32[]{:S(2)}) collective-permute-start(bf16[8,1280]{1,0:T(8,128)(2,1)S(1)} %add_convert_fusion.6), channel_id=1, source_target_pairs={{0,32},{32,64},{64,96},{96,0},{128,160},{160,192},{192,224},{224,1... | collective-permute-start | bytes 61448 | tf_op jit(solution)/shard_map/ppermute | solution.py:34
  152.1 8.4 %collective-permute-start.32 = (bf16[32,1280]{1,0:T(8,128)(2,1)S(1)}, bf16[32,1280]{1,0:T(8,128)(2,1)S(1)}, u32[]{:S(2)}, u32[]{:S(2)}) collective-permute-start(bf16[32,1280]{1,0:T(8,128)(2,1)S(1)} %constant_dynamic-slice_fusion), channel_id=1, source_target_pairs={{0,1},{1,0},{2,3},{3,2},{4,5},{5,4},{6,7},{7,6},{8,9},{9,8},{10,11... | collective-permute-start | bytes 245768 | tf_op jit(solution)/shard_map/ppermute | solution.py:48
  (17 other events, 163.1 us)

commit v3 on v2

--- a/solution.py
+++ b/solution.py
@@ -85,10 +85,11 @@
 LANES = 128
 
 
-def local_kernel(kernel, outs, scratch, flops, moved, name):
+def local_kernel(kernel, outs, scratch, flops, moved, name, **specs):
     return pl.pallas_call(
         kernel,
         out_shape=outs,
+        **specs,
         scratch_shapes=scratch,
         compiler_params=pltpu.CompilerParams(vmem_limit_bytes=32 * 1024 * 1024),
         cost_estimate=pl.CostEstimate(flops=flops, bytes_accessed=moved, transcendentals=0),
@@ -100,7 +101,30 @@
     return lax.dot_general(a, b, (((1,), (1,)), ((), ())), preferred_element_type=F32)
 
 
-def front_kernel(each, tok_ref, cot_ref, par_ref, rows_ref, disp_ref, comb_ref, slots_ref, flat_ref):
+PIECES = 4
+
+
+def tn(a, b):
+    return lax.dot_general(a, b, (((0,), (0,)), ((), ())), preferred_element_type=F32)
+
+
+def front_kernel(
+    each, tok_hbm, cot_hbm, par_hbm, rows_ref, disp_ref, comb_ref,
+    slots_ref, flat_ref, tok_ref, cot_ref, par_ref, sems,
+):
+    def loads(source, target, which):
+        rows = source.shape[0] // PIECES
+        for i in range(PIECES):
+            part = pl.ds(i * rows, rows)
+            copy = pltpu.make_async_copy(source.at[part], target.at[part], sems.at[which, i])
+            copy.start()
+            yield copy
+
+    par_loads = list(loads(par_hbm, par_ref, 0))
+    tok_loads = list(loads(tok_hbm, tok_ref, 1))
+    cot_loads = list(loads(cot_hbm, cot_ref, 2))
+    for copy in par_loads + tok_loads:
+        copy.wait()
     tiles = slots_ref.shape[0]
     groups = slots_ref.shape[1] // each
     stride = 2 * each * tiles
@@ -112,6 +136,9 @@
     disp_ref[...] = dispatch
     comb_ref[...] = combine
     for kind, (weights, values) in enumerate(((dispatch, tok_ref), (combine, cot_ref))):
+        if kind == 1:
+            for copy in cot_loads:
+                copy.wait()
         mixed = jnp.dot(weights.astype(BF16), values[...], preferred_element_type=F32)
         for k in range(tiles):
             slots_ref[k] = mixed[:, k * LANES : (k + 1) * LANES]
@@ -196,26 +223,37 @@
     return parts[0, 0], got_01, got_03, got_10
 
 
-def sum_all(partial):
+def crossed_send(value, step, turn):
+    pairs = []
+    for z in range(ZL):
+        for x in range(X):
+            for y in range(Y):
+                for h in range(ZH):
+                    for c in range(CORE):
+                        along_x = (c + turn) % 2 == 0
+                        tx = (x + step) % X if along_x else x
+                        ty = y if along_x else (y + step) % Y
+                        here = ((z * X + x) * Y + y) * ZH + h
+                        there = ((z * X + tx) * Y + ty) * ZH + h
+                        pairs.append((here * CORE + c, there * CORE + c))
+    return lax.ppermute(value, ("batch", "expert"), pairs)
+
+
+def sum_all(partial, beside):
     core = lax.axis_index("expert") % CORE
-    x = lax.axis_index("batch") % X
     half = partial.shape[0] // CORE
-    rows = half // X
     keep = lax.dynamic_slice_in_dim(partial, core * half, half)
     give = lax.dynamic_slice_in_dim(partial, (1 - core) * half, half)
     total = add(keep, expert_send(give, 0, 0, 1))
-    chunks = [lax.dynamic_slice_in_dim(total, (x + k) % X * rows, rows) for k in range(X)]
-    total = add(chunks[0], *[batch_send(chunks[k], 0, k) for k in range(1, X)])
-    total = add(total, *[expert_send(total, k, 0, 0) for k in range(1, Y)])
+    total = add(total, *[crossed_send(total, k, 0) for k in range(1, X)])
+    total = add(total, *[crossed_send(total, k, 1) for k in range(1, X)])
     total = add(total, batch_send(total, 1, 0))
+    total, beside = lax.optimization_barrier((total, beside))
     total = add(total, *[expert_send(total, 0, k, 0) for k in range(1, ZH)])
-    around = [batch_send(total, 0, k) for k in range(X - 1, 0, -1)] + [total]
-    ring = jnp.concatenate(around + around, axis=0)
-    total = lax.dynamic_slice_in_dim(ring, (X - 1 - x) * rows, half)
     other = expert_send(total, 0, 0, 1)
     first = jnp.where(core == 0, total, other)
     second = jnp.where(core == 0, other, total)
-    return jnp.concatenate([first, second], axis=0).astype(F32)
+    return jnp.concatenate([first, second], axis=0).astype(F32), beside
 
 
 def body(tokens, slot_params, weight_in, weight_out, output_grad):
@@ -233,10 +271,18 @@
     rows, dispatch, combine = local_kernel(
         functools.partial(front_kernel, each),
         (flat_shape, square, square),
-        [pltpu.VMEM((tiles, slots, LANES), F32), pltpu.VMEM((flat, LANES), F32)],
+        [
+            pltpu.VMEM((tiles, slots, LANES), F32),
+            pltpu.VMEM((flat, LANES), F32),
+            pltpu.VMEM((patches, width), BF16),
+            pltpu.VMEM((patches, width), BF16),
+            pltpu.VMEM((slots, width), BF16),
+            pltpu.SemaphoreType.DMA((3, PIECES)),
+        ],
         3 * dot_flops,
         4 * patches * width + 2 * flat * LANES,
         "front",
+        in_specs=[pl.BlockSpec(memory_space=pltpu.HBM)] * 3,
     )(tokens, output_grad, params)
     routed = lax.all_to_all(
         rows.reshape(groups, 2 * each * tiles, LANES), "expert", split_axis=0, concat_axis=0,
@@ -252,7 +298,7 @@
     )(routed)
     blocks = gather_blocks(mine)
     gathered = jnp.concatenate([blocks[o] for o in OFFSETS], axis=0)
-    out_cols, in_cols, in_grads, out_grads = [], [], [], []
+    out_cols, in_cols, acts, pres = [], [], [], []
     for j in range(each):
         rows_in = gathered[:, j * width : (j + 1) * width]
         rows_cot = gathered[:, (each + j) * width : (each + j + 1) * width]
@@ -269,16 +315,8 @@
                 pre_grad, weight_in[j], (((1,), (1,)), ((), ())), preferred_element_type=F32
             ).astype(BF16)
         )
-        out_grads.append(
-            lax.dot_general(
-                activation, rows_cot, (((0,), (0,)), ((), ())), preferred_element_type=F32
-            ).astype(BF16)
-        )
-        in_grads.append(
-            lax.dot_general(
-                rows_in, pre_grad, (((0,), (0,)), ((), ())), preferred_element_type=F32
-            ).astype(BF16)
-        )
+        acts.append(activation)
+        pres.append(pre_grad)
     partial = jnp.concatenate(out_cols + in_cols, axis=1)
     parts = {o: partial[i * groups : (i + 1) * groups] for i, o in enumerate(OFFSETS)}
     share = scatter_blocks(parts)
@@ -290,10 +328,19 @@
         10 * flat * LANES,
         "pack_sum",
     )(*share)
+    packed, gathered, acts, pres = lax.optimization_barrier((packed, gathered, acts, pres))
     back = lax.all_to_all(
         packed.reshape(groups, 2 * each * tiles, LANES), "expert", split_axis=0, concat_axis=0,
         tiled=True,
     ).reshape(flat, LANES)
+    in_grads, out_grads = [], []
+    for j in range(each):
+        rows_in = gathered[:, j * width : (j + 1) * width]
+        rows_cot = gathered[:, (each + j) * width : (each + j + 1) * width]
+        in_grads.append(tn(rows_in, pres[j]).astype(BF16))
+        out_grads.append(tn(acts[j], rows_cot).astype(BF16))
+    weight_grads = (jnp.stack(in_grads), jnp.stack(out_grads))
+    back, weight_grads = lax.optimization_barrier((back, weight_grads))
     row_shape = jax.ShapeDtypeStruct((slots, width), BF16)
     slot_in_grad, logits_grad, local_params = local_kernel(
         functools.partial(final_kernel, each),
@@ -312,8 +359,9 @@
         + jnp.einsum("sm,sd->md", logits_grad, params, preferred_element_type=F32)
     ).astype(BF16)
     total_images = lax.axis_size("batch") * groups
-    params_grad = (sum_all(local_params) / total_images).T
-    return (tokens_grad[None], params_grad, jnp.stack(in_grads), jnp.stack(out_grads))
+    params_sum, tokens_grad = sum_all(local_params, tokens_grad)
+    params_grad = (params_sum / total_images).T
+    return (tokens_grad[None], params_grad, *weight_grads)
 
 
 def solution(mesh):

time: 162 us -> 162 us (level)
  Pallas kernels: 3.08 us -> 5.2 us
  starting transfers between devices: 52.2 us -> 50.3 us
    ppermute x0 -> x6, starting transfers between devices: none -> 7.25 us  [crossed_send(): return lax.ppermute(value, ('batch', 'expert'), pairs)]
    ppermute x25 -> x19, starting transfers between devices: 26.2 us -> 19.3 us  [batch_send(): return lax.ppermute(value, 'batch', pairs)]
    ppermute x25 -> x19, waiting for transfers between devices: 38.4 us -> 31.6 us  [batch_send(): return lax.ppermute(value, 'batch', pairs)]
    ppermute x0 -> x6, waiting for transfers between devices: none -> 5.51 us  [crossed_send(): return lax.ppermute(value, ('batch', 'expert'), pairs)]
    ppermute x8 -> x5, starting transfers between devices: 13.7 us -> 8.89 us  [expert_send(): return lax.ppermute(value, 'expert', pairs)]
    all_to_all x1, waiting for transfers between devices: 12.5 us -> 9.89 us  [body(): lax.all_to_all(packed.reshape(groups, 2 * each * tiles, LANES), 'expert',...]
    all_to_all x1, starting transfers between devices: 12.4 us -> 14.9 us  [body(): lax.all_to_all(packed.reshape(groups, 2 * each * tiles, LANES), 'expert',...]
    ppermute x8 -> x5, waiting for transfers between devices: 5.61 us -> 7.9 us  [expert_send(): return lax.ppermute(value, 'expert', pairs)]
  transfers between devices with their start and end apart: 34 -> 31, of which waited for: 18 -> 25; matrix products, arithmetic and copies ran while one was open for 6% -> 3% of each run, Pallas kernels for 0% -> 0%
where the time goes in v3:
time: 162 us; the launch traced here: 161 us
  waiting for transfers between devices  54.9 us (34%)
  starting transfers between devices  50.3 us (31%)
  blocking collectives  27.3 us (17%)
  matrix products  11.7 us (7%)
  local copies, waits for them, and re-layouts  5.59 us (3%)
  Pallas kernels  5.2 us (3%)
  other arithmetic  4.85 us (3%)
    ppermute x19, waiting for transfers between devices, batch_send(): return lax.ppermute(value, 'batch', pairs)  31.6 us
    all_to_all x1, blocking collectives, body(): lax.all_to_all(rows.reshape(groups, 2 * each * tiles, LANES), 'expert', s...  27.3 us
    ppermute x19, starting transfers between devices, batch_send(): return lax.ppermute(value, 'batch', pairs)  19.3 us
    all_to_all x1, starting transfers between devices, body(): lax.all_to_all(packed.reshape(groups, 2 * each * tiles, LANES), 'expert',...  14.9 us
    all_to_all x1, waiting for transfers between devices, body(): lax.all_to_all(packed.reshape(groups, 2 * each * tiles, LANES), 'expert',...  9.89 us
    ppermute x5, starting transfers between devices, expert_send(): return lax.ppermute(value, 'expert', pairs)  8.89 us
    ppermute x5, waiting for transfers between devices, expert_send(): return lax.ppermute(value, 'expert', pairs)  7.9 us
    ppermute x6, starting transfers between devices, crossed_send(): return lax.ppermute(value, ('batch', 'expert'), pairs)  7.25 us
  transfers between devices with their start and end apart: 31, of which 25 were waited for; matrix products, arithmetic and copies ran while one was open for 3% of the time, Pallas kernels for 0%

profile of v3, /device:TPU:1, one launch (start us, length us, event | category | flops | bytes accessed | tf_op | source)
XLA Modules:
  0.0 160.9 jit_solution(10806049810656285209)
XLA Ops:
  3.7 3.3 %front.1 = (bf16[1280,128]{1,0:T(8,128)(2,1)S(1)}, f32[64,256]{1,0:T(8,128)S(1)}, f32[64,256]{1,0:T(8,128)S(1)}) custom-call(bf16[256,1280]{1,0:T(8,128)(2,1)S(1)} %bitcast.61, bf16[256,1280]{1,0:T(8,128)(2,1)S(1)} %bitcast.63, bf16[64,1280]{1,0:T(8,128)(2,1)S(1)} %bitcast.67), custom_call_target="tpu_custom_call" | custom-call | flops 125829120 | bytes 1638400 | tf_op jit(solution)/shard_map/front/pallas_call | solution.py:271
  7.0 27.3 %all_to_all.10 = bf16[32,40,128]{2,1,0:T(8,128)(2,1)S(1)} all-to-all(bf16[32,40,128]{2,1,0:T(8,128)(2,1)S(1)} %bitcast.68), channel_id=1, replica_groups=mesh['batch'=8,'expert'=32] {'expert'}, dimensions={0} | all-to-all | bytes 655360 | tf_op jit(solution)/shard_map/all_to_all | solution.py:287
  34.5 2.6 %collective-permute-start = (bf16[32,5120]{1,0:T(8,128)(2,1)S(1)}, bf16[32,5120]{1,0:T(8,128)(2,1)S(1)}, u32[]{:S(2)}, u32[]{:S(2)}) collective-permute-start(bf16[32,5120]{1,0:T(8,128)(2,1)S(1)} %unpack.1), channel_id=1, source_target_pairs={{0,96},{32,0},{64,32},{96,64},{128,224},{160,128},{192,160},{224,1... | collective-permute-start | bytes 983048 | tf_op jit(solution)/shard_map/ppermute | solution.py:34
  38.0 5.6 %collective-permute-done = bf16[32,5120]{1,0:T(8,128)(2,1)S(1)} collective-permute-done((bf16[32,5120]{1,0:T(8,128)(2,1)S(1)}, bf16[32,5120]{1,0:T(8,128)(2,1)S(1)}, u32[]{:S(2)}, u32[]{:S(2)}) %collective-permute-start) | collective-permute-done | bytes 327712 | tf_op jit(solution)/shard_map/ppermute | solution.py:34
  43.7 3.4 %collective-permute-start.1 = (bf16[32,5120]{1,0:T(8,128)(2,1)S(1)}, bf16[32,5120]{1,0:T(8,128)(2,1)S(1)}, u32[]{:S(2)}, u32[]{:S(2)}) collective-permute-start(bf16[32,5120]{1,0:T(8,128)(2,1)S(1)} %collective-permute-done), channel_id=1, source_target_pairs={{0,96},{32,0},{64,32},{96,64},{128,224},{160,128},{192,160},{224,1... | collective-permute-start | bytes 983048 | tf_op jit(solution)/shard_map/ppermute | solution.py:34
  48.3 6.4 %collective-permute-done.4 = bf16[32,5120]{1,0:T(8,128)(2,1)S(1)} collective-permute-done((bf16[32,5120]{1,0:T(8,128)(2,1)S(1)}, bf16[32,5120]{1,0:T(8,128)(2,1)S(1)}, u32[]{:S(2)}, u32[]{:S(2)}) %collective-permute-start.4) | collective-permute-done | bytes 327712 | tf_op jit(solution)/shard_map/ppermute | solution.py:34
  55.1 1.5 collective-permute-start.8
  59.0 2.8 %collective-permute-done.7 = bf16[32,1664]{1,0:T(8,128)(2,1)S(1)} collective-permute-done((bf16[32,1664]{1,0:T(8,128)(2,1)S(1)}, bf16[32,1664]{1,0:T(8,128)(2,1)S(1)}, u32[]{:S(2)}, u32[]{:S(2)}) %collective-permute-start.7) | collective-permute-done | bytes 106528 | tf_op jit(solution)/shard_map/ppermute | solution.py:34
  63.3 1.4 copy-done.10
  68.6 1.5 collective-permute-start.9
  70.1 1.7 %collective-permute-done.11 = bf16[32,1664]{1,0:T(8,128)(2,1)S(1)} collective-permute-done((bf16[32,1664]{1,0:T(8,128)(2,1)S(1)}, bf16[32,1664]{1,0:T(8,128)(2,1)S(1)}, u32[]{:S(2)}, u32[]{:S(2)}) %collective-permute-start.11) | collective-permute-done | bytes 106528 | tf_op jit(solution)/shard_map/ppermute | solution.py:34
  72.4 2.7 %collective-permute-start.16 = (bf16[32,5120]{1,0:T(8,128)(2,1)S(1)}, bf16[32,5120]{1,0:T(8,128)(2,1)S(1)}, u32[]{:S(2)}, u32[]{:S(2)}) collective-permute-start(bf16[32,5120]{1,0:T(8,128)(2,1)S(1)} %get-tuple-element.40), channel_id=1, source_target_pairs={{0,96},{32,0},{64,32},{96,64},{128,224},{160,128},{192,160},{224,1... | collective-permute-start | bytes 983048 | tf_op jit(solution)/shard_map/ppermute | solution.py:34
  75.1 1.3 collective-permute-start.10
  76.4 4.3 %collective-permute-done.12 = bf16[32,5120]{1,0:T(8,128)(2,1)S(1)} collective-permute-done((bf16[32,5120]{1,0:T(8,128)(2,1)S(1)}, bf16[32,5120]{1,0:T(8,128)(2,1)S(1)}, u32[]{:S(2)}, u32[]{:S(2)}) %collective-permute-start.12) | collective-permute-done | bytes 327712 | tf_op jit(solution)/shard_map/ppermute | solution.py:34
  82.7 2.0 %collective-permute-done.14.c_ref = bf16[32,5120]{1,0:T(8,128)(2,1)S(1)} collective-permute-done((bf16[32,5120]{1,0:T(8,128)(2,1)S(1)}, bf16[32,5120]{1,0:T(8,128)(2,1)S(1)}, u32[]{:S(2)}, u32[]{:S(2)}) %collective-permute-start.14) | collective-permute-done | bytes 327712 | tf_op jit(solution)/shard_map/ppermute | solution.py:34
  84.7 5.1 %collective-permute-done.13.b_ref = bf16[32,5120]{1,0:T(8,128)(2,1)S(1)} collective-permute-done((bf16[32,5120]{1,0:T(8,128)(2,1)S(1)}, bf16[32,5120]{1,0:T(8,128)(2,1)S(1)}, u32[]{:S(2)}, u32[]{:S(2)}) %collective-permute-start.13) | collective-permute-done | bytes 327712 | tf_op jit(solution)/shard_map/ppermute | solution.py:34
  91.2 1.6 %fusion.2 = bf16[1,512,1280]{2,1,0:T(8,128)(2,1)S(1)} fusion(bf16[256,512]{1,0:T(8,128)(2,1)S(1)} %get-tuple-element.26, bf16[256,5120]{1,0:T(8,128)(2,1)} %copy-done.8), kind=kOutput, calls=%fused_computation.7 | convolution fusion | flops 336199680 | bytes 2228224 | tf_op jit(solution)/shard_map/dot_general | solution.py:108
  93.4 1.6 %fusion = bf16[1,1280,512]{2,1,0:T(8,128)(2,1)} fusion(bf16[256,512]{1,0:T(8,128)(2,1)S(1)} %fusion.26, bf16[256,5120]{1,0:T(8,128)(2,1)S(1)} %copy-done.9), kind=kOutput, calls=%fused_computation.5 | convolution fusion | flops 336199680 | bytes 2228224 | tf_op jit(solution)/shard_map/dot_general | solution.py:108
  95.0 1.6 fusion.1
  96.6 14.9 %all-to-all-start.1 = ((bf16[32,40,128]{2,1,0:T(8,128)(2,1)}), bf16[32,40,128]{2,1,0:T(8,128)(2,1)S(1)}, u32[]{:S(2)}, u32[]{:S(2)}) async-start(bf16[32,40,128]{2,1,0:T(8,128)(2,1)} %bitcast.9), calls=%async_computation.1 | async-start | bytes 655360 | tf_op jit(solution)/shard_map/all_to_all | solution.py:332
  111.5 1.7 %pad_maximum_fusion.1 = bf16[2,512,1280]{2,1,0:T(8,128)(2,1)} fusion(bf16[1,512,1280]{2,1,0:T(8,128)(2,1)S(1)} %fusion.3, bf16[1,512,1280]{2,1,0:T(8,128)(2,1)S(1)} %fusion.2), kind=kLoop, calls=%fused_computation.10 | loop fusion | flops 1310720 | bytes 5242880 | tf_op jit(solution)/shard_map/stack | solution.py:342
  114.1 1.7 %pad_maximum_fusion = bf16[2,1280,512]{2,1,0:T(8,128)(2,1)} fusion(bf16[1,1280,512]{2,1,0:T(8,128)(2,1)S(1)} %copy-done.7, bf16[1,1280,512]{2,1,0:T(8,128)(2,1)S(1)} %copy-done.6), kind=kLoop, calls=%fused_computation.9 | loop fusion | flops 1310720 | bytes 5242880 | tf_op jit(solution)/shard_map/stack | solution.py:342
  115.9 9.9 %all-to-all-done.1 = bf16[32,40,128]{2,1,0:T(8,128)(2,1)S(1)} async-done(((bf16[32,40,128]{2,1,0:T(8,128)(2,1)}), bf16[32,40,128]{2,1,0:T(8,128)(2,1)S(1)}, u32[]{:S(2)}, u32[]{:S(2)}) %all-to-all-start.1) | async-done | bytes 327712 | tf_op jit(solution)/shard_map/all_to_all | solution.py:332
  129.2 1.5 collective-permute-start.20
  130.6 1.9 %collective-permute-start.21 = (bf16[32,1280]{1,0:T(8,128)(2,1)S(1)}, bf16[32,1280]{1,0:T(8,128)(2,1)S(1)}, u32[]{:S(2)}, u32[]{:S(2)}) collective-permute-start(bf16[32,1280]{1,0:T(8,128)(2,1)S(1)} %add_convert_fusion.9), channel_id=1, source_target_pairs={{0,96},{1,25},{2,98},{3,27},{4,100},{5,29},{6,102},{7,31},{8,104},... | collective-permute-start | bytes 245768 | tf_op jit(solution)/shard_map/ppermute | solution.py:239
  135.1 2.9 %collective-permute-start.23 = (bf16[32,1280]{1,0:T(8,128)(2,1)S(1)}, bf16[32,1280]{1,0:T(8,128)(2,1)S(1)}, u32[]{:S(2)}, u32[]{:S(2)}) collective-permute-start(bf16[32,1280]{1,0:T(8,128)(2,1)S(1)} %add_convert_fusion.8), channel_id=1, source_target_pairs={{0,16},{1,65},{2,18},{3,67},{4,20},{5,69},{6,22},{7,71},{8,24},{9,... | collective-permute-start | bytes 245768 | tf_op jit(solution)/shard_map/ppermute | solution.py:239
  141.7 1.3 collective-permute-start.25
  145.2 3.3 %collective-permute-start.27 = (bf16[32,1280]{1,0:T(8,128)(2,1)S(1)}, bf16[32,1280]{1,0:T(8,128)(2,1)S(1)}, u32[]{:S(2)}, u32[]{:S(2)}) collective-permute-start(bf16[32,1280]{1,0:T(8,128)(2,1)S(1)} %add_convert_fusion.6), channel_id=1, source_target_pairs={{0,4},{1,5},{2,6},{3,7},{4,0},{5,1},{6,2},{7,3},{8,12},{9,13},{10,... | collective-permute-start | bytes 245768 | tf_op jit(solution)/shard_map/ppermute | solution.py:48
  149.4 1.6 collective-permute-done.26
  151.0 1.7 %collective-permute-done.27 = bf16[32,1280]{1,0:T(8,128)(2,1)S(1)} collective-permute-done((bf16[32,1280]{1,0:T(8,128)(2,1)S(1)}, bf16[32,1280]{1,0:T(8,128)(2,1)S(1)}, u32[]{:S(2)}, u32[]{:S(2)}) %collective-permute-start.27) | collective-permute-done | bytes 81952 | tf_op jit(solution)/shard_map/ppermute | solution.py:48
  152.7 2.7 %collective-permute-done.28 = bf16[32,1280]{1,0:T(8,128)(2,1)S(1)} collective-permute-done((bf16[32,1280]{1,0:T(8,128)(2,1)S(1)}, bf16[32,1280]{1,0:T(8,128)(2,1)S(1)}, u32[]{:S(2)}, u32[]{:S(2)}) %collective-permute-start.28) | collective-permute-done | bytes 81952 | tf_op jit(solution)/shard_map/ppermute | solution.py:48
  155.5 3.7 %collective-permute-start.29 = (bf16[32,1280]{1,0:T(8,128)(2,1)S(1)}, bf16[32,1280]{1,0:T(8,128)(2,1)S(1)}, u32[]{:S(2)}, u32[]{:S(2)}) collective-permute-start(bf16[32,1280]{1,0:T(8,128)(2,1)S(1)} %add_convert_fusion.5), channel_id=1, source_target_pairs={{0,1},{1,0},{2,3},{3,2},{4,5},{5,4},{6,7},{7,6},{8,9},{9,8},{10,11... | collective-permute-start | bytes 245768 | tf_op jit(solution)/shard_map/ppermute | solution.py:48
  (101 shorter events, 33.3 us)
Async XLA Ops:
  34.5 9.2 %collective-permute-start = (bf16[32,5120]{1,0:T(8,128)(2,1)S(1)}, bf16[32,5120]{1,0:T(8,128)(2,1)S(1)}, u32[]{:S(2)}, u32[]{:S(2)}) collective-permute-start(bf16[32,5120]{1,0:T(8,128)(2,1)S(1)} %unpack.1), channel_id=1, source_target_pairs={{0,96},{32,0},{64,32},{96,64},{128,224},{160,128},{192,160},{224,1... | collective-permute-start | bytes 983048 | tf_op jit(solution)/shard_map/ppermute | solution.py:34
  37.1 20.8 %collective-permute-start.2 = (bf16[32,5120]{1,0:T(8,128)(2,1)S(1)}, bf16[32,5120]{1,0:T(8,128)(2,1)S(1)}, u32[]{:S(2)}, u32[]{:S(2)}) collective-permute-start(bf16[32,5120]{1,0:T(8,128)(2,1)S(1)} %unpack.1), channel_id=1, source_target_pairs={{0,32},{32,64},{64,96},{96,0},{128,160},{160,192},{192,224},{224,1... | collective-permute-start | bytes 983048 | tf_op jit(solution)/shard_map/ppermute | solution.py:34
  37.1 11.2 %collective-permute-start.3 = (bf16[32,5120]{1,0:T(8,128)(2,1)S(1)}, bf16[32,5120]{1,0:T(8,128)(2,1)S(1)}, u32[]{:S(2)}, u32[]{:S(2)}) collective-permute-start(bf16[32,5120]{1,0:T(8,128)(2,1)S(1)} %unpack.1), channel_id=1, source_target_pairs={{0,128},{32,160},{64,192},{96,224},{128,0},{160,32},{192,64},{224,... | collective-permute-start | bytes 983048 | tf_op jit(solution)/shard_map/ppermute | solution.py:34
  43.7 11.4 %collective-permute-start.1 = (bf16[32,5120]{1,0:T(8,128)(2,1)S(1)}, bf16[32,5120]{1,0:T(8,128)(2,1)S(1)}, u32[]{:S(2)}, u32[]{:S(2)}) collective-permute-start(bf16[32,5120]{1,0:T(8,128)(2,1)S(1)} %collective-permute-done), channel_id=1, source_target_pairs={{0,96},{32,0},{64,32},{96,64},{128,224},{160,128},{192,160},{224,1... | collective-permute-start | bytes 983048 | tf_op jit(solution)/shard_map/ppermute | solution.py:34
  47.1 7.6 %collective-permute-start.4 = (bf16[32,5120]{1,0:T(8,128)(2,1)S(1)}, bf16[32,5120]{1,0:T(8,128)(2,1)S(1)}, u32[]{:S(2)}, u32[]{:S(2)}) collective-permute-start(bf16[32,5120]{1,0:T(8,128)(2,1)S(1)} %collective-permute-done), channel_id=1, source_target_pairs={{0,128},{32,160},{64,192},{96,224},{128,0},{160,32},{192,64},{224,... | collective-permute-start | bytes 983048 | tf_op jit(solution)/shard_map/ppermute | solution.py:34
  48.3 8.8 %collective-permute-start.6 = (bf16[32,5120]{1,0:T(8,128)(2,1)S(1)}, bf16[32,5120]{1,0:T(8,128)(2,1)S(1)}, u32[]{:S(2)}, u32[]{:S(2)}) collective-permute-start(bf16[32,5120]{1,0:T(8,128)(2,1)S(1)} %collective-permute-done.3), channel_id=1, source_target_pairs={{0,32},{32,64},{64,96},{96,0},{128,160},{160,192},{192,224},{224,1... | collective-permute-start | bytes 983048 | tf_op jit(solution)/shard_map/ppermute | solution.py:34
  54.7 7.2 %collective-permute-start.5 = (bf16[32,1792]{1,0:T(8,128)(2,1)S(1)}, bf16[32,1792]{1,0:T(8,128)(2,1)S(1)}, u32[]{:S(2)}, u32[]{:S(2)}) collective-permute-start(bf16[32,1792]{1,0:T(8,128)(2,1)S(1)} %slice.144), channel_id=1, source_target_pairs={{0,96},{32,0},{64,32},{96,64},{128,224},{160,128},{192,160},{224,1... | collective-permute-start | bytes 344072 | tf_op jit(solution)/shard_map/ppermute | solution.py:34
  55.1 3.9 %collective-permute-start.8 = (bf16[32,1664]{1,0:T(8,128)(2,1)S(1)}, bf16[32,1664]{1,0:T(8,128)(2,1)S(1)}, u32[]{:S(2)}, u32[]{:S(2)}) collective-permute-start(bf16[32,1664]{1,0:T(8,128)(2,1)S(1)} %slice.146), channel_id=1, source_target_pairs={{0,128},{32,160},{64,192},{96,224},{128,0},{160,32},{192,64},{224,... | collective-permute-start | bytes 319496 | tf_op jit(solution)/shard_map/ppermute | solution.py:34
  57.0 4.8 %collective-permute-start.7 = (bf16[32,1664]{1,0:T(8,128)(2,1)S(1)}, bf16[32,1664]{1,0:T(8,128)(2,1)S(1)}, u32[]{:S(2)}, u32[]{:S(2)}) collective-permute-start(bf16[32,1664]{1,0:T(8,128)(2,1)S(1)} %slice.145), channel_id=1, source_target_pairs={{0,32},{32,64},{64,96},{96,0},{128,160},{160,192},{192,224},{224,1... | collective-permute-start | bytes 319496 | tf_op jit(solution)/shard_map/ppermute | solution.py:34
  68.2 3.6 %collective-permute-start.11 = (bf16[32,1664]{1,0:T(8,128)(2,1)S(1)}, bf16[32,1664]{1,0:T(8,128)(2,1)S(1)}, u32[]{:S(2)}, u32[]{:S(2)}) collective-permute-start(bf16[32,1664]{1,0:T(8,128)(2,1)S(1)} %get-tuple-element.47), channel_id=1, source_target_pairs={{0,128},{32,160},{64,192},{96,224},{128,0},{160,32},{192,64},{224,... | collective-permute-start | bytes 319496 | tf_op jit(solution)/shard_map/ppermute | solution.py:34
  68.4 3.7 %collective-permute-start.15 = (bf16[32,1664]{1,0:T(8,128)(2,1)S(1)}, bf16[32,1664]{1,0:T(8,128)(2,1)S(1)}, u32[]{:S(2)}, u32[]{:S(2)}) collective-permute-start(bf16[32,1664]{1,0:T(8,128)(2,1)S(1)} %get-tuple-element.46), channel_id=1, source_target_pairs={{0,96},{32,0},{64,32},{96,64},{128,224},{160,128},{192,160},{224,1... | collective-permute-start | bytes 319496 | tf_op jit(solution)/shard_map/ppermute | solution.py:34
  68.6 6.4 %collective-permute-start.9 = (bf16[32,1792]{1,0:T(8,128)(2,1)S(1)}, bf16[32,1792]{1,0:T(8,128)(2,1)S(1)}, u32[]{:S(2)}, u32[]{:S(2)}) collective-permute-start(bf16[32,1792]{1,0:T(8,128)(2,1)S(1)} %pad_maximum_fusion.8), channel_id=1, source_target_pairs={{0,32},{32,64},{64,96},{96,0},{128,160},{160,192},{192,224},{224,1... | collective-permute-start | bytes 344072 | tf_op jit(solution)/shard_map/ppermute | solution.py:34
  72.3 8.4 %collective-permute-start.12 = (bf16[32,5120]{1,0:T(8,128)(2,1)S(1)}, bf16[32,5120]{1,0:T(8,128)(2,1)S(1)}, u32[]{:S(2)}, u32[]{:S(2)}) collective-permute-start(bf16[32,5120]{1,0:T(8,128)(2,1)S(1)} %get-tuple-element.43), channel_id=1, source_target_pairs={{0,32},{32,64},{64,96},{96,0},{128,160},{160,192},{192,224},{224,1... | collective-permute-start | bytes 983048 | tf_op jit(solution)/shard_map/ppermute | solution.py:34
  72.4 8.4 %collective-permute-start.16 = (bf16[32,5120]{1,0:T(8,128)(2,1)S(1)}, bf16[32,5120]{1,0:T(8,128)(2,1)S(1)}, u32[]{:S(2)}, u32[]{:S(2)}) collective-permute-start(bf16[32,5120]{1,0:T(8,128)(2,1)S(1)} %get-tuple-element.40), channel_id=1, source_target_pairs={{0,96},{32,0},{64,32},{96,64},{128,224},{160,128},{192,160},{224,1... | collective-permute-start | bytes 983048 | tf_op jit(solution)/shard_map/ppermute | solution.py:34
  75.1 6.0 %collective-permute-start.10 = (bf16[32,5120]{1,0:T(8,128)(2,1)S(1)}, bf16[32,5120]{1,0:T(8,128)(2,1)S(1)}, u32[]{:S(2)}, u32[]{:S(2)}) collective-permute-start(bf16[32,5120]{1,0:T(8,128)(2,1)S(1)} %fusion.67), channel_id=1, source_target_pairs={{0,128},{32,160},{64,192},{96,224},{128,0},{160,32},{192,64},{224,... | collective-permute-start | bytes 983048 | tf_op jit(solution)/shard_map/ppermute | solution.py:34
  76.4 8.3 %collective-permute-start.14 = (bf16[32,5120]{1,0:T(8,128)(2,1)S(1)}, bf16[32,5120]{1,0:T(8,128)(2,1)S(1)}, u32[]{:S(2)}, u32[]{:S(2)}) collective-permute-start(bf16[32,5120]{1,0:T(8,128)(2,1)S(1)} %get-tuple-element.42), channel_id=1, source_target_pairs={{0,96},{32,0},{64,32},{96,64},{128,224},{160,128},{192,160},{224,1... | collective-permute-start | bytes 983048 | tf_op jit(solution)/shard_map/ppermute | solution.py:34
  81.3 8.4 %collective-permute-start.13 = (bf16[32,5120]{1,0:T(8,128)(2,1)S(1)}, bf16[32,5120]{1,0:T(8,128)(2,1)S(1)}, u32[]{:S(2)}, u32[]{:S(2)}) collective-permute-start(bf16[32,5120]{1,0:T(8,128)(2,1)S(1)} %get-tuple-element.39), channel_id=1, source_target_pairs={{0,32},{32,64},{64,96},{96,0},{128,160},{160,192},{192,224},{224,1... | collective-permute-start | bytes 983048 | tf_op jit(solution)/shard_map/ppermute | solution.py:34
  81.4 8.8 %collective-permute-start.17 = (bf16[32,5120]{1,0:T(8,128)(2,1)S(1)}, bf16[32,5120]{1,0:T(8,128)(2,1)S(1)}, u32[]{:S(2)}, u32[]{:S(2)}) collective-permute-start(bf16[32,5120]{1,0:T(8,128)(2,1)S(1)} %get-tuple-element.38), channel_id=1, source_target_pairs={{0,128},{32,160},{64,192},{96,224},{128,0},{160,32},{192,64},{224,... | collective-permute-start | bytes 983048 | tf_op jit(solution)/shard_map/ppermute | solution.py:34
  96.6 29.1 %all-to-all-start.1 = ((bf16[32,40,128]{2,1,0:T(8,128)(2,1)}), bf16[32,40,128]{2,1,0:T(8,128)(2,1)S(1)}, u32[]{:S(2)}, u32[]{:S(2)}) async-start(bf16[32,40,128]{2,1,0:T(8,128)(2,1)} %bitcast.9), calls=%async_computation.1 | async-start | bytes 655360 | tf_op jit(solution)/shard_map/all_to_all | solution.py:332
  115.9 27.2 %copy-start.5 = (bf16[1280,64]{0,1:T(8,128)(2,1)S(1)}, bf16[1280,64]{0,1:T(8,128)(2,1)}, u32[]{:S(2)}) copy-start(bf16[1280,64]{0,1:T(8,128)(2,1)} %param.6) | copy-start | bytes 491524
  126.6 1.8 %collective-permute-start.18 = (bf16[32,1280]{1,0:T(8,128)(2,1)S(1)}, bf16[32,1280]{1,0:T(8,128)(2,1)S(1)}, u32[]{:S(2)}, u32[]{:S(2)}) collective-permute-start(bf16[32,1280]{1,0:T(8,128)(2,1)S(1)} %constant_dynamic-slice_fusion), channel_id=1, source_target_pairs={{0,1},{1,0},{2,3},{3,2},{4,5},{5,4},{6,7},{7,6},{8,9},{9,8},{10,11... | collective-permute-start | bytes 245768 | tf_op jit(solution)/shard_map/ppermute | solution.py:48
  128.5 4.9 %collective-permute-start.19 = (bf16[32,1280]{1,0:T(8,128)(2,1)S(1)}, bf16[32,1280]{1,0:T(8,128)(2,1)S(1)}, u32[]{:S(2)}, u32[]{:S(2)}) collective-permute-start(bf16[32,1280]{1,0:T(8,128)(2,1)S(1)} %add_convert_fusion.9), channel_id=1, source_target_pairs={{0,32},{1,9},{2,34},{3,11},{4,36},{5,13},{6,38},{7,15},{8,40},{9,1... | collective-permute-start | bytes 245768 | tf_op jit(solution)/shard_map/ppermute | solution.py:239
  129.2 4.8 %collective-permute-start.20 = (bf16[32,1280]{1,0:T(8,128)(2,1)S(1)}, bf16[32,1280]{1,0:T(8,128)(2,1)S(1)}, u32[]{:S(2)}, u32[]{:S(2)}) collective-permute-start(bf16[32,1280]{1,0:T(8,128)(2,1)S(1)} %add_convert_fusion.9), channel_id=1, source_target_pairs={{0,64},{1,17},{2,66},{3,19},{4,68},{5,21},{6,70},{7,23},{8,72},{9,... | collective-permute-start | bytes 245768 | tf_op jit(solution)/shard_map/ppermute | solution.py:239
  130.6 4.2 %collective-permute-start.21 = (bf16[32,1280]{1,0:T(8,128)(2,1)S(1)}, bf16[32,1280]{1,0:T(8,128)(2,1)S(1)}, u32[]{:S(2)}, u32[]{:S(2)}) collective-permute-start(bf16[32,1280]{1,0:T(8,128)(2,1)S(1)} %add_convert_fusion.9), channel_id=1, source_target_pairs={{0,96},{1,25},{2,98},{3,27},{4,100},{5,29},{6,102},{7,31},{8,104},... | collective-permute-start | bytes 245768 | tf_op jit(solution)/shard_map/ppermute | solution.py:239
  134.8 4.8 %collective-permute-start.22 = (bf16[32,1280]{1,0:T(8,128)(2,1)S(1)}, bf16[32,1280]{1,0:T(8,128)(2,1)S(1)}, u32[]{:S(2)}, u32[]{:S(2)}) collective-permute-start(bf16[32,1280]{1,0:T(8,128)(2,1)S(1)} %add_convert_fusion.8), channel_id=1, source_target_pairs={{0,8},{1,33},{2,10},{3,35},{4,12},{5,37},{6,14},{7,39},{8,16},{9,4... | collective-permute-start | bytes 245768 | tf_op jit(solution)/shard_map/ppermute | solution.py:239
  135.1 5.6 %collective-permute-start.23 = (bf16[32,1280]{1,0:T(8,128)(2,1)S(1)}, bf16[32,1280]{1,0:T(8,128)(2,1)S(1)}, u32[]{:S(2)}, u32[]{:S(2)}) collective-permute-start(bf16[32,1280]{1,0:T(8,128)(2,1)S(1)} %add_convert_fusion.8), channel_id=1, source_target_pairs={{0,16},{1,65},{2,18},{3,67},{4,20},{5,69},{6,22},{7,71},{8,24},{9,... | collective-permute-start | bytes 245768 | tf_op jit(solution)/shard_map/ppermute | solution.py:239
  138.1 3.6 %collective-permute-start.24 = (bf16[32,1280]{1,0:T(8,128)(2,1)S(1)}, bf16[32,1280]{1,0:T(8,128)(2,1)S(1)}, u32[]{:S(2)}, u32[]{:S(2)}) collective-permute-start(bf16[32,1280]{1,0:T(8,128)(2,1)S(1)} %add_convert_fusion.8), channel_id=1, source_target_pairs={{0,24},{1,97},{2,26},{3,99},{4,28},{5,101},{6,30},{7,103},{8,0},{9... | collective-permute-start | bytes 245768 | tf_op jit(solution)/shard_map/ppermute | solution.py:239
  141.7 3.4 %collective-permute-start.25 = (bf16[32,1280]{1,0:T(8,128)(2,1)S(1)}, bf16[32,1280]{1,0:T(8,128)(2,1)S(1)}, u32[]{:S(2)}, u32[]{:S(2)}) collective-permute-start(bf16[32,1280]{1,0:T(8,128)(2,1)S(1)} %add_convert_fusion.7), channel_id=1, source_target_pairs={{0,128},{32,160},{64,192},{96,224},{128,0},{160,32},{192,64},{224,... | collective-permute-start | bytes 245768 | tf_op jit(solution)/shard_map/ppermute | solution.py:34
  145.1 5.9 %collective-permute-start.26 = (bf16[32,1280]{1,0:T(8,128)(2,1)S(1)}, bf16[32,1280]{1,0:T(8,128)(2,1)S(1)}, u32[]{:S(2)}, u32[]{:S(2)}) collective-permute-start(bf16[32,1280]{1,0:T(8,128)(2,1)S(1)} %add_convert_fusion.6), channel_id=1, source_target_pairs={{0,2},{1,3},{2,4},{3,5},{4,6},{5,7},{6,0},{7,1},{8,10},{9,11},{10,... | collective-permute-start | bytes 245768 | tf_op jit(solution)/shard_map/ppermute | solution.py:48
  145.2 7.5 %collective-permute-start.27 = (bf16[32,1280]{1,0:T(8,128)(2,1)S(1)}, bf16[32,1280]{1,0:T(8,128)(2,1)S(1)}, u32[]{:S(2)}, u32[]{:S(2)}) collective-permute-start(bf16[32,1280]{1,0:T(8,128)(2,1)S(1)} %add_convert_fusion.6), channel_id=1, source_target_pairs={{0,4},{1,5},{2,6},{3,7},{4,0},{5,1},{6,2},{7,3},{8,12},{9,13},{10,... | collective-permute-start | bytes 245768 | tf_op jit(solution)/shard_map/ppermute | solution.py:48
  148.5 7.0 %collective-permute-start.28 = (bf16[32,1280]{1,0:T(8,128)(2,1)S(1)}, bf16[32,1280]{1,0:T(8,128)(2,1)S(1)}, u32[]{:S(2)}, u32[]{:S(2)}) collective-permute-start(bf16[32,1280]{1,0:T(8,128)(2,1)S(1)} %add_convert_fusion.6), channel_id=1, source_target_pairs={{0,6},{1,7},{2,0},{3,1},{4,2},{5,3},{6,4},{7,5},{8,14},{9,15},{10,... | collective-permute-start | bytes 245768 | tf_op jit(solution)/shard_map/ppermute | solution.py:48
  155.5 4.7 %collective-permute-start.29 = (bf16[32,1280]{1,0:T(8,128)(2,1)S(1)}, bf16[32,1280]{1,0:T(8,128)(2,1)S(1)}, u32[]{:S(2)}, u32[]{:S(2)}) collective-permute-start(bf16[32,1280]{1,0:T(8,128)(2,1)S(1)} %add_convert_fusion.5), channel_id=1, source_target_pairs={{0,1},{1,0},{2,3},{3,2},{4,5},{5,4},{6,7},{7,6},{8,9},{9,8},{10,11... | collective-permute-start | bytes 245768 | tf_op jit(solution)/shard_map/ppermute | solution.py:48
  (11 other events, 71.7 us)

commit v4 on v3

--- a/solution.py
+++ b/solution.py
@@ -85,13 +85,30 @@
 LANES = 128
 
 
-def local_kernel(kernel, outs, scratch, flops, moved, name, **specs):
+PIECES = 4
+
+
+def start_loads(source, target, sems):
+    rows = source.shape[0] // PIECES
+    copies = []
+    for i in range(PIECES):
+        part = pl.ds(i * rows, rows)
+        copies.append(pltpu.make_async_copy(source.at[part], target.at[part], sems.at[i]))
+        copies[-1].start()
+    return copies
+
+
+def in_hbm(value):
+    return pltpu.with_memory_space_constraint(value, pltpu.HBM)
+
+
+def local_kernel(kernel, outs, scratch, flops, moved, name, vmem=16, **specs):
     return pl.pallas_call(
         kernel,
         out_shape=outs,
         **specs,
         scratch_shapes=scratch,
-        compiler_params=pltpu.CompilerParams(vmem_limit_bytes=32 * 1024 * 1024),
+        compiler_params=pltpu.CompilerParams(vmem_limit_bytes=vmem * 1024 * 1024),
         cost_estimate=pl.CostEstimate(flops=flops, bytes_accessed=moved, transcendentals=0),
         name=name,
     )
@@ -112,17 +129,9 @@
     each, tok_hbm, cot_hbm, par_hbm, rows_ref, disp_ref, comb_ref,
     slots_ref, flat_ref, tok_ref, cot_ref, par_ref, sems,
 ):
-    def loads(source, target, which):
-        rows = source.shape[0] // PIECES
-        for i in range(PIECES):
-            part = pl.ds(i * rows, rows)
-            copy = pltpu.make_async_copy(source.at[part], target.at[part], sems.at[which, i])
-            copy.start()
-            yield copy
-
-    par_loads = list(loads(par_hbm, par_ref, 0))
-    tok_loads = list(loads(tok_hbm, tok_ref, 1))
-    cot_loads = list(loads(cot_hbm, cot_ref, 2))
+    par_loads = start_loads(par_hbm, par_ref, sems.at[0])
+    tok_loads = start_loads(tok_hbm, tok_ref, sems.at[1])
+    cot_loads = start_loads(cot_hbm, cot_ref, sems.at[2])
     for copy in par_loads + tok_loads:
         copy.wait()
     tiles = slots_ref.shape[0]
@@ -202,6 +211,106 @@
     par_ref[...] = jnp.dot(logits_grad, tok_ref[...], preferred_element_type=F32).astype(BF16)
 
 
+def expert_kernel(count, each, *refs):
+    blocks, (win_hbm, wout_hbm) = refs[:count], refs[count : count + 2]
+    parts = refs[count + 2 : 2 * count + 2]
+    act_ref, pre_ref, win_ref, wout_ref, sems = refs[2 * count + 2 :]
+    loads = [
+        (
+            start_loads(win_hbm.at[j], win_ref.at[j], sems.at[0, j]),
+            start_loads(wout_hbm.at[j], wout_ref.at[j], sems.at[1, j]),
+        )
+        for j in range(each)
+    ]
+    groups = blocks[0].shape[0]
+    width, hidden = win_ref.shape[1:]
+
+    def gathered(kind, j):
+        cols = slice((kind * each + j) * width, (kind * each + j + 1) * width)
+        return jnp.concatenate([block[:, cols] for block in blocks], axis=0)
+
+    def spread(value, kind, j):
+        cols = slice((kind * each + j) * width, (kind * each + j + 1) * width)
+        value = value.astype(BF16)
+        for i, part in enumerate(parts):
+            part[:, cols] = value[i * groups : (i + 1) * groups]
+
+    for j in range(each):
+        hid = slice(j * hidden, (j + 1) * hidden)
+        for copy in loads[j][0]:
+            copy.wait()
+        pre_act = jnp.dot(gathered(0, j), win_ref[j], preferred_element_type=F32)
+        gelu_value, gelu_slope = gelu_pair(pre_act)
+        activation = gelu_value.astype(BF16)
+        act_ref[:, hid] = activation
+        for copy in loads[j][1]:
+            copy.wait()
+        spread(jnp.dot(activation, wout_ref[j], preferred_element_type=F32), 0, j)
+        pre_grad = (nt(gathered(1, j), wout_ref[j]) * gelu_slope).astype(BF16)
+        pre_ref[:, hid] = pre_grad
+        spread(nt(pre_grad, win_ref[j]), 1, j)
+
+
+def expert_step(blocks, weight_in, weight_out):
+    count = len(blocks)
+    each, width, hidden = weight_in.shape
+    rows = count * blocks[0].shape[0]
+    kept = jax.ShapeDtypeStruct((rows, each * hidden), BF16)
+    outs = local_kernel(
+        functools.partial(expert_kernel, count, each),
+        [jax.ShapeDtypeStruct(b.shape, BF16) for b in blocks] + [kept, kept],
+        [
+            pltpu.VMEM(weight_in.shape, BF16),
+            pltpu.VMEM(weight_out.shape, BF16),
+            pltpu.SemaphoreType.DMA((2, each, PIECES)),
+        ],
+        8 * rows * each * width * hidden,
+        4 * each * width * hidden + 8 * rows * each * width,
+        "expert",
+        in_specs=[pl.BlockSpec(memory_space=pltpu.VMEM)] * count
+        + [pl.BlockSpec(memory_space=pltpu.HBM)] * 2,
+    )(*blocks, in_hbm(weight_in), in_hbm(weight_out))
+    return outs[:count], outs[count], outs[count + 1]
+
+
+def weights_kernel(count, kept, *refs):
+    rows_in, rows_cot = refs[:count], refs[count : 2 * count]
+    acts, pres = refs[2 * count : 2 * count + kept], refs[2 * count + kept : 2 * count + 2 * kept]
+    gin_ref, gout_ref = refs[2 * count + 2 * kept :]
+
+    def whole(parts):
+        return jnp.concatenate([part[...] for part in parts], axis=0)
+
+    gin_ref[0] = tn(whole(rows_in), whole(pres)).astype(BF16)
+    gout_ref[0] = tn(whole(acts), whole(rows_cot)).astype(BF16)
+
+
+def weight_gradients(blocks, acts, pres, each, width, hidden):
+    count, kept, cuts = len(blocks), len(acts), 2
+    groups = blocks[0].shape[0]
+    rows = count * groups
+    return local_kernel(
+        functools.partial(weights_kernel, count, kept),
+        (
+            jax.ShapeDtypeStruct((each, width, hidden), BF16),
+            jax.ShapeDtypeStruct((each, hidden, width), BF16),
+        ),
+        [],
+        4 * rows * each * width * hidden,
+        4 * each * width * hidden + 8 * rows * each * width,
+        "weight_grads",
+        grid=(each, cuts),
+        in_specs=[pl.BlockSpec((groups, width // cuts), lambda e, i: (0, e * cuts + i))] * count
+        + [pl.BlockSpec((groups, width), lambda e, i: (0, each + e))] * count
+        + [pl.BlockSpec((a.shape[0], hidden // cuts), lambda e, i: (0, e * cuts + i)) for a in acts]
+        + [pl.BlockSpec((p.shape[0], hidden), lambda e, i: (0, e)) for p in pres],
+        out_specs=(
+            pl.BlockSpec((1, width // cuts, hidden), lambda e, i: (e, i, 0)),
+            pl.BlockSpec((1, hidden // cuts, width), lambda e, i: (e, i, 0)),
+        ),
+    )(*blocks, *blocks, *acts, *pres)
+
+
 def scatter_blocks(parts):
     a, b, c = thirds(parts[0, 0].shape[1])
     far = parts[1, 2]
@@ -283,7 +392,7 @@
         4 * patches * width + 2 * flat * LANES,
         "front",
         in_specs=[pl.BlockSpec(memory_space=pltpu.HBM)] * 3,
-    )(tokens, output_grad, params)
+    )(in_hbm(tokens), in_hbm(output_grad), in_hbm(params))
     routed = lax.all_to_all(
         rows.reshape(groups, 2 * each * tiles, LANES), "expert", split_axis=0, concat_axis=0,
         tiled=True,
@@ -297,28 +406,9 @@
         "unpack",
     )(routed)
     blocks = gather_blocks(mine)
-    gathered = jnp.concatenate([blocks[o] for o in OFFSETS], axis=0)
-    out_cols, in_cols, acts, pres = [], [], [], []
-    for j in range(each):
-        rows_in = gathered[:, j * width : (j + 1) * width]
-        rows_cot = gathered[:, (each + j) * width : (each + j + 1) * width]
-        pre_act = jnp.dot(rows_in, weight_in[j], preferred_element_type=F32)
-        gelu_value, gelu_slope = gelu_pair(pre_act)
-        activation = gelu_value.astype(BF16)
-        out_cols.append(jnp.dot(activation, weight_out[j], preferred_element_type=F32).astype(BF16))
-        act_grad = lax.dot_general(
-            rows_cot, weight_out[j], (((1,), (1,)), ((), ())), preferred_element_type=F32
-        )
-        pre_grad = (act_grad * gelu_slope).astype(BF16)
-        in_cols.append(
-            lax.dot_general(
-                pre_grad, weight_in[j], (((1,), (1,)), ((), ())), preferred_element_type=F32
-            ).astype(BF16)
-        )
-        acts.append(activation)
-        pres.append(pre_grad)
-    partial = jnp.concatenate(out_cols + in_cols, axis=1)
-    parts = {o: partial[i * groups : (i + 1) * groups] for i, o in enumerate(OFFSETS)}
+    blocks = [blocks[o] for o in OFFSETS]
+    partial, act, pre = expert_step(blocks, weight_in, weight_out)
+    parts = dict(zip(OFFSETS, partial))
     share = scatter_blocks(parts)
     packed = local_kernel(
         pack_sum_kernel,
@@ -328,18 +418,13 @@
         10 * flat * LANES,
         "pack_sum",
     )(*share)
-    packed, gathered, acts, pres = lax.optimization_barrier((packed, gathered, acts, pres))
+    packed, act, pre = lax.optimization_barrier((packed, act, pre))
     back = lax.all_to_all(
         packed.reshape(groups, 2 * each * tiles, LANES), "expert", split_axis=0, concat_axis=0,
         tiled=True,
     ).reshape(flat, LANES)
-    in_grads, out_grads = [], []
-    for j in range(each):
-        rows_in = gathered[:, j * width : (j + 1) * width]
-        rows_cot = gathered[:, (each + j) * width : (each + j + 1) * width]
-        in_grads.append(tn(rows_in, pres[j]).astype(BF16))
-        out_grads.append(tn(acts[j], rows_cot).astype(BF16))
-    weight_grads = (jnp.stack(in_grads), jnp.stack(out_grads))
+    hidden = weight_in.shape[2]
+    weight_grads = weight_gradients(blocks, [act], [pre], each, width, hidden)
     back, weight_grads = lax.optimization_barrier((back, weight_grads))
     row_shape = jax.ShapeDtypeStruct((slots, width), BF16)
     slot_in_grad, logits_grad, local_params = local_kernel(

time: 162 us -> 165 us (1.019)
  matrix products: 11.7 us -> 1.55 us
  Pallas kernels: 5.2 us -> 15.3 us
  waiting for transfers between devices: 54.9 us -> 60.7 us
  other arithmetic: 4.85 us -> 1.3 us
  starting transfers between devices: 50.3 us -> 53.3 us
    dot_general x12 -> x0, matrix products: 10.2 us -> none  [the longest x4 5.4 us: tn(): lax.dot_general(a, b, (((0,), (0,)), ((), ())), preferred_element_type=F32)]
    pallas_call x0 -> x2, Pallas kernels: none -> 9.8 us  [the longest x1 5.76 us: expert_step(): local_kernel(functools.partial(expert_kernel, count, each), [jax.ShapeDty...]
    ppermute x19, waiting for transfers between devices: 31.6 us -> 37.1 us  [batch_send(): return lax.ppermute(value, 'batch', pairs)]
    ppermute x6, starting transfers between devices: 7.25 us -> 3.74 us  [crossed_send(): return lax.ppermute(value, ('batch', 'expert'), pairs)]
    ppermute x19, starting transfers between devices: 19.3 us -> 22.8 us  [batch_send(): return lax.ppermute(value, 'batch', pairs)]
    another operation x2 -> x0, other arithmetic: 3.44 us -> none  [body(): weight_grads = (jnp.stack(in_grads), jnp.stack(out_grads))]
    ppermute x6, waiting for transfers between devices: 5.51 us -> 8.59 us  [crossed_send(): return lax.ppermute(value, ('batch', 'expert'), pairs)]
    all_to_all x1, waiting for transfers between devices: 9.89 us -> 6.83 us  [body(): lax.all_to_all(packed.reshape(groups, 2 * each * tiles, LANES), 'expert',...]
  transfers between devices with their start and end apart: 31 -> 31, of which waited for: 25 -> 23; matrix products, arithmetic and copies ran while one was open for 3% -> 1% of each run, Pallas kernels for 0% -> 2%
where the time goes in v4:
time: 165 us
  waiting for transfers between devices  60.7 us (37%)
  starting transfers between devices  53.3 us (32%)
  blocking collectives  27.3 us (17%)
  Pallas kernels  15.3 us (9%)
  local copies, waits for them, and re-layouts  4.21 us (3%)
    ppermute x19, waiting for transfers between devices, batch_send(): return lax.ppermute(value, 'batch', pairs)  37.1 us
    all_to_all x1, blocking collectives, body(): lax.all_to_all(rows.reshape(groups, 2 * each * tiles, LANES), 'expert', s...  27.3 us
    ppermute x19, starting transfers between devices, batch_send(): return lax.ppermute(value, 'batch', pairs)  22.8 us
    all_to_all x1, starting transfers between devices, body(): lax.all_to_all(packed.reshape(groups, 2 * each * tiles, LANES), 'expert',...  15.2 us
    ppermute x5, starting transfers between devices, expert_send(): return lax.ppermute(value, 'expert', pairs)  11.7 us
    ppermute x6, waiting for transfers between devices, crossed_send(): return lax.ppermute(value, ('batch', 'expert'), pairs)  8.59 us
    ppermute x5, waiting for transfers between devices, expert_send(): return lax.ppermute(value, 'expert', pairs)  8.16 us
    all_to_all x1, waiting for transfers between devices, body(): lax.all_to_all(packed.reshape(groups, 2 * each * tiles, LANES), 'expert',...  6.83 us
  transfers between devices with their start and end apart: 31, of which 23 were waited for; matrix products, arithmetic and copies ran while one was open for 1% of the time, Pallas kernels for 2%

profile of v4, /device:TPU:1, one launch (start us, length us, event | category | flops | bytes accessed | tf_op | source)
XLA Modules:
  0.0 164.7 jit_solution(16510305704392973023)
XLA Ops:
  0.6 2.6 %front.1 = (bf16[1280,128]{1,0:T(8,128)(2,1)S(1)}, f32[64,256]{1,0:T(8,128)S(1)}, f32[64,256]{1,0:T(8,128)S(1)}) custom-call(bf16[256,1280]{1,0:T(8,128)(2,1)} %bitcast.13, bf16[256,1280]{1,0:T(8,128)(2,1)} %bitcast.15, bf16[64,1280]{1,0:T(8,128)(2,1)} %bitcast.19), custom_call_target="tpu_custom_call" | custom-call | flops 125829120 | bytes 1638400 | tf_op jit(solution)/shard_map/front/pallas_call | solution.py:380
  3.3 27.3 %all_to_all.10 = bf16[32,40,128]{2,1,0:T(8,128)(2,1)S(1)} all-to-all(bf16[32,40,128]{2,1,0:T(8,128)(2,1)S(1)} %bitcast.18), channel_id=1, replica_groups=mesh['batch'=8,'expert'=32] {'expert'}, dimensions={0} | all-to-all | bytes 655360 | tf_op jit(solution)/shard_map/all_to_all | solution.py:396
  30.8 2.6 %collective-permute-start = (bf16[32,5120]{1,0:T(8,128)(2,1)S(1)}, bf16[32,5120]{1,0:T(8,128)(2,1)S(1)}, u32[]{:S(2)}, u32[]{:S(2)}) collective-permute-start(bf16[32,5120]{1,0:T(8,128)(2,1)S(1)} %unpack.1.refs_0_.refs_8_), channel_id=1, source_target_pairs={{0,96},{32,0},{64,32},{96,64},{128,224},{160,128},{192,160},{224,1... | collective-permute-start | bytes 983048 | tf_op jit(solution)/shard_map/ppermute | solution.py:34
  34.3 5.7 %collective-permute-done.refs_1_.refs_9_ = bf16[32,5120]{1,0:T(8,128)(2,1)S(1)} collective-permute-done((bf16[32,5120]{1,0:T(8,128)(2,1)S(1)}, bf16[32,5120]{1,0:T(8,128)(2,1)S(1)}, u32[]{:S(2)}, u32[]{:S(2)}) %collective-permute-start) | collective-permute-done | bytes 327712 | tf_op jit(solution)/shard_map/ppermute | solution.py:34
  42.1 2.5 %collective-permute-start.1 = (bf16[32,5120]{1,0:T(8,128)(2,1)S(1)}, bf16[32,5120]{1,0:T(8,128)(2,1)S(1)}, u32[]{:S(2)}, u32[]{:S(2)}) collective-permute-start(bf16[32,5120]{1,0:T(8,128)(2,1)S(1)} %collective-permute-done.refs_1_.refs_9_), channel_id=1, source_target_pairs={{0,96},{32,0},{64,32},{96,64},{128,224},{160,128},{192,160},{224,1... | collective-permute-start | bytes 983048 | tf_op jit(solution)/shard_map/ppermute | solution.py:34
  44.6 4.0 %collective-permute-done.4.refs_5_.refs_13_ = bf16[32,5120]{1,0:T(8,128)(2,1)S(1)} collective-permute-done((bf16[32,5120]{1,0:T(8,128)(2,1)S(1)}, bf16[32,5120]{1,0:T(8,128)(2,1)S(1)}, u32[]{:S(2)}, u32[]{:S(2)}) %collective-permute-start.4) | collective-permute-done | bytes 327712 | tf_op jit(solution)/shard_map/ppermute | solution.py:34
  48.7 2.7 %collective-permute-start.5 = (bf16[32,1792]{1,0:T(8,128)(2,1)S(1)}, bf16[32,1792]{1,0:T(8,128)(2,1)S(1)}, u32[]{:S(2)}, u32[]{:S(2)}) collective-permute-start(bf16[32,1792]{1,0:T(8,128)(2,1)S(1)} %slice.52), channel_id=1, source_target_pairs={{0,96},{32,0},{64,32},{96,64},{128,224},{160,128},{192,160},{224,1... | collective-permute-start | bytes 344072 | tf_op jit(solution)/shard_map/ppermute | solution.py:34
  51.5 1.5 collective-permute-start.8
  53.4 8.2 %collective-permute-done.7 = bf16[32,1664]{1,0:T(8,128)(2,1)S(1)} collective-permute-done((bf16[32,1664]{1,0:T(8,128)(2,1)S(1)}, bf16[32,1664]{1,0:T(8,128)(2,1)S(1)}, u32[]{:S(2)}, u32[]{:S(2)}) %collective-permute-start.7) | collective-permute-done | bytes 106528 | tf_op jit(solution)/shard_map/ppermute | solution.py:34
  61.6 5.8 %expert.1 = (bf16[32,5120]{1,0:T(8,128)(2,1)S(1)}, bf16[32,5120]{1,0:T(8,128)(2,1)S(1)}, bf16[32,5120]{1,0:T(8,128)(2,1)S(1)}, bf16[32,5120]{1,0:T(8,128)(2,1)S(...) custom-call(bf16[32,5120]{1,0:T(8,128)(2,1)S(1)} %unpack.1.refs_0_.r, ...), custom_call_target="tpu_custom_call" | custom-call | flops 2684354560 | bytes 10485760 | tf_op jit(solution)/shard_map/expert/pallas_call | solution.py:259
  67.5 1.7 %collective-permute-start.11 = (bf16[32,1664]{1,0:T(8,128)(2,1)S(1)}, bf16[32,1664]{1,0:T(8,128)(2,1)S(1)}, u32[]{:S(2)}, u32[]{:S(2)}) collective-permute-start(bf16[32,1664]{1,0:T(8,128)(2,1)S(1)} %get-tuple-element.57), channel_id=1, source_target_pairs={{0,128},{32,160},{64,192},{96,224},{128,0},{160,32},{192,64},{224,... | collective-permute-start | bytes 319496 | tf_op jit(solution)/shard_map/ppermute | solution.py:34
  69.5 2.7 %collective-permute-start.14 = (bf16[32,5120]{1,0:T(8,128)(2,1)S(1)}, bf16[32,5120]{1,0:T(8,128)(2,1)S(1)}, u32[]{:S(2)}, u32[]{:S(2)}) collective-permute-start(bf16[32,5120]{1,0:T(8,128)(2,1)S(1)} %get-tuple-element.36), channel_id=1, source_target_pairs={{0,96},{32,0},{64,32},{96,64},{128,224},{160,128},{192,160},{224,1... | collective-permute-start | bytes 983048 | tf_op jit(solution)/shard_map/ppermute | solution.py:34
  72.3 1.5 collective-permute-start.12
  73.8 3.9 %collective-permute-done.15 = bf16[32,1664]{1,0:T(8,128)(2,1)S(1)} collective-permute-done((bf16[32,1664]{1,0:T(8,128)(2,1)S(1)}, bf16[32,1664]{1,0:T(8,128)(2,1)S(1)}, u32[]{:S(2)}, u32[]{:S(2)}) %collective-permute-start.15) | collective-permute-done | bytes 106528 | tf_op jit(solution)/shard_map/ppermute | solution.py:34
  77.8 3.5 %collective-permute-start.16 = (bf16[32,5120]{1,0:T(8,128)(2,1)S(1)}, bf16[32,5120]{1,0:T(8,128)(2,1)S(1)}, u32[]{:S(2)}, u32[]{:S(2)}) collective-permute-start(bf16[32,5120]{1,0:T(8,128)(2,1)S(1)} %pad_maximum_fusion.2), channel_id=1, source_target_pairs={{0,96},{32,0},{64,32},{96,64},{128,224},{160,128},{192,160},{224,1... | collective-permute-start | bytes 983048 | tf_op jit(solution)/shard_map/ppermute | solution.py:34
  81.4 4.1 %collective-permute-done.16 = bf16[32,5120]{1,0:T(8,128)(2,1)S(1)} collective-permute-done((bf16[32,5120]{1,0:T(8,128)(2,1)S(1)}, bf16[32,5120]{1,0:T(8,128)(2,1)S(1)}, u32[]{:S(2)}, u32[]{:S(2)}) %collective-permute-start.16) | collective-permute-done | bytes 327712 | tf_op jit(solution)/shard_map/ppermute | solution.py:34
  85.7 1.9 %collective-permute-done.10 = bf16[32,5120]{1,0:T(8,128)(2,1)S(1)} collective-permute-done((bf16[32,5120]{1,0:T(8,128)(2,1)S(1)}, bf16[32,5120]{1,0:T(8,128)(2,1)S(1)}, u32[]{:S(2)}, u32[]{:S(2)}) %collective-permute-start.10) | collective-permute-done | bytes 327712 | tf_op jit(solution)/shard_map/ppermute | solution.py:34
  87.9 6.2 %collective-permute-done.17.d_ref = bf16[32,5120]{1,0:T(8,128)(2,1)S(1)} collective-permute-done((bf16[32,5120]{1,0:T(8,128)(2,1)S(1)}, bf16[32,5120]{1,0:T(8,128)(2,1)S(1)}, u32[]{:S(2)}, u32[]{:S(2)}) %collective-permute-start.17) | collective-permute-done | bytes 327712 | tf_op jit(solution)/shard_map/ppermute | solution.py:34
  95.9 15.2 %all-to-all-start.1 = ((bf16[32,40,128]{2,1,0:T(8,128)(2,1)}), bf16[32,40,128]{2,1,0:T(8,128)(2,1)}, u32[]{:S(2)}, u32[]{:S(2)}) async-start(bf16[32,40,128]{2,1,0:T(8,128)(2,1)} %bitcast.5), calls=%async_computation.1 | async-start | bytes 655360 | tf_op jit(solution)/shard_map/all_to_all | solution.py:422
  115.1 4.0 %weight_grads.1 = (bf16[2,1280,512]{2,1,0:T(8,128)(2,1)}, bf16[2,512,1280]{2,1,0:T(8,128)(2,1)}) custom-call(bf16[32,5120]{1,0:T(8,128)(2,1)S(1)} %unpack.1.refs_0_.refs_8_, bf16[32,5120]{1,0:T(8,128)(2,1)S(1)} %collective-permute-done.refs_1_.refs_9_, bf16[32,5120]{1,0:T(8,128)(2,1)S(1)} %collective-permute-done.1.refs_2_.refs_10_, ...), custom_call_target="tpu_custom_call" | custom-call | flops 1342177280 | bytes 10485760 | tf_op jit(solution)/shard_map/weight_grads/pallas_call | solution.py:292
  119.1 6.8 %all-to-all-done.1 = bf16[32,40,128]{2,1,0:T(8,128)(2,1)} async-done(((bf16[32,40,128]{2,1,0:T(8,128)(2,1)}), bf16[32,40,128]{2,1,0:T(8,128)(2,1)}, u32[]{:S(2)}, u32[]{:S(2)}) %all-to-all-start.1) | async-done | bytes 327712 | tf_op jit(solution)/shard_map/all_to_all | solution.py:422
  126.0 1.8 %final.1 = (bf16[64,1280]{1,0:T(8,128)(2,1)S(1)}, bf16[64,256]{1,0:T(8,128)(2,1)S(1)}, bf16[64,1280]{1,0:T(8,128)(2,1)S(1)}) custom-call(bf16[1280,128]{1,0:T(8,128)(2,1)} %bitcast.6.flat_in_ref, bf16[256,1280]{1,0:T(8,128)(2,1)S(1)} %bitcast.14, bf16[256,1280]{1,0:T(8,128)(2,1)S(1)} %bitcast.16, f32[64,256]{1,0:T(8,128)S(1)} %get-tuple-element.47.disp_ref, ...), custom_call_target="tpu_custom_call" | custom-call | flops 125829120 | bytes 1638400 | tf_op jit(solution)/shard_map/final/pallas_call | solution.py:430
  130.2 1.2 collective-permute-start.20
  131.5 1.4 collective-permute-done.21
  133.0 2.3 %collective-permute-done.20 = bf16[32,1280]{1,0:T(8,128)(2,1)S(1)} collective-permute-done((bf16[32,1280]{1,0:T(8,128)(2,1)S(1)}, bf16[32,1280]{1,0:T(8,128)(2,1)S(1)}, u32[]{:S(2)}, u32[]{:S(2)}) %collective-permute-start.20) | collective-permute-done | bytes 81952 | tf_op jit(solution)/shard_map/ppermute | solution.py:348
  136.4 1.4 collective-permute-start.22
  138.1 1.5 collective-permute-done.24
  139.6 1.6 collective-permute-done.23
  143.3 1.2 fusion
  146.3 2.4 %collective-permute-start.27 = (bf16[32,1280]{1,0:T(8,128)(2,1)S(1)}, bf16[32,1280]{1,0:T(8,128)(2,1)S(1)}, u32[]{:S(2)}, u32[]{:S(2)}) collective-permute-start(bf16[32,1280]{1,0:T(8,128)(2,1)S(1)} %add_convert_fusion.6), channel_id=1, source_target_pairs={{0,4},{1,5},{2,6},{3,7},{4,0},{5,1},{6,2},{7,3},{8,12},{9,13},{10,... | collective-permute-start | bytes 245768 | tf_op jit(solution)/shard_map/ppermute | solution.py:48
  149.9 4.5 %collective-permute-done.27 = bf16[32,1280]{1,0:T(8,128)(2,1)S(1)} collective-permute-done((bf16[32,1280]{1,0:T(8,128)(2,1)S(1)}, bf16[32,1280]{1,0:T(8,128)(2,1)S(1)}, u32[]{:S(2)}, u32[]{:S(2)}) %collective-permute-start.27) | collective-permute-done | bytes 81952 | tf_op jit(solution)/shard_map/ppermute | solution.py:48
  155.1 7.9 %collective-permute-start.29 = (bf16[32,1280]{1,0:T(8,128)(2,1)S(1)}, bf16[32,1280]{1,0:T(8,128)(2,1)S(1)}, u32[]{:S(2)}, u32[]{:S(2)}) collective-permute-start(bf16[32,1280]{1,0:T(8,128)(2,1)S(1)} %add_convert_fusion.5), channel_id=1, source_target_pairs={{0,1},{1,0},{2,3},{3,2},{4,5},{5,4},{6,7},{7,6},{8,9},{9,8},{10,11... | collective-permute-start | bytes 245768 | tf_op jit(solution)/shard_map/ppermute | solution.py:48
  (89 shorter events, 22.2 us)
Async XLA Ops:
  30.8 9.2 %collective-permute-start = (bf16[32,5120]{1,0:T(8,128)(2,1)S(1)}, bf16[32,5120]{1,0:T(8,128)(2,1)S(1)}, u32[]{:S(2)}, u32[]{:S(2)}) collective-permute-start(bf16[32,5120]{1,0:T(8,128)(2,1)S(1)} %unpack.1.refs_0_.refs_8_), channel_id=1, source_target_pairs={{0,96},{32,0},{64,32},{96,64},{128,224},{160,128},{192,160},{224,1... | collective-permute-start | bytes 983048 | tf_op jit(solution)/shard_map/ppermute | solution.py:34
  33.3 8.5 %collective-permute-start.3 = (bf16[32,5120]{1,0:T(8,128)(2,1)S(1)}, bf16[32,5120]{1,0:T(8,128)(2,1)S(1)}, u32[]{:S(2)}, u32[]{:S(2)}) collective-permute-start(bf16[32,5120]{1,0:T(8,128)(2,1)S(1)} %unpack.1.refs_0_.refs_8_), channel_id=1, source_target_pairs={{0,128},{32,160},{64,192},{96,224},{128,0},{160,32},{192,64},{224,... | collective-permute-start | bytes 983048 | tf_op jit(solution)/shard_map/ppermute | solution.py:34
  40.0 8.7 %collective-permute-start.4 = (bf16[32,5120]{1,0:T(8,128)(2,1)S(1)}, bf16[32,5120]{1,0:T(8,128)(2,1)S(1)}, u32[]{:S(2)}, u32[]{:S(2)}) collective-permute-start(bf16[32,5120]{1,0:T(8,128)(2,1)S(1)} %collective-permute-done.refs_1_.refs_9_), channel_id=1, source_target_pairs={{0,128},{32,160},{64,192},{96,224},{128,0},{160,32},{192,64},{224,... | collective-permute-start | bytes 983048 | tf_op jit(solution)/shard_map/ppermute | solution.py:34
  41.8 25.6 %copy-start.2 = (bf16[32,5120]{1,0:T(8,128)(2,1)}, bf16[32,5120]{1,0:T(8,128)(2,1)S(1)}, u32[]{:S(2)}) copy-start(bf16[32,5120]{1,0:T(8,128)(2,1)S(1)} %collective-permute-done.3.refs_4_.refs_12_) | copy-start | bytes 983044
  41.8 9.5 %collective-permute-start.6 = (bf16[32,5120]{1,0:T(8,128)(2,1)S(1)}, bf16[32,5120]{1,0:T(8,128)(2,1)S(1)}, u32[]{:S(2)}, u32[]{:S(2)}) collective-permute-start(bf16[32,5120]{1,0:T(8,128)(2,1)S(1)} %collective-permute-done.3.refs_4_.refs_12_), channel_id=1, source_target_pairs={{0,32},{32,64},{64,96},{96,0},{128,160},{160,192},{192,224},{224,1... | collective-permute-start | bytes 983048 | tf_op jit(solution)/shard_map/ppermute | solution.py:34
  42.1 9.4 %collective-permute-start.1 = (bf16[32,5120]{1,0:T(8,128)(2,1)S(1)}, bf16[32,5120]{1,0:T(8,128)(2,1)S(1)}, u32[]{:S(2)}, u32[]{:S(2)}) collective-permute-start(bf16[32,5120]{1,0:T(8,128)(2,1)S(1)} %collective-permute-done.refs_1_.refs_9_), channel_id=1, source_target_pairs={{0,96},{32,0},{64,32},{96,64},{128,224},{160,128},{192,160},{224,1... | collective-permute-start | bytes 983048 | tf_op jit(solution)/shard_map/ppermute | solution.py:34
  48.7 4.7 %collective-permute-start.5 = (bf16[32,1792]{1,0:T(8,128)(2,1)S(1)}, bf16[32,1792]{1,0:T(8,128)(2,1)S(1)}, u32[]{:S(2)}, u32[]{:S(2)}) collective-permute-start(bf16[32,1792]{1,0:T(8,128)(2,1)S(1)} %slice.52), channel_id=1, source_target_pairs={{0,96},{32,0},{64,32},{96,64},{128,224},{160,128},{192,160},{224,1... | collective-permute-start | bytes 344072 | tf_op jit(solution)/shard_map/ppermute | solution.py:34
  51.4 10.2 %collective-permute-start.2 = (bf16[32,5120]{1,0:T(8,128)(2,1)S(1)}, bf16[32,5120]{1,0:T(8,128)(2,1)S(1)}, u32[]{:S(2)}, u32[]{:S(2)}) collective-permute-start(bf16[32,5120]{1,0:T(8,128)(2,1)S(1)} %unpack.1.refs_0_.refs_8_), channel_id=1, source_target_pairs={{0,32},{32,64},{64,96},{96,0},{128,160},{160,192},{192,224},{224,1... | collective-permute-start | bytes 983048 | tf_op jit(solution)/shard_map/ppermute | solution.py:34
  51.4 10.2 %collective-permute-start.7 = (bf16[32,1664]{1,0:T(8,128)(2,1)S(1)}, bf16[32,1664]{1,0:T(8,128)(2,1)S(1)}, u32[]{:S(2)}, u32[]{:S(2)}) collective-permute-start(bf16[32,1664]{1,0:T(8,128)(2,1)S(1)} %slice.53), channel_id=1, source_target_pairs={{0,32},{32,64},{64,96},{96,0},{128,160},{160,192},{192,224},{224,1... | collective-permute-start | bytes 319496 | tf_op jit(solution)/shard_map/ppermute | solution.py:34
  51.5 10.1 %collective-permute-start.8 = (bf16[32,1664]{1,0:T(8,128)(2,1)S(1)}, bf16[32,1664]{1,0:T(8,128)(2,1)S(1)}, u32[]{:S(2)}, u32[]{:S(2)}) collective-permute-start(bf16[32,1664]{1,0:T(8,128)(2,1)S(1)} %slice.54), channel_id=1, source_target_pairs={{0,128},{32,160},{64,192},{96,224},{128,0},{160,32},{192,64},{224,... | collective-permute-start | bytes 319496 | tf_op jit(solution)/shard_map/ppermute | solution.py:34
  67.5 4.8 %collective-permute-start.11 = (bf16[32,1664]{1,0:T(8,128)(2,1)S(1)}, bf16[32,1664]{1,0:T(8,128)(2,1)S(1)}, u32[]{:S(2)}, u32[]{:S(2)}) collective-permute-start(bf16[32,1664]{1,0:T(8,128)(2,1)S(1)} %get-tuple-element.57), channel_id=1, source_target_pairs={{0,128},{32,160},{64,192},{96,224},{128,0},{160,32},{192,64},{224,... | collective-permute-start | bytes 319496 | tf_op jit(solution)/shard_map/ppermute | solution.py:34
  69.2 12.0 %collective-permute-start.9 = (bf16[32,1792]{1,0:T(8,128)(2,1)S(1)}, bf16[32,1792]{1,0:T(8,128)(2,1)S(1)}, u32[]{:S(2)}, u32[]{:S(2)}) collective-permute-start(bf16[32,1792]{1,0:T(8,128)(2,1)S(1)} %slice.43), channel_id=1, source_target_pairs={{0,32},{32,64},{64,96},{96,0},{128,160},{160,192},{192,224},{224,1... | collective-permute-start | bytes 344072 | tf_op jit(solution)/shard_map/ppermute | solution.py:34
  69.5 18.3 %collective-permute-start.14 = (bf16[32,5120]{1,0:T(8,128)(2,1)S(1)}, bf16[32,5120]{1,0:T(8,128)(2,1)S(1)}, u32[]{:S(2)}, u32[]{:S(2)}) collective-permute-start(bf16[32,5120]{1,0:T(8,128)(2,1)S(1)} %get-tuple-element.36), channel_id=1, source_target_pairs={{0,96},{32,0},{64,32},{96,64},{128,224},{160,128},{192,160},{224,1... | collective-permute-start | bytes 983048 | tf_op jit(solution)/shard_map/ppermute | solution.py:34
  72.2 5.5 %collective-permute-start.15 = (bf16[32,1664]{1,0:T(8,128)(2,1)S(1)}, bf16[32,1664]{1,0:T(8,128)(2,1)S(1)}, u32[]{:S(2)}, u32[]{:S(2)}) collective-permute-start(bf16[32,1664]{1,0:T(8,128)(2,1)S(1)} %get-tuple-element.56), channel_id=1, source_target_pairs={{0,96},{32,0},{64,32},{96,64},{128,224},{160,128},{192,160},{224,1... | collective-permute-start | bytes 319496 | tf_op jit(solution)/shard_map/ppermute | solution.py:34
  72.3 13.4 %collective-permute-start.12 = (bf16[32,5120]{1,0:T(8,128)(2,1)S(1)}, bf16[32,5120]{1,0:T(8,128)(2,1)S(1)}, u32[]{:S(2)}, u32[]{:S(2)}) collective-permute-start(bf16[32,5120]{1,0:T(8,128)(2,1)S(1)} %pad_maximum_fusion.1), channel_id=1, source_target_pairs={{0,32},{32,64},{64,96},{96,0},{128,160},{160,192},{192,224},{224,1... | collective-permute-start | bytes 983048 | tf_op jit(solution)/shard_map/ppermute | solution.py:34
  77.8 7.7 %collective-permute-start.16 = (bf16[32,5120]{1,0:T(8,128)(2,1)S(1)}, bf16[32,5120]{1,0:T(8,128)(2,1)S(1)}, u32[]{:S(2)}, u32[]{:S(2)}) collective-permute-start(bf16[32,5120]{1,0:T(8,128)(2,1)S(1)} %pad_maximum_fusion.2), channel_id=1, source_target_pairs={{0,96},{32,0},{64,32},{96,64},{128,224},{160,128},{192,160},{224,1... | collective-permute-start | bytes 983048 | tf_op jit(solution)/shard_map/ppermute | solution.py:34
  81.3 6.3 %collective-permute-start.10 = (bf16[32,5120]{1,0:T(8,128)(2,1)S(1)}, bf16[32,5120]{1,0:T(8,128)(2,1)S(1)}, u32[]{:S(2)}, u32[]{:S(2)}) collective-permute-start(bf16[32,5120]{1,0:T(8,128)(2,1)S(1)} %pad_maximum_fusion), channel_id=1, source_target_pairs={{0,128},{32,160},{64,192},{96,224},{128,0},{160,32},{192,64},{224,... | collective-permute-start | bytes 983048 | tf_op jit(solution)/shard_map/ppermute | solution.py:34
  85.6 8.4 %collective-permute-start.17 = (bf16[32,5120]{1,0:T(8,128)(2,1)S(1)}, bf16[32,5120]{1,0:T(8,128)(2,1)S(1)}, u32[]{:S(2)}, u32[]{:S(2)}) collective-permute-start(bf16[32,5120]{1,0:T(8,128)(2,1)S(1)} %add_convert_fusion), channel_id=1, source_target_pairs={{0,128},{32,160},{64,192},{96,224},{128,0},{160,32},{192,64},{224,... | collective-permute-start | bytes 983048 | tf_op jit(solution)/shard_map/ppermute | solution.py:34
  87.8 7.2 %collective-permute-start.13 = (bf16[32,5120]{1,0:T(8,128)(2,1)S(1)}, bf16[32,5120]{1,0:T(8,128)(2,1)S(1)}, u32[]{:S(2)}, u32[]{:S(2)}) collective-permute-start(bf16[32,5120]{1,0:T(8,128)(2,1)S(1)} %add_convert_fusion.1), channel_id=1, source_target_pairs={{0,32},{32,64},{64,96},{96,0},{128,160},{160,192},{192,224},{224,1... | collective-permute-start | bytes 983048 | tf_op jit(solution)/shard_map/ppermute | solution.py:34
  95.9 30.1 %all-to-all-start.1 = ((bf16[32,40,128]{2,1,0:T(8,128)(2,1)}), bf16[32,40,128]{2,1,0:T(8,128)(2,1)}, u32[]{:S(2)}, u32[]{:S(2)}) async-start(bf16[32,40,128]{2,1,0:T(8,128)(2,1)} %bitcast.5), calls=%async_computation.1 | async-start | bytes 655360 | tf_op jit(solution)/shard_map/all_to_all | solution.py:422
  127.8 1.5 collective-permute-start.18
  129.3 3.7 %collective-permute-start.21 = (bf16[32,1280]{1,0:T(8,128)(2,1)S(1)}, bf16[32,1280]{1,0:T(8,128)(2,1)S(1)}, u32[]{:S(2)}, u32[]{:S(2)}) collective-permute-start(bf16[32,1280]{1,0:T(8,128)(2,1)S(1)} %add_convert_fusion.9), channel_id=1, source_target_pairs={{0,96},{1,25},{2,98},{3,27},{4,100},{5,29},{6,102},{7,31},{8,104},... | collective-permute-start | bytes 245768 | tf_op jit(solution)/shard_map/ppermute | solution.py:348
  130.2 5.1 %collective-permute-start.20 = (bf16[32,1280]{1,0:T(8,128)(2,1)S(1)}, bf16[32,1280]{1,0:T(8,128)(2,1)S(1)}, u32[]{:S(2)}, u32[]{:S(2)}) collective-permute-start(bf16[32,1280]{1,0:T(8,128)(2,1)S(1)} %add_convert_fusion.9), channel_id=1, source_target_pairs={{0,64},{1,17},{2,66},{3,19},{4,68},{5,21},{6,70},{7,23},{8,72},{9,... | collective-permute-start | bytes 245768 | tf_op jit(solution)/shard_map/ppermute | solution.py:348
  131.4 4.8 %collective-permute-start.19 = (bf16[32,1280]{1,0:T(8,128)(2,1)S(1)}, bf16[32,1280]{1,0:T(8,128)(2,1)S(1)}, u32[]{:S(2)}, u32[]{:S(2)}) collective-permute-start(bf16[32,1280]{1,0:T(8,128)(2,1)S(1)} %add_convert_fusion.9), channel_id=1, source_target_pairs={{0,32},{1,9},{2,34},{3,11},{4,36},{5,13},{6,38},{7,15},{8,40},{9,1... | collective-permute-start | bytes 245768 | tf_op jit(solution)/shard_map/ppermute | solution.py:348
  136.2 3.4 %collective-permute-start.24 = (bf16[32,1280]{1,0:T(8,128)(2,1)S(1)}, bf16[32,1280]{1,0:T(8,128)(2,1)S(1)}, u32[]{:S(2)}, u32[]{:S(2)}) collective-permute-start(bf16[32,1280]{1,0:T(8,128)(2,1)S(1)} %add_convert_fusion.8), channel_id=1, source_target_pairs={{0,24},{1,97},{2,26},{3,99},{4,28},{5,101},{6,30},{7,103},{8,0},{9... | collective-permute-start | bytes 245768 | tf_op jit(solution)/shard_map/ppermute | solution.py:348
  136.3 4.9 %collective-permute-start.23 = (bf16[32,1280]{1,0:T(8,128)(2,1)S(1)}, bf16[32,1280]{1,0:T(8,128)(2,1)S(1)}, u32[]{:S(2)}, u32[]{:S(2)}) collective-permute-start(bf16[32,1280]{1,0:T(8,128)(2,1)S(1)} %add_convert_fusion.8), channel_id=1, source_target_pairs={{0,16},{1,65},{2,18},{3,67},{4,20},{5,69},{6,22},{7,71},{8,24},{9,... | collective-permute-start | bytes 245768 | tf_op jit(solution)/shard_map/ppermute | solution.py:348
  136.4 5.7 %collective-permute-start.22 = (bf16[32,1280]{1,0:T(8,128)(2,1)S(1)}, bf16[32,1280]{1,0:T(8,128)(2,1)S(1)}, u32[]{:S(2)}, u32[]{:S(2)}) collective-permute-start(bf16[32,1280]{1,0:T(8,128)(2,1)S(1)} %add_convert_fusion.8), channel_id=1, source_target_pairs={{0,8},{1,33},{2,10},{3,35},{4,12},{5,37},{6,14},{7,39},{8,16},{9,4... | collective-permute-start | bytes 245768 | tf_op jit(solution)/shard_map/ppermute | solution.py:348
  142.1 3.4 %collective-permute-start.25 = (bf16[32,1280]{1,0:T(8,128)(2,1)S(1)}, bf16[32,1280]{1,0:T(8,128)(2,1)S(1)}, u32[]{:S(2)}, u32[]{:S(2)}) collective-permute-start(bf16[32,1280]{1,0:T(8,128)(2,1)S(1)} %add_convert_fusion.7), channel_id=1, source_target_pairs={{0,128},{32,160},{64,192},{96,224},{128,0},{160,32},{192,64},{224,... | collective-permute-start | bytes 245768 | tf_op jit(solution)/shard_map/ppermute | solution.py:34
  145.5 4.4 %collective-permute-start.28 = (bf16[32,1280]{1,0:T(8,128)(2,1)S(1)}, bf16[32,1280]{1,0:T(8,128)(2,1)S(1)}, u32[]{:S(2)}, u32[]{:S(2)}) collective-permute-start(bf16[32,1280]{1,0:T(8,128)(2,1)S(1)} %add_convert_fusion.6), channel_id=1, source_target_pairs={{0,6},{1,7},{2,0},{3,1},{4,2},{5,3},{6,4},{7,5},{8,14},{9,15},{10,... | collective-permute-start | bytes 245768 | tf_op jit(solution)/shard_map/ppermute | solution.py:48
  146.3 8.1 %collective-permute-start.27 = (bf16[32,1280]{1,0:T(8,128)(2,1)S(1)}, bf16[32,1280]{1,0:T(8,128)(2,1)S(1)}, u32[]{:S(2)}, u32[]{:S(2)}) collective-permute-start(bf16[32,1280]{1,0:T(8,128)(2,1)S(1)} %add_convert_fusion.6), channel_id=1, source_target_pairs={{0,4},{1,5},{2,6},{3,7},{4,0},{5,1},{6,2},{7,3},{8,12},{9,13},{10,... | collective-permute-start | bytes 245768 | tf_op jit(solution)/shard_map/ppermute | solution.py:48
  148.7 6.3 %collective-permute-start.26 = (bf16[32,1280]{1,0:T(8,128)(2,1)S(1)}, bf16[32,1280]{1,0:T(8,128)(2,1)S(1)}, u32[]{:S(2)}, u32[]{:S(2)}) collective-permute-start(bf16[32,1280]{1,0:T(8,128)(2,1)S(1)} %add_convert_fusion.6), channel_id=1, source_target_pairs={{0,2},{1,3},{2,4},{3,5},{4,6},{5,7},{6,0},{7,1},{8,10},{9,11},{10,... | collective-permute-start | bytes 245768 | tf_op jit(solution)/shard_map/ppermute | solution.py:48
  155.1 8.9 %collective-permute-start.29 = (bf16[32,1280]{1,0:T(8,128)(2,1)S(1)}, bf16[32,1280]{1,0:T(8,128)(2,1)S(1)}, u32[]{:S(2)}, u32[]{:S(2)}) collective-permute-start(bf16[32,1280]{1,0:T(8,128)(2,1)S(1)} %add_convert_fusion.5), channel_id=1, source_target_pairs={{0,1},{1,0},{2,3},{3,2},{4,5},{5,4},{6,7},{7,6},{8,9},{9,8},{10,11... | collective-permute-start | bytes 245768 | tf_op jit(solution)/shard_map/ppermute | solution.py:48
  (10 other events, 56.8 us)

commit v5 on v4

--- a/solution.py
+++ b/solution.py
@@ -14,7 +14,6 @@
 F32 = jnp.float32
 
 X, ZL, Y, ZH, CORE = 4, 2, 4, 4, 2
-OFFSETS = [(dz, dx) for dz in range(ZL) for dx in range(X)]
 
 
 def gelu_pair(pre_act):
@@ -48,38 +47,53 @@
     return lax.ppermute(value, "expert", pairs)
 
 
-def thirds(width):
-    tiles = width // 128
-    first = -(-tiles // 3) * 128
-    second = first + (tiles - first // 128 + 1) // 2 * 128
-    return (slice(0, first), slice(first, second), slice(second, width))
-
-
-def gather_blocks(mine):
-    blocks = {(0, 0): mine}
-    blocks[0, 1] = batch_fetch(mine, 0, 1)
-    blocks[0, 3] = batch_fetch(mine, 0, 3)
-    blocks[1, 0] = batch_fetch(mine, 1, 0)
-    blocks[0, 2] = batch_fetch(blocks[0, 1], 0, 1)
-    blocks[1, 3] = batch_fetch(blocks[1, 0], 0, 3)
-    blocks[1, 1] = batch_fetch(blocks[0, 1], 1, 0)
-    a, b, c = thirds(mine.shape[1])
-    blocks[1, 2] = jnp.concatenate(
-        [
-            batch_fetch(blocks[1, 1][:, a], 0, 1),
-            batch_fetch(blocks[1, 3][:, b], 0, 3),
-            batch_fetch(blocks[0, 2][:, c], 1, 0),
-        ],
-        axis=1,
-    )
-    return blocks
-
-
 def add(*terms):
     total = terms[0].astype(F32)
     for term in terms[1:]:
         total = total + term.astype(F32)
     return total.astype(BF16)
+
+
+def together(*values):
+    return lax.optimization_barrier(values)
+
+
+def gather_near(mine):
+    return batch_fetch(mine, 0, 1), batch_fetch(mine, 0, 3), batch_fetch(mine, 1, 0)
+
+
+def gather_next(near):
+    b01, b03, b10 = near
+    return batch_fetch(b01, 0, 1), batch_fetch(b10, 0, 3), batch_fetch(b01, 1, 0)
+
+
+def gather_far(nexts, side):
+    b02, b13, b11 = nexts
+    return batch_fetch(b11, 0, 1) if side == 0 else batch_fetch(b13, 0, 3)
+
+
+def by_offset(mine, near, nexts, far):
+    return [mine, near[0], nexts[0], near[1], near[2], nexts[2], far, nexts[1]]
+
+
+def scatter_far(parts, side):
+    p00, p01, p02, p03, p10, p11, p12, p13 = parts
+    return batch_send(p12, 0, 1 if side == 0 else 3), batch_send(p03, 0, 3)
+
+
+def scatter_next(parts, got, side):
+    p00, p01, p02, p03, p10, p11, p12, p13 = parts
+    if side == 0:
+        p11 = add(p11, got)
+    else:
+        p13 = add(p13, got)
+    return batch_send(p02, 0, 1), batch_send(p13, 0, 3), batch_send(p11, 1, 0)
+
+
+def scatter_near(parts, got):
+    p01 = add(parts[1], got[0], got[2])
+    p10 = add(parts[4], got[1])
+    return batch_send(p01, 0, 1), batch_send(p10, 1, 0)
 
 
 LANES = 128
@@ -159,24 +173,29 @@
     rows_ref[...] = flat_ref[...].astype(BF16)
 
 
-def unpack_kernel(flat_in_ref, out_ref, flat_ref):
-    groups = out_ref.shape[0]
-    stride = out_ref.shape[1] // LANES
+def unpack_kernel(flat_in_ref, ins_ref, cots_ref, flat_ref):
+    groups = ins_ref.shape[0]
+    tiles = ins_ref.shape[1] // LANES
     flat_ref[...] = flat_in_ref[...].astype(F32)
-    for c in range(stride):
-        out_ref[:, c * LANES : (c + 1) * LANES] = flat_ref[
-            pl.ds(c, groups, stride=stride), :
-        ].astype(BF16)
-
-
-def pack_sum_kernel(a_ref, b_ref, c_ref, d_ref, out_ref, flat_ref):
-    groups = a_ref.shape[0]
-    stride = a_ref.shape[1] // LANES
-    for c in range(stride):
-        cols = slice(c * LANES, (c + 1) * LANES)
-        total = a_ref[:, cols].astype(F32) + b_ref[:, cols].astype(F32)
-        total = total + c_ref[:, cols].astype(F32) + d_ref[:, cols].astype(F32)
-        flat_ref[pl.ds(c, groups, stride=stride), :] = total
+    for kind, out_ref in enumerate((ins_ref, cots_ref)):
+        for c in range(tiles):
+            out_ref[:, c * LANES : (c + 1) * LANES] = flat_ref[
+                pl.ds(kind * tiles + c, groups, stride=2 * tiles), :
+            ].astype(BF16)
+
+
+def pack_sum_kernel(*refs):
+    out_ref, flat_ref = refs[-2:]
+    groups = refs[0].shape[0]
+    tiles = refs[0].shape[1] // LANES
+    for kind in range(2):
+        terms = refs[4 * kind : 4 * kind + 4]
+        for c in range(tiles):
+            cols = slice(c * LANES, (c + 1) * LANES)
+            total = terms[0][:, cols].astype(F32)
+            for term in terms[1:]:
+                total = total + term[:, cols].astype(F32)
+            flat_ref[pl.ds(kind * tiles + c, groups, stride=2 * tiles), :] = total
     out_ref[...] = flat_ref[...].astype(BF16)
 
 
@@ -211,66 +230,79 @@
     par_ref[...] = jnp.dot(logits_grad, tok_ref[...], preferred_element_type=F32).astype(BF16)
 
 
-def expert_kernel(count, each, *refs):
+def gathered(blocks, j, width):
+    return jnp.concatenate([b[:, j * width : (j + 1) * width] for b in blocks], axis=0)
+
+
+def spread(parts, value, j, width):
+    value = value.astype(BF16)
+    groups = parts[0].shape[0]
+    for i, part in enumerate(parts):
+        part[:, j * width : (j + 1) * width] = value[i * groups : (i + 1) * groups]
+
+
+def wait_all(copies):
+    for copy in copies:
+        copy.wait()
+
+
+def forward_kernel(count, each, *refs):
     blocks, (win_hbm, wout_hbm) = refs[:count], refs[count : count + 2]
     parts = refs[count + 2 : 2 * count + 2]
-    act_ref, pre_ref, win_ref, wout_ref, sems = refs[2 * count + 2 :]
-    loads = [
-        (
-            start_loads(win_hbm.at[j], win_ref.at[j], sems.at[0, j]),
-            start_loads(wout_hbm.at[j], wout_ref.at[j], sems.at[1, j]),
-        )
-        for j in range(each)
-    ]
-    groups = blocks[0].shape[0]
+    act_ref, slope_ref, win_ref, wout_ref, sems = refs[2 * count + 2 :]
     width, hidden = win_ref.shape[1:]
-
-    def gathered(kind, j):
-        cols = slice((kind * each + j) * width, (kind * each + j + 1) * width)
-        return jnp.concatenate([block[:, cols] for block in blocks], axis=0)
-
-    def spread(value, kind, j):
-        cols = slice((kind * each + j) * width, (kind * each + j + 1) * width)
-        value = value.astype(BF16)
-        for i, part in enumerate(parts):
-            part[:, cols] = value[i * groups : (i + 1) * groups]
-
+    win_loads = [start_loads(win_hbm.at[j], win_ref.at[j], sems.at[0, j]) for j in range(each)]
+    wout_loads = [start_loads(wout_hbm.at[j], wout_ref.at[j], sems.at[1, j]) for j in range(each)]
     for j in range(each):
         hid = slice(j * hidden, (j + 1) * hidden)
-        for copy in loads[j][0]:
-            copy.wait()
-        pre_act = jnp.dot(gathered(0, j), win_ref[j], preferred_element_type=F32)
-        gelu_value, gelu_slope = gelu_pair(pre_act)
-        activation = gelu_value.astype(BF16)
-        act_ref[:, hid] = activation
-        for copy in loads[j][1]:
-            copy.wait()
-        spread(jnp.dot(activation, wout_ref[j], preferred_element_type=F32), 0, j)
-        pre_grad = (nt(gathered(1, j), wout_ref[j]) * gelu_slope).astype(BF16)
-        pre_ref[:, hid] = pre_grad
-        spread(nt(pre_grad, win_ref[j]), 1, j)
-
-
-def expert_step(blocks, weight_in, weight_out):
+        wait_all(win_loads[j])
+        pre_act = jnp.dot(gathered(blocks, j, width), win_ref[j], preferred_element_type=F32)
+        gelu_value, slope_ref[:, hid] = gelu_pair(pre_act)
+        act_ref[:, hid] = gelu_value.astype(BF16)
+    for j in range(each):
+        hid = slice(j * hidden, (j + 1) * hidden)
+        wait_all(wout_loads[j])
+        spread(parts, jnp.dot(act_ref[:, hid], wout_ref[j], preferred_element_type=F32), j, width)
+
+
+def backward_kernel(count, each, *refs):
+    blocks, (slope_ref, win_hbm, wout_hbm) = refs[:count], refs[count : count + 3]
+    parts = refs[count + 3 : 2 * count + 3]
+    pre_ref, win_ref, wout_ref, sems = refs[2 * count + 3 :]
+    width, hidden = win_ref.shape[1:]
+    wout_loads = [start_loads(wout_hbm.at[j], wout_ref.at[j], sems.at[1, j]) for j in range(each)]
+    win_loads = [start_loads(win_hbm.at[j], win_ref.at[j], sems.at[0, j]) for j in range(each)]
+    for j in range(each):
+        hid = slice(j * hidden, (j + 1) * hidden)
+        wait_all(wout_loads[j])
+        act_grad = nt(gathered(blocks, j, width), wout_ref[j])
+        pre_ref[:, hid] = (act_grad * slope_ref[:, hid]).astype(BF16)
+    for j in range(each):
+        hid = slice(j * hidden, (j + 1) * hidden)
+        wait_all(win_loads[j])
+        spread(parts, nt(pre_ref[:, hid], win_ref[j]), j, width)
+
+
+def expert_step(kernel, name, blocks, extra, kept, weight_in, weight_out):
     count = len(blocks)
     each, width, hidden = weight_in.shape
     rows = count * blocks[0].shape[0]
-    kept = jax.ShapeDtypeStruct((rows, each * hidden), BF16)
+    in_vmem, hbm = pl.BlockSpec(memory_space=pltpu.VMEM), pl.BlockSpec(memory_space=pltpu.HBM)
     outs = local_kernel(
-        functools.partial(expert_kernel, count, each),
-        [jax.ShapeDtypeStruct(b.shape, BF16) for b in blocks] + [kept, kept],
+        functools.partial(kernel, count, each),
+        [jax.ShapeDtypeStruct(b.shape, BF16) for b in blocks]
+        + [jax.ShapeDtypeStruct((rows, each * hidden), t) for t in kept],
         [
             pltpu.VMEM(weight_in.shape, BF16),
             pltpu.VMEM(weight_out.shape, BF16),
             pltpu.SemaphoreType.DMA((2, each, PIECES)),
         ],
-        8 * rows * each * width * hidden,
-        4 * each * width * hidden + 8 * rows * each * width,
-        "expert",
-        in_specs=[pl.BlockSpec(memory_space=pltpu.VMEM)] * count
-        + [pl.BlockSpec(memory_space=pltpu.HBM)] * 2,
-    )(*blocks, in_hbm(weight_in), in_hbm(weight_out))
-    return outs[:count], outs[count], outs[count + 1]
+        4 * rows * each * width * hidden,
+        4 * each * width * hidden + 4 * rows * each * width,
+        name,
+        in_specs=[in_vmem] * (count + len(extra)) + [hbm] * 2,
+    )(*blocks, *extra, in_hbm(weight_in), in_hbm(weight_out))
+    return outs[:count], *outs[count:]
 
 
 def weights_kernel(count, kept, *refs):
@@ -285,9 +317,9 @@
     gout_ref[0] = tn(whole(acts), whole(rows_cot)).astype(BF16)
 
 
-def weight_gradients(blocks, acts, pres, each, width, hidden):
-    count, kept, cuts = len(blocks), len(acts), 2
-    groups = blocks[0].shape[0]
+def weight_gradients(ins, cots, acts, pres, each, width, hidden):
+    count, kept, cuts = len(ins), len(acts), 2
+    groups = ins[0].shape[0]
     rows = count * groups
     return local_kernel(
         functools.partial(weights_kernel, count, kept),
@@ -301,35 +333,14 @@
         "weight_grads",
         grid=(each, cuts),
         in_specs=[pl.BlockSpec((groups, width // cuts), lambda e, i: (0, e * cuts + i))] * count
-        + [pl.BlockSpec((groups, width), lambda e, i: (0, each + e))] * count
+        + [pl.BlockSpec((groups, width), lambda e, i: (0, e))] * count
         + [pl.BlockSpec((a.shape[0], hidden // cuts), lambda e, i: (0, e * cuts + i)) for a in acts]
         + [pl.BlockSpec((p.shape[0], hidden), lambda e, i: (0, e)) for p in pres],
         out_specs=(
             pl.BlockSpec((1, width // cuts, hidden), lambda e, i: (e, i, 0)),
             pl.BlockSpec((1, hidden // cuts, width), lambda e, i: (e, i, 0)),
         ),
-    )(*blocks, *blocks, *acts, *pres)
-
-
-def scatter_blocks(parts):
-    a, b, c = thirds(parts[0, 0].shape[1])
-    far = parts[1, 2]
-    got_a = batch_send(far[:, a], 0, 1)
-    got_b = batch_send(far[:, b], 0, 3)
-    got_c = batch_send(far[:, c], 1, 0)
-
-    def add_cols(part, got, cols):
-        return jnp.concatenate(
-            [part[:, : cols.start], add(part[:, cols], got), part[:, cols.stop :]], axis=1
-        )
-
-    got_11 = batch_send(add_cols(parts[1, 1], got_a, a), 1, 0)
-    got_13 = batch_send(add_cols(parts[1, 3], got_b, b), 0, 3)
-    got_02 = batch_send(add_cols(parts[0, 2], got_c, c), 0, 1)
-    got_01 = batch_send(add(parts[0, 1], got_11, got_02), 0, 1)
-    got_03 = batch_send(parts[0, 3], 0, 3)
-    got_10 = batch_send(add(parts[1, 0], got_13), 1, 0)
-    return parts[0, 0], got_01, got_03, got_10
+    )(*ins, *cots, *acts, *pres)
 
 
 def crossed_send(value, step, turn):
@@ -397,19 +408,44 @@
         rows.reshape(groups, 2 * each * tiles, LANES), "expert", split_axis=0, concat_axis=0,
         tiled=True,
     ).reshape(flat, LANES)
-    mine = local_kernel(
+    half_shape = jax.ShapeDtypeStruct((groups, each * width), BF16)
+    ins, cots = local_kernel(
         unpack_kernel,
-        jax.ShapeDtypeStruct((groups, 2 * each * width), BF16),
+        (half_shape, half_shape),
         [pltpu.VMEM((flat, LANES), F32)],
         0,
         4 * flat * LANES,
         "unpack",
     )(routed)
-    blocks = gather_blocks(mine)
-    blocks = [blocks[o] for o in OFFSETS]
-    partial, act, pre = expert_step(blocks, weight_in, weight_out)
-    parts = dict(zip(OFFSETS, partial))
-    share = scatter_blocks(parts)
+    near_a = gather_near(ins)
+    near_b = gather_near(cots)
+    near_a = together(*near_a)
+    next_a = gather_next(near_a)
+    near_b = together(*near_b)
+    next_b = gather_next(near_b)
+    next_a = together(*next_a)
+    far_a = gather_far(next_a, 0)
+    next_b = together(*next_b)
+    far_b = gather_far(next_b, 1)
+    blocks_a = by_offset(ins, near_a, next_a, far_a)
+    blocks_b = by_offset(cots, near_b, next_b, far_b)
+    parts_a, act, slope = expert_step(
+        forward_kernel, "expert_forward", blocks_a, [], [BF16, F32], weight_in, weight_out
+    )
+    got_a, near_from_a = scatter_far(parts_a, 0)
+    parts_b, pre = expert_step(
+        backward_kernel, "expert_backward", blocks_b, [slope], [BF16], weight_in, weight_out
+    )
+    got_b, near_from_b = scatter_far(parts_b, 1)
+    got_a, near_from_a = together(got_a, near_from_a)
+    next_got_a = scatter_next(parts_a, got_a, 0)
+    got_b, near_from_b = together(got_b, near_from_b)
+    next_got_b = scatter_next(parts_b, got_b, 1)
+    next_got_a = together(*next_got_a)
+    near_got_a = scatter_near(parts_a, next_got_a)
+    next_got_b = together(*next_got_b)
+    near_got_b = scatter_near(parts_b, next_got_b)
+    share = (parts_a[0], near_from_a, *near_got_a, parts_b[0], near_from_b, *near_got_b)
     packed = local_kernel(
         pack_sum_kernel,
         flat_shape,
@@ -424,7 +460,7 @@
         tiled=True,
     ).reshape(flat, LANES)
     hidden = weight_in.shape[2]
-    weight_grads = weight_gradients(blocks, [act], [pre], each, width, hidden)
+    weight_grads = weight_gradients(blocks_a, blocks_b, [act], [pre], each, width, hidden)
     back, weight_grads = lax.optimization_barrier((back, weight_grads))
     row_shape = jax.ShapeDtypeStruct((slots, width), BF16)
     slot_in_grad, logits_grad, local_params = local_kernel(

time: 165 us -> 157 us (0.952)
  waiting for transfers between devices: 60.7 us -> 36.8 us
  starting transfers between devices: 53.3 us -> 62.8 us
  local copies, waits for them, and re-layouts: 4.21 us -> 8.94 us
    ppermute x19 -> x29, waiting for transfers between devices: 37.1 us -> 16.8 us  [batch_send(): return lax.ppermute(value, 'batch', pairs)]
    ppermute x19 -> x29, starting transfers between devices: 22.8 us -> 31.8 us  [batch_send(): return lax.ppermute(value, 'batch', pairs)]
    unnamed x24 -> x38, local copies, waits for them, and re-layouts: 4.08 us -> 8.93 us
    all_to_all x1, waiting for transfers between devices: 6.83 us -> 4.04 us  [body(): lax.all_to_all(packed.reshape(groups, 2 * each * tiles, LANES), 'expert',...]
    pallas_call x2 -> x3, Pallas kernels: 5.93 us -> 8.08 us  [the longest x2 7.91 us: expert_step(): local_kernel(functools.partial(kernel, count, each), [jax.ShapeDtypeStruc...]
    all_to_all x1, starting transfers between devices: 15.2 us -> 13.1 us  [body(): lax.all_to_all(packed.reshape(groups, 2 * each * tiles, LANES), 'expert',...]
    ppermute x6, starting transfers between devices: 3.74 us -> 5.67 us  [crossed_send(): return lax.ppermute(value, ('batch', 'expert'), pairs)]
  transfers between devices with their start and end apart: 31 -> 41, of which waited for: 23 -> 25; matrix products, arithmetic and copies ran while one was open for 1% -> 1% of each run, Pallas kernels for 2% -> 8%
where the time goes in v5:
time: 157 us; the launch traced here: 156 us
  starting transfers between devices  62.8 us (40%)
  waiting for transfers between devices  36.8 us (23%)
  blocking collectives  27.3 us (17%)
  Pallas kernels  16.5 us (11%)
  local copies, waits for them, and re-layouts  8.94 us (6%)
    ppermute x29, starting transfers between devices, batch_send(): return lax.ppermute(value, 'batch', pairs)  31.8 us
    all_to_all x1, blocking collectives, body(): lax.all_to_all(rows.reshape(groups, 2 * each * tiles, LANES), 'expert', s...  27.3 us
    ppermute x29, waiting for transfers between devices, batch_send(): return lax.ppermute(value, 'batch', pairs)  16.8 us
    all_to_all x1, starting transfers between devices, body(): lax.all_to_all(packed.reshape(groups, 2 * each * tiles, LANES), 'expert',...  13.1 us
    ppermute x5, starting transfers between devices, expert_send(): return lax.ppermute(value, 'expert', pairs)  12.3 us
    unnamed x38, local copies, waits for them, and re-layouts  8.93 us
    ppermute x6, waiting for transfers between devices, crossed_send(): return lax.ppermute(value, ('batch', 'expert'), pairs)  8.76 us
    pallas_call x2, Pallas kernels, expert_step(): local_kernel(functools.partial(kernel, count, each), [jax.ShapeDtypeStruc...  7.91 us
  transfers between devices with their start and end apart: 41, of which 25 were waited for; matrix products, arithmetic and copies ran while one was open for 1% of the time, Pallas kernels for 8%

profile of v5, /device:TPU:1, one launch (start us, length us, event | category | flops | bytes accessed | tf_op | source)
XLA Modules:
  0.0 156.0 jit_solution(14675130449625327465)
XLA Ops:
  0.6 2.6 %front.1 = (bf16[1280,128]{1,0:T(8,128)(2,1)S(1)}, f32[64,256]{1,0:T(8,128)S(1)}, f32[64,256]{1,0:T(8,128)S(1)}) custom-call(bf16[256,1280]{1,0:T(8,128)(2,1)} %bitcast.13, bf16[256,1280]{1,0:T(8,128)(2,1)} %bitcast.15, bf16[64,1280]{1,0:T(8,128)(2,1)} %bitcast.20), custom_call_target="tpu_custom_call" | custom-call | flops 125829120 | bytes 1638400 | tf_op jit(solution)/shard_map/front/pallas_call | solution.py:391
  3.9 27.3 %all_to_all.10 = bf16[32,40,128]{2,1,0:T(8,128)(2,1)S(1)} all-to-all(bf16[32,40,128]{2,1,0:T(8,128)(2,1)S(1)} %bitcast.19), channel_id=1, replica_groups=mesh['batch'=8,'expert'=32] {'expert'}, dimensions={0} | all-to-all | bytes 655360 | tf_op jit(solution)/shard_map/all_to_all | solution.py:407
  31.4 2.6 %collective-permute-start = (bf16[32,2560]{1,0:T(8,128)(2,1)S(1)}, bf16[32,2560]{1,0:T(8,128)(2,1)S(1)}, u32[]{:S(2)}, u32[]{:S(2)}) collective-permute-start(bf16[32,2560]{1,0:T(8,128)(2,1)S(1)} %get-tuple-element.64.refs_0_), channel_id=1, source_target_pairs={{0,96},{32,0},{64,32},{96,64},{128,224},{160,128},{192,160},{224,1... | collective-permute-start | bytes 491528 | tf_op jit(solution)/shard_map/ppermute | solution.py:33
  34.9 2.7 %collective-permute-start.14 = (bf16[32,2560]{1,0:T(8,128)(2,1)S(1)}, bf16[32,2560]{1,0:T(8,128)(2,1)S(1)}, u32[]{:S(2)}, u32[]{:S(2)}) collective-permute-start(bf16[32,2560]{1,0:T(8,128)(2,1)S(1)} %get-tuple-element.84.refs_0_.refs_8_), channel_id=1, source_target_pairs={{0,96},{32,0},{64,32},{96,64},{128,224},{160,128},{192,160},{224,1... | collective-permute-start | bytes 491528 | tf_op jit(solution)/shard_map/ppermute | solution.py:33
  38.2 1.9 %collective-permute-done.1.refs_3_ = bf16[32,2560]{1,0:T(8,128)(2,1)S(1)} collective-permute-done((bf16[32,2560]{1,0:T(8,128)(2,1)S(1)}, bf16[32,2560]{1,0:T(8,128)(2,1)S(1)}, u32[]{:S(2)}, u32[]{:S(2)}) %collective-permute-start.1) | collective-permute-done | bytes 163872 | tf_op jit(solution)/shard_map/ppermute | solution.py:33
  40.1 1.5 collective-permute-start.3
  42.9 2.3 %collective-permute-start.17 = (bf16[32,2560]{1,0:T(8,128)(2,1)S(1)}, bf16[32,2560]{1,0:T(8,128)(2,1)S(1)}, u32[]{:S(2)}, u32[]{:S(2)}) collective-permute-start(bf16[32,2560]{1,0:T(8,128)(2,1)S(1)} %collective-permute-done.14.refs_1_.refs_9_), channel_id=1, source_target_pairs={{0,96},{32,0},{64,32},{96,64},{128,224},{160,128},{192,160},{224,1... | collective-permute-start | bytes 491528 | tf_op jit(solution)/shard_map/ppermute | solution.py:33
  47.0 1.8 %collective-permute-start.6 = (bf16[32,2560]{1,0:T(8,128)(2,1)S(1)}, bf16[32,2560]{1,0:T(8,128)(2,1)S(1)}, u32[]{:S(2)}, u32[]{:S(2)}) collective-permute-start(bf16[32,2560]{1,0:T(8,128)(2,1)S(1)} %collective-permute-done.5.refs_5_), channel_id=1, source_target_pairs={{0,96},{32,0},{64,32},{96,64},{128,224},{160,128},{192,160},{224,1... | collective-permute-start | bytes 491528 | tf_op jit(solution)/shard_map/ppermute | solution.py:33
  48.8 2.5 %collective-permute-done.18.refs_7_.refs_15_ = bf16[32,2560]{1,0:T(8,128)(2,1)S(1)} collective-permute-done((bf16[32,2560]{1,0:T(8,128)(2,1)S(1)}, bf16[32,2560]{1,0:T(8,128)(2,1)S(1)}, u32[]{:S(2)}, u32[]{:S(2)}) %collective-permute-start.18) | collective-permute-done | bytes 163872 | tf_op jit(solution)/shard_map/ppermute | solution.py:33
  52.3 4.1 %expert_forward.1 = (bf16[32,2560]{1,0:T(8,128)(2,1)S(1)}, bf16[32,2560]{1,0:T(8,128)(2,1)S(1)}, bf16[32,2560]{1,0:T(8,128)(2,1)S(1)}, bf16[32,2560]{1,0:T(8,128...) custom-call(bf16[32,2560]{1,0:T(8,128)(2,1)S(1)} %get-tuple-element., ...), custom_call_target="tpu_custom_call" | custom-call | flops 1342177280 | bytes 7864320 | tf_op jit(solution)/shard_map/expert_forward/pallas_call | solution.py:291
  57.9 2.4 %collective-permute-start.8 = (bf16[32,2560]{1,0:T(8,128)(2,1)S(1)}, bf16[32,2560]{1,0:T(8,128)(2,1)S(1)}, u32[]{:S(2)}, u32[]{:S(2)}) collective-permute-start(bf16[32,2560]{1,0:T(8,128)(2,1)S(1)} %get-tuple-element.73), channel_id=1, source_target_pairs={{0,96},{32,0},{64,32},{96,64},{128,224},{160,128},{192,160},{224,1... | collective-permute-start | bytes 491528 | tf_op jit(solution)/shard_map/ppermute | solution.py:33
  60.3 2.7 %collective-permute-start.10 = (bf16[32,2560]{1,0:T(8,128)(2,1)S(1)}, bf16[32,2560]{1,0:T(8,128)(2,1)S(1)}, u32[]{:S(2)}, u32[]{:S(2)}) collective-permute-start(bf16[32,2560]{1,0:T(8,128)(2,1)S(1)} %get-tuple-element.77), channel_id=1, source_target_pairs={{0,96},{32,0},{64,32},{96,64},{128,224},{160,128},{192,160},{224,1... | collective-permute-start | bytes 491528 | tf_op jit(solution)/shard_map/ppermute | solution.py:33
  63.0 3.8 %expert_backward.1 = (bf16[32,2560]{1,0:T(8,128)(2,1)S(1)}, bf16[32,2560]{1,0:T(8,128)(2,1)S(1)}, bf16[32,2560]{1,0:T(8,128)(2,1)S(1)}, bf16[32,2560]{1,0:T(8,12...) custom-call(bf16[32,2560]{1,0:T(8,128)(2,1)S(1)} %get-tuple-element., ...), custom_call_target="tpu_custom_call" | custom-call | flops 1342177280 | bytes 7864320 | tf_op jit(solution)/shard_map/expert_backward/pallas_call | solution.py:291
  67.3 1.4 collective-permute-start.23
  68.7 2.4 %collective-permute-done.21 = bf16[32,2560]{1,0:T(8,128)(2,1)S(1)} collective-permute-done((bf16[32,2560]{1,0:T(8,128)(2,1)S(1)}, bf16[32,2560]{1,0:T(8,128)(2,1)S(1)}, u32[]{:S(2)}, u32[]{:S(2)}) %collective-permute-start.21) | collective-permute-done | bytes 163872 | tf_op jit(solution)/shard_map/ppermute | solution.py:33
  73.5 3.2 %collective-permute-start.24 = (bf16[32,2560]{1,0:T(8,128)(2,1)S(1)}, bf16[32,2560]{1,0:T(8,128)(2,1)S(1)}, u32[]{:S(2)}, u32[]{:S(2)}) collective-permute-start(bf16[32,2560]{1,0:T(8,128)(2,1)S(1)} %add_convert_fusion.2), channel_id=1, source_target_pairs={{0,96},{32,0},{64,32},{96,64},{128,224},{160,128},{192,160},{224,1... | collective-permute-start | bytes 491528 | tf_op jit(solution)/shard_map/ppermute | solution.py:33
  80.0 1.6 collective-permute-start.26
  83.7 1.8 %collective-permute-done.26.refs_6_ = bf16[32,2560]{1,0:T(8,128)(2,1)S(1)} collective-permute-done((bf16[32,2560]{1,0:T(8,128)(2,1)S(1)}, bf16[32,2560]{1,0:T(8,128)(2,1)S(1)}, u32[]{:S(2)}, u32[]{:S(2)}) %collective-permute-start.26) | collective-permute-done | bytes 163872 | tf_op jit(solution)/shard_map/ppermute | solution.py:33
  85.5 1.4 collective-permute-done.27.refs_7_
  87.8 13.1 %all-to-all-start.1 = ((bf16[32,40,128]{2,1,0:T(8,128)(2,1)}), bf16[32,40,128]{2,1,0:T(8,128)(2,1)S(1)}, u32[]{:S(2)}, u32[]{:S(2)}) async-start(bf16[32,40,128]{2,1,0:T(8,128)(2,1)} %bitcast.5), calls=%async_computation.1 | async-start | bytes 655360 | tf_op jit(solution)/shard_map/all_to_all | solution.py:458
  107.6 4.0 %weight_grads.1 = (bf16[2,1280,512]{2,1,0:T(8,128)(2,1)}, bf16[2,512,1280]{2,1,0:T(8,128)(2,1)}) custom-call(bf16[32,2560]{1,0:T(8,128)(2,1)S(1)} %get-tuple-element.64.refs_0_, bf16[32,2560]{1,0:T(8,128)(2,1)S(1)} %collective-permute-done.refs_1_, bf16[32,2560]{1,0:T(8,128)(2,1)S(1)} %collective-permute-done.3.refs_2_, ...), custom_call_target="tpu_custom_call" | custom-call | flops 1342177280 | bytes 10485760 | tf_op jit(solution)/shard_map/weight_grads/pallas_call | solution.py:324
  111.7 4.0 %all-to-all-done.1 = bf16[32,40,128]{2,1,0:T(8,128)(2,1)S(1)} async-done(((bf16[32,40,128]{2,1,0:T(8,128)(2,1)}), bf16[32,40,128]{2,1,0:T(8,128)(2,1)S(1)}, u32[]{:S(2)}, u32[]{:S(2)}) %all-to-all-start.1) | async-done | bytes 327712 | tf_op jit(solution)/shard_map/all_to_all | solution.py:458
  119.7 1.3 collective-permute-start.30
  121.4 1.5 collective-permute-done.31
  122.8 1.7 %collective-permute-done.30 = bf16[32,1280]{1,0:T(8,128)(2,1)S(1)} collective-permute-done((bf16[32,1280]{1,0:T(8,128)(2,1)S(1)}, bf16[32,1280]{1,0:T(8,128)(2,1)S(1)}, u32[]{:S(2)}, u32[]{:S(2)}) %collective-permute-start.30) | collective-permute-done | bytes 81952 | tf_op jit(solution)/shard_map/ppermute | solution.py:359
  125.6 2.4 %collective-permute-start.34 = (bf16[32,1280]{1,0:T(8,128)(2,1)S(1)}, bf16[32,1280]{1,0:T(8,128)(2,1)S(1)}, u32[]{:S(2)}, u32[]{:S(2)}) collective-permute-start(bf16[32,1280]{1,0:T(8,128)(2,1)S(1)} %add_convert_fusion.9), channel_id=1, source_target_pairs={{0,24},{1,97},{2,26},{3,99},{4,28},{5,101},{6,30},{7,103},{8,0},{9... | collective-permute-start | bytes 245768 | tf_op jit(solution)/shard_map/ppermute | solution.py:359
  129.5 3.4 %collective-permute-done.33 = bf16[32,1280]{1,0:T(8,128)(2,1)S(1)} collective-permute-done((bf16[32,1280]{1,0:T(8,128)(2,1)S(1)}, bf16[32,1280]{1,0:T(8,128)(2,1)S(1)}, u32[]{:S(2)}, u32[]{:S(2)}) %collective-permute-start.33) | collective-permute-done | bytes 81952 | tf_op jit(solution)/shard_map/ppermute | solution.py:359
  135.7 1.7 %collective-permute-done.35 = bf16[32,1280]{1,0:T(8,128)(2,1)S(1)} collective-permute-done((bf16[32,1280]{1,0:T(8,128)(2,1)S(1)}, bf16[32,1280]{1,0:T(8,128)(2,1)S(1)}, u32[]{:S(2)}, u32[]{:S(2)}) %collective-permute-start.35) | collective-permute-done | bytes 81952 | tf_op jit(solution)/shard_map/ppermute | solution.py:33
  138.1 3.4 %collective-permute-start.37 = (bf16[32,1280]{1,0:T(8,128)(2,1)S(1)}, bf16[32,1280]{1,0:T(8,128)(2,1)S(1)}, u32[]{:S(2)}, u32[]{:S(2)}) collective-permute-start(bf16[32,1280]{1,0:T(8,128)(2,1)S(1)} %add_convert_fusion.7), channel_id=1, source_target_pairs={{0,4},{1,5},{2,6},{3,7},{4,0},{5,1},{6,2},{7,3},{8,12},{9,13},{10,... | collective-permute-start | bytes 245768 | tf_op jit(solution)/shard_map/ppermute | solution.py:47
  142.5 3.0 %collective-permute-done.37 = bf16[32,1280]{1,0:T(8,128)(2,1)S(1)} collective-permute-done((bf16[32,1280]{1,0:T(8,128)(2,1)S(1)}, bf16[32,1280]{1,0:T(8,128)(2,1)S(1)}, u32[]{:S(2)}, u32[]{:S(2)}) %collective-permute-start.37) | collective-permute-done | bytes 81952 | tf_op jit(solution)/shard_map/ppermute | solution.py:47
  145.5 2.2 %collective-permute-done.36 = bf16[32,1280]{1,0:T(8,128)(2,1)S(1)} collective-permute-done((bf16[32,1280]{1,0:T(8,128)(2,1)S(1)}, bf16[32,1280]{1,0:T(8,128)(2,1)S(1)}, u32[]{:S(2)}, u32[]{:S(2)}) %collective-permute-start.36) | collective-permute-done | bytes 81952 | tf_op jit(solution)/shard_map/ppermute | solution.py:47
  147.7 6.7 %collective-permute-start.39 = (bf16[32,1280]{1,0:T(8,128)(2,1)S(1)}, bf16[32,1280]{1,0:T(8,128)(2,1)S(1)}, u32[]{:S(2)}, u32[]{:S(2)}) collective-permute-start(bf16[32,1280]{1,0:T(8,128)(2,1)S(1)} %add_convert_fusion.6), channel_id=1, source_target_pairs={{0,1},{1,0},{2,3},{3,2},{4,5},{5,4},{6,7},{7,6},{8,9},{9,8},{10,11... | collective-permute-start | bytes 245768 | tf_op jit(solution)/shard_map/ppermute | solution.py:47
  (112 shorter events, 36.9 us)
Async XLA Ops:
  31.4 6.2 %collective-permute-start = (bf16[32,2560]{1,0:T(8,128)(2,1)S(1)}, bf16[32,2560]{1,0:T(8,128)(2,1)S(1)}, u32[]{:S(2)}, u32[]{:S(2)}) collective-permute-start(bf16[32,2560]{1,0:T(8,128)(2,1)S(1)} %get-tuple-element.64.refs_0_), channel_id=1, source_target_pairs={{0,96},{32,0},{64,32},{96,64},{128,224},{160,128},{192,160},{224,1... | collective-permute-start | bytes 491528 | tf_op jit(solution)/shard_map/ppermute | solution.py:33
  33.9 6.2 %collective-permute-start.1 = (bf16[32,2560]{1,0:T(8,128)(2,1)S(1)}, bf16[32,2560]{1,0:T(8,128)(2,1)S(1)}, u32[]{:S(2)}, u32[]{:S(2)}) collective-permute-start(bf16[32,2560]{1,0:T(8,128)(2,1)S(1)} %get-tuple-element.64.refs_0_), channel_id=1, source_target_pairs={{0,32},{32,64},{64,96},{96,0},{128,160},{160,192},{192,224},{224,1... | collective-permute-start | bytes 491528 | tf_op jit(solution)/shard_map/ppermute | solution.py:33
  33.9 6.2 %collective-permute-start.2 = (bf16[32,2560]{1,0:T(8,128)(2,1)S(1)}, bf16[32,2560]{1,0:T(8,128)(2,1)S(1)}, u32[]{:S(2)}, u32[]{:S(2)}) collective-permute-start(bf16[32,2560]{1,0:T(8,128)(2,1)S(1)} %get-tuple-element.64.refs_0_), channel_id=1, source_target_pairs={{0,128},{32,160},{64,192},{96,224},{128,0},{160,32},{192,64},{224,... | collective-permute-start | bytes 491528 | tf_op jit(solution)/shard_map/ppermute | solution.py:33
  34.9 6.8 %collective-permute-start.14 = (bf16[32,2560]{1,0:T(8,128)(2,1)S(1)}, bf16[32,2560]{1,0:T(8,128)(2,1)S(1)}, u32[]{:S(2)}, u32[]{:S(2)}) collective-permute-start(bf16[32,2560]{1,0:T(8,128)(2,1)S(1)} %get-tuple-element.84.refs_0_.refs_8_), channel_id=1, source_target_pairs={{0,96},{32,0},{64,32},{96,64},{128,224},{160,128},{192,160},{224,1... | collective-permute-start | bytes 491528 | tf_op jit(solution)/shard_map/ppermute | solution.py:33
  37.6 5.4 %collective-permute-start.15 = (bf16[32,2560]{1,0:T(8,128)(2,1)S(1)}, bf16[32,2560]{1,0:T(8,128)(2,1)S(1)}, u32[]{:S(2)}, u32[]{:S(2)}) collective-permute-start(bf16[32,2560]{1,0:T(8,128)(2,1)S(1)} %get-tuple-element.84.refs_0_.refs_8_), channel_id=1, source_target_pairs={{0,32},{32,64},{64,96},{96,0},{128,160},{160,192},{192,224},{224,1... | collective-permute-start | bytes 491528 | tf_op jit(solution)/shard_map/ppermute | solution.py:33
  37.6 5.4 %collective-permute-start.16 = (bf16[32,2560]{1,0:T(8,128)(2,1)S(1)}, bf16[32,2560]{1,0:T(8,128)(2,1)S(1)}, u32[]{:S(2)}, u32[]{:S(2)}) collective-permute-start(bf16[32,2560]{1,0:T(8,128)(2,1)S(1)} %get-tuple-element.84.refs_0_.refs_8_), channel_id=1, source_target_pairs={{0,128},{32,160},{64,192},{96,224},{128,0},{160,32},{192,64},{224,... | collective-permute-start | bytes 491528 | tf_op jit(solution)/shard_map/ppermute | solution.py:33
  40.1 5.7 %collective-permute-start.3 = (bf16[32,2560]{1,0:T(8,128)(2,1)S(1)}, bf16[32,2560]{1,0:T(8,128)(2,1)S(1)}, u32[]{:S(2)}, u32[]{:S(2)}) collective-permute-start(bf16[32,2560]{1,0:T(8,128)(2,1)S(1)} %collective-permute-done.refs_1_), channel_id=1, source_target_pairs={{0,96},{32,0},{64,32},{96,64},{128,224},{160,128},{192,160},{224,1... | collective-permute-start | bytes 491528 | tf_op jit(solution)/shard_map/ppermute | solution.py:33
  41.6 5.4 %collective-permute-start.4 = (bf16[32,2560]{1,0:T(8,128)(2,1)S(1)}, bf16[32,2560]{1,0:T(8,128)(2,1)S(1)}, u32[]{:S(2)}, u32[]{:S(2)}) collective-permute-start(bf16[32,2560]{1,0:T(8,128)(2,1)S(1)} %collective-permute-done.2.refs_4_), channel_id=1, source_target_pairs={{0,32},{32,64},{64,96},{96,0},{128,160},{160,192},{192,224},{224,1... | collective-permute-start | bytes 491528 | tf_op jit(solution)/shard_map/ppermute | solution.py:33
  41.6 5.4 %collective-permute-start.5 = (bf16[32,2560]{1,0:T(8,128)(2,1)S(1)}, bf16[32,2560]{1,0:T(8,128)(2,1)S(1)}, u32[]{:S(2)}, u32[]{:S(2)}) collective-permute-start(bf16[32,2560]{1,0:T(8,128)(2,1)S(1)} %collective-permute-done.refs_1_), channel_id=1, source_target_pairs={{0,128},{32,160},{64,192},{96,224},{128,0},{160,32},{192,64},{224,... | collective-permute-start | bytes 491528 | tf_op jit(solution)/shard_map/ppermute | solution.py:33
  42.9 5.8 %collective-permute-start.17 = (bf16[32,2560]{1,0:T(8,128)(2,1)S(1)}, bf16[32,2560]{1,0:T(8,128)(2,1)S(1)}, u32[]{:S(2)}, u32[]{:S(2)}) collective-permute-start(bf16[32,2560]{1,0:T(8,128)(2,1)S(1)} %collective-permute-done.14.refs_1_.refs_9_), channel_id=1, source_target_pairs={{0,96},{32,0},{64,32},{96,64},{128,224},{160,128},{192,160},{224,1... | collective-permute-start | bytes 491528 | tf_op jit(solution)/shard_map/ppermute | solution.py:33
  45.2 6.0 %collective-permute-start.19 = (bf16[32,2560]{1,0:T(8,128)(2,1)S(1)}, bf16[32,2560]{1,0:T(8,128)(2,1)S(1)}, u32[]{:S(2)}, u32[]{:S(2)}) collective-permute-start(bf16[32,2560]{1,0:T(8,128)(2,1)S(1)} %collective-permute-done.14.refs_1_.refs_9_), channel_id=1, source_target_pairs={{0,128},{32,160},{64,192},{96,224},{128,0},{160,32},{192,64},{224,... | collective-permute-start | bytes 491528 | tf_op jit(solution)/shard_map/ppermute | solution.py:33
  45.9 5.4 %collective-permute-start.18 = (bf16[32,2560]{1,0:T(8,128)(2,1)S(1)}, bf16[32,2560]{1,0:T(8,128)(2,1)S(1)}, u32[]{:S(2)}, u32[]{:S(2)}) collective-permute-start(bf16[32,2560]{1,0:T(8,128)(2,1)S(1)} %collective-permute-done.16.refs_4_.refs_12_), channel_id=1, source_target_pairs={{0,32},{32,64},{64,96},{96,0},{128,160},{160,192},{192,224},{224,1... | collective-permute-start | bytes 491528 | tf_op jit(solution)/shard_map/ppermute | solution.py:33
  47.0 5.2 %collective-permute-start.6 = (bf16[32,2560]{1,0:T(8,128)(2,1)S(1)}, bf16[32,2560]{1,0:T(8,128)(2,1)S(1)}, u32[]{:S(2)}, u32[]{:S(2)}) collective-permute-start(bf16[32,2560]{1,0:T(8,128)(2,1)S(1)} %collective-permute-done.5.refs_5_), channel_id=1, source_target_pairs={{0,96},{32,0},{64,32},{96,64},{128,224},{160,128},{192,160},{224,1... | collective-permute-start | bytes 491528 | tf_op jit(solution)/shard_map/ppermute | solution.py:33
  51.3 11.7 %collective-permute-start.20 = (bf16[32,2560]{1,0:T(8,128)(2,1)S(1)}, bf16[32,2560]{1,0:T(8,128)(2,1)S(1)}, u32[]{:S(2)}, u32[]{:S(2)}) collective-permute-start(bf16[32,2560]{1,0:T(8,128)(2,1)S(1)} %collective-permute-done.18.refs_7_.refs_15_), channel_id=1, source_target_pairs={{0,32},{32,64},{64,96},{96,0},{128,160},{160,192},{192,224},{224,1... | collective-permute-start | bytes 491528 | tf_op jit(solution)/shard_map/ppermute | solution.py:33
  57.2 10.0 %collective-permute-start.7 = (bf16[32,2560]{1,0:T(8,128)(2,1)S(1)}, bf16[32,2560]{1,0:T(8,128)(2,1)S(1)}, u32[]{:S(2)}, u32[]{:S(2)}) collective-permute-start(bf16[32,2560]{1,0:T(8,128)(2,1)S(1)} %get-tuple-element.72), channel_id=1, source_target_pairs={{0,32},{32,64},{64,96},{96,0},{128,160},{160,192},{192,224},{224,1... | collective-permute-start | bytes 491528 | tf_op jit(solution)/shard_map/ppermute | solution.py:33
  57.9 9.3 %collective-permute-start.8 = (bf16[32,2560]{1,0:T(8,128)(2,1)S(1)}, bf16[32,2560]{1,0:T(8,128)(2,1)S(1)}, u32[]{:S(2)}, u32[]{:S(2)}) collective-permute-start(bf16[32,2560]{1,0:T(8,128)(2,1)S(1)} %get-tuple-element.73), channel_id=1, source_target_pairs={{0,96},{32,0},{64,32},{96,64},{128,224},{160,128},{192,160},{224,1... | collective-permute-start | bytes 491528 | tf_op jit(solution)/shard_map/ppermute | solution.py:33
  60.3 13.2 %collective-permute-start.9 = (bf16[32,2560]{1,0:T(8,128)(2,1)S(1)}, bf16[32,2560]{1,0:T(8,128)(2,1)S(1)}, u32[]{:S(2)}, u32[]{:S(2)}) collective-permute-start(bf16[32,2560]{1,0:T(8,128)(2,1)S(1)} %get-tuple-element.76), channel_id=1, source_target_pairs={{0,32},{32,64},{64,96},{96,0},{128,160},{160,192},{192,224},{224,1... | collective-permute-start | bytes 491528 | tf_op jit(solution)/shard_map/ppermute | solution.py:33
  60.3 16.4 %collective-permute-start.10 = (bf16[32,2560]{1,0:T(8,128)(2,1)S(1)}, bf16[32,2560]{1,0:T(8,128)(2,1)S(1)}, u32[]{:S(2)}, u32[]{:S(2)}) collective-permute-start(bf16[32,2560]{1,0:T(8,128)(2,1)S(1)} %get-tuple-element.77), channel_id=1, source_target_pairs={{0,96},{32,0},{64,32},{96,64},{128,224},{160,128},{192,160},{224,1... | collective-permute-start | bytes 491528 | tf_op jit(solution)/shard_map/ppermute | solution.py:33
  67.2 5.8 %collective-permute-start.22 = (bf16[32,2560]{1,0:T(8,128)(2,1)S(1)}, bf16[32,2560]{1,0:T(8,128)(2,1)S(1)}, u32[]{:S(2)}, u32[]{:S(2)}) collective-permute-start(bf16[32,2560]{1,0:T(8,128)(2,1)S(1)} %get-tuple-element.94), channel_id=1, source_target_pairs={{0,96},{32,0},{64,32},{96,64},{128,224},{160,128},{192,160},{224,1... | collective-permute-start | bytes 491528 | tf_op jit(solution)/shard_map/ppermute | solution.py:33
  67.3 12.7 %collective-permute-start.23 = (bf16[32,2560]{1,0:T(8,128)(2,1)S(1)}, bf16[32,2560]{1,0:T(8,128)(2,1)S(1)}, u32[]{:S(2)}, u32[]{:S(2)}) collective-permute-start(bf16[32,2560]{1,0:T(8,128)(2,1)S(1)} %get-tuple-element.97), channel_id=1, source_target_pairs={{0,32},{32,64},{64,96},{96,0},{128,160},{160,192},{192,224},{224,1... | collective-permute-start | bytes 491528 | tf_op jit(solution)/shard_map/ppermute | solution.py:33
  71.1 8.9 %collective-permute-start.25 = (bf16[32,2560]{1,0:T(8,128)(2,1)S(1)}, bf16[32,2560]{1,0:T(8,128)(2,1)S(1)}, u32[]{:S(2)}, u32[]{:S(2)}) collective-permute-start(bf16[32,2560]{1,0:T(8,128)(2,1)S(1)} %get-tuple-element.100), channel_id=1, source_target_pairs={{0,128},{32,160},{64,192},{96,224},{128,0},{160,32},{192,64},{224,... | collective-permute-start | bytes 491528 | tf_op jit(solution)/shard_map/ppermute | solution.py:33
  73.5 6.4 %collective-permute-start.24 = (bf16[32,2560]{1,0:T(8,128)(2,1)S(1)}, bf16[32,2560]{1,0:T(8,128)(2,1)S(1)}, u32[]{:S(2)}, u32[]{:S(2)}) collective-permute-start(bf16[32,2560]{1,0:T(8,128)(2,1)S(1)} %add_convert_fusion.2), channel_id=1, source_target_pairs={{0,96},{32,0},{64,32},{96,64},{128,224},{160,128},{192,160},{224,1... | collective-permute-start | bytes 491528 | tf_op jit(solution)/shard_map/ppermute | solution.py:33
  77.5 5.6 %collective-permute-start.12 = (bf16[32,2560]{1,0:T(8,128)(2,1)S(1)}, bf16[32,2560]{1,0:T(8,128)(2,1)S(1)}, u32[]{:S(2)}, u32[]{:S(2)}) collective-permute-start(bf16[32,2560]{1,0:T(8,128)(2,1)S(1)} %add_convert_fusion.4), channel_id=1, source_target_pairs={{0,32},{32,64},{64,96},{96,0},{128,160},{160,192},{192,224},{224,1... | collective-permute-start | bytes 491528 | tf_op jit(solution)/shard_map/ppermute | solution.py:33
  78.8 4.9 %collective-permute-start.13 = (bf16[32,2560]{1,0:T(8,128)(2,1)S(1)}, bf16[32,2560]{1,0:T(8,128)(2,1)S(1)}, u32[]{:S(2)}, u32[]{:S(2)}) collective-permute-start(bf16[32,2560]{1,0:T(8,128)(2,1)S(1)} %add_convert_fusion.3), channel_id=1, source_target_pairs={{0,128},{32,160},{64,192},{96,224},{128,0},{160,32},{192,64},{224,... | collective-permute-start | bytes 491528 | tf_op jit(solution)/shard_map/ppermute | solution.py:33
  80.0 5.5 %collective-permute-start.26 = (bf16[32,2560]{1,0:T(8,128)(2,1)S(1)}, bf16[32,2560]{1,0:T(8,128)(2,1)S(1)}, u32[]{:S(2)}, u32[]{:S(2)}) collective-permute-start(bf16[32,2560]{1,0:T(8,128)(2,1)S(1)} %add_convert_fusion.1), channel_id=1, source_target_pairs={{0,32},{32,64},{64,96},{96,0},{128,160},{160,192},{192,224},{224,1... | collective-permute-start | bytes 491528 | tf_op jit(solution)/shard_map/ppermute | solution.py:33
  81.6 5.3 %collective-permute-start.27 = (bf16[32,2560]{1,0:T(8,128)(2,1)S(1)}, bf16[32,2560]{1,0:T(8,128)(2,1)S(1)}, u32[]{:S(2)}, u32[]{:S(2)}) collective-permute-start(bf16[32,2560]{1,0:T(8,128)(2,1)S(1)} %add_convert_fusion), channel_id=1, source_target_pairs={{0,128},{32,160},{64,192},{96,224},{128,0},{160,32},{192,64},{224,... | collective-permute-start | bytes 491528 | tf_op jit(solution)/shard_map/ppermute | solution.py:33
  87.8 27.9 %all-to-all-start.1 = ((bf16[32,40,128]{2,1,0:T(8,128)(2,1)}), bf16[32,40,128]{2,1,0:T(8,128)(2,1)S(1)}, u32[]{:S(2)}, u32[]{:S(2)}) async-start(bf16[32,40,128]{2,1,0:T(8,128)(2,1)} %bitcast.5), calls=%async_computation.1 | async-start | bytes 655360 | tf_op jit(solution)/shard_map/all_to_all | solution.py:458
  128.3 5.7 %collective-permute-start.32 = (bf16[32,1280]{1,0:T(8,128)(2,1)S(1)}, bf16[32,1280]{1,0:T(8,128)(2,1)S(1)}, u32[]{:S(2)}, u32[]{:S(2)}) collective-permute-start(bf16[32,1280]{1,0:T(8,128)(2,1)S(1)} %add_convert_fusion.9), channel_id=1, source_target_pairs={{0,8},{1,33},{2,10},{3,35},{4,12},{5,37},{6,14},{7,39},{8,16},{9,4... | collective-permute-start | bytes 245768 | tf_op jit(solution)/shard_map/ppermute | solution.py:359
  137.4 5.0 %collective-permute-start.38 = (bf16[32,1280]{1,0:T(8,128)(2,1)S(1)}, bf16[32,1280]{1,0:T(8,128)(2,1)S(1)}, u32[]{:S(2)}, u32[]{:S(2)}) collective-permute-start(bf16[32,1280]{1,0:T(8,128)(2,1)S(1)} %add_convert_fusion.7), channel_id=1, source_target_pairs={{0,6},{1,7},{2,0},{3,1},{4,2},{5,3},{6,4},{7,5},{8,14},{9,15},{10,... | collective-permute-start | bytes 245768 | tf_op jit(solution)/shard_map/ppermute | solution.py:47
  138.1 7.4 %collective-permute-start.37 = (bf16[32,1280]{1,0:T(8,128)(2,1)S(1)}, bf16[32,1280]{1,0:T(8,128)(2,1)S(1)}, u32[]{:S(2)}, u32[]{:S(2)}) collective-permute-start(bf16[32,1280]{1,0:T(8,128)(2,1)S(1)} %add_convert_fusion.7), channel_id=1, source_target_pairs={{0,4},{1,5},{2,6},{3,7},{4,0},{5,1},{6,2},{7,3},{8,12},{9,13},{10,... | collective-permute-start | bytes 245768 | tf_op jit(solution)/shard_map/ppermute | solution.py:47
  141.5 6.2 %collective-permute-start.36 = (bf16[32,1280]{1,0:T(8,128)(2,1)S(1)}, bf16[32,1280]{1,0:T(8,128)(2,1)S(1)}, u32[]{:S(2)}, u32[]{:S(2)}) collective-permute-start(bf16[32,1280]{1,0:T(8,128)(2,1)S(1)} %add_convert_fusion.7), channel_id=1, source_target_pairs={{0,2},{1,3},{2,4},{3,5},{4,6},{5,7},{6,0},{7,1},{8,10},{9,11},{10,... | collective-permute-start | bytes 245768 | tf_op jit(solution)/shard_map/ppermute | solution.py:47
  147.7 7.6 %collective-permute-start.39 = (bf16[32,1280]{1,0:T(8,128)(2,1)S(1)}, bf16[32,1280]{1,0:T(8,128)(2,1)S(1)}, u32[]{:S(2)}, u32[]{:S(2)}) collective-permute-start(bf16[32,1280]{1,0:T(8,128)(2,1)S(1)} %add_convert_fusion.6), channel_id=1, source_target_pairs={{0,1},{1,0},{2,3},{3,2},{4,5},{5,4},{6,7},{7,6},{8,9},{9,8},{10,11... | collective-permute-start | bytes 245768 | tf_op jit(solution)/shard_map/ppermute | solution.py:47
  (28 other events, 152.5 us)

commit v6 on v5

--- a/solution.py
+++ b/solution.py
@@ -110,6 +110,15 @@
         copies.append(pltpu.make_async_copy(source.at[part], target.at[part], sems.at[i]))
         copies[-1].start()
     return copies
+
+
+def wait_all(copies):
+    for copy in copies:
+        copy.wait()
+
+
+in_vmem_spec = pl.BlockSpec(memory_space=pltpu.VMEM)
+in_hbm_spec = pl.BlockSpec(memory_space=pltpu.HBM)
 
 
 def in_hbm(value):
@@ -140,14 +149,13 @@
 
 
 def front_kernel(
-    each, tok_hbm, cot_hbm, par_hbm, rows_ref, disp_ref, comb_ref,
-    slots_ref, flat_ref, tok_ref, cot_ref, par_ref, sems,
+    each, tok_hbm, cot_hbm, par_hbm, rows_ref, disp_hbm, comb_hbm,
+    slots_ref, flat_ref, tok_ref, cot_ref, par_ref, disp_ref, comb_ref, sems, out_sems,
 ):
     par_loads = start_loads(par_hbm, par_ref, sems.at[0])
     tok_loads = start_loads(tok_hbm, tok_ref, sems.at[1])
     cot_loads = start_loads(cot_hbm, cot_ref, sems.at[2])
-    for copy in par_loads + tok_loads:
-        copy.wait()
+    wait_all(par_loads + tok_loads)
     tiles = slots_ref.shape[0]
     groups = slots_ref.shape[1] // each
     stride = 2 * each * tiles
@@ -158,10 +166,15 @@
     combine = raised / jnp.sum(raised, axis=0, keepdims=True)
     disp_ref[...] = dispatch
     comb_ref[...] = combine
+    stores = [
+        pltpu.make_async_copy(disp_ref, disp_hbm, out_sems.at[0]),
+        pltpu.make_async_copy(comb_ref, comb_hbm, out_sems.at[1]),
+    ]
+    for copy in stores:
+        copy.start()
     for kind, (weights, values) in enumerate(((dispatch, tok_ref), (combine, cot_ref))):
         if kind == 1:
-            for copy in cot_loads:
-                copy.wait()
+            wait_all(cot_loads)
         mixed = jnp.dot(weights.astype(BF16), values[...], preferred_element_type=F32)
         for k in range(tiles):
             slots_ref[k] = mixed[:, k * LANES : (k + 1) * LANES]
@@ -171,6 +184,7 @@
                     k, pl.ds(j, groups, stride=each), :
                 ]
     rows_ref[...] = flat_ref[...].astype(BF16)
+    wait_all(stores)
 
 
 def unpack_kernel(flat_in_ref, ins_ref, cots_ref, flat_ref):
@@ -200,9 +214,15 @@
 
 
 def final_kernel(
-    each, flat_in_ref, tok_ref, cot_ref, disp_ref, comb_ref, sig_ref, grad_ref, par_ref,
-    flat_ref, out_f_ref, sig_f_ref,
+    each, flat_in_ref, tok_ref, cot_ref, disp_hbm, comb_hbm, sig_ref, grad_ref, par_ref,
+    flat_ref, out_f_ref, sig_f_ref, disp_ref, comb_ref, sems,
 ):
+    loads = [
+        pltpu.make_async_copy(disp_hbm, disp_ref, sems.at[0]),
+        pltpu.make_async_copy(comb_hbm, comb_ref, sems.at[1]),
+    ]
+    for copy in loads:
+        copy.start()
     groups = sig_ref.shape[0] // each
     tiles = sig_ref.shape[1] // LANES
     stride = 2 * each * tiles
@@ -219,6 +239,7 @@
     sig_ref[...] = sig
     combine_grad = nt(slot_out, cot_ref[...])
     dispatch_grad = nt(sig, tok_ref[...])
+    wait_all(loads)
     combine = comb_ref[...]
     dispatch = disp_ref[...]
     combine_part = combine * (combine_grad - jnp.sum(combine * combine_grad, axis=0, keepdims=True))
@@ -241,88 +262,97 @@
         part[:, j * width : (j + 1) * width] = value[i * groups : (i + 1) * groups]
 
 
-def wait_all(copies):
-    for copy in copies:
-        copy.wait()
+def start_stores(sources, target, sems):
+    rows = sources[0].shape[0]
+    copies = []
+    for i, source in enumerate(sources):
+        part = target.at[pl.ds(i * rows, rows)]
+        copies.append(pltpu.make_async_copy(source, part, sems.at[i]))
+        copies[-1].start()
+    return copies
 
 
 def forward_kernel(count, each, *refs):
     blocks, (win_hbm, wout_hbm) = refs[:count], refs[count : count + 2]
-    parts = refs[count + 2 : 2 * count + 2]
-    act_ref, slope_ref, win_ref, wout_ref, sems = refs[2 * count + 2 :]
+    parts, (slope_ref, rows_hbm, act_hbm) = refs[count + 2 : 2 * count + 2], refs[-9:-6]
+    win_ref, wout_ref, act_ref, sems, row_sems, kept_sems = refs[-6:]
     width, hidden = win_ref.shape[1:]
     win_loads = [start_loads(win_hbm.at[j], win_ref.at[j], sems.at[0, j]) for j in range(each)]
     wout_loads = [start_loads(wout_hbm.at[j], wout_ref.at[j], sems.at[1, j]) for j in range(each)]
+    stores = start_stores(blocks, rows_hbm, row_sems)
     for j in range(each):
         hid = slice(j * hidden, (j + 1) * hidden)
         wait_all(win_loads[j])
         pre_act = jnp.dot(gathered(blocks, j, width), win_ref[j], preferred_element_type=F32)
         gelu_value, slope_ref[:, hid] = gelu_pair(pre_act)
         act_ref[:, hid] = gelu_value.astype(BF16)
+    stores += start_stores([act_ref], act_hbm, kept_sems)
     for j in range(each):
         hid = slice(j * hidden, (j + 1) * hidden)
         wait_all(wout_loads[j])
         spread(parts, jnp.dot(act_ref[:, hid], wout_ref[j], preferred_element_type=F32), j, width)
+    wait_all(stores)
 
 
 def backward_kernel(count, each, *refs):
     blocks, (slope_ref, win_hbm, wout_hbm) = refs[:count], refs[count : count + 3]
-    parts = refs[count + 3 : 2 * count + 3]
-    pre_ref, win_ref, wout_ref, sems = refs[2 * count + 3 :]
+    parts, (rows_hbm, pre_hbm) = refs[count + 3 : 2 * count + 3], refs[-8:-6]
+    win_ref, wout_ref, pre_ref, sems, row_sems, kept_sems = refs[-6:]
     width, hidden = win_ref.shape[1:]
     wout_loads = [start_loads(wout_hbm.at[j], wout_ref.at[j], sems.at[1, j]) for j in range(each)]
     win_loads = [start_loads(win_hbm.at[j], win_ref.at[j], sems.at[0, j]) for j in range(each)]
+    stores = start_stores(blocks, rows_hbm, row_sems)
     for j in range(each):
         hid = slice(j * hidden, (j + 1) * hidden)
         wait_all(wout_loads[j])
         act_grad = nt(gathered(blocks, j, width), wout_ref[j])
         pre_ref[:, hid] = (act_grad * slope_ref[:, hid]).astype(BF16)
+    stores += start_stores([pre_ref], pre_hbm, kept_sems)
     for j in range(each):
         hid = slice(j * hidden, (j + 1) * hidden)
         wait_all(win_loads[j])
         spread(parts, nt(pre_ref[:, hid], win_ref[j]), j, width)
-
-
-def expert_step(kernel, name, blocks, extra, kept, weight_in, weight_out):
+    wait_all(stores)
+
+
+def expert_step(kernel, name, blocks, extra, in_place, weight_in, weight_out):
     count = len(blocks)
     each, width, hidden = weight_in.shape
     rows = count * blocks[0].shape[0]
-    in_vmem, hbm = pl.BlockSpec(memory_space=pltpu.VMEM), pl.BlockSpec(memory_space=pltpu.HBM)
+    kept = jax.ShapeDtypeStruct((rows, each * hidden), BF16)
     outs = local_kernel(
         functools.partial(kernel, count, each),
         [jax.ShapeDtypeStruct(b.shape, BF16) for b in blocks]
-        + [jax.ShapeDtypeStruct((rows, each * hidden), t) for t in kept],
+        + [jax.ShapeDtypeStruct((rows, each * hidden), F32)] * in_place
+        + [pltpu.HBM((rows, each * width), BF16), pltpu.HBM(kept.shape, BF16)],
         [
             pltpu.VMEM(weight_in.shape, BF16),
             pltpu.VMEM(weight_out.shape, BF16),
+            pltpu.VMEM(kept.shape, BF16),
             pltpu.SemaphoreType.DMA((2, each, PIECES)),
+            pltpu.SemaphoreType.DMA((count,)),
+            pltpu.SemaphoreType.DMA((1,)),
         ],
         4 * rows * each * width * hidden,
         4 * each * width * hidden + 4 * rows * each * width,
         name,
-        in_specs=[in_vmem] * (count + len(extra)) + [hbm] * 2,
+        in_specs=[in_vmem_spec] * (count + len(extra)) + [in_hbm_spec] * 2,
+        out_specs=[in_vmem_spec] * (count + in_place) + [in_hbm_spec] * 2,
     )(*blocks, *extra, in_hbm(weight_in), in_hbm(weight_out))
     return outs[:count], *outs[count:]
 
 
-def weights_kernel(count, kept, *refs):
-    rows_in, rows_cot = refs[:count], refs[count : 2 * count]
-    acts, pres = refs[2 * count : 2 * count + kept], refs[2 * count + kept : 2 * count + 2 * kept]
-    gin_ref, gout_ref = refs[2 * count + 2 * kept :]
-
-    def whole(parts):
-        return jnp.concatenate([part[...] for part in parts], axis=0)
-
-    gin_ref[0] = tn(whole(rows_in), whole(pres)).astype(BF16)
-    gout_ref[0] = tn(whole(acts), whole(rows_cot)).astype(BF16)
-
-
-def weight_gradients(ins, cots, acts, pres, each, width, hidden):
-    count, kept, cuts = len(ins), len(acts), 2
-    groups = ins[0].shape[0]
-    rows = count * groups
+def weights_kernel(ins_ref, cots_ref, act_ref, pre_ref, gin_ref, gout_ref):
+    gin_ref[0] = tn(ins_ref[...], pre_ref[...]).astype(BF16)
+    gout_ref[0] = tn(act_ref[...], cots_ref[...]).astype(BF16)
+
+
+def weight_gradients(ins, cots, act, pre, each):
+    cuts = 2
+    rows = ins.shape[0]
+    width, hidden = ins.shape[1] // each, act.shape[1] // each
     return local_kernel(
-        functools.partial(weights_kernel, count, kept),
+        weights_kernel,
         (
             jax.ShapeDtypeStruct((each, width, hidden), BF16),
             jax.ShapeDtypeStruct((each, hidden, width), BF16),
@@ -332,15 +362,17 @@
         4 * each * width * hidden + 8 * rows * each * width,
         "weight_grads",
         grid=(each, cuts),
-        in_specs=[pl.BlockSpec((groups, width // cuts), lambda e, i: (0, e * cuts + i))] * count
-        + [pl.BlockSpec((groups, width), lambda e, i: (0, e))] * count
-        + [pl.BlockSpec((a.shape[0], hidden // cuts), lambda e, i: (0, e * cuts + i)) for a in acts]
-        + [pl.BlockSpec((p.shape[0], hidden), lambda e, i: (0, e)) for p in pres],
+        in_specs=[
+            pl.BlockSpec((rows, width // cuts), lambda e, i: (0, e * cuts + i)),
+            pl.BlockSpec((rows, width), lambda e, i: (0, e)),
+            pl.BlockSpec((rows, hidden // cuts), lambda e, i: (0, e * cuts + i)),
+            pl.BlockSpec((rows, hidden), lambda e, i: (0, e)),
+        ],
         out_specs=(
             pl.BlockSpec((1, width // cuts, hidden), lambda e, i: (e, i, 0)),
             pl.BlockSpec((1, hidden // cuts, width), lambda e, i: (e, i, 0)),
         ),
-    )(*ins, *cots, *acts, *pres)
+    )(in_hbm(ins), in_hbm(cots), in_hbm(act), in_hbm(pre))
 
 
 def crossed_send(value, step, turn):
@@ -359,6 +391,21 @@
     return lax.ppermute(value, ("batch", "expert"), pairs)
 
 
+def depth_swap(value, step):
+    depth = ZL * ZH
+    pairs = []
+    for z in range(depth):
+        to = (z + (step if z % 2 else -step)) % depth
+        for x in range(X):
+            for y in range(Y):
+                for c in range(CORE):
+                    here, there = (
+                        ((k % ZL * X + x) * Y + y) * ZH * CORE + k // ZL * CORE + c for k in (z, to)
+                    )
+                    pairs.append((here, there))
+    return lax.ppermute(value, ("batch", "expert"), pairs)
+
+
 def sum_all(partial, beside):
     core = lax.axis_index("expert") % CORE
     half = partial.shape[0] // CORE
@@ -368,8 +415,9 @@
     total = add(total, *[crossed_send(total, k, 0) for k in range(1, X)])
     total = add(total, *[crossed_send(total, k, 1) for k in range(1, X)])
     total = add(total, batch_send(total, 1, 0))
-    total, beside = lax.optimization_barrier((total, beside))
-    total = add(total, *[expert_send(total, 0, k, 0) for k in range(1, ZH)])
+    total, beside = together(total, beside)
+    total = add(total, depth_swap(total, 1))
+    total = add(total, depth_swap(total, -3))
     other = expert_send(total, 0, 0, 1)
     first = jnp.where(core == 0, total, other)
     second = jnp.where(core == 0, other, total)
@@ -386,7 +434,7 @@
     flat = groups * 2 * each * tiles
     params = slot_params.T
     flat_shape = jax.ShapeDtypeStruct((flat, LANES), BF16)
-    square = jax.ShapeDtypeStruct((slots, patches), F32)
+    square = pltpu.HBM((slots, patches), F32)
     dot_flops = 2 * slots * patches * width
     rows, dispatch, combine = local_kernel(
         functools.partial(front_kernel, each),
@@ -397,12 +445,16 @@
             pltpu.VMEM((patches, width), BF16),
             pltpu.VMEM((patches, width), BF16),
             pltpu.VMEM((slots, width), BF16),
+            pltpu.VMEM((slots, patches), F32),
+            pltpu.VMEM((slots, patches), F32),
             pltpu.SemaphoreType.DMA((3, PIECES)),
+            pltpu.SemaphoreType.DMA((2,)),
         ],
         3 * dot_flops,
         4 * patches * width + 2 * flat * LANES,
         "front",
-        in_specs=[pl.BlockSpec(memory_space=pltpu.HBM)] * 3,
+        in_specs=[in_hbm_spec] * 3,
+        out_specs=(in_vmem_spec, in_hbm_spec, in_hbm_spec),
     )(in_hbm(tokens), in_hbm(output_grad), in_hbm(params))
     routed = lax.all_to_all(
         rows.reshape(groups, 2 * each * tiles, LANES), "expert", split_axis=0, concat_axis=0,
@@ -429,15 +481,15 @@
     far_b = gather_far(next_b, 1)
     blocks_a = by_offset(ins, near_a, next_a, far_a)
     blocks_b = by_offset(cots, near_b, next_b, far_b)
-    parts_a, act, slope = expert_step(
-        forward_kernel, "expert_forward", blocks_a, [], [BF16, F32], weight_in, weight_out
+    parts_a, slope, rows_a, act = expert_step(
+        forward_kernel, "expert_forward", blocks_a, [], 1, weight_in, weight_out
     )
     got_a, near_from_a = scatter_far(parts_a, 0)
-    parts_b, pre = expert_step(
-        backward_kernel, "expert_backward", blocks_b, [slope], [BF16], weight_in, weight_out
+    parts_b, rows_b, pre = expert_step(
+        backward_kernel, "expert_backward", blocks_b, [slope], 0, weight_in, weight_out
     )
+    got_a, near_from_a, parts_a, pre = together(got_a, near_from_a, parts_a, pre)
     got_b, near_from_b = scatter_far(parts_b, 1)
-    got_a, near_from_a = together(got_a, near_from_a)
     next_got_a = scatter_next(parts_a, got_a, 0)
     got_b, near_from_b = together(got_b, near_from_b)
     next_got_b = scatter_next(parts_b, got_b, 1)
@@ -454,13 +506,12 @@
         10 * flat * LANES,
         "pack_sum",
     )(*share)
-    packed, act, pre = lax.optimization_barrier((packed, act, pre))
+    packed, act, pre = together(packed, act, pre)
     back = lax.all_to_all(
         packed.reshape(groups, 2 * each * tiles, LANES), "expert", split_axis=0, concat_axis=0,
         tiled=True,
     ).reshape(flat, LANES)
-    hidden = weight_in.shape[2]
-    weight_grads = weight_gradients(blocks_a, blocks_b, [act], [pre], each, width, hidden)
+    weight_grads = weight_gradients(rows_a, rows_b, act, pre, each)
     back, weight_grads = lax.optimization_barrier((back, weight_grads))
     row_shape = jax.ShapeDtypeStruct((slots, width), BF16)
     slot_in_grad, logits_grad, local_params = local_kernel(
@@ -470,11 +521,15 @@
             pltpu.VMEM((flat, LANES), F32),
             pltpu.VMEM((tiles, slots, LANES), F32),
             pltpu.VMEM((tiles, slots, LANES), F32),
+            pltpu.VMEM((slots, patches), F32),
+            pltpu.VMEM((slots, patches), F32),
+            pltpu.SemaphoreType.DMA((2,)),
         ],
         3 * dot_flops,
         4 * patches * width + 2 * flat * LANES,
         "final",
-    )(back, tokens, output_grad, dispatch, combine)
+        in_specs=[in_vmem_spec] * 3 + [in_hbm_spec] * 2,
+    )(back, tokens, output_grad, in_hbm(dispatch), in_hbm(combine))
     tokens_grad = (
         jnp.einsum("sm,sd->md", dispatch.astype(BF16), slot_in_grad, preferred_element_type=F32)
         + jnp.einsum("sm,sd->md", logits_grad, params, preferred_element_type=F32)

time: 157 us -> 155 us (0.987)
  local copies, waits for them, and re-layouts: 8.94 us -> 0.04 us
  waiting for transfers between devices: 36.8 us -> 42.7 us
  Pallas kernels: 16.5 us -> 20.5 us
  starting transfers between devices: 62.8 us -> 60.5 us
    unnamed x38 -> x8, local copies, waits for them, and re-layouts: 8.93 us -> 0.02 us
    ppermute x0 -> x2, waiting for transfers between devices: none -> 8.34 us  [depth_swap(): return lax.ppermute(value, ('batch', 'expert'), pairs)]
    ppermute x5 -> x2, waiting for transfers between devices: 7.23 us -> 1.85 us  [expert_send(): return lax.ppermute(value, 'expert', pairs)]
    all_to_all x1, waiting for transfers between devices: 4.04 us -> 8.34 us  [body(): lax.all_to_all(packed.reshape(groups, 2 * each * tiles, LANES), 'expert',...]
    ppermute x5 -> x2, starting transfers between devices: 12.3 us -> 8.46 us  [expert_send(): return lax.ppermute(value, 'expert', pairs)]
    pallas_call x1, Pallas kernels: 4.03 us -> 6.14 us  [weight_gradients(): local_kernel(weights_kernel, (jax.ShapeDtypeStruct((each, width, hidden),...]
    all_to_all x1, starting transfers between devices: 13.1 us -> 11.2 us  [body(): lax.all_to_all(packed.reshape(groups, 2 * each * tiles, LANES), 'expert',...]
    ppermute x6, starting transfers between devices: 5.67 us -> 7.54 us  [crossed_send(): return lax.ppermute(value, ('batch', 'expert'), pairs)]
  transfers between devices with their start and end apart: 41 -> 40, of which waited for: 25 -> 23; matrix products, arithmetic and copies ran while one was open for 1% -> 1% of each run, Pallas kernels for 8% -> 10%
where the time goes in v6:
time: 155 us
  starting transfers between devices  60.5 us (39%)
  waiting for transfers between devices  42.7 us (28%)
  blocking collectives  27.3 us (18%)
  Pallas kernels  20.5 us (13%)
    ppermute x29, starting transfers between devices, batch_send(): return lax.ppermute(value, 'batch', pairs)  31.9 us
    all_to_all x1, blocking collectives, body(): lax.all_to_all(rows.reshape(groups, 2 * each * tiles, LANES), 'expert', s...  27.3 us
    ppermute x29, waiting for transfers between devices, batch_send(): return lax.ppermute(value, 'batch', pairs)  15.9 us
    all_to_all x1, starting transfers between devices, body(): lax.all_to_all(packed.reshape(groups, 2 * each * tiles, LANES), 'expert',...  11.2 us
    pallas_call x2, Pallas kernels, expert_step(): local_kernel(functools.partial(kernel, count, each), [jax.ShapeDtypeStruc...  8.99 us
    ppermute x2, starting transfers between devices, expert_send(): return lax.ppermute(value, 'expert', pairs)  8.46 us
    ppermute x2, waiting for transfers between devices, depth_swap(): return lax.ppermute(value, ('batch', 'expert'), pairs)  8.34 us
    all_to_all x1, waiting for transfers between devices, body(): lax.all_to_all(packed.reshape(groups, 2 * each * tiles, LANES), 'expert',...  8.34 us
  transfers between devices with their start and end apart: 40, of which 23 were waited for; matrix products, arithmetic and copies ran while one was open for 1% of the time, Pallas kernels for 10%

profile of v6, /device:TPU:1, one launch (start us, length us, event | category | flops | bytes accessed | tf_op | source)
XLA Modules:
  0.0 154.6 jit_solution(7871330482173001506)
XLA Ops:
  0.6 2.7 %front.1 = (bf16[1280,128]{1,0:T(8,128)(2,1)S(1)}, f32[64,256]{1,0:T(8,128)}, f32[64,256]{1,0:T(8,128)}) custom-call(bf16[256,1280]{1,0:T(8,128)(2,1)} %bitcast.13, bf16[256,1280]{1,0:T(8,128)(2,1)} %bitcast.15, bf16[64,1280]{1,0:T(8,128)(2,1)} %bitcast.20), custom_call_target="tpu_custom_call" | custom-call | flops 125829120 | bytes 1638400 | tf_op jit(solution)/shard_map/front/pallas_call | solution.py:439
  3.3 27.3 %all_to_all.10 = bf16[32,40,128]{2,1,0:T(8,128)(2,1)S(1)} all-to-all(bf16[32,40,128]{2,1,0:T(8,128)(2,1)S(1)} %bitcast.19), channel_id=1, replica_groups=mesh['batch'=8,'expert'=32] {'expert'}, dimensions={0} | all-to-all | bytes 655360 | tf_op jit(solution)/shard_map/all_to_all | solution.py:459
  30.8 2.6 %collective-permute-start = (bf16[32,2560]{1,0:T(8,128)(2,1)S(1)}, bf16[32,2560]{1,0:T(8,128)(2,1)S(1)}, u32[]{:S(2)}, u32[]{:S(2)}) collective-permute-start(bf16[32,2560]{1,0:T(8,128)(2,1)S(1)} %get-tuple-element.73.refs_0_), channel_id=1, source_target_pairs={{0,96},{32,0},{64,32},{96,64},{128,224},{160,128},{192,160},{224,1... | collective-permute-start | bytes 491528 | tf_op jit(solution)/shard_map/ppermute | solution.py:33
  34.3 2.7 %collective-permute-start.9 = (bf16[32,2560]{1,0:T(8,128)(2,1)S(1)}, bf16[32,2560]{1,0:T(8,128)(2,1)S(1)}, u32[]{:S(2)}, u32[]{:S(2)}) collective-permute-start(bf16[32,2560]{1,0:T(8,128)(2,1)S(1)} %get-tuple-element.88.refs_0_), channel_id=1, source_target_pairs={{0,96},{32,0},{64,32},{96,64},{128,224},{160,128},{192,160},{224,1... | collective-permute-start | bytes 491528 | tf_op jit(solution)/shard_map/ppermute | solution.py:33
  37.6 1.9 %collective-permute-done.1.refs_3_ = bf16[32,2560]{1,0:T(8,128)(2,1)S(1)} collective-permute-done((bf16[32,2560]{1,0:T(8,128)(2,1)S(1)}, bf16[32,2560]{1,0:T(8,128)(2,1)S(1)}, u32[]{:S(2)}, u32[]{:S(2)}) %collective-permute-start.1) | collective-permute-done | bytes 163872 | tf_op jit(solution)/shard_map/ppermute | solution.py:33
  39.6 1.5 collective-permute-start.3
  42.4 2.2 %collective-permute-start.12 = (bf16[32,2560]{1,0:T(8,128)(2,1)S(1)}, bf16[32,2560]{1,0:T(8,128)(2,1)S(1)}, u32[]{:S(2)}, u32[]{:S(2)}) collective-permute-start(bf16[32,2560]{1,0:T(8,128)(2,1)S(1)} %collective-permute-done.9.refs_1_), channel_id=1, source_target_pairs={{0,96},{32,0},{64,32},{96,64},{128,224},{160,128},{192,160},{224,1... | collective-permute-start | bytes 491528 | tf_op jit(solution)/shard_map/ppermute | solution.py:33
  46.4 1.8 %collective-permute-start.6 = (bf16[32,2560]{1,0:T(8,128)(2,1)S(1)}, bf16[32,2560]{1,0:T(8,128)(2,1)S(1)}, u32[]{:S(2)}, u32[]{:S(2)}) collective-permute-start(bf16[32,2560]{1,0:T(8,128)(2,1)S(1)} %collective-permute-done.5.refs_5_), channel_id=1, source_target_pairs={{0,96},{32,0},{64,32},{96,64},{128,224},{160,128},{192,160},{224,1... | collective-permute-start | bytes 491528 | tf_op jit(solution)/shard_map/ppermute | solution.py:33
  48.2 2.3 %collective-permute-done.13.refs_7_ = bf16[32,2560]{1,0:T(8,128)(2,1)S(1)} collective-permute-done((bf16[32,2560]{1,0:T(8,128)(2,1)S(1)}, bf16[32,2560]{1,0:T(8,128)(2,1)S(1)}, u32[]{:S(2)}, u32[]{:S(2)}) %collective-permute-start.13) | collective-permute-done | bytes 163872 | tf_op jit(solution)/shard_map/ppermute | solution.py:33
  51.6 4.7 %expert_forward.1 = (bf16[32,2560]{1,0:T(8,128)(2,1)S(1)}, bf16[32,2560]{1,0:T(8,128)(2,1)S(1)}, bf16[32,2560]{1,0:T(8,128)(2,1)S(1)}, bf16[32,2560]{1,0:T(8,128...) custom-call(bf16[32,2560]{1,0:T(8,128)(2,1)S(1)} %get-tuple-element., ...), custom_call_target="tpu_custom_call" | custom-call | flops 1342177280 | bytes 7864320 | tf_op jit(solution)/shard_map/expert_forward/pallas_call | solution.py:323
  57.2 2.4 %collective-permute-start.8 = (bf16[32,2560]{1,0:T(8,128)(2,1)S(1)}, bf16[32,2560]{1,0:T(8,128)(2,1)S(1)}, u32[]{:S(2)}, u32[]{:S(2)}) collective-permute-start(bf16[32,2560]{1,0:T(8,128)(2,1)S(1)} %get-tuple-element.81), channel_id=1, source_target_pairs={{0,96},{32,0},{64,32},{96,64},{128,224},{160,128},{192,160},{224,1... | collective-permute-start | bytes 491528 | tf_op jit(solution)/shard_map/ppermute | solution.py:33
  59.6 4.3 %expert_backward.1 = (bf16[32,2560]{1,0:T(8,128)(2,1)S(1)}, bf16[32,2560]{1,0:T(8,128)(2,1)S(1)}, bf16[32,2560]{1,0:T(8,128)(2,1)S(1)}, bf16[32,2560]{1,0:T(8,12...) custom-call(bf16[32,2560]{1,0:T(8,128)(2,1)S(1)} %get-tuple-element., ...), custom_call_target="tpu_custom_call" | custom-call | flops 1342177280 | bytes 7864320 | tf_op jit(solution)/shard_map/expert_backward/pallas_call | solution.py:323
  68.1 3.0 %collective-permute-start.17 = (bf16[32,2560]{1,0:T(8,128)(2,1)S(1)}, bf16[32,2560]{1,0:T(8,128)(2,1)S(1)}, u32[]{:S(2)}, u32[]{:S(2)}) collective-permute-start(bf16[32,2560]{1,0:T(8,128)(2,1)S(1)} %get-tuple-element.101), channel_id=1, source_target_pairs={{0,96},{32,0},{64,32},{96,64},{128,224},{160,128},{192,160},{224,1... | collective-permute-start | bytes 491528 | tf_op jit(solution)/shard_map/ppermute | solution.py:33
  72.8 1.5 collective-permute-start.24
  75.8 2.2 %collective-permute-start.19 = (bf16[32,2560]{1,0:T(8,128)(2,1)S(1)}, bf16[32,2560]{1,0:T(8,128)(2,1)S(1)}, u32[]{:S(2)}, u32[]{:S(2)}) collective-permute-start(bf16[32,2560]{1,0:T(8,128)(2,1)S(1)} %add_convert_fusion.4), channel_id=1, source_target_pairs={{0,32},{32,64},{64,96},{96,0},{128,160},{160,192},{192,224},{224,1... | collective-permute-start | bytes 491528 | tf_op jit(solution)/shard_map/ppermute | solution.py:33
  78.5 1.5 collective-permute-start.26
  81.4 2.9 %collective-permute-done.20.refs_3_ = bf16[32,2560]{1,0:T(8,128)(2,1)S(1)} collective-permute-done((bf16[32,2560]{1,0:T(8,128)(2,1)S(1)}, bf16[32,2560]{1,0:T(8,128)(2,1)S(1)}, u32[]{:S(2)}, u32[]{:S(2)}) %collective-permute-start.20) | collective-permute-done | bytes 163872 | tf_op jit(solution)/shard_map/ppermute | solution.py:33
  84.3 1.5 collective-permute-done.27.refs_7_
  86.6 11.2 %all-to-all-start.1 = ((bf16[32,40,128]{2,1,0:T(8,128)(2,1)}), bf16[32,40,128]{2,1,0:T(8,128)(2,1)S(1)}, u32[]{:S(2)}, u32[]{:S(2)}) async-start(bf16[32,40,128]{2,1,0:T(8,128)(2,1)} %bitcast.5), calls=%async_computation.1 | async-start | bytes 655360 | tf_op jit(solution)/shard_map/all_to_all | solution.py:510
  97.9 6.1 %weight_grads.1 = (bf16[2,1280,512]{2,1,0:T(8,128)(2,1)}, bf16[2,512,1280]{2,1,0:T(8,128)(2,1)}) custom-call(bf16[256,2560]{1,0:T(8,128)(2,1)} %get-tuple-element.124.ins_ref, bf16[256,2560]{1,0:T(8,128)(2,1)} %get-tuple-element.125.cots_ref, bf16[256,1024]{1,0:T(8,128)(2,1)} %get-tuple-element.126.act_ref, bf16[256,1024]{1,0:T(8,128)(2,1)} %get-tuple-element.127.pre_ref), custom_call_target="tpu_custom_call" | custom-call | flops 1342177280 | bytes 10485760 | tf_op jit(solution)/shard_map/weight_grads/pallas_call | solution.py:354
  104.0 8.3 %all-to-all-done.1 = bf16[32,40,128]{2,1,0:T(8,128)(2,1)S(1)} async-done(((bf16[32,40,128]{2,1,0:T(8,128)(2,1)}), bf16[32,40,128]{2,1,0:T(8,128)(2,1)S(1)}, u32[]{:S(2)}, u32[]{:S(2)}) %all-to-all-start.1) | async-done | bytes 327712 | tf_op jit(solution)/shard_map/all_to_all | solution.py:510
  112.4 1.6 %final.1 = (bf16[64,1280]{1,0:T(8,128)(2,1)S(1)}, bf16[64,256]{1,0:T(8,128)(2,1)S(1)}, bf16[64,1280]{1,0:T(8,128)(2,1)S(1)}) custom-call(bf16[1280,128]{1,0:T(8,128)(2,1)S(1)} %bitcast.17, bf16[256,1280]{1,0:T(8,128)(2,1)S(1)} %bitcast.14, bf16[256,1280]{1,0:T(8,128)(2,1)S(1)} %bitcast.16, f32[64,256]{1,0:T(8,128)} %get-tuple-element.131.disp_hbm, ...), custom_call_target="tpu_custom_call" | custom-call | flops 125829120 | bytes 1638400 | tf_op jit(solution)/shard_map/final/pallas_call | solution.py:517
  116.6 1.6 %collective-permute-start.30 = (bf16[32,1280]{1,0:T(8,128)(2,1)S(1)}, bf16[32,1280]{1,0:T(8,128)(2,1)S(1)}, u32[]{:S(2)}, u32[]{:S(2)}) collective-permute-start(bf16[32,1280]{1,0:T(8,128)(2,1)S(1)} %add_convert_fusion.11), channel_id=1, source_target_pairs={{0,64},{1,17},{2,66},{3,19},{4,68},{5,21},{6,70},{7,23},{8,72},{9,... | collective-permute-start | bytes 245768 | tf_op jit(solution)/shard_map/ppermute | solution.py:391
  118.9 2.5 %collective-permute-done.30 = bf16[32,1280]{1,0:T(8,128)(2,1)S(1)} collective-permute-done((bf16[32,1280]{1,0:T(8,128)(2,1)S(1)}, bf16[32,1280]{1,0:T(8,128)(2,1)S(1)}, u32[]{:S(2)}, u32[]{:S(2)}) %collective-permute-start.30) | collective-permute-done | bytes 81952 | tf_op jit(solution)/shard_map/ppermute | solution.py:391
  122.7 1.9 %collective-permute-start.34 = (bf16[32,1280]{1,0:T(8,128)(2,1)S(1)}, bf16[32,1280]{1,0:T(8,128)(2,1)S(1)}, u32[]{:S(2)}, u32[]{:S(2)}) collective-permute-start(bf16[32,1280]{1,0:T(8,128)(2,1)S(1)} %add_convert_fusion.10), channel_id=1, source_target_pairs={{0,24},{1,97},{2,26},{3,99},{4,28},{5,101},{6,30},{7,103},{8,0},{9... | collective-permute-start | bytes 245768 | tf_op jit(solution)/shard_map/ppermute | solution.py:391
  124.7 2.6 %collective-permute-start.33 = (bf16[32,1280]{1,0:T(8,128)(2,1)S(1)}, bf16[32,1280]{1,0:T(8,128)(2,1)S(1)}, u32[]{:S(2)}, u32[]{:S(2)}) collective-permute-start(bf16[32,1280]{1,0:T(8,128)(2,1)S(1)} %add_convert_fusion.10), channel_id=1, source_target_pairs={{0,16},{1,65},{2,18},{3,67},{4,20},{5,69},{6,22},{7,71},{8,24},{9,... | collective-permute-start | bytes 245768 | tf_op jit(solution)/shard_map/ppermute | solution.py:391
  127.6 1.8 %collective-permute-done.33 = bf16[32,1280]{1,0:T(8,128)(2,1)S(1)} collective-permute-done((bf16[32,1280]{1,0:T(8,128)(2,1)S(1)}, bf16[32,1280]{1,0:T(8,128)(2,1)S(1)}, u32[]{:S(2)}, u32[]{:S(2)}) %collective-permute-start.33) | collective-permute-done | bytes 81952 | tf_op jit(solution)/shard_map/ppermute | solution.py:391
  129.5 2.3 %collective-permute-done.32 = bf16[32,1280]{1,0:T(8,128)(2,1)S(1)} collective-permute-done((bf16[32,1280]{1,0:T(8,128)(2,1)S(1)}, bf16[32,1280]{1,0:T(8,128)(2,1)S(1)}, u32[]{:S(2)}, u32[]{:S(2)}) %collective-permute-start.32) | collective-permute-done | bytes 81952 | tf_op jit(solution)/shard_map/ppermute | solution.py:391
  133.7 1.5 collective-permute-done.35
  135.3 4.5 %collective-permute-done.36 = bf16[32,1280]{1,0:T(8,128)(2,1)S(1)} collective-permute-done((bf16[32,1280]{1,0:T(8,128)(2,1)S(1)}, bf16[32,1280]{1,0:T(8,128)(2,1)S(1)}, u32[]{:S(2)}, u32[]{:S(2)}) %collective-permute-start.36) | collective-permute-done | bytes 81952 | tf_op jit(solution)/shard_map/ppermute | solution.py:406
  141.2 3.8 %collective-permute-done.37 = bf16[32,1280]{1,0:T(8,128)(2,1)S(1)} collective-permute-done((bf16[32,1280]{1,0:T(8,128)(2,1)S(1)}, bf16[32,1280]{1,0:T(8,128)(2,1)S(1)}, u32[]{:S(2)}, u32[]{:S(2)}) %collective-permute-start.37) | collective-permute-done | bytes 81952 | tf_op jit(solution)/shard_map/ppermute | solution.py:406
  145.0 7.9 %collective-permute-start.38 = (bf16[32,1280]{1,0:T(8,128)(2,1)S(1)}, bf16[32,1280]{1,0:T(8,128)(2,1)S(1)}, u32[]{:S(2)}, u32[]{:S(2)}) collective-permute-start(bf16[32,1280]{1,0:T(8,128)(2,1)S(1)} %add_convert_fusion.6), channel_id=1, source_target_pairs={{0,1},{1,0},{2,3},{3,2},{4,5},{5,4},{6,7},{7,6},{8,9},{9,8},{10,11... | collective-permute-start | bytes 245768 | tf_op jit(solution)/shard_map/ppermute | solution.py:47
  (81 shorter events, 27.2 us)
Async XLA Ops:
  30.8 6.2 %collective-permute-start = (bf16[32,2560]{1,0:T(8,128)(2,1)S(1)}, bf16[32,2560]{1,0:T(8,128)(2,1)S(1)}, u32[]{:S(2)}, u32[]{:S(2)}) collective-permute-start(bf16[32,2560]{1,0:T(8,128)(2,1)S(1)} %get-tuple-element.73.refs_0_), channel_id=1, source_target_pairs={{0,96},{32,0},{64,32},{96,64},{128,224},{160,128},{192,160},{224,1... | collective-permute-start | bytes 491528 | tf_op jit(solution)/shard_map/ppermute | solution.py:33
  33.4 6.2 %collective-permute-start.1 = (bf16[32,2560]{1,0:T(8,128)(2,1)S(1)}, bf16[32,2560]{1,0:T(8,128)(2,1)S(1)}, u32[]{:S(2)}, u32[]{:S(2)}) collective-permute-start(bf16[32,2560]{1,0:T(8,128)(2,1)S(1)} %get-tuple-element.73.refs_0_), channel_id=1, source_target_pairs={{0,32},{32,64},{64,96},{96,0},{128,160},{160,192},{192,224},{224,1... | collective-permute-start | bytes 491528 | tf_op jit(solution)/shard_map/ppermute | solution.py:33
  33.4 6.2 %collective-permute-start.2 = (bf16[32,2560]{1,0:T(8,128)(2,1)S(1)}, bf16[32,2560]{1,0:T(8,128)(2,1)S(1)}, u32[]{:S(2)}, u32[]{:S(2)}) collective-permute-start(bf16[32,2560]{1,0:T(8,128)(2,1)S(1)} %get-tuple-element.73.refs_0_), channel_id=1, source_target_pairs={{0,128},{32,160},{64,192},{96,224},{128,0},{160,32},{192,64},{224,... | collective-permute-start | bytes 491528 | tf_op jit(solution)/shard_map/ppermute | solution.py:33
  34.3 6.8 %collective-permute-start.9 = (bf16[32,2560]{1,0:T(8,128)(2,1)S(1)}, bf16[32,2560]{1,0:T(8,128)(2,1)S(1)}, u32[]{:S(2)}, u32[]{:S(2)}) collective-permute-start(bf16[32,2560]{1,0:T(8,128)(2,1)S(1)} %get-tuple-element.88.refs_0_), channel_id=1, source_target_pairs={{0,96},{32,0},{64,32},{96,64},{128,224},{160,128},{192,160},{224,1... | collective-permute-start | bytes 491528 | tf_op jit(solution)/shard_map/ppermute | solution.py:33
  37.0 5.4 %collective-permute-start.10 = (bf16[32,2560]{1,0:T(8,128)(2,1)S(1)}, bf16[32,2560]{1,0:T(8,128)(2,1)S(1)}, u32[]{:S(2)}, u32[]{:S(2)}) collective-permute-start(bf16[32,2560]{1,0:T(8,128)(2,1)S(1)} %get-tuple-element.88.refs_0_), channel_id=1, source_target_pairs={{0,32},{32,64},{64,96},{96,0},{128,160},{160,192},{192,224},{224,1... | collective-permute-start | bytes 491528 | tf_op jit(solution)/shard_map/ppermute | solution.py:33
  37.0 5.4 %collective-permute-start.11 = (bf16[32,2560]{1,0:T(8,128)(2,1)S(1)}, bf16[32,2560]{1,0:T(8,128)(2,1)S(1)}, u32[]{:S(2)}, u32[]{:S(2)}) collective-permute-start(bf16[32,2560]{1,0:T(8,128)(2,1)S(1)} %get-tuple-element.88.refs_0_), channel_id=1, source_target_pairs={{0,128},{32,160},{64,192},{96,224},{128,0},{160,32},{192,64},{224,... | collective-permute-start | bytes 491528 | tf_op jit(solution)/shard_map/ppermute | solution.py:33
  39.6 5.0 %collective-permute-start.3 = (bf16[32,2560]{1,0:T(8,128)(2,1)S(1)}, bf16[32,2560]{1,0:T(8,128)(2,1)S(1)}, u32[]{:S(2)}, u32[]{:S(2)}) collective-permute-start(bf16[32,2560]{1,0:T(8,128)(2,1)S(1)} %collective-permute-done.refs_1_), channel_id=1, source_target_pairs={{0,96},{32,0},{64,32},{96,64},{128,224},{160,128},{192,160},{224,1... | collective-permute-start | bytes 491528 | tf_op jit(solution)/shard_map/ppermute | solution.py:33
  41.0 5.4 %collective-permute-start.4 = (bf16[32,2560]{1,0:T(8,128)(2,1)S(1)}, bf16[32,2560]{1,0:T(8,128)(2,1)S(1)}, u32[]{:S(2)}, u32[]{:S(2)}) collective-permute-start(bf16[32,2560]{1,0:T(8,128)(2,1)S(1)} %collective-permute-done.2.refs_4_), channel_id=1, source_target_pairs={{0,32},{32,64},{64,96},{96,0},{128,160},{160,192},{192,224},{224,1... | collective-permute-start | bytes 491528 | tf_op jit(solution)/shard_map/ppermute | solution.py:33
  41.1 5.4 %collective-permute-start.5 = (bf16[32,2560]{1,0:T(8,128)(2,1)S(1)}, bf16[32,2560]{1,0:T(8,128)(2,1)S(1)}, u32[]{:S(2)}, u32[]{:S(2)}) collective-permute-start(bf16[32,2560]{1,0:T(8,128)(2,1)S(1)} %collective-permute-done.refs_1_), channel_id=1, source_target_pairs={{0,128},{32,160},{64,192},{96,224},{128,0},{160,32},{192,64},{224,... | collective-permute-start | bytes 491528 | tf_op jit(solution)/shard_map/ppermute | solution.py:33
  42.4 5.8 %collective-permute-start.12 = (bf16[32,2560]{1,0:T(8,128)(2,1)S(1)}, bf16[32,2560]{1,0:T(8,128)(2,1)S(1)}, u32[]{:S(2)}, u32[]{:S(2)}) collective-permute-start(bf16[32,2560]{1,0:T(8,128)(2,1)S(1)} %collective-permute-done.9.refs_1_), channel_id=1, source_target_pairs={{0,96},{32,0},{64,32},{96,64},{128,224},{160,128},{192,160},{224,1... | collective-permute-start | bytes 491528 | tf_op jit(solution)/shard_map/ppermute | solution.py:33
  44.6 6.0 %collective-permute-start.13 = (bf16[32,2560]{1,0:T(8,128)(2,1)S(1)}, bf16[32,2560]{1,0:T(8,128)(2,1)S(1)}, u32[]{:S(2)}, u32[]{:S(2)}) collective-permute-start(bf16[32,2560]{1,0:T(8,128)(2,1)S(1)} %collective-permute-done.11.refs_4_), channel_id=1, source_target_pairs={{0,32},{32,64},{64,96},{96,0},{128,160},{160,192},{192,224},{224,1... | collective-permute-start | bytes 491528 | tf_op jit(solution)/shard_map/ppermute | solution.py:33
  44.6 6.0 %collective-permute-start.14 = (bf16[32,2560]{1,0:T(8,128)(2,1)S(1)}, bf16[32,2560]{1,0:T(8,128)(2,1)S(1)}, u32[]{:S(2)}, u32[]{:S(2)}) collective-permute-start(bf16[32,2560]{1,0:T(8,128)(2,1)S(1)} %collective-permute-done.9.refs_1_), channel_id=1, source_target_pairs={{0,128},{32,160},{64,192},{96,224},{128,0},{160,32},{192,64},{224,... | collective-permute-start | bytes 491528 | tf_op jit(solution)/shard_map/ppermute | solution.py:33
  46.4 5.2 %collective-permute-start.6 = (bf16[32,2560]{1,0:T(8,128)(2,1)S(1)}, bf16[32,2560]{1,0:T(8,128)(2,1)S(1)}, u32[]{:S(2)}, u32[]{:S(2)}) collective-permute-start(bf16[32,2560]{1,0:T(8,128)(2,1)S(1)} %collective-permute-done.5.refs_5_), channel_id=1, source_target_pairs={{0,96},{32,0},{64,32},{96,64},{128,224},{160,128},{192,160},{224,1... | collective-permute-start | bytes 491528 | tf_op jit(solution)/shard_map/ppermute | solution.py:33
  50.5 9.1 %collective-permute-start.15 = (bf16[32,2560]{1,0:T(8,128)(2,1)S(1)}, bf16[32,2560]{1,0:T(8,128)(2,1)S(1)}, u32[]{:S(2)}, u32[]{:S(2)}) collective-permute-start(bf16[32,2560]{1,0:T(8,128)(2,1)S(1)} %collective-permute-done.13.refs_7_), channel_id=1, source_target_pairs={{0,32},{32,64},{64,96},{96,0},{128,160},{160,192},{192,224},{224,1... | collective-permute-start | bytes 491528 | tf_op jit(solution)/shard_map/ppermute | solution.py:33
  56.3 10.5 %collective-permute-start.7 = (bf16[32,2560]{1,0:T(8,128)(2,1)S(1)}, bf16[32,2560]{1,0:T(8,128)(2,1)S(1)}, u32[]{:S(2)}, u32[]{:S(2)}) collective-permute-start(bf16[32,2560]{1,0:T(8,128)(2,1)S(1)} %get-tuple-element.80), channel_id=1, source_target_pairs={{0,32},{32,64},{64,96},{96,0},{128,160},{160,192},{192,224},{224,1... | collective-permute-start | bytes 491528 | tf_op jit(solution)/shard_map/ppermute | solution.py:33
  57.2 10.2 %collective-permute-start.8 = (bf16[32,2560]{1,0:T(8,128)(2,1)S(1)}, bf16[32,2560]{1,0:T(8,128)(2,1)S(1)}, u32[]{:S(2)}, u32[]{:S(2)}) collective-permute-start(bf16[32,2560]{1,0:T(8,128)(2,1)S(1)} %get-tuple-element.81), channel_id=1, source_target_pairs={{0,96},{32,0},{64,32},{96,64},{128,224},{160,128},{192,160},{224,1... | collective-permute-start | bytes 491528 | tf_op jit(solution)/shard_map/ppermute | solution.py:33
  65.3 5.8 %collective-permute-start.22 = (bf16[32,2560]{1,0:T(8,128)(2,1)S(1)}, bf16[32,2560]{1,0:T(8,128)(2,1)S(1)}, u32[]{:S(2)}, u32[]{:S(2)}) collective-permute-start(bf16[32,2560]{1,0:T(8,128)(2,1)S(1)} %get-tuple-element.110), channel_id=1, source_target_pairs={{0,96},{32,0},{64,32},{96,64},{128,224},{160,128},{192,160},{224,1... | collective-permute-start | bytes 491528 | tf_op jit(solution)/shard_map/ppermute | solution.py:33
  65.4 13.0 %collective-permute-start.23 = (bf16[32,2560]{1,0:T(8,128)(2,1)S(1)}, bf16[32,2560]{1,0:T(8,128)(2,1)S(1)}, u32[]{:S(2)}, u32[]{:S(2)}) collective-permute-start(bf16[32,2560]{1,0:T(8,128)(2,1)S(1)} %get-tuple-element.113), channel_id=1, source_target_pairs={{0,32},{32,64},{64,96},{96,0},{128,160},{160,192},{192,224},{224,1... | collective-permute-start | bytes 491528 | tf_op jit(solution)/shard_map/ppermute | solution.py:33
  66.8 11.6 %collective-permute-start.25 = (bf16[32,2560]{1,0:T(8,128)(2,1)S(1)}, bf16[32,2560]{1,0:T(8,128)(2,1)S(1)}, u32[]{:S(2)}, u32[]{:S(2)}) collective-permute-start(bf16[32,2560]{1,0:T(8,128)(2,1)S(1)} %get-tuple-element.116), channel_id=1, source_target_pairs={{0,128},{32,160},{64,192},{96,224},{128,0},{160,32},{192,64},{224,... | collective-permute-start | bytes 491528 | tf_op jit(solution)/shard_map/ppermute | solution.py:33
  67.4 5.4 %collective-permute-start.16 = (bf16[32,2560]{1,0:T(8,128)(2,1)S(1)}, bf16[32,2560]{1,0:T(8,128)(2,1)S(1)}, u32[]{:S(2)}, u32[]{:S(2)}) collective-permute-start(bf16[32,2560]{1,0:T(8,128)(2,1)S(1)} %get-tuple-element.100), channel_id=1, source_target_pairs={{0,32},{32,64},{64,96},{96,0},{128,160},{160,192},{192,224},{224,1... | collective-permute-start | bytes 491528 | tf_op jit(solution)/shard_map/ppermute | solution.py:33
  68.1 7.0 %collective-permute-start.17 = (bf16[32,2560]{1,0:T(8,128)(2,1)S(1)}, bf16[32,2560]{1,0:T(8,128)(2,1)S(1)}, u32[]{:S(2)}, u32[]{:S(2)}) collective-permute-start(bf16[32,2560]{1,0:T(8,128)(2,1)S(1)} %get-tuple-element.101), channel_id=1, source_target_pairs={{0,96},{32,0},{64,32},{96,64},{128,224},{160,128},{192,160},{224,1... | collective-permute-start | bytes 491528 | tf_op jit(solution)/shard_map/ppermute | solution.py:33
  72.8 5.7 %collective-permute-start.24 = (bf16[32,2560]{1,0:T(8,128)(2,1)S(1)}, bf16[32,2560]{1,0:T(8,128)(2,1)S(1)}, u32[]{:S(2)}, u32[]{:S(2)}) collective-permute-start(bf16[32,2560]{1,0:T(8,128)(2,1)S(1)} %add_convert_fusion.2), channel_id=1, source_target_pairs={{0,96},{32,0},{64,32},{96,64},{128,224},{160,128},{192,160},{224,1... | collective-permute-start | bytes 491528 | tf_op jit(solution)/shard_map/ppermute | solution.py:33
  75.8 5.5 %collective-permute-start.19 = (bf16[32,2560]{1,0:T(8,128)(2,1)S(1)}, bf16[32,2560]{1,0:T(8,128)(2,1)S(1)}, u32[]{:S(2)}, u32[]{:S(2)}) collective-permute-start(bf16[32,2560]{1,0:T(8,128)(2,1)S(1)} %add_convert_fusion.4), channel_id=1, source_target_pairs={{0,32},{32,64},{64,96},{96,0},{128,160},{160,192},{192,224},{224,1... | collective-permute-start | bytes 491528 | tf_op jit(solution)/shard_map/ppermute | solution.py:33
  78.1 6.1 %collective-permute-start.20 = (bf16[32,2560]{1,0:T(8,128)(2,1)S(1)}, bf16[32,2560]{1,0:T(8,128)(2,1)S(1)}, u32[]{:S(2)}, u32[]{:S(2)}) collective-permute-start(bf16[32,2560]{1,0:T(8,128)(2,1)S(1)} %add_convert_fusion.3), channel_id=1, source_target_pairs={{0,128},{32,160},{64,192},{96,224},{128,0},{160,32},{192,64},{224,... | collective-permute-start | bytes 491528 | tf_op jit(solution)/shard_map/ppermute | solution.py:33
  78.5 5.7 %collective-permute-start.26 = (bf16[32,2560]{1,0:T(8,128)(2,1)S(1)}, bf16[32,2560]{1,0:T(8,128)(2,1)S(1)}, u32[]{:S(2)}, u32[]{:S(2)}) collective-permute-start(bf16[32,2560]{1,0:T(8,128)(2,1)S(1)} %add_convert_fusion.1), channel_id=1, source_target_pairs={{0,32},{32,64},{64,96},{96,0},{128,160},{160,192},{192,224},{224,1... | collective-permute-start | bytes 491528 | tf_op jit(solution)/shard_map/ppermute | solution.py:33
  80.1 5.6 %collective-permute-start.27 = (bf16[32,2560]{1,0:T(8,128)(2,1)S(1)}, bf16[32,2560]{1,0:T(8,128)(2,1)S(1)}, u32[]{:S(2)}, u32[]{:S(2)}) collective-permute-start(bf16[32,2560]{1,0:T(8,128)(2,1)S(1)} %add_convert_fusion), channel_id=1, source_target_pairs={{0,128},{32,160},{64,192},{96,224},{128,0},{160,32},{192,64},{224,... | collective-permute-start | bytes 491528 | tf_op jit(solution)/shard_map/ppermute | solution.py:33
  86.6 25.7 %all-to-all-start.1 = ((bf16[32,40,128]{2,1,0:T(8,128)(2,1)}), bf16[32,40,128]{2,1,0:T(8,128)(2,1)S(1)}, u32[]{:S(2)}, u32[]{:S(2)}) async-start(bf16[32,40,128]{2,1,0:T(8,128)(2,1)} %bitcast.5), calls=%async_computation.1 | async-start | bytes 655360 | tf_op jit(solution)/shard_map/all_to_all | solution.py:510
  116.6 4.8 %collective-permute-start.30 = (bf16[32,1280]{1,0:T(8,128)(2,1)S(1)}, bf16[32,1280]{1,0:T(8,128)(2,1)S(1)}, u32[]{:S(2)}, u32[]{:S(2)}) collective-permute-start(bf16[32,1280]{1,0:T(8,128)(2,1)S(1)} %add_convert_fusion.11), channel_id=1, source_target_pairs={{0,64},{1,17},{2,66},{3,19},{4,68},{5,21},{6,70},{7,23},{8,72},{9,... | collective-permute-start | bytes 245768 | tf_op jit(solution)/shard_map/ppermute | solution.py:391
  122.7 4.9 %collective-permute-start.34 = (bf16[32,1280]{1,0:T(8,128)(2,1)S(1)}, bf16[32,1280]{1,0:T(8,128)(2,1)S(1)}, u32[]{:S(2)}, u32[]{:S(2)}) collective-permute-start(bf16[32,1280]{1,0:T(8,128)(2,1)S(1)} %add_convert_fusion.10), channel_id=1, source_target_pairs={{0,24},{1,97},{2,26},{3,99},{4,28},{5,101},{6,30},{7,103},{8,0},{9... | collective-permute-start | bytes 245768 | tf_op jit(solution)/shard_map/ppermute | solution.py:391
  124.7 4.8 %collective-permute-start.33 = (bf16[32,1280]{1,0:T(8,128)(2,1)S(1)}, bf16[32,1280]{1,0:T(8,128)(2,1)S(1)}, u32[]{:S(2)}, u32[]{:S(2)}) collective-permute-start(bf16[32,1280]{1,0:T(8,128)(2,1)S(1)} %add_convert_fusion.10), channel_id=1, source_target_pairs={{0,16},{1,65},{2,18},{3,67},{4,20},{5,69},{6,22},{7,71},{8,24},{9,... | collective-permute-start | bytes 245768 | tf_op jit(solution)/shard_map/ppermute | solution.py:391
  139.8 5.2 %collective-permute-start.37 = (bf16[32,1280]{1,0:T(8,128)(2,1)S(1)}, bf16[32,1280]{1,0:T(8,128)(2,1)S(1)}, u32[]{:S(2)}, u32[]{:S(2)}) collective-permute-start(bf16[32,1280]{1,0:T(8,128)(2,1)S(1)} %add_convert_fusion.7), channel_id=1, source_target_pairs={{0,130},{1,131},{8,138},{9,139},{16,146},{17,147},{24,154},{25,155... | collective-permute-start | bytes 245768 | tf_op jit(solution)/shard_map/ppermute | solution.py:406
  145.0 8.8 %collective-permute-start.38 = (bf16[32,1280]{1,0:T(8,128)(2,1)S(1)}, bf16[32,1280]{1,0:T(8,128)(2,1)S(1)}, u32[]{:S(2)}, u32[]{:S(2)}) collective-permute-start(bf16[32,1280]{1,0:T(8,128)(2,1)S(1)} %add_convert_fusion.6), channel_id=1, source_target_pairs={{0,1},{1,0},{2,3},{3,2},{4,5},{5,4},{6,7},{7,6},{8,9},{9,8},{10,11... | collective-permute-start | bytes 245768 | tf_op jit(solution)/shard_map/ppermute | solution.py:47
  (12 other events, 101.5 us)

commit v7 on v6

--- a/solution.py
+++ b/solution.py
@@ -76,24 +76,24 @@
     return [mine, near[0], nexts[0], near[1], near[2], nexts[2], far, nexts[1]]
 
 
-def scatter_far(parts, side):
+def scatter_first(parts):
     p00, p01, p02, p03, p10, p11, p12, p13 = parts
-    return batch_send(p12, 0, 1 if side == 0 else 3), batch_send(p03, 0, 3)
-
-
-def scatter_next(parts, got, side):
+    return batch_send(p11, 0, 1), batch_send(p13, 0, 3), batch_send(p12, 1, 0)
+
+
+def scatter_second(parts, got, side):
     p00, p01, p02, p03, p10, p11, p12, p13 = parts
+    p10 = add(p10, got[0], got[1])
+    p02 = add(p02, got[2])
     if side == 0:
-        p11 = add(p11, got)
-    else:
-        p13 = add(p13, got)
-    return batch_send(p02, 0, 1), batch_send(p13, 0, 3), batch_send(p11, 1, 0)
-
-
-def scatter_near(parts, got):
-    p01 = add(parts[1], got[0], got[2])
-    p10 = add(parts[4], got[1])
-    return batch_send(p01, 0, 1), batch_send(p10, 1, 0)
+        return batch_send(p02, 0, 1), batch_send(p03, 0, 3), batch_send(p10, 1, 0)
+    return batch_send(p02, 0, 3), batch_send(p01, 0, 1), batch_send(p10, 1, 0)
+
+
+def scatter_third(parts, got, side):
+    if side == 0:
+        return batch_send(add(parts[1], got), 0, 1)
+    return batch_send(add(parts[3], got), 0, 3)
 
 
 LANES = 128
@@ -273,16 +273,14 @@
 
 
 def forward_kernel(count, each, *refs):
-    blocks, (win_hbm, wout_hbm) = refs[:count], refs[count : count + 2]
-    parts, (slope_ref, rows_hbm, act_hbm) = refs[count + 2 : 2 * count + 2], refs[-9:-6]
-    win_ref, wout_ref, act_ref, sems, row_sems, kept_sems = refs[-6:]
+    blocks, (win_ref, wout_hbm) = refs[:count], refs[count : count + 2]
+    parts, (slope_ref, rows_hbm, act_hbm) = refs[count + 2 : 2 * count + 2], refs[-8:-5]
+    wout_ref, act_ref, sems, row_sems, kept_sems = refs[-5:]
     width, hidden = win_ref.shape[1:]
-    win_loads = [start_loads(win_hbm.at[j], win_ref.at[j], sems.at[0, j]) for j in range(each)]
-    wout_loads = [start_loads(wout_hbm.at[j], wout_ref.at[j], sems.at[1, j]) for j in range(each)]
+    wout_loads = [start_loads(wout_hbm.at[j], wout_ref.at[j], sems.at[j]) for j in range(each)]
     stores = start_stores(blocks, rows_hbm, row_sems)
     for j in range(each):
         hid = slice(j * hidden, (j + 1) * hidden)
-        wait_all(win_loads[j])
         pre_act = jnp.dot(gathered(blocks, j, width), win_ref[j], preferred_element_type=F32)
         gelu_value, slope_ref[:, hid] = gelu_pair(pre_act)
         act_ref[:, hid] = gelu_value.astype(BF16)
@@ -295,16 +293,14 @@
 
 
 def backward_kernel(count, each, *refs):
-    blocks, (slope_ref, win_hbm, wout_hbm) = refs[:count], refs[count : count + 3]
-    parts, (rows_hbm, pre_hbm) = refs[count + 3 : 2 * count + 3], refs[-8:-6]
-    win_ref, wout_ref, pre_ref, sems, row_sems, kept_sems = refs[-6:]
+    blocks, (slope_ref, wout_ref, win_hbm) = refs[:count], refs[count : count + 3]
+    parts, (rows_hbm, pre_hbm) = refs[count + 3 : 2 * count + 3], refs[-7:-5]
+    win_ref, pre_ref, sems, row_sems, kept_sems = refs[-5:]
     width, hidden = win_ref.shape[1:]
-    wout_loads = [start_loads(wout_hbm.at[j], wout_ref.at[j], sems.at[1, j]) for j in range(each)]
-    win_loads = [start_loads(win_hbm.at[j], win_ref.at[j], sems.at[0, j]) for j in range(each)]
+    win_loads = [start_loads(win_hbm.at[j], win_ref.at[j], sems.at[j]) for j in range(each)]
     stores = start_stores(blocks, rows_hbm, row_sems)
     for j in range(each):
         hid = slice(j * hidden, (j + 1) * hidden)
-        wait_all(wout_loads[j])
         act_grad = nt(gathered(blocks, j, width), wout_ref[j])
         pre_ref[:, hid] = (act_grad * slope_ref[:, hid]).astype(BF16)
     stores += start_stores([pre_ref], pre_hbm, kept_sems)
@@ -315,9 +311,9 @@
     wait_all(stores)
 
 
-def expert_step(kernel, name, blocks, extra, in_place, weight_in, weight_out):
+def expert_step(kernel, name, blocks, extra, in_place, first, second, hidden):
     count = len(blocks)
-    each, width, hidden = weight_in.shape
+    each, width = first.shape[0], first.shape[1] * first.shape[2] // hidden
     rows = count * blocks[0].shape[0]
     kept = jax.ShapeDtypeStruct((rows, each * hidden), BF16)
     outs = local_kernel(
@@ -326,19 +322,18 @@
         + [jax.ShapeDtypeStruct((rows, each * hidden), F32)] * in_place
         + [pltpu.HBM((rows, each * width), BF16), pltpu.HBM(kept.shape, BF16)],
         [
-            pltpu.VMEM(weight_in.shape, BF16),
-            pltpu.VMEM(weight_out.shape, BF16),
+            pltpu.VMEM(second.shape, BF16),
             pltpu.VMEM(kept.shape, BF16),
-            pltpu.SemaphoreType.DMA((2, each, PIECES)),
+            pltpu.SemaphoreType.DMA((each, PIECES)),
             pltpu.SemaphoreType.DMA((count,)),
             pltpu.SemaphoreType.DMA((1,)),
         ],
         4 * rows * each * width * hidden,
         4 * each * width * hidden + 4 * rows * each * width,
         name,
-        in_specs=[in_vmem_spec] * (count + len(extra)) + [in_hbm_spec] * 2,
+        in_specs=[in_vmem_spec] * (count + len(extra) + 1) + [in_hbm_spec],
         out_specs=[in_vmem_spec] * (count + in_place) + [in_hbm_spec] * 2,
-    )(*blocks, *extra, in_hbm(weight_in), in_hbm(weight_out))
+    )(*blocks, *extra, first, in_hbm(second))
     return outs[:count], *outs[count:]
 
 
@@ -469,6 +464,7 @@
         4 * flat * LANES,
         "unpack",
     )(routed)
+    hidden = weight_in.shape[2]
     near_a = gather_near(ins)
     near_b = gather_near(cots)
     near_a = together(*near_a)
@@ -482,22 +478,22 @@
     blocks_a = by_offset(ins, near_a, next_a, far_a)
     blocks_b = by_offset(cots, near_b, next_b, far_b)
     parts_a, slope, rows_a, act = expert_step(
-        forward_kernel, "expert_forward", blocks_a, [], 1, weight_in, weight_out
+        forward_kernel, "expert_forward", blocks_a, [], 1, weight_in, weight_out, hidden
     )
-    got_a, near_from_a = scatter_far(parts_a, 0)
+    first_a = scatter_first(parts_a)
     parts_b, rows_b, pre = expert_step(
-        backward_kernel, "expert_backward", blocks_b, [slope], 0, weight_in, weight_out
+        backward_kernel, "expert_backward", blocks_b, [slope], 0, weight_out, weight_in, hidden
     )
-    got_a, near_from_a, parts_a, pre = together(got_a, near_from_a, parts_a, pre)
-    got_b, near_from_b = scatter_far(parts_b, 1)
-    next_got_a = scatter_next(parts_a, got_a, 0)
-    got_b, near_from_b = together(got_b, near_from_b)
-    next_got_b = scatter_next(parts_b, got_b, 1)
-    next_got_a = together(*next_got_a)
-    near_got_a = scatter_near(parts_a, next_got_a)
-    next_got_b = together(*next_got_b)
-    near_got_b = scatter_near(parts_b, next_got_b)
-    share = (parts_a[0], near_from_a, *near_got_a, parts_b[0], near_from_b, *near_got_b)
+    first_b = scatter_first(parts_b)
+    first_a, parts_a, pre = together(first_a, parts_a, pre)
+    second_a = scatter_second(parts_a, first_a, 0)
+    first_b, parts_b = together(first_b, parts_b)
+    second_b = scatter_second(parts_b, first_b, 1)
+    second_a = together(*second_a)
+    third_a = scatter_third(parts_a, second_a[0], 0)
+    second_b = together(*second_b)
+    third_b = scatter_third(parts_b, second_b[0], 1)
+    share = (parts_a[0], *second_a[1:], third_a, parts_b[0], *second_b[1:], third_b)
     packed = local_kernel(
         pack_sum_kernel,
         flat_shape,

time: 155 us -> 153 us (0.987)
  starting transfers between devices: 60.5 us -> 54.9 us
  waiting for transfers between devices: 42.7 us -> 45.6 us
  local copies, waits for them, and re-layouts: 0.04 us -> 1.78 us
    ppermute x29, starting transfers between devices: 31.9 us -> 29 us  [batch_send(): return lax.ppermute(value, 'batch', pairs)]
    ppermute x29, waiting for transfers between devices: 15.9 us -> 18.4 us  [batch_send(): return lax.ppermute(value, 'batch', pairs)]
    ppermute x6, starting transfers between devices: 7.54 us -> 5.56 us  [crossed_send(): return lax.ppermute(value, ('batch', 'expert'), pairs)]
    unnamed x8 -> x12, local copies, waits for them, and re-layouts: 0.02 us -> 1.77 us
  transfers between devices with their start and end apart: 40 -> 40, of which waited for: 23 -> 24; matrix products, arithmetic and copies ran while one was open for 1% -> 1% of each run, Pallas kernels for 10% -> 9%
where the time goes in v7:
time: 153 us; the launch traced here: 152 us
  starting transfers between devices  54.9 us (36%)
  waiting for transfers between devices  45.6 us (30%)
  blocking collectives  27.3 us (18%)
  Pallas kernels  19 us (12%)
  local copies, waits for them, and re-layouts  1.78 us (1%)
  matrix products  1.55 us (1%)
    ppermute x29, starting transfers between devices, batch_send(): return lax.ppermute(value, 'batch', pairs)  29 us
    all_to_all x1, blocking collectives, body(): lax.all_to_all(rows.reshape(groups, 2 * each * tiles, LANES), 'expert', s...  27.3 us
    ppermute x29, waiting for transfers between devices, batch_send(): return lax.ppermute(value, 'batch', pairs)  18.4 us
    all_to_all x1, starting transfers between devices, body(): lax.all_to_all(packed.reshape(groups, 2 * each * tiles, LANES), 'expert',...  11.1 us
    ppermute x6, waiting for transfers between devices, crossed_send(): return lax.ppermute(value, ('batch', 'expert'), pairs)  8.69 us
    all_to_all x1, waiting for transfers between devices, body(): lax.all_to_all(packed.reshape(groups, 2 * each * tiles, LANES), 'expert',...  8.59 us
    ppermute x2, waiting for transfers between devices, depth_swap(): return lax.ppermute(value, ('batch', 'expert'), pairs)  8.08 us
    pallas_call x2, Pallas kernels, expert_step(): local_kernel(functools.partial(kernel, count, each), [jax.ShapeDtypeStruc...  7.5 us
  transfers between devices with their start and end apart: 40, of which 24 were waited for; matrix products, arithmetic and copies ran while one was open for 1% of the time, Pallas kernels for 9%

profile of v7, /device:TPU:1, one launch (start us, length us, event | category | flops | bytes accessed | tf_op | source)
XLA Modules:
  0.0 152.1 jit_solution(138982202308512493)
XLA Ops:
  0.6 2.7 %front.1 = (bf16[1280,128]{1,0:T(8,128)(2,1)S(1)}, f32[64,256]{1,0:T(8,128)}, f32[64,256]{1,0:T(8,128)}) custom-call(bf16[256,1280]{1,0:T(8,128)(2,1)} %bitcast.13, bf16[256,1280]{1,0:T(8,128)(2,1)} %bitcast.15, bf16[64,1280]{1,0:T(8,128)(2,1)} %bitcast.20), custom_call_target="tpu_custom_call" | custom-call | flops 125829120 | bytes 1638400 | tf_op jit(solution)/shard_map/front/pallas_call | solution.py:434
  3.3 27.3 %all_to_all.10 = bf16[32,40,128]{2,1,0:T(8,128)(2,1)S(1)} all-to-all(bf16[32,40,128]{2,1,0:T(8,128)(2,1)S(1)} %bitcast.19), channel_id=1, replica_groups=mesh['batch'=8,'expert'=32] {'expert'}, dimensions={0} | all-to-all | bytes 655360 | tf_op jit(solution)/shard_map/all_to_all | solution.py:454
  30.8 2.6 %collective-permute-start = (bf16[32,2560]{1,0:T(8,128)(2,1)S(1)}, bf16[32,2560]{1,0:T(8,128)(2,1)S(1)}, u32[]{:S(2)}, u32[]{:S(2)}) collective-permute-start(bf16[32,2560]{1,0:T(8,128)(2,1)S(1)} %get-tuple-element.79.refs_0_), channel_id=1, source_target_pairs={{0,96},{32,0},{64,32},{96,64},{128,224},{160,128},{192,160},{224,1... | collective-permute-start | bytes 491528 | tf_op jit(solution)/shard_map/ppermute | solution.py:33
  34.3 2.7 %collective-permute-start.10 = (bf16[32,2560]{1,0:T(8,128)(2,1)S(1)}, bf16[32,2560]{1,0:T(8,128)(2,1)S(1)}, u32[]{:S(2)}, u32[]{:S(2)}) collective-permute-start(bf16[32,2560]{1,0:T(8,128)(2,1)S(1)} %get-tuple-element.94.refs_0_), channel_id=1, source_target_pairs={{0,96},{32,0},{64,32},{96,64},{128,224},{160,128},{192,160},{224,1... | collective-permute-start | bytes 491528 | tf_op jit(solution)/shard_map/ppermute | solution.py:33
  37.6 1.9 %collective-permute-done.1.refs_3_ = bf16[32,2560]{1,0:T(8,128)(2,1)S(1)} collective-permute-done((bf16[32,2560]{1,0:T(8,128)(2,1)S(1)}, bf16[32,2560]{1,0:T(8,128)(2,1)S(1)}, u32[]{:S(2)}, u32[]{:S(2)}) %collective-permute-start.1) | collective-permute-done | bytes 163872 | tf_op jit(solution)/shard_map/ppermute | solution.py:33
  39.6 1.5 collective-permute-start.3
  42.4 2.2 %collective-permute-start.13 = (bf16[32,2560]{1,0:T(8,128)(2,1)S(1)}, bf16[32,2560]{1,0:T(8,128)(2,1)S(1)}, u32[]{:S(2)}, u32[]{:S(2)}) collective-permute-start(bf16[32,2560]{1,0:T(8,128)(2,1)S(1)} %collective-permute-done.10.refs_1_), channel_id=1, source_target_pairs={{0,96},{32,0},{64,32},{96,64},{128,224},{160,128},{192,160},{224,1... | collective-permute-start | bytes 491528 | tf_op jit(solution)/shard_map/ppermute | solution.py:33
  46.4 1.8 %collective-permute-start.6 = (bf16[32,2560]{1,0:T(8,128)(2,1)S(1)}, bf16[32,2560]{1,0:T(8,128)(2,1)S(1)}, u32[]{:S(2)}, u32[]{:S(2)}) collective-permute-start(bf16[32,2560]{1,0:T(8,128)(2,1)S(1)} %collective-permute-done.5.refs_5_), channel_id=1, source_target_pairs={{0,96},{32,0},{64,32},{96,64},{128,224},{160,128},{192,160},{224,1... | collective-permute-start | bytes 491528 | tf_op jit(solution)/shard_map/ppermute | solution.py:33
  48.2 2.3 %collective-permute-done.14.refs_7_ = bf16[32,2560]{1,0:T(8,128)(2,1)S(1)} collective-permute-done((bf16[32,2560]{1,0:T(8,128)(2,1)S(1)}, bf16[32,2560]{1,0:T(8,128)(2,1)S(1)}, u32[]{:S(2)}, u32[]{:S(2)}) %collective-permute-start.14) | collective-permute-done | bytes 163872 | tf_op jit(solution)/shard_map/ppermute | solution.py:33
  51.6 1.7 %copy-done = bf16[2,1280,512]{2,1,0:T(8,128)(2,1)S(1)} copy-done((bf16[2,1280,512]{2,1,0:T(8,128)(2,1)S(1)}, bf16[2,1280,512]{2,1,0:T(8,128)(2,1)}, u32[]{:S(2)}) %copy-start) | copy-done | bytes 2621464
  53.3 4.0 %expert_forward.1 = (bf16[32,2560]{1,0:T(8,128)(2,1)S(1)}, bf16[32,2560]{1,0:T(8,128)(2,1)S(1)}, bf16[32,2560]{1,0:T(8,128)(2,1)S(1)}, bf16[32,2560]{1,0:T(8,128...) custom-call(bf16[32,2560]{1,0:T(8,128)(2,1)S(1)} %get-tuple-element., ...), custom_call_target="tpu_custom_call" | custom-call | flops 1342177280 | bytes 7864320 | tf_op jit(solution)/shard_map/expert_forward/pallas_call | solution.py:319
  58.3 2.4 %collective-permute-start.8 = (bf16[32,2560]{1,0:T(8,128)(2,1)S(1)}, bf16[32,2560]{1,0:T(8,128)(2,1)S(1)}, u32[]{:S(2)}, u32[]{:S(2)}) collective-permute-start(bf16[32,2560]{1,0:T(8,128)(2,1)S(1)} %get-tuple-element.87), channel_id=1, source_target_pairs={{0,96},{32,0},{64,32},{96,64},{128,224},{160,128},{192,160},{224,1... | collective-permute-start | bytes 491528 | tf_op jit(solution)/shard_map/ppermute | solution.py:33
  61.2 3.5 %expert_backward.1 = (bf16[32,2560]{1,0:T(8,128)(2,1)S(1)}, bf16[32,2560]{1,0:T(8,128)(2,1)S(1)}, bf16[32,2560]{1,0:T(8,128)(2,1)S(1)}, bf16[32,2560]{1,0:T(8,12...) custom-call(bf16[32,2560]{1,0:T(8,128)(2,1)S(1)} %get-tuple-element., ...), custom_call_target="tpu_custom_call" | custom-call | flops 1342177280 | bytes 7864320 | tf_op jit(solution)/shard_map/expert_backward/pallas_call | solution.py:319
  64.8 2.7 %collective-permute-start.22 = (bf16[32,2560]{1,0:T(8,128)(2,1)S(1)}, bf16[32,2560]{1,0:T(8,128)(2,1)S(1)}, u32[]{:S(2)}, u32[]{:S(2)}) collective-permute-start(bf16[32,2560]{1,0:T(8,128)(2,1)S(1)} %get-tuple-element.115), channel_id=1, source_target_pairs={{0,96},{32,0},{64,32},{96,64},{128,224},{160,128},{192,160},{224,1... | collective-permute-start | bytes 491528 | tf_op jit(solution)/shard_map/ppermute | solution.py:33
  68.5 2.7 %collective-permute-start.18 = (bf16[32,2560]{1,0:T(8,128)(2,1)S(1)}, bf16[32,2560]{1,0:T(8,128)(2,1)S(1)}, u32[]{:S(2)}, u32[]{:S(2)}) collective-permute-start(bf16[32,2560]{1,0:T(8,128)(2,1)S(1)} %get-tuple-element.106), channel_id=1, source_target_pairs={{0,96},{32,0},{64,32},{96,64},{128,224},{160,128},{192,160},{224,1... | collective-permute-start | bytes 491528 | tf_op jit(solution)/shard_map/ppermute | solution.py:33
  76.7 2.4 %collective-permute-done.25.refs_5_ = bf16[32,2560]{1,0:T(8,128)(2,1)S(1)} collective-permute-done((bf16[32,2560]{1,0:T(8,128)(2,1)S(1)}, bf16[32,2560]{1,0:T(8,128)(2,1)S(1)}, u32[]{:S(2)}, u32[]{:S(2)}) %collective-permute-start.25) | collective-permute-done | bytes 163872 | tf_op jit(solution)/shard_map/ppermute | solution.py:33
  80.5 1.5 collective-permute-done.20.refs_3_
  81.9 3.7 %collective-permute-done.27.refs_7_ = bf16[32,2560]{1,0:T(8,128)(2,1)S(1)} collective-permute-done((bf16[32,2560]{1,0:T(8,128)(2,1)S(1)}, bf16[32,2560]{1,0:T(8,128)(2,1)S(1)}, u32[]{:S(2)}, u32[]{:S(2)}) %collective-permute-start.27) | collective-permute-done | bytes 163872 | tf_op jit(solution)/shard_map/ppermute | solution.py:33
  86.5 11.1 %all-to-all-start.1 = ((bf16[32,40,128]{2,1,0:T(8,128)(2,1)}), bf16[32,40,128]{2,1,0:T(8,128)(2,1)S(1)}, u32[]{:S(2)}, u32[]{:S(2)}) async-start(bf16[32,40,128]{2,1,0:T(8,128)(2,1)} %bitcast.5), calls=%async_computation.1 | async-start | bytes 655360 | tf_op jit(solution)/shard_map/all_to_all | solution.py:506
  97.7 6.1 %weight_grads.1 = (bf16[2,1280,512]{2,1,0:T(8,128)(2,1)}, bf16[2,512,1280]{2,1,0:T(8,128)(2,1)}) custom-call(bf16[256,2560]{1,0:T(8,128)(2,1)} %get-tuple-element.136.ins_ref, bf16[256,2560]{1,0:T(8,128)(2,1)} %get-tuple-element.137.cots_ref, bf16[256,1024]{1,0:T(8,128)(2,1)} %get-tuple-element.138.act_ref, bf16[256,1024]{1,0:T(8,128)(2,1)} %get-tuple-element.139.pre_ref), custom_call_target="tpu_custom_call" | custom-call | flops 1342177280 | bytes 10485760 | tf_op jit(solution)/shard_map/weight_grads/pallas_call | solution.py:349
  103.9 8.6 %all-to-all-done.1 = bf16[32,40,128]{2,1,0:T(8,128)(2,1)S(1)} async-done(((bf16[32,40,128]{2,1,0:T(8,128)(2,1)}), bf16[32,40,128]{2,1,0:T(8,128)(2,1)S(1)}, u32[]{:S(2)}, u32[]{:S(2)}) %all-to-all-start.1) | async-done | bytes 327712 | tf_op jit(solution)/shard_map/all_to_all | solution.py:506
  112.5 1.6 %final.1 = (bf16[64,1280]{1,0:T(8,128)(2,1)S(1)}, bf16[64,256]{1,0:T(8,128)(2,1)S(1)}, bf16[64,1280]{1,0:T(8,128)(2,1)S(1)}) custom-call(bf16[1280,128]{1,0:T(8,128)(2,1)S(1)} %bitcast.17, bf16[256,1280]{1,0:T(8,128)(2,1)S(1)} %bitcast.14, bf16[256,1280]{1,0:T(8,128)(2,1)S(1)} %bitcast.16, f32[64,256]{1,0:T(8,128)} %get-tuple-element.143.disp_hbm, ...), custom_call_target="tpu_custom_call" | custom-call | flops 125829120 | bytes 1638400 | tf_op jit(solution)/shard_map/final/pallas_call | solution.py:513
  116.4 1.3 collective-permute-start.30
  117.8 1.4 collective-permute-done.31
  119.3 1.9 %collective-permute-done.30 = bf16[32,1280]{1,0:T(8,128)(2,1)S(1)} collective-permute-done((bf16[32,1280]{1,0:T(8,128)(2,1)S(1)}, bf16[32,1280]{1,0:T(8,128)(2,1)S(1)}, u32[]{:S(2)}, u32[]{:S(2)}) %collective-permute-start.30) | collective-permute-done | bytes 81952 | tf_op jit(solution)/shard_map/ppermute | solution.py:386
  122.2 2.7 %collective-permute-start.34 = (bf16[32,1280]{1,0:T(8,128)(2,1)S(1)}, bf16[32,1280]{1,0:T(8,128)(2,1)S(1)}, u32[]{:S(2)}, u32[]{:S(2)}) collective-permute-start(bf16[32,1280]{1,0:T(8,128)(2,1)S(1)} %add_convert_fusion.10), channel_id=1, source_target_pairs={{0,24},{1,97},{2,26},{3,99},{4,28},{5,101},{6,30},{7,103},{8,0},{9... | collective-permute-start | bytes 245768 | tf_op jit(solution)/shard_map/ppermute | solution.py:386
  127.2 2.6 %collective-permute-done.33 = bf16[32,1280]{1,0:T(8,128)(2,1)S(1)} collective-permute-done((bf16[32,1280]{1,0:T(8,128)(2,1)S(1)}, bf16[32,1280]{1,0:T(8,128)(2,1)S(1)}, u32[]{:S(2)}, u32[]{:S(2)}) %collective-permute-start.33) | collective-permute-done | bytes 81952 | tf_op jit(solution)/shard_map/ppermute | solution.py:386
  132.2 1.5 collective-permute-done.35
  133.8 4.5 %collective-permute-done.36 = bf16[32,1280]{1,0:T(8,128)(2,1)S(1)} collective-permute-done((bf16[32,1280]{1,0:T(8,128)(2,1)S(1)}, bf16[32,1280]{1,0:T(8,128)(2,1)S(1)}, u32[]{:S(2)}, u32[]{:S(2)}) %collective-permute-start.36) | collective-permute-done | bytes 81952 | tf_op jit(solution)/shard_map/ppermute | solution.py:401
  138.3 1.6 %collective-permute-start.37 = (bf16[32,1280]{1,0:T(8,128)(2,1)S(1)}, bf16[32,1280]{1,0:T(8,128)(2,1)S(1)}, u32[]{:S(2)}, u32[]{:S(2)}) collective-permute-start(bf16[32,1280]{1,0:T(8,128)(2,1)S(1)} %add_convert_fusion.7), channel_id=1, source_target_pairs={{0,130},{1,131},{8,138},{9,139},{16,146},{17,147},{24,154},{25,155... | collective-permute-start | bytes 245768 | tf_op jit(solution)/shard_map/ppermute | solution.py:401
  139.9 3.6 %collective-permute-done.37 = bf16[32,1280]{1,0:T(8,128)(2,1)S(1)} collective-permute-done((bf16[32,1280]{1,0:T(8,128)(2,1)S(1)}, bf16[32,1280]{1,0:T(8,128)(2,1)S(1)}, u32[]{:S(2)}, u32[]{:S(2)}) %collective-permute-start.37) | collective-permute-done | bytes 81952 | tf_op jit(solution)/shard_map/ppermute | solution.py:401
  143.6 6.9 %collective-permute-start.38 = (bf16[32,1280]{1,0:T(8,128)(2,1)S(1)}, bf16[32,1280]{1,0:T(8,128)(2,1)S(1)}, u32[]{:S(2)}, u32[]{:S(2)}) collective-permute-start(bf16[32,1280]{1,0:T(8,128)(2,1)S(1)} %add_convert_fusion.6), channel_id=1, source_target_pairs={{0,1},{1,0},{2,3},{3,2},{4,5},{5,4},{6,7},{7,6},{8,9},{9,8},{10,11... | collective-permute-start | bytes 245768 | tf_op jit(solution)/shard_map/ppermute | solution.py:47
  (85 shorter events, 26.3 us)
Async XLA Ops:
  30.8 6.2 %collective-permute-start = (bf16[32,2560]{1,0:T(8,128)(2,1)S(1)}, bf16[32,2560]{1,0:T(8,128)(2,1)S(1)}, u32[]{:S(2)}, u32[]{:S(2)}) collective-permute-start(bf16[32,2560]{1,0:T(8,128)(2,1)S(1)} %get-tuple-element.79.refs_0_), channel_id=1, source_target_pairs={{0,96},{32,0},{64,32},{96,64},{128,224},{160,128},{192,160},{224,1... | collective-permute-start | bytes 491528 | tf_op jit(solution)/shard_map/ppermute | solution.py:33
  33.4 6.2 %collective-permute-start.1 = (bf16[32,2560]{1,0:T(8,128)(2,1)S(1)}, bf16[32,2560]{1,0:T(8,128)(2,1)S(1)}, u32[]{:S(2)}, u32[]{:S(2)}) collective-permute-start(bf16[32,2560]{1,0:T(8,128)(2,1)S(1)} %get-tuple-element.79.refs_0_), channel_id=1, source_target_pairs={{0,32},{32,64},{64,96},{96,0},{128,160},{160,192},{192,224},{224,1... | collective-permute-start | bytes 491528 | tf_op jit(solution)/shard_map/ppermute | solution.py:33
  33.4 6.2 %collective-permute-start.2 = (bf16[32,2560]{1,0:T(8,128)(2,1)S(1)}, bf16[32,2560]{1,0:T(8,128)(2,1)S(1)}, u32[]{:S(2)}, u32[]{:S(2)}) collective-permute-start(bf16[32,2560]{1,0:T(8,128)(2,1)S(1)} %get-tuple-element.79.refs_0_), channel_id=1, source_target_pairs={{0,128},{32,160},{64,192},{96,224},{128,0},{160,32},{192,64},{224,... | collective-permute-start | bytes 491528 | tf_op jit(solution)/shard_map/ppermute | solution.py:33
  34.3 6.8 %collective-permute-start.10 = (bf16[32,2560]{1,0:T(8,128)(2,1)S(1)}, bf16[32,2560]{1,0:T(8,128)(2,1)S(1)}, u32[]{:S(2)}, u32[]{:S(2)}) collective-permute-start(bf16[32,2560]{1,0:T(8,128)(2,1)S(1)} %get-tuple-element.94.refs_0_), channel_id=1, source_target_pairs={{0,96},{32,0},{64,32},{96,64},{128,224},{160,128},{192,160},{224,1... | collective-permute-start | bytes 491528 | tf_op jit(solution)/shard_map/ppermute | solution.py:33
  37.0 5.4 %collective-permute-start.11 = (bf16[32,2560]{1,0:T(8,128)(2,1)S(1)}, bf16[32,2560]{1,0:T(8,128)(2,1)S(1)}, u32[]{:S(2)}, u32[]{:S(2)}) collective-permute-start(bf16[32,2560]{1,0:T(8,128)(2,1)S(1)} %get-tuple-element.94.refs_0_), channel_id=1, source_target_pairs={{0,32},{32,64},{64,96},{96,0},{128,160},{160,192},{192,224},{224,1... | collective-permute-start | bytes 491528 | tf_op jit(solution)/shard_map/ppermute | solution.py:33
  37.0 5.4 %collective-permute-start.12 = (bf16[32,2560]{1,0:T(8,128)(2,1)S(1)}, bf16[32,2560]{1,0:T(8,128)(2,1)S(1)}, u32[]{:S(2)}, u32[]{:S(2)}) collective-permute-start(bf16[32,2560]{1,0:T(8,128)(2,1)S(1)} %get-tuple-element.94.refs_0_), channel_id=1, source_target_pairs={{0,128},{32,160},{64,192},{96,224},{128,0},{160,32},{192,64},{224,... | collective-permute-start | bytes 491528 | tf_op jit(solution)/shard_map/ppermute | solution.py:33
  39.6 5.0 %collective-permute-start.3 = (bf16[32,2560]{1,0:T(8,128)(2,1)S(1)}, bf16[32,2560]{1,0:T(8,128)(2,1)S(1)}, u32[]{:S(2)}, u32[]{:S(2)}) collective-permute-start(bf16[32,2560]{1,0:T(8,128)(2,1)S(1)} %collective-permute-done.refs_1_), channel_id=1, source_target_pairs={{0,96},{32,0},{64,32},{96,64},{128,224},{160,128},{192,160},{224,1... | collective-permute-start | bytes 491528 | tf_op jit(solution)/shard_map/ppermute | solution.py:33
  41.1 5.4 %collective-permute-start.4 = (bf16[32,2560]{1,0:T(8,128)(2,1)S(1)}, bf16[32,2560]{1,0:T(8,128)(2,1)S(1)}, u32[]{:S(2)}, u32[]{:S(2)}) collective-permute-start(bf16[32,2560]{1,0:T(8,128)(2,1)S(1)} %collective-permute-done.2.refs_4_), channel_id=1, source_target_pairs={{0,32},{32,64},{64,96},{96,0},{128,160},{160,192},{192,224},{224,1... | collective-permute-start | bytes 491528 | tf_op jit(solution)/shard_map/ppermute | solution.py:33
  41.1 5.4 %collective-permute-start.5 = (bf16[32,2560]{1,0:T(8,128)(2,1)S(1)}, bf16[32,2560]{1,0:T(8,128)(2,1)S(1)}, u32[]{:S(2)}, u32[]{:S(2)}) collective-permute-start(bf16[32,2560]{1,0:T(8,128)(2,1)S(1)} %collective-permute-done.refs_1_), channel_id=1, source_target_pairs={{0,128},{32,160},{64,192},{96,224},{128,0},{160,32},{192,64},{224,... | collective-permute-start | bytes 491528 | tf_op jit(solution)/shard_map/ppermute | solution.py:33
  42.4 5.8 %collective-permute-start.13 = (bf16[32,2560]{1,0:T(8,128)(2,1)S(1)}, bf16[32,2560]{1,0:T(8,128)(2,1)S(1)}, u32[]{:S(2)}, u32[]{:S(2)}) collective-permute-start(bf16[32,2560]{1,0:T(8,128)(2,1)S(1)} %collective-permute-done.10.refs_1_), channel_id=1, source_target_pairs={{0,96},{32,0},{64,32},{96,64},{128,224},{160,128},{192,160},{224,1... | collective-permute-start | bytes 491528 | tf_op jit(solution)/shard_map/ppermute | solution.py:33
  44.6 6.0 %collective-permute-start.14 = (bf16[32,2560]{1,0:T(8,128)(2,1)S(1)}, bf16[32,2560]{1,0:T(8,128)(2,1)S(1)}, u32[]{:S(2)}, u32[]{:S(2)}) collective-permute-start(bf16[32,2560]{1,0:T(8,128)(2,1)S(1)} %collective-permute-done.12.refs_4_), channel_id=1, source_target_pairs={{0,32},{32,64},{64,96},{96,0},{128,160},{160,192},{192,224},{224,1... | collective-permute-start | bytes 491528 | tf_op jit(solution)/shard_map/ppermute | solution.py:33
  44.6 6.0 %collective-permute-start.15 = (bf16[32,2560]{1,0:T(8,128)(2,1)S(1)}, bf16[32,2560]{1,0:T(8,128)(2,1)S(1)}, u32[]{:S(2)}, u32[]{:S(2)}) collective-permute-start(bf16[32,2560]{1,0:T(8,128)(2,1)S(1)} %collective-permute-done.10.refs_1_), channel_id=1, source_target_pairs={{0,128},{32,160},{64,192},{96,224},{128,0},{160,32},{192,64},{224,... | collective-permute-start | bytes 491528 | tf_op jit(solution)/shard_map/ppermute | solution.py:33
  46.4 5.2 %collective-permute-start.6 = (bf16[32,2560]{1,0:T(8,128)(2,1)S(1)}, bf16[32,2560]{1,0:T(8,128)(2,1)S(1)}, u32[]{:S(2)}, u32[]{:S(2)}) collective-permute-start(bf16[32,2560]{1,0:T(8,128)(2,1)S(1)} %collective-permute-done.5.refs_5_), channel_id=1, source_target_pairs={{0,96},{32,0},{64,32},{96,64},{128,224},{160,128},{192,160},{224,1... | collective-permute-start | bytes 491528 | tf_op jit(solution)/shard_map/ppermute | solution.py:33
  50.5 10.7 %collective-permute-start.16 = (bf16[32,2560]{1,0:T(8,128)(2,1)S(1)}, bf16[32,2560]{1,0:T(8,128)(2,1)S(1)}, u32[]{:S(2)}, u32[]{:S(2)}) collective-permute-start(bf16[32,2560]{1,0:T(8,128)(2,1)S(1)} %collective-permute-done.14.refs_7_), channel_id=1, source_target_pairs={{0,32},{32,64},{64,96},{96,0},{128,160},{160,192},{192,224},{224,1... | collective-permute-start | bytes 491528 | tf_op jit(solution)/shard_map/ppermute | solution.py:33
  57.4 10.1 %collective-permute-start.7 = (bf16[32,2560]{1,0:T(8,128)(2,1)S(1)}, bf16[32,2560]{1,0:T(8,128)(2,1)S(1)}, u32[]{:S(2)}, u32[]{:S(2)}) collective-permute-start(bf16[32,2560]{1,0:T(8,128)(2,1)S(1)} %get-tuple-element.86), channel_id=1, source_target_pairs={{0,32},{32,64},{64,96},{96,0},{128,160},{160,192},{192,224},{224,1... | collective-permute-start | bytes 491528 | tf_op jit(solution)/shard_map/ppermute | solution.py:33
  58.3 10.1 %collective-permute-start.8 = (bf16[32,2560]{1,0:T(8,128)(2,1)S(1)}, bf16[32,2560]{1,0:T(8,128)(2,1)S(1)}, u32[]{:S(2)}, u32[]{:S(2)}) collective-permute-start(bf16[32,2560]{1,0:T(8,128)(2,1)S(1)} %get-tuple-element.87), channel_id=1, source_target_pairs={{0,96},{32,0},{64,32},{96,64},{128,224},{160,128},{192,160},{224,1... | collective-permute-start | bytes 491528 | tf_op jit(solution)/shard_map/ppermute | solution.py:33
  60.7 7.7 %collective-permute-start.9 = (bf16[32,2560]{1,0:T(8,128)(2,1)S(1)}, bf16[32,2560]{1,0:T(8,128)(2,1)S(1)}, u32[]{:S(2)}, u32[]{:S(2)}) collective-permute-start(bf16[32,2560]{1,0:T(8,128)(2,1)S(1)} %get-tuple-element.88), channel_id=1, source_target_pairs={{0,128},{32,160},{64,192},{96,224},{128,0},{160,32},{192,64},{224,... | collective-permute-start | bytes 491528 | tf_op jit(solution)/shard_map/ppermute | solution.py:33
  64.7 6.5 %collective-permute-start.21 = (bf16[32,2560]{1,0:T(8,128)(2,1)S(1)}, bf16[32,2560]{1,0:T(8,128)(2,1)S(1)}, u32[]{:S(2)}, u32[]{:S(2)}) collective-permute-start(bf16[32,2560]{1,0:T(8,128)(2,1)S(1)} %get-tuple-element.114), channel_id=1, source_target_pairs={{0,32},{32,64},{64,96},{96,0},{128,160},{160,192},{192,224},{224,1... | collective-permute-start | bytes 491528 | tf_op jit(solution)/shard_map/ppermute | solution.py:33
  64.8 7.1 %collective-permute-start.22 = (bf16[32,2560]{1,0:T(8,128)(2,1)S(1)}, bf16[32,2560]{1,0:T(8,128)(2,1)S(1)}, u32[]{:S(2)}, u32[]{:S(2)}) collective-permute-start(bf16[32,2560]{1,0:T(8,128)(2,1)S(1)} %get-tuple-element.115), channel_id=1, source_target_pairs={{0,96},{32,0},{64,32},{96,64},{128,224},{160,128},{192,160},{224,1... | collective-permute-start | bytes 491528 | tf_op jit(solution)/shard_map/ppermute | solution.py:33
  68.4 5.5 %collective-permute-start.17 = (bf16[32,2560]{1,0:T(8,128)(2,1)S(1)}, bf16[32,2560]{1,0:T(8,128)(2,1)S(1)}, u32[]{:S(2)}, u32[]{:S(2)}) collective-permute-start(bf16[32,2560]{1,0:T(8,128)(2,1)S(1)} %add_convert_fusion.5), channel_id=1, source_target_pairs={{0,32},{32,64},{64,96},{96,0},{128,160},{160,192},{192,224},{224,1... | collective-permute-start | bytes 491528 | tf_op jit(solution)/shard_map/ppermute | solution.py:33
  68.5 6.3 %collective-permute-start.18 = (bf16[32,2560]{1,0:T(8,128)(2,1)S(1)}, bf16[32,2560]{1,0:T(8,128)(2,1)S(1)}, u32[]{:S(2)}, u32[]{:S(2)}) collective-permute-start(bf16[32,2560]{1,0:T(8,128)(2,1)S(1)} %get-tuple-element.106), channel_id=1, source_target_pairs={{0,96},{32,0},{64,32},{96,64},{128,224},{160,128},{192,160},{224,1... | collective-permute-start | bytes 491528 | tf_op jit(solution)/shard_map/ppermute | solution.py:33
  73.0 6.1 %collective-permute-start.25 = (bf16[32,2560]{1,0:T(8,128)(2,1)S(1)}, bf16[32,2560]{1,0:T(8,128)(2,1)S(1)}, u32[]{:S(2)}, u32[]{:S(2)}) collective-permute-start(bf16[32,2560]{1,0:T(8,128)(2,1)S(1)} %get-tuple-element.125), channel_id=1, source_target_pairs={{0,32},{32,64},{64,96},{96,0},{128,160},{160,192},{192,224},{224,1... | collective-permute-start | bytes 491528 | tf_op jit(solution)/shard_map/ppermute | solution.py:33
  73.9 6.0 %collective-permute-start.26 = (bf16[32,2560]{1,0:T(8,128)(2,1)S(1)}, bf16[32,2560]{1,0:T(8,128)(2,1)S(1)}, u32[]{:S(2)}, u32[]{:S(2)}) collective-permute-start(bf16[32,2560]{1,0:T(8,128)(2,1)S(1)} %add_convert_fusion.1), channel_id=1, source_target_pairs={{0,128},{32,160},{64,192},{96,224},{128,0},{160,32},{192,64},{224,... | collective-permute-start | bytes 491528 | tf_op jit(solution)/shard_map/ppermute | solution.py:33
  75.9 6.1 %collective-permute-start.20 = (bf16[32,2560]{1,0:T(8,128)(2,1)S(1)}, bf16[32,2560]{1,0:T(8,128)(2,1)S(1)}, u32[]{:S(2)}, u32[]{:S(2)}) collective-permute-start(bf16[32,2560]{1,0:T(8,128)(2,1)S(1)} %add_convert_fusion.3), channel_id=1, source_target_pairs={{0,32},{32,64},{64,96},{96,0},{128,160},{160,192},{192,224},{224,1... | collective-permute-start | bytes 491528 | tf_op jit(solution)/shard_map/ppermute | solution.py:33
  79.9 5.7 %collective-permute-start.27 = (bf16[32,2560]{1,0:T(8,128)(2,1)S(1)}, bf16[32,2560]{1,0:T(8,128)(2,1)S(1)}, u32[]{:S(2)}, u32[]{:S(2)}) collective-permute-start(bf16[32,2560]{1,0:T(8,128)(2,1)S(1)} %add_convert_fusion), channel_id=1, source_target_pairs={{0,96},{32,0},{64,32},{96,64},{128,224},{160,128},{192,160},{224,1... | collective-permute-start | bytes 491528 | tf_op jit(solution)/shard_map/ppermute | solution.py:33
  86.5 25.9 %all-to-all-start.1 = ((bf16[32,40,128]{2,1,0:T(8,128)(2,1)}), bf16[32,40,128]{2,1,0:T(8,128)(2,1)S(1)}, u32[]{:S(2)}, u32[]{:S(2)}) async-start(bf16[32,40,128]{2,1,0:T(8,128)(2,1)} %bitcast.5), calls=%async_computation.1 | async-start | bytes 655360 | tf_op jit(solution)/shard_map/all_to_all | solution.py:506
  116.4 4.8 %collective-permute-start.30 = (bf16[32,1280]{1,0:T(8,128)(2,1)S(1)}, bf16[32,1280]{1,0:T(8,128)(2,1)S(1)}, u32[]{:S(2)}, u32[]{:S(2)}) collective-permute-start(bf16[32,1280]{1,0:T(8,128)(2,1)S(1)} %add_convert_fusion.11), channel_id=1, source_target_pairs={{0,64},{1,17},{2,66},{3,19},{4,68},{5,21},{6,70},{7,23},{8,72},{9,... | collective-permute-start | bytes 245768 | tf_op jit(solution)/shard_map/ppermute | solution.py:386
  122.2 4.9 %collective-permute-start.34 = (bf16[32,1280]{1,0:T(8,128)(2,1)S(1)}, bf16[32,1280]{1,0:T(8,128)(2,1)S(1)}, u32[]{:S(2)}, u32[]{:S(2)}) collective-permute-start(bf16[32,1280]{1,0:T(8,128)(2,1)S(1)} %add_convert_fusion.10), channel_id=1, source_target_pairs={{0,24},{1,97},{2,26},{3,99},{4,28},{5,101},{6,30},{7,103},{8,0},{9... | collective-permute-start | bytes 245768 | tf_op jit(solution)/shard_map/ppermute | solution.py:386
  124.9 4.9 %collective-permute-start.33 = (bf16[32,1280]{1,0:T(8,128)(2,1)S(1)}, bf16[32,1280]{1,0:T(8,128)(2,1)S(1)}, u32[]{:S(2)}, u32[]{:S(2)}) collective-permute-start(bf16[32,1280]{1,0:T(8,128)(2,1)S(1)} %add_convert_fusion.10), channel_id=1, source_target_pairs={{0,16},{1,65},{2,18},{3,67},{4,20},{5,69},{6,22},{7,71},{8,24},{9,... | collective-permute-start | bytes 245768 | tf_op jit(solution)/shard_map/ppermute | solution.py:386
  124.9 5.4 %collective-permute-start.32 = (bf16[32,1280]{1,0:T(8,128)(2,1)S(1)}, bf16[32,1280]{1,0:T(8,128)(2,1)S(1)}, u32[]{:S(2)}, u32[]{:S(2)}) collective-permute-start(bf16[32,1280]{1,0:T(8,128)(2,1)S(1)} %add_convert_fusion.10), channel_id=1, source_target_pairs={{0,8},{1,33},{2,10},{3,35},{4,12},{5,37},{6,14},{7,39},{8,16},{9,4... | collective-permute-start | bytes 245768 | tf_op jit(solution)/shard_map/ppermute | solution.py:386
  138.3 5.2 %collective-permute-start.37 = (bf16[32,1280]{1,0:T(8,128)(2,1)S(1)}, bf16[32,1280]{1,0:T(8,128)(2,1)S(1)}, u32[]{:S(2)}, u32[]{:S(2)}) collective-permute-start(bf16[32,1280]{1,0:T(8,128)(2,1)S(1)} %add_convert_fusion.7), channel_id=1, source_target_pairs={{0,130},{1,131},{8,138},{9,139},{16,146},{17,147},{24,154},{25,155... | collective-permute-start | bytes 245768 | tf_op jit(solution)/shard_map/ppermute | solution.py:401
  143.6 7.8 %collective-permute-start.38 = (bf16[32,1280]{1,0:T(8,128)(2,1)S(1)}, bf16[32,1280]{1,0:T(8,128)(2,1)S(1)}, u32[]{:S(2)}, u32[]{:S(2)}) collective-permute-start(bf16[32,1280]{1,0:T(8,128)(2,1)S(1)} %add_convert_fusion.6), channel_id=1, source_target_pairs={{0,1},{1,0},{2,3},{3,2},{4,5},{5,4},{6,7},{7,6},{8,9},{9,8},{10,11... | collective-permute-start | bytes 245768 | tf_op jit(solution)/shard_map/ppermute | solution.py:47
  (14 other events, 109.2 us)

commit v8 on v7

--- a/solution.py
+++ b/solution.py
@@ -149,8 +149,8 @@
 
 
 def front_kernel(
-    each, tok_hbm, cot_hbm, par_hbm, rows_ref, disp_hbm, comb_hbm,
-    slots_ref, flat_ref, tok_ref, cot_ref, par_ref, disp_ref, comb_ref, sems, out_sems,
+    each, tok_hbm, cot_hbm, par_hbm, rows_ref, disp_ref, comb_ref,
+    slots_ref, flat_ref, tok_ref, cot_ref, par_ref, sems,
 ):
     par_loads = start_loads(par_hbm, par_ref, sems.at[0])
     tok_loads = start_loads(tok_hbm, tok_ref, sems.at[1])
@@ -166,12 +166,6 @@
     combine = raised / jnp.sum(raised, axis=0, keepdims=True)
     disp_ref[...] = dispatch
     comb_ref[...] = combine
-    stores = [
-        pltpu.make_async_copy(disp_ref, disp_hbm, out_sems.at[0]),
-        pltpu.make_async_copy(comb_ref, comb_hbm, out_sems.at[1]),
-    ]
-    for copy in stores:
-        copy.start()
     for kind, (weights, values) in enumerate(((dispatch, tok_ref), (combine, cot_ref))):
         if kind == 1:
             wait_all(cot_loads)
@@ -184,7 +178,6 @@
                     k, pl.ds(j, groups, stride=each), :
                 ]
     rows_ref[...] = flat_ref[...].astype(BF16)
-    wait_all(stores)
 
 
 def unpack_kernel(flat_in_ref, ins_ref, cots_ref, flat_ref):
@@ -214,15 +207,9 @@
 
 
 def final_kernel(
-    each, flat_in_ref, tok_ref, cot_ref, disp_hbm, comb_hbm, sig_ref, grad_ref, par_ref,
-    flat_ref, out_f_ref, sig_f_ref, disp_ref, comb_ref, sems,
+    each, flat_in_ref, tok_ref, cot_ref, disp_ref, comb_ref, sig_ref, grad_ref, par_ref,
+    flat_ref, out_f_ref, sig_f_ref,
 ):
-    loads = [
-        pltpu.make_async_copy(disp_hbm, disp_ref, sems.at[0]),
-        pltpu.make_async_copy(comb_hbm, comb_ref, sems.at[1]),
-    ]
-    for copy in loads:
-        copy.start()
     groups = sig_ref.shape[0] // each
     tiles = sig_ref.shape[1] // LANES
     stride = 2 * each * tiles
@@ -239,7 +226,6 @@
     sig_ref[...] = sig
     combine_grad = nt(slot_out, cot_ref[...])
     dispatch_grad = nt(sig, tok_ref[...])
-    wait_all(loads)
     combine = comb_ref[...]
     dispatch = disp_ref[...]
     combine_part = combine * (combine_grad - jnp.sum(combine * combine_grad, axis=0, keepdims=True))
@@ -273,14 +259,16 @@
 
 
 def forward_kernel(count, each, *refs):
-    blocks, (win_ref, wout_hbm) = refs[:count], refs[count : count + 2]
-    parts, (slope_ref, rows_hbm, act_hbm) = refs[count + 2 : 2 * count + 2], refs[-8:-5]
-    wout_ref, act_ref, sems, row_sems, kept_sems = refs[-5:]
+    blocks, (win_hbm, wout_hbm) = refs[:count], refs[count : count + 2]
+    parts, (slope_ref, rows_hbm, act_hbm) = refs[count + 2 : 2 * count + 2], refs[-10:-7]
+    win_ref, wout_ref, act_ref, sems, row_sems, kept_sems, win_sems = refs[-7:]
     width, hidden = win_ref.shape[1:]
+    win_loads = [start_loads(win_hbm.at[j], win_ref.at[j], win_sems.at[j]) for j in range(each)]
     wout_loads = [start_loads(wout_hbm.at[j], wout_ref.at[j], sems.at[j]) for j in range(each)]
     stores = start_stores(blocks, rows_hbm, row_sems)
     for j in range(each):
         hid = slice(j * hidden, (j + 1) * hidden)
+        wait_all(win_loads[j])
         pre_act = jnp.dot(gathered(blocks, j, width), win_ref[j], preferred_element_type=F32)
         gelu_value, slope_ref[:, hid] = gelu_pair(pre_act)
         act_ref[:, hid] = gelu_value.astype(BF16)
@@ -311,7 +299,7 @@
     wait_all(stores)
 
 
-def expert_step(kernel, name, blocks, extra, in_place, first, second, hidden):
+def expert_step(kernel, name, blocks, extra, in_place, first, second, hidden, load_first):
     count = len(blocks)
     each, width = first.shape[0], first.shape[1] * first.shape[2] // hidden
     rows = count * blocks[0].shape[0]
@@ -321,19 +309,22 @@
         [jax.ShapeDtypeStruct(b.shape, BF16) for b in blocks]
         + [jax.ShapeDtypeStruct((rows, each * hidden), F32)] * in_place
         + [pltpu.HBM((rows, each * width), BF16), pltpu.HBM(kept.shape, BF16)],
-        [
+        [pltpu.VMEM(first.shape, BF16)] * load_first
+        + [
             pltpu.VMEM(second.shape, BF16),
             pltpu.VMEM(kept.shape, BF16),
             pltpu.SemaphoreType.DMA((each, PIECES)),
             pltpu.SemaphoreType.DMA((count,)),
             pltpu.SemaphoreType.DMA((1,)),
-        ],
+        ]
+        + [pltpu.SemaphoreType.DMA((each, PIECES))] * load_first,
         4 * rows * each * width * hidden,
         4 * each * width * hidden + 4 * rows * each * width,
         name,
-        in_specs=[in_vmem_spec] * (count + len(extra) + 1) + [in_hbm_spec],
+        in_specs=[in_vmem_spec] * (count + len(extra) + 1 - load_first)
+        + [in_hbm_spec] * (1 + load_first),
         out_specs=[in_vmem_spec] * (count + in_place) + [in_hbm_spec] * 2,
-    )(*blocks, *extra, first, in_hbm(second))
+    )(*blocks, *extra, in_hbm(first) if load_first else first, in_hbm(second))
     return outs[:count], *outs[count:]
 
 
@@ -429,7 +420,7 @@
     flat = groups * 2 * each * tiles
     params = slot_params.T
     flat_shape = jax.ShapeDtypeStruct((flat, LANES), BF16)
-    square = pltpu.HBM((slots, patches), F32)
+    square = pltpu.VMEM((slots, patches), F32)
     dot_flops = 2 * slots * patches * width
     rows, dispatch, combine = local_kernel(
         functools.partial(front_kernel, each),
@@ -440,16 +431,13 @@
             pltpu.VMEM((patches, width), BF16),
             pltpu.VMEM((patches, width), BF16),
             pltpu.VMEM((slots, width), BF16),
-            pltpu.VMEM((slots, patches), F32),
-            pltpu.VMEM((slots, patches), F32),
             pltpu.SemaphoreType.DMA((3, PIECES)),
-            pltpu.SemaphoreType.DMA((2,)),
         ],
         3 * dot_flops,
         4 * patches * width + 2 * flat * LANES,
         "front",
         in_specs=[in_hbm_spec] * 3,
-        out_specs=(in_vmem_spec, in_hbm_spec, in_hbm_spec),
+        out_specs=(in_vmem_spec,) * 3,
     )(in_hbm(tokens), in_hbm(output_grad), in_hbm(params))
     routed = lax.all_to_all(
         rows.reshape(groups, 2 * each * tiles, LANES), "expert", split_axis=0, concat_axis=0,
@@ -469,20 +457,19 @@
     near_b = gather_near(cots)
     near_a = together(*near_a)
     next_a = gather_next(near_a)
-    near_b = together(*near_b)
+    next_a, near_b = together(next_a, near_b)
+    far_a = gather_far(next_a, 0)
     next_b = gather_next(near_b)
-    next_a = together(*next_a)
-    far_a = gather_far(next_a, 0)
-    next_b = together(*next_b)
+    blocks_a = by_offset(ins, near_a, next_a, far_a)
+    parts_a, slope, rows_a, act = expert_step(
+        forward_kernel, "expert_forward", blocks_a, [], 1, weight_in, weight_out, hidden, 1
+    )
+    next_b, parts_a = together(next_b, parts_a)
     far_b = gather_far(next_b, 1)
-    blocks_a = by_offset(ins, near_a, next_a, far_a)
     blocks_b = by_offset(cots, near_b, next_b, far_b)
-    parts_a, slope, rows_a, act = expert_step(
-        forward_kernel, "expert_forward", blocks_a, [], 1, weight_in, weight_out, hidden
-    )
     first_a = scatter_first(parts_a)
     parts_b, rows_b, pre = expert_step(
-        backward_kernel, "expert_backward", blocks_b, [slope], 0, weight_out, weight_in, hidden
+        backward_kernel, "expert_backward", blocks_b, [slope], 0, weight_out, weight_in, hidden, 0
     )
     first_b = scatter_first(parts_b)
     first_a, parts_a, pre = together(first_a, parts_a, pre)
@@ -517,15 +504,11 @@
             pltpu.VMEM((flat, LANES), F32),
             pltpu.VMEM((tiles, slots, LANES), F32),
             pltpu.VMEM((tiles, slots, LANES), F32),
-            pltpu.VMEM((slots, patches), F32),
-            pltpu.VMEM((slots, patches), F32),
-            pltpu.SemaphoreType.DMA((2,)),
         ],
         3 * dot_flops,
         4 * patches * width + 2 * flat * LANES,
         "final",
-        in_specs=[in_vmem_spec] * 3 + [in_hbm_spec] * 2,
-    )(back, tokens, output_grad, in_hbm(dispatch), in_hbm(combine))
+    )(back, tokens, output_grad, dispatch, combine)
     tokens_grad = (
         jnp.einsum("sm,sd->md", dispatch.astype(BF16), slot_in_grad, preferred_element_type=F32)
         + jnp.einsum("sm,sd->md", logits_grad, params, preferred_element_type=F32)

time: 153 us -> 157 us (1.026)
  starting transfers between devices: 54.9 us -> 58 us
  waiting for transfers between devices: 45.6 us -> 48.2 us
  local copies, waits for them, and re-layouts: 1.78 us -> 0.03 us
    ppermute x29, waiting for transfers between devices: 18.4 us -> 21.2 us  [batch_send(): return lax.ppermute(value, 'batch', pairs)]
    all_to_all x1, starting transfers between devices: 11.1 us -> 13.8 us  [body(): lax.all_to_all(packed.reshape(groups, 2 * each * tiles, LANES), 'expert',...]
    unnamed x12 -> x8, local copies, waits for them, and re-layouts: 1.77 us -> 0.02 us
where the time goes in v8:
time: 157 us; the launch traced here: 156 us
  starting transfers between devices  58 us (37%)
  waiting for transfers between devices  48.2 us (31%)
  blocking collectives  27.3 us (17%)
  Pallas kernels  19.2 us (12%)
    ppermute x29, starting transfers between devices, batch_send(): return lax.ppermute(value, 'batch', pairs)  29 us
    all_to_all x1, blocking collectives, body(): lax.all_to_all(rows.reshape(groups, 2 * each * tiles, LANES), 'expert', s...  27.3 us
    ppermute x29, waiting for transfers between devices, batch_send(): return lax.ppermute(value, 'batch', pairs)  21.2 us
    all_to_all x1, starting transfers between devices, body(): lax.all_to_all(packed.reshape(groups, 2 * each * tiles, LANES), 'expert',...  13.8 us
    ppermute x6, waiting for transfers between devices, crossed_send(): return lax.ppermute(value, ('batch', 'expert'), pairs)  8.72 us
    pallas_call x2, Pallas kernels, expert_step(): local_kernel(functools.partial(kernel, count, each), [jax.ShapeDtypeStruc...  8.52 us
    all_to_all x1, waiting for transfers between devices, body(): lax.all_to_all(packed.reshape(groups, 2 * each * tiles, LANES), 'expert',...  8.31 us
    ppermute x2, waiting for transfers between devices, depth_swap(): return lax.ppermute(value, ('batch', 'expert'), pairs)  8.07 us
  transfers between devices with their start and end apart: 40, of which 24 were waited for; matrix products, arithmetic and copies ran while one was open for 1% of the time, Pallas kernels for 9%

profile of v8, /device:TPU:1, one launch (start us, length us, event | category | flops | bytes accessed | tf_op | source)
XLA Modules:
  0.0 156.4 jit_solution(14557117179337586806)
XLA Ops:
  0.6 2.6 %front.1 = (bf16[1280,128]{1,0:T(8,128)(2,1)S(1)}, f32[64,256]{1,0:T(8,128)S(1)}, f32[64,256]{1,0:T(8,128)S(1)}) custom-call(bf16[256,1280]{1,0:T(8,128)(2,1)} %bitcast.13, bf16[256,1280]{1,0:T(8,128)(2,1)} %bitcast.15, bf16[64,1280]{1,0:T(8,128)(2,1)} %bitcast.20), custom_call_target="tpu_custom_call" | custom-call | flops 125829120 | bytes 1638400 | tf_op jit(solution)/shard_map/front/pallas_call | solution.py:425
  3.3 27.3 %all_to_all.10 = bf16[32,40,128]{2,1,0:T(8,128)(2,1)S(1)} all-to-all(bf16[32,40,128]{2,1,0:T(8,128)(2,1)S(1)} %bitcast.19), channel_id=1, replica_groups=mesh['batch'=8,'expert'=32] {'expert'}, dimensions={0} | all-to-all | bytes 655360 | tf_op jit(solution)/shard_map/all_to_all | solution.py:442
  30.8 2.6 %collective-permute-start = (bf16[32,2560]{1,0:T(8,128)(2,1)S(1)}, bf16[32,2560]{1,0:T(8,128)(2,1)S(1)}, u32[]{:S(2)}, u32[]{:S(2)}) collective-permute-start(bf16[32,2560]{1,0:T(8,128)(2,1)S(1)} %get-tuple-element.87.refs_0_), channel_id=1, source_target_pairs={{0,96},{32,0},{64,32},{96,64},{128,224},{160,128},{192,160},{224,1... | collective-permute-start | bytes 491528 | tf_op jit(solution)/shard_map/ppermute | solution.py:33
  34.3 2.7 %collective-permute-start.6 = (bf16[32,2560]{1,0:T(8,128)(2,1)S(1)}, bf16[32,2560]{1,0:T(8,128)(2,1)S(1)}, u32[]{:S(2)}, u32[]{:S(2)}) collective-permute-start(bf16[32,2560]{1,0:T(8,128)(2,1)S(1)} %get-tuple-element.90.refs_0_), channel_id=1, source_target_pairs={{0,96},{32,0},{64,32},{96,64},{128,224},{160,128},{192,160},{224,1... | collective-permute-start | bytes 491528 | tf_op jit(solution)/shard_map/ppermute | solution.py:33
  37.6 1.9 %collective-permute-done.1.refs_3_ = bf16[32,2560]{1,0:T(8,128)(2,1)S(1)} collective-permute-done((bf16[32,2560]{1,0:T(8,128)(2,1)S(1)}, bf16[32,2560]{1,0:T(8,128)(2,1)S(1)}, u32[]{:S(2)}, u32[]{:S(2)}) %collective-permute-start.1) | collective-permute-done | bytes 163872 | tf_op jit(solution)/shard_map/ppermute | solution.py:33
  39.5 1.5 collective-permute-start.3
  42.3 1.7 %collective-permute-done.3.refs_2_ = bf16[32,2560]{1,0:T(8,128)(2,1)S(1)} collective-permute-done((bf16[32,2560]{1,0:T(8,128)(2,1)S(1)}, bf16[32,2560]{1,0:T(8,128)(2,1)S(1)}, u32[]{:S(2)}, u32[]{:S(2)}) %collective-permute-start.3) | collective-permute-done | bytes 163872 | tf_op jit(solution)/shard_map/ppermute | solution.py:33
  44.0 2.4 %collective-permute-done.4.refs_7_ = bf16[32,2560]{1,0:T(8,128)(2,1)S(1)} collective-permute-done((bf16[32,2560]{1,0:T(8,128)(2,1)S(1)}, bf16[32,2560]{1,0:T(8,128)(2,1)S(1)}, u32[]{:S(2)}, u32[]{:S(2)}) %collective-permute-start.4) | collective-permute-done | bytes 163872 | tf_op jit(solution)/shard_map/ppermute | solution.py:33
  46.4 1.8 %collective-permute-start.12 = (bf16[32,2560]{1,0:T(8,128)(2,1)S(1)}, bf16[32,2560]{1,0:T(8,128)(2,1)S(1)}, u32[]{:S(2)}, u32[]{:S(2)}) collective-permute-start(bf16[32,2560]{1,0:T(8,128)(2,1)S(1)} %collective-permute-done.5.refs_5_), channel_id=1, source_target_pairs={{0,96},{32,0},{64,32},{96,64},{128,224},{160,128},{192,160},{224,1... | collective-permute-start | bytes 491528 | tf_op jit(solution)/shard_map/ppermute | solution.py:33
  48.2 1.4 collective-permute-start.10
  50.6 5.1 %expert_forward.1 = (bf16[32,2560]{1,0:T(8,128)(2,1)S(1)}, bf16[32,2560]{1,0:T(8,128)(2,1)S(1)}, bf16[32,2560]{1,0:T(8,128)(2,1)S(1)}, bf16[32,2560]{1,0:T(8,128...) custom-call(bf16[32,2560]{1,0:T(8,128)(2,1)S(1)} %get-tuple-element., ...), custom_call_target="tpu_custom_call" | custom-call | flops 1342177280 | bytes 7864320 | tf_op jit(solution)/shard_map/expert_forward/pallas_call | solution.py:307
  56.9 2.0 %collective-permute-start.14 = (bf16[32,2560]{1,0:T(8,128)(2,1)S(1)}, bf16[32,2560]{1,0:T(8,128)(2,1)S(1)}, u32[]{:S(2)}, u32[]{:S(2)}) collective-permute-start(bf16[32,2560]{1,0:T(8,128)(2,1)S(1)} %get-tuple-element.106), channel_id=1, source_target_pairs={{0,96},{32,0},{64,32},{96,64},{128,224},{160,128},{192,160},{224,1... | collective-permute-start | bytes 491528 | tf_op jit(solution)/shard_map/ppermute | solution.py:33
  59.7 1.7 %collective-permute-done.16.refs_6_ = bf16[32,2560]{1,0:T(8,128)(2,1)S(1)} collective-permute-done((bf16[32,2560]{1,0:T(8,128)(2,1)S(1)}, bf16[32,2560]{1,0:T(8,128)(2,1)S(1)}, u32[]{:S(2)}, u32[]{:S(2)}) %collective-permute-start.16) | collective-permute-done | bytes 163872 | tf_op jit(solution)/shard_map/ppermute | solution.py:33
  61.4 3.5 %expert_backward.1 = (bf16[32,2560]{1,0:T(8,128)(2,1)S(1)}, bf16[32,2560]{1,0:T(8,128)(2,1)S(1)}, bf16[32,2560]{1,0:T(8,128)(2,1)S(1)}, bf16[32,2560]{1,0:T(8,12...) custom-call(bf16[32,2560]{1,0:T(8,128)(2,1)S(1)} %get-tuple-element., ...), custom_call_target="tpu_custom_call" | custom-call | flops 1342177280 | bytes 7864320 | tf_op jit(solution)/shard_map/expert_backward/pallas_call | solution.py:307
  65.1 2.7 %collective-permute-start.18 = (bf16[32,2560]{1,0:T(8,128)(2,1)S(1)}, bf16[32,2560]{1,0:T(8,128)(2,1)S(1)}, u32[]{:S(2)}, u32[]{:S(2)}) collective-permute-start(bf16[32,2560]{1,0:T(8,128)(2,1)S(1)} %get-tuple-element.122), channel_id=1, source_target_pairs={{0,96},{32,0},{64,32},{96,64},{128,224},{160,128},{192,160},{224,1... | collective-permute-start | bytes 491528 | tf_op jit(solution)/shard_map/ppermute | solution.py:33
  68.7 2.7 %collective-permute-start.22 = (bf16[32,2560]{1,0:T(8,128)(2,1)S(1)}, bf16[32,2560]{1,0:T(8,128)(2,1)S(1)}, u32[]{:S(2)}, u32[]{:S(2)}) collective-permute-start(bf16[32,2560]{1,0:T(8,128)(2,1)S(1)} %get-tuple-element.131), channel_id=1, source_target_pairs={{0,96},{32,0},{64,32},{96,64},{128,224},{160,128},{192,160},{224,1... | collective-permute-start | bytes 491528 | tf_op jit(solution)/shard_map/ppermute | solution.py:33
  72.1 2.0 %collective-permute-done.21 = bf16[32,2560]{1,0:T(8,128)(2,1)S(1)} collective-permute-done((bf16[32,2560]{1,0:T(8,128)(2,1)S(1)}, bf16[32,2560]{1,0:T(8,128)(2,1)S(1)}, u32[]{:S(2)}, u32[]{:S(2)}) %collective-permute-start.21) | collective-permute-done | bytes 163872 | tf_op jit(solution)/shard_map/ppermute | solution.py:33
  74.1 1.8 %collective-permute-done.23 = bf16[32,2560]{1,0:T(8,128)(2,1)S(1)} collective-permute-done((bf16[32,2560]{1,0:T(8,128)(2,1)S(1)}, bf16[32,2560]{1,0:T(8,128)(2,1)S(1)}, u32[]{:S(2)}, u32[]{:S(2)}) %collective-permute-start.23) | collective-permute-done | bytes 163872 | tf_op jit(solution)/shard_map/ppermute | solution.py:33
  78.4 3.0 %collective-permute-done.24 = bf16[32,2560]{1,0:T(8,128)(2,1)S(1)} collective-permute-done((bf16[32,2560]{1,0:T(8,128)(2,1)S(1)}, bf16[32,2560]{1,0:T(8,128)(2,1)S(1)}, u32[]{:S(2)}, u32[]{:S(2)}) %collective-permute-start.24) | collective-permute-done | bytes 163872 | tf_op jit(solution)/shard_map/ppermute | solution.py:33
  84.5 3.3 %collective-permute-done.27.refs_7_ = bf16[32,2560]{1,0:T(8,128)(2,1)S(1)} collective-permute-done((bf16[32,2560]{1,0:T(8,128)(2,1)S(1)}, bf16[32,2560]{1,0:T(8,128)(2,1)S(1)}, u32[]{:S(2)}, u32[]{:S(2)}) %collective-permute-start.27) | collective-permute-done | bytes 163872 | tf_op jit(solution)/shard_map/ppermute | solution.py:33
  88.7 13.8 %all-to-all-start.1 = ((bf16[32,40,128]{2,1,0:T(8,128)(2,1)}), bf16[32,40,128]{2,1,0:T(8,128)(2,1)S(1)}, u32[]{:S(2)}, u32[]{:S(2)}) async-start(bf16[32,40,128]{2,1,0:T(8,128)(2,1)} %bitcast.5), calls=%async_computation.1 | async-start | bytes 655360 | tf_op jit(solution)/shard_map/all_to_all | solution.py:493
  102.5 6.1 %weight_grads.1 = (bf16[2,1280,512]{2,1,0:T(8,128)(2,1)}, bf16[2,512,1280]{2,1,0:T(8,128)(2,1)}) custom-call(bf16[256,2560]{1,0:T(8,128)(2,1)} %get-tuple-element.152.ins_ref, bf16[256,2560]{1,0:T(8,128)(2,1)} %get-tuple-element.153.cots_ref, bf16[256,1024]{1,0:T(8,128)(2,1)} %get-tuple-element.154.act_ref, bf16[256,1024]{1,0:T(8,128)(2,1)} %get-tuple-element.155.pre_ref), custom_call_target="tpu_custom_call" | custom-call | flops 1342177280 | bytes 10485760 | tf_op jit(solution)/shard_map/weight_grads/pallas_call | solution.py:340
  108.7 8.3 %all-to-all-done.1 = bf16[32,40,128]{2,1,0:T(8,128)(2,1)S(1)} async-done(((bf16[32,40,128]{2,1,0:T(8,128)(2,1)}), bf16[32,40,128]{2,1,0:T(8,128)(2,1)S(1)}, u32[]{:S(2)}, u32[]{:S(2)}) %all-to-all-start.1) | async-done | bytes 327712 | tf_op jit(solution)/shard_map/all_to_all | solution.py:493
  121.6 1.4 collective-permute-done.31
  123.0 2.0 %collective-permute-done.30 = bf16[32,1280]{1,0:T(8,128)(2,1)S(1)} collective-permute-done((bf16[32,1280]{1,0:T(8,128)(2,1)S(1)}, bf16[32,1280]{1,0:T(8,128)(2,1)S(1)}, u32[]{:S(2)}, u32[]{:S(2)}) %collective-permute-start.30) | collective-permute-done | bytes 81952 | tf_op jit(solution)/shard_map/ppermute | solution.py:377
  126.0 3.0 %collective-permute-start.34 = (bf16[32,1280]{1,0:T(8,128)(2,1)S(1)}, bf16[32,1280]{1,0:T(8,128)(2,1)S(1)}, u32[]{:S(2)}, u32[]{:S(2)}) collective-permute-start(bf16[32,1280]{1,0:T(8,128)(2,1)S(1)} %add_convert_fusion.10), channel_id=1, source_target_pairs={{0,24},{1,97},{2,26},{3,99},{4,28},{5,101},{6,30},{7,103},{8,0},{9... | collective-permute-start | bytes 245768 | tf_op jit(solution)/shard_map/ppermute | solution.py:377
  131.3 2.6 %collective-permute-done.33 = bf16[32,1280]{1,0:T(8,128)(2,1)S(1)} collective-permute-done((bf16[32,1280]{1,0:T(8,128)(2,1)S(1)}, bf16[32,1280]{1,0:T(8,128)(2,1)S(1)}, u32[]{:S(2)}, u32[]{:S(2)}) %collective-permute-start.33) | collective-permute-done | bytes 81952 | tf_op jit(solution)/shard_map/ppermute | solution.py:377
  136.4 1.5 collective-permute-done.35
  138.0 4.5 %collective-permute-done.36 = bf16[32,1280]{1,0:T(8,128)(2,1)S(1)} collective-permute-done((bf16[32,1280]{1,0:T(8,128)(2,1)S(1)}, bf16[32,1280]{1,0:T(8,128)(2,1)S(1)}, u32[]{:S(2)}, u32[]{:S(2)}) %collective-permute-start.36) | collective-permute-done | bytes 81952 | tf_op jit(solution)/shard_map/ppermute | solution.py:392
  142.5 1.6 %collective-permute-start.37 = (bf16[32,1280]{1,0:T(8,128)(2,1)S(1)}, bf16[32,1280]{1,0:T(8,128)(2,1)S(1)}, u32[]{:S(2)}, u32[]{:S(2)}) collective-permute-start(bf16[32,1280]{1,0:T(8,128)(2,1)S(1)} %add_convert_fusion.7), channel_id=1, source_target_pairs={{0,130},{1,131},{8,138},{9,139},{16,146},{17,147},{24,154},{25,155... | collective-permute-start | bytes 245768 | tf_op jit(solution)/shard_map/ppermute | solution.py:392
  144.1 3.6 %collective-permute-done.37 = bf16[32,1280]{1,0:T(8,128)(2,1)S(1)} collective-permute-done((bf16[32,1280]{1,0:T(8,128)(2,1)S(1)}, bf16[32,1280]{1,0:T(8,128)(2,1)S(1)}, u32[]{:S(2)}, u32[]{:S(2)}) %collective-permute-start.37) | collective-permute-done | bytes 81952 | tf_op jit(solution)/shard_map/ppermute | solution.py:392
  147.7 7.0 %collective-permute-start.38 = (bf16[32,1280]{1,0:T(8,128)(2,1)S(1)}, bf16[32,1280]{1,0:T(8,128)(2,1)S(1)}, u32[]{:S(2)}, u32[]{:S(2)}) collective-permute-start(bf16[32,1280]{1,0:T(8,128)(2,1)S(1)} %add_convert_fusion.6), channel_id=1, source_target_pairs={{0,1},{1,0},{2,3},{3,2},{4,5},{5,4},{6,7},{7,6},{8,9},{9,8},{10,11... | collective-permute-start | bytes 245768 | tf_op jit(solution)/shard_map/ppermute | solution.py:47
  (81 shorter events, 26.5 us)
Async XLA Ops:
  30.8 6.2 %collective-permute-start = (bf16[32,2560]{1,0:T(8,128)(2,1)S(1)}, bf16[32,2560]{1,0:T(8,128)(2,1)S(1)}, u32[]{:S(2)}, u32[]{:S(2)}) collective-permute-start(bf16[32,2560]{1,0:T(8,128)(2,1)S(1)} %get-tuple-element.87.refs_0_), channel_id=1, source_target_pairs={{0,96},{32,0},{64,32},{96,64},{128,224},{160,128},{192,160},{224,1... | collective-permute-start | bytes 491528 | tf_op jit(solution)/shard_map/ppermute | solution.py:33
  33.3 6.2 %collective-permute-start.1 = (bf16[32,2560]{1,0:T(8,128)(2,1)S(1)}, bf16[32,2560]{1,0:T(8,128)(2,1)S(1)}, u32[]{:S(2)}, u32[]{:S(2)}) collective-permute-start(bf16[32,2560]{1,0:T(8,128)(2,1)S(1)} %get-tuple-element.87.refs_0_), channel_id=1, source_target_pairs={{0,32},{32,64},{64,96},{96,0},{128,160},{160,192},{192,224},{224,1... | collective-permute-start | bytes 491528 | tf_op jit(solution)/shard_map/ppermute | solution.py:33
  33.3 6.2 %collective-permute-start.2 = (bf16[32,2560]{1,0:T(8,128)(2,1)S(1)}, bf16[32,2560]{1,0:T(8,128)(2,1)S(1)}, u32[]{:S(2)}, u32[]{:S(2)}) collective-permute-start(bf16[32,2560]{1,0:T(8,128)(2,1)S(1)} %get-tuple-element.87.refs_0_), channel_id=1, source_target_pairs={{0,128},{32,160},{64,192},{96,224},{128,0},{160,32},{192,64},{224,... | collective-permute-start | bytes 491528 | tf_op jit(solution)/shard_map/ppermute | solution.py:33
  34.3 6.8 %collective-permute-start.6 = (bf16[32,2560]{1,0:T(8,128)(2,1)S(1)}, bf16[32,2560]{1,0:T(8,128)(2,1)S(1)}, u32[]{:S(2)}, u32[]{:S(2)}) collective-permute-start(bf16[32,2560]{1,0:T(8,128)(2,1)S(1)} %get-tuple-element.90.refs_0_), channel_id=1, source_target_pairs={{0,96},{32,0},{64,32},{96,64},{128,224},{160,128},{192,160},{224,1... | collective-permute-start | bytes 491528 | tf_op jit(solution)/shard_map/ppermute | solution.py:33
  36.9 5.4 %collective-permute-start.7 = (bf16[32,2560]{1,0:T(8,128)(2,1)S(1)}, bf16[32,2560]{1,0:T(8,128)(2,1)S(1)}, u32[]{:S(2)}, u32[]{:S(2)}) collective-permute-start(bf16[32,2560]{1,0:T(8,128)(2,1)S(1)} %get-tuple-element.90.refs_0_), channel_id=1, source_target_pairs={{0,32},{32,64},{64,96},{96,0},{128,160},{160,192},{192,224},{224,1... | collective-permute-start | bytes 491528 | tf_op jit(solution)/shard_map/ppermute | solution.py:33
  37.0 5.4 %collective-permute-start.8 = (bf16[32,2560]{1,0:T(8,128)(2,1)S(1)}, bf16[32,2560]{1,0:T(8,128)(2,1)S(1)}, u32[]{:S(2)}, u32[]{:S(2)}) collective-permute-start(bf16[32,2560]{1,0:T(8,128)(2,1)S(1)} %get-tuple-element.90.refs_0_), channel_id=1, source_target_pairs={{0,128},{32,160},{64,192},{96,224},{128,0},{160,32},{192,64},{224,... | collective-permute-start | bytes 491528 | tf_op jit(solution)/shard_map/ppermute | solution.py:33
  41.0 5.4 %collective-permute-start.4 = (bf16[32,2560]{1,0:T(8,128)(2,1)S(1)}, bf16[32,2560]{1,0:T(8,128)(2,1)S(1)}, u32[]{:S(2)}, u32[]{:S(2)}) collective-permute-start(bf16[32,2560]{1,0:T(8,128)(2,1)S(1)} %collective-permute-done.2.refs_4_), channel_id=1, source_target_pairs={{0,32},{32,64},{64,96},{96,0},{128,160},{160,192},{192,224},{224,1... | collective-permute-start | bytes 491528 | tf_op jit(solution)/shard_map/ppermute | solution.py:33
  41.0 5.4 %collective-permute-start.5 = (bf16[32,2560]{1,0:T(8,128)(2,1)S(1)}, bf16[32,2560]{1,0:T(8,128)(2,1)S(1)}, u32[]{:S(2)}, u32[]{:S(2)}) collective-permute-start(bf16[32,2560]{1,0:T(8,128)(2,1)S(1)} %collective-permute-done.refs_1_), channel_id=1, source_target_pairs={{0,128},{32,160},{64,192},{96,224},{128,0},{160,32},{192,64},{224,... | collective-permute-start | bytes 491528 | tf_op jit(solution)/shard_map/ppermute | solution.py:33
  48.2 7.5 %collective-permute-start.9 = (bf16[32,2560]{1,0:T(8,128)(2,1)S(1)}, bf16[32,2560]{1,0:T(8,128)(2,1)S(1)}, u32[]{:S(2)}, u32[]{:S(2)}) collective-permute-start(bf16[32,2560]{1,0:T(8,128)(2,1)S(1)} %collective-permute-done.6.refs_1_), channel_id=1, source_target_pairs={{0,96},{32,0},{64,32},{96,64},{128,224},{160,128},{192,160},{224,1... | collective-permute-start | bytes 491528 | tf_op jit(solution)/shard_map/ppermute | solution.py:33
  48.2 7.5 %collective-permute-start.10 = (bf16[32,2560]{1,0:T(8,128)(2,1)S(1)}, bf16[32,2560]{1,0:T(8,128)(2,1)S(1)}, u32[]{:S(2)}, u32[]{:S(2)}) collective-permute-start(bf16[32,2560]{1,0:T(8,128)(2,1)S(1)} %collective-permute-done.8.refs_4_), channel_id=1, source_target_pairs={{0,32},{32,64},{64,96},{96,0},{128,160},{160,192},{192,224},{224,1... | collective-permute-start | bytes 491528 | tf_op jit(solution)/shard_map/ppermute | solution.py:33
  49.6 6.0 %collective-permute-start.11 = (bf16[32,2560]{1,0:T(8,128)(2,1)S(1)}, bf16[32,2560]{1,0:T(8,128)(2,1)S(1)}, u32[]{:S(2)}, u32[]{:S(2)}) collective-permute-start(bf16[32,2560]{1,0:T(8,128)(2,1)S(1)} %collective-permute-done.6.refs_1_), channel_id=1, source_target_pairs={{0,128},{32,160},{64,192},{96,224},{128,0},{160,32},{192,64},{224,... | collective-permute-start | bytes 491528 | tf_op jit(solution)/shard_map/ppermute | solution.py:33
  55.7 5.8 %collective-permute-start.16 = (bf16[32,2560]{1,0:T(8,128)(2,1)S(1)}, bf16[32,2560]{1,0:T(8,128)(2,1)S(1)}, u32[]{:S(2)}, u32[]{:S(2)}) collective-permute-start(bf16[32,2560]{1,0:T(8,128)(2,1)S(1)} %collective-permute-done.10.refs_7_), channel_id=1, source_target_pairs={{0,32},{32,64},{64,96},{96,0},{128,160},{160,192},{192,224},{224,1... | collective-permute-start | bytes 491528 | tf_op jit(solution)/shard_map/ppermute | solution.py:33
  55.8 9.1 %collective-permute-start.13 = (bf16[32,2560]{1,0:T(8,128)(2,1)S(1)}, bf16[32,2560]{1,0:T(8,128)(2,1)S(1)}, u32[]{:S(2)}, u32[]{:S(2)}) collective-permute-start(bf16[32,2560]{1,0:T(8,128)(2,1)S(1)} %get-tuple-element.105), channel_id=1, source_target_pairs={{0,32},{32,64},{64,96},{96,0},{128,160},{160,192},{192,224},{224,1... | collective-permute-start | bytes 491528 | tf_op jit(solution)/shard_map/ppermute | solution.py:33
  56.9 8.0 %collective-permute-start.14 = (bf16[32,2560]{1,0:T(8,128)(2,1)S(1)}, bf16[32,2560]{1,0:T(8,128)(2,1)S(1)}, u32[]{:S(2)}, u32[]{:S(2)}) collective-permute-start(bf16[32,2560]{1,0:T(8,128)(2,1)S(1)} %get-tuple-element.106), channel_id=1, source_target_pairs={{0,96},{32,0},{64,32},{96,64},{128,224},{160,128},{192,160},{224,1... | collective-permute-start | bytes 491528 | tf_op jit(solution)/shard_map/ppermute | solution.py:33
  58.9 6.0 %collective-permute-start.15 = (bf16[32,2560]{1,0:T(8,128)(2,1)S(1)}, bf16[32,2560]{1,0:T(8,128)(2,1)S(1)}, u32[]{:S(2)}, u32[]{:S(2)}) collective-permute-start(bf16[32,2560]{1,0:T(8,128)(2,1)S(1)} %get-tuple-element.107), channel_id=1, source_target_pairs={{0,128},{32,160},{64,192},{96,224},{128,0},{160,32},{192,64},{224,... | collective-permute-start | bytes 491528 | tf_op jit(solution)/shard_map/ppermute | solution.py:33
  65.0 6.4 %collective-permute-start.17 = (bf16[32,2560]{1,0:T(8,128)(2,1)S(1)}, bf16[32,2560]{1,0:T(8,128)(2,1)S(1)}, u32[]{:S(2)}, u32[]{:S(2)}) collective-permute-start(bf16[32,2560]{1,0:T(8,128)(2,1)S(1)} %add_convert_fusion.5), channel_id=1, source_target_pairs={{0,32},{32,64},{64,96},{96,0},{128,160},{160,192},{192,224},{224,1... | collective-permute-start | bytes 491528 | tf_op jit(solution)/shard_map/ppermute | solution.py:33
  65.1 7.0 %collective-permute-start.18 = (bf16[32,2560]{1,0:T(8,128)(2,1)S(1)}, bf16[32,2560]{1,0:T(8,128)(2,1)S(1)}, u32[]{:S(2)}, u32[]{:S(2)}) collective-permute-start(bf16[32,2560]{1,0:T(8,128)(2,1)S(1)} %get-tuple-element.122), channel_id=1, source_target_pairs={{0,96},{32,0},{64,32},{96,64},{128,224},{160,128},{192,160},{224,1... | collective-permute-start | bytes 491528 | tf_op jit(solution)/shard_map/ppermute | solution.py:33
  68.7 5.4 %collective-permute-start.21 = (bf16[32,2560]{1,0:T(8,128)(2,1)S(1)}, bf16[32,2560]{1,0:T(8,128)(2,1)S(1)}, u32[]{:S(2)}, u32[]{:S(2)}) collective-permute-start(bf16[32,2560]{1,0:T(8,128)(2,1)S(1)} %get-tuple-element.130), channel_id=1, source_target_pairs={{0,32},{32,64},{64,96},{96,0},{128,160},{160,192},{192,224},{224,1... | collective-permute-start | bytes 491528 | tf_op jit(solution)/shard_map/ppermute | solution.py:33
  68.7 5.4 %collective-permute-start.22 = (bf16[32,2560]{1,0:T(8,128)(2,1)S(1)}, bf16[32,2560]{1,0:T(8,128)(2,1)S(1)}, u32[]{:S(2)}, u32[]{:S(2)}) collective-permute-start(bf16[32,2560]{1,0:T(8,128)(2,1)S(1)} %get-tuple-element.131), channel_id=1, source_target_pairs={{0,96},{32,0},{64,32},{96,64},{128,224},{160,128},{192,160},{224,1... | collective-permute-start | bytes 491528 | tf_op jit(solution)/shard_map/ppermute | solution.py:33
  75.9 5.5 %collective-permute-start.24 = (bf16[32,2560]{1,0:T(8,128)(2,1)S(1)}, bf16[32,2560]{1,0:T(8,128)(2,1)S(1)}, u32[]{:S(2)}, u32[]{:S(2)}) collective-permute-start(bf16[32,2560]{1,0:T(8,128)(2,1)S(1)} %add_convert_fusion.2), channel_id=1, source_target_pairs={{0,96},{32,0},{64,32},{96,64},{128,224},{160,128},{192,160},{224,1... | collective-permute-start | bytes 491528 | tf_op jit(solution)/shard_map/ppermute | solution.py:33
  76.9 5.4 %collective-permute-start.25 = (bf16[32,2560]{1,0:T(8,128)(2,1)S(1)}, bf16[32,2560]{1,0:T(8,128)(2,1)S(1)}, u32[]{:S(2)}, u32[]{:S(2)}) collective-permute-start(bf16[32,2560]{1,0:T(8,128)(2,1)S(1)} %get-tuple-element.141), channel_id=1, source_target_pairs={{0,32},{32,64},{64,96},{96,0},{128,160},{160,192},{192,224},{224,1... | collective-permute-start | bytes 491528 | tf_op jit(solution)/shard_map/ppermute | solution.py:33
  77.5 5.5 %collective-permute-start.26 = (bf16[32,2560]{1,0:T(8,128)(2,1)S(1)}, bf16[32,2560]{1,0:T(8,128)(2,1)S(1)}, u32[]{:S(2)}, u32[]{:S(2)}) collective-permute-start(bf16[32,2560]{1,0:T(8,128)(2,1)S(1)} %add_convert_fusion.1), channel_id=1, source_target_pairs={{0,128},{32,160},{64,192},{96,224},{128,0},{160,32},{192,64},{224,... | collective-permute-start | bytes 491528 | tf_op jit(solution)/shard_map/ppermute | solution.py:33
  78.3 6.2 %collective-permute-start.20 = (bf16[32,2560]{1,0:T(8,128)(2,1)S(1)}, bf16[32,2560]{1,0:T(8,128)(2,1)S(1)}, u32[]{:S(2)}, u32[]{:S(2)}) collective-permute-start(bf16[32,2560]{1,0:T(8,128)(2,1)S(1)} %add_convert_fusion.3), channel_id=1, source_target_pairs={{0,32},{32,64},{64,96},{96,0},{128,160},{160,192},{192,224},{224,1... | collective-permute-start | bytes 491528 | tf_op jit(solution)/shard_map/ppermute | solution.py:33
  83.1 4.6 %collective-permute-start.27 = (bf16[32,2560]{1,0:T(8,128)(2,1)S(1)}, bf16[32,2560]{1,0:T(8,128)(2,1)S(1)}, u32[]{:S(2)}, u32[]{:S(2)}) collective-permute-start(bf16[32,2560]{1,0:T(8,128)(2,1)S(1)} %add_convert_fusion), channel_id=1, source_target_pairs={{0,96},{32,0},{64,32},{96,64},{128,224},{160,128},{192,160},{224,1... | collective-permute-start | bytes 491528 | tf_op jit(solution)/shard_map/ppermute | solution.py:33
  88.7 28.3 %all-to-all-start.1 = ((bf16[32,40,128]{2,1,0:T(8,128)(2,1)}), bf16[32,40,128]{2,1,0:T(8,128)(2,1)S(1)}, u32[]{:S(2)}, u32[]{:S(2)}) async-start(bf16[32,40,128]{2,1,0:T(8,128)(2,1)} %bitcast.5), calls=%async_computation.1 | async-start | bytes 655360 | tf_op jit(solution)/shard_map/all_to_all | solution.py:493
  120.2 4.8 %collective-permute-start.30 = (bf16[32,1280]{1,0:T(8,128)(2,1)S(1)}, bf16[32,1280]{1,0:T(8,128)(2,1)S(1)}, u32[]{:S(2)}, u32[]{:S(2)}) collective-permute-start(bf16[32,1280]{1,0:T(8,128)(2,1)S(1)} %add_convert_fusion.11), channel_id=1, source_target_pairs={{0,64},{1,17},{2,66},{3,19},{4,68},{5,21},{6,70},{7,23},{8,72},{9,... | collective-permute-start | bytes 245768 | tf_op jit(solution)/shard_map/ppermute | solution.py:377
  126.0 5.3 %collective-permute-start.34 = (bf16[32,1280]{1,0:T(8,128)(2,1)S(1)}, bf16[32,1280]{1,0:T(8,128)(2,1)S(1)}, u32[]{:S(2)}, u32[]{:S(2)}) collective-permute-start(bf16[32,1280]{1,0:T(8,128)(2,1)S(1)} %add_convert_fusion.10), channel_id=1, source_target_pairs={{0,24},{1,97},{2,26},{3,99},{4,28},{5,101},{6,30},{7,103},{8,0},{9... | collective-permute-start | bytes 245768 | tf_op jit(solution)/shard_map/ppermute | solution.py:377
  129.0 4.9 %collective-permute-start.33 = (bf16[32,1280]{1,0:T(8,128)(2,1)S(1)}, bf16[32,1280]{1,0:T(8,128)(2,1)S(1)}, u32[]{:S(2)}, u32[]{:S(2)}) collective-permute-start(bf16[32,1280]{1,0:T(8,128)(2,1)S(1)} %add_convert_fusion.10), channel_id=1, source_target_pairs={{0,16},{1,65},{2,18},{3,67},{4,20},{5,69},{6,22},{7,71},{8,24},{9,... | collective-permute-start | bytes 245768 | tf_op jit(solution)/shard_map/ppermute | solution.py:377
  129.0 5.4 %collective-permute-start.32 = (bf16[32,1280]{1,0:T(8,128)(2,1)S(1)}, bf16[32,1280]{1,0:T(8,128)(2,1)S(1)}, u32[]{:S(2)}, u32[]{:S(2)}) collective-permute-start(bf16[32,1280]{1,0:T(8,128)(2,1)S(1)} %add_convert_fusion.10), channel_id=1, source_target_pairs={{0,8},{1,33},{2,10},{3,35},{4,12},{5,37},{6,14},{7,39},{8,16},{9,4... | collective-permute-start | bytes 245768 | tf_op jit(solution)/shard_map/ppermute | solution.py:377
  137.9 4.6 %collective-permute-start.36 = (bf16[32,1280]{1,0:T(8,128)(2,1)S(1)}, bf16[32,1280]{1,0:T(8,128)(2,1)S(1)}, u32[]{:S(2)}, u32[]{:S(2)}) collective-permute-start(bf16[32,1280]{1,0:T(8,128)(2,1)S(1)} %add_convert_fusion.8), channel_id=1, source_target_pairs={{0,134},{1,135},{8,142},{9,143},{16,150},{17,151},{24,158},{25,159... | collective-permute-start | bytes 245768 | tf_op jit(solution)/shard_map/ppermute | solution.py:392
  142.5 5.2 %collective-permute-start.37 = (bf16[32,1280]{1,0:T(8,128)(2,1)S(1)}, bf16[32,1280]{1,0:T(8,128)(2,1)S(1)}, u32[]{:S(2)}, u32[]{:S(2)}) collective-permute-start(bf16[32,1280]{1,0:T(8,128)(2,1)S(1)} %add_convert_fusion.7), channel_id=1, source_target_pairs={{0,130},{1,131},{8,138},{9,139},{16,146},{17,147},{24,154},{25,155... | collective-permute-start | bytes 245768 | tf_op jit(solution)/shard_map/ppermute | solution.py:392
  147.7 7.9 %collective-permute-start.38 = (bf16[32,1280]{1,0:T(8,128)(2,1)S(1)}, bf16[32,1280]{1,0:T(8,128)(2,1)S(1)}, u32[]{:S(2)}, u32[]{:S(2)}) collective-permute-start(bf16[32,1280]{1,0:T(8,128)(2,1)S(1)} %add_convert_fusion.6), channel_id=1, source_target_pairs={{0,1},{1,0},{2,3},{3,2},{4,5},{5,4},{6,7},{7,6},{8,9},{9,8},{10,11... | collective-permute-start | bytes 245768 | tf_op jit(solution)/shard_map/ppermute | solution.py:47
  (12 other events, 87.5 us)

commit v9 on v8

--- a/solution.py
+++ b/solution.py
@@ -457,16 +457,17 @@
     near_b = gather_near(cots)
     near_a = together(*near_a)
     next_a = gather_next(near_a)
-    next_a, near_b = together(next_a, near_b)
+    near_b = together(*near_b)
+    next_b = gather_next(near_b)
+    next_a = together(*next_a)
     far_a = gather_far(next_a, 0)
-    next_b = gather_next(near_b)
+    next_b = together(*next_b)
+    far_b = gather_far(next_b, 1)
     blocks_a = by_offset(ins, near_a, next_a, far_a)
+    blocks_b = by_offset(cots, near_b, next_b, far_b)
     parts_a, slope, rows_a, act = expert_step(
         forward_kernel, "expert_forward", blocks_a, [], 1, weight_in, weight_out, hidden, 1
     )
-    next_b, parts_a = together(next_b, parts_a)
-    far_b = gather_far(next_b, 1)
-    blocks_b = by_offset(cots, near_b, next_b, far_b)
     first_a = scatter_first(parts_a)
     parts_b, rows_b, pre = expert_step(
         backward_kernel, "expert_backward", blocks_b, [slope], 0, weight_out, weight_in, hidden, 0

time: 157 us -> 151 us (0.962)
  starting transfers between devices: 58 us -> 54.8 us
  waiting for transfers between devices: 48.2 us -> 45.6 us
    ppermute x29, waiting for transfers between devices: 21.2 us -> 18.4 us  [batch_send(): return lax.ppermute(value, 'batch', pairs)]
    all_to_all x1, starting transfers between devices: 13.8 us -> 11.1 us  [body(): lax.all_to_all(packed.reshape(groups, 2 * each * tiles, LANES), 'expert',...]
  transfers between devices with their start and end apart: 40 -> 40, of which waited for: 24 -> 24; matrix products, arithmetic and copies ran while one was open for 1% -> 1% of each run, Pallas kernels for 9% -> 10%
where the time goes in v9:
time: 151 us
  starting transfers between devices  54.8 us (36%)
  waiting for transfers between devices  45.6 us (30%)
  blocking collectives  27.3 us (18%)
  Pallas kernels  19.2 us (13%)
  matrix products  1.54 us (1%)
    ppermute x29, starting transfers between devices, batch_send(): return lax.ppermute(value, 'batch', pairs)  29 us
    all_to_all x1, blocking collectives, body(): lax.all_to_all(rows.reshape(groups, 2 * each * tiles, LANES), 'expert', s...  27.3 us
    ppermute x29, waiting for transfers between devices, batch_send(): return lax.ppermute(value, 'batch', pairs)  18.4 us
    all_to_all x1, starting transfers between devices, body(): lax.all_to_all(packed.reshape(groups, 2 * each * tiles, LANES), 'expert',...  11.1 us
    ppermute x6, waiting for transfers between devices, crossed_send(): return lax.ppermute(value, ('batch', 'expert'), pairs)  8.69 us
    all_to_all x1, waiting for transfers between devices, body(): lax.all_to_all(packed.reshape(groups, 2 * each * tiles, LANES), 'expert',...  8.6 us
    pallas_call x2, Pallas kernels, expert_step(): local_kernel(functools.partial(kernel, count, each), [jax.ShapeDtypeStruc...  8.52 us
    ppermute x2, waiting for transfers between devices, depth_swap(): return lax.ppermute(value, ('batch', 'expert'), pairs)  8.08 us
  transfers between devices with their start and end apart: 40, of which 24 were waited for; matrix products, arithmetic and copies ran while one was open for 1% of the time, Pallas kernels for 10%

profile of v9, /device:TPU:1, one launch (start us, length us, event | category | flops | bytes accessed | tf_op | source)
XLA Modules:
  0.0 150.6 jit_solution(1028961720904854778)
XLA Ops:
  0.6 2.6 %front.1 = (bf16[1280,128]{1,0:T(8,128)(2,1)S(1)}, f32[64,256]{1,0:T(8,128)S(1)}, f32[64,256]{1,0:T(8,128)S(1)}) custom-call(bf16[256,1280]{1,0:T(8,128)(2,1)} %bitcast.13, bf16[256,1280]{1,0:T(8,128)(2,1)} %bitcast.15, bf16[64,1280]{1,0:T(8,128)(2,1)} %bitcast.20), custom_call_target="tpu_custom_call" | custom-call | flops 125829120 | bytes 1638400 | tf_op jit(solution)/shard_map/front/pallas_call | solution.py:425
  3.3 27.3 %all_to_all.10 = bf16[32,40,128]{2,1,0:T(8,128)(2,1)S(1)} all-to-all(bf16[32,40,128]{2,1,0:T(8,128)(2,1)S(1)} %bitcast.19), channel_id=1, replica_groups=mesh['batch'=8,'expert'=32] {'expert'}, dimensions={0} | all-to-all | bytes 655360 | tf_op jit(solution)/shard_map/all_to_all | solution.py:442
  30.8 2.6 %collective-permute-start = (bf16[32,2560]{1,0:T(8,128)(2,1)S(1)}, bf16[32,2560]{1,0:T(8,128)(2,1)S(1)}, u32[]{:S(2)}, u32[]{:S(2)}) collective-permute-start(bf16[32,2560]{1,0:T(8,128)(2,1)S(1)} %get-tuple-element.79.refs_0_), channel_id=1, source_target_pairs={{0,96},{32,0},{64,32},{96,64},{128,224},{160,128},{192,160},{224,1... | collective-permute-start | bytes 491528 | tf_op jit(solution)/shard_map/ppermute | solution.py:33
  34.3 2.7 %collective-permute-start.10 = (bf16[32,2560]{1,0:T(8,128)(2,1)S(1)}, bf16[32,2560]{1,0:T(8,128)(2,1)S(1)}, u32[]{:S(2)}, u32[]{:S(2)}) collective-permute-start(bf16[32,2560]{1,0:T(8,128)(2,1)S(1)} %get-tuple-element.94.refs_0_), channel_id=1, source_target_pairs={{0,96},{32,0},{64,32},{96,64},{128,224},{160,128},{192,160},{224,1... | collective-permute-start | bytes 491528 | tf_op jit(solution)/shard_map/ppermute | solution.py:33
  37.6 1.9 %collective-permute-done.1.refs_3_ = bf16[32,2560]{1,0:T(8,128)(2,1)S(1)} collective-permute-done((bf16[32,2560]{1,0:T(8,128)(2,1)S(1)}, bf16[32,2560]{1,0:T(8,128)(2,1)S(1)}, u32[]{:S(2)}, u32[]{:S(2)}) %collective-permute-start.1) | collective-permute-done | bytes 163872 | tf_op jit(solution)/shard_map/ppermute | solution.py:33
  39.5 1.5 collective-permute-start.3
  42.3 2.2 %collective-permute-start.13 = (bf16[32,2560]{1,0:T(8,128)(2,1)S(1)}, bf16[32,2560]{1,0:T(8,128)(2,1)S(1)}, u32[]{:S(2)}, u32[]{:S(2)}) collective-permute-start(bf16[32,2560]{1,0:T(8,128)(2,1)S(1)} %collective-permute-done.10.refs_1_), channel_id=1, source_target_pairs={{0,96},{32,0},{64,32},{96,64},{128,224},{160,128},{192,160},{224,1... | collective-permute-start | bytes 491528 | tf_op jit(solution)/shard_map/ppermute | solution.py:33
  46.4 1.8 %collective-permute-start.6 = (bf16[32,2560]{1,0:T(8,128)(2,1)S(1)}, bf16[32,2560]{1,0:T(8,128)(2,1)S(1)}, u32[]{:S(2)}, u32[]{:S(2)}) collective-permute-start(bf16[32,2560]{1,0:T(8,128)(2,1)S(1)} %collective-permute-done.5.refs_5_), channel_id=1, source_target_pairs={{0,96},{32,0},{64,32},{96,64},{128,224},{160,128},{192,160},{224,1... | collective-permute-start | bytes 491528 | tf_op jit(solution)/shard_map/ppermute | solution.py:33
  48.2 2.3 %collective-permute-done.14.refs_7_ = bf16[32,2560]{1,0:T(8,128)(2,1)S(1)} collective-permute-done((bf16[32,2560]{1,0:T(8,128)(2,1)S(1)}, bf16[32,2560]{1,0:T(8,128)(2,1)S(1)}, u32[]{:S(2)}, u32[]{:S(2)}) %collective-permute-start.14) | collective-permute-done | bytes 163872 | tf_op jit(solution)/shard_map/ppermute | solution.py:33
  51.6 5.1 %expert_forward.1 = (bf16[32,2560]{1,0:T(8,128)(2,1)S(1)}, bf16[32,2560]{1,0:T(8,128)(2,1)S(1)}, bf16[32,2560]{1,0:T(8,128)(2,1)S(1)}, bf16[32,2560]{1,0:T(8,128...) custom-call(bf16[32,2560]{1,0:T(8,128)(2,1)S(1)} %get-tuple-element., ...), custom_call_target="tpu_custom_call" | custom-call | flops 1342177280 | bytes 7864320 | tf_op jit(solution)/shard_map/expert_forward/pallas_call | solution.py:307
  57.5 2.4 %collective-permute-start.8 = (bf16[32,2560]{1,0:T(8,128)(2,1)S(1)}, bf16[32,2560]{1,0:T(8,128)(2,1)S(1)}, u32[]{:S(2)}, u32[]{:S(2)}) collective-permute-start(bf16[32,2560]{1,0:T(8,128)(2,1)S(1)} %get-tuple-element.87), channel_id=1, source_target_pairs={{0,96},{32,0},{64,32},{96,64},{128,224},{160,128},{192,160},{224,1... | collective-permute-start | bytes 491528 | tf_op jit(solution)/shard_map/ppermute | solution.py:33
  60.5 3.5 %expert_backward.1 = (bf16[32,2560]{1,0:T(8,128)(2,1)S(1)}, bf16[32,2560]{1,0:T(8,128)(2,1)S(1)}, bf16[32,2560]{1,0:T(8,128)(2,1)S(1)}, bf16[32,2560]{1,0:T(8,12...) custom-call(bf16[32,2560]{1,0:T(8,128)(2,1)S(1)} %get-tuple-element., ...), custom_call_target="tpu_custom_call" | custom-call | flops 1342177280 | bytes 7864320 | tf_op jit(solution)/shard_map/expert_backward/pallas_call | solution.py:307
  64.0 2.7 %collective-permute-start.22 = (bf16[32,2560]{1,0:T(8,128)(2,1)S(1)}, bf16[32,2560]{1,0:T(8,128)(2,1)S(1)}, u32[]{:S(2)}, u32[]{:S(2)}) collective-permute-start(bf16[32,2560]{1,0:T(8,128)(2,1)S(1)} %get-tuple-element.115), channel_id=1, source_target_pairs={{0,96},{32,0},{64,32},{96,64},{128,224},{160,128},{192,160},{224,1... | collective-permute-start | bytes 491528 | tf_op jit(solution)/shard_map/ppermute | solution.py:33
  67.8 2.7 %collective-permute-start.18 = (bf16[32,2560]{1,0:T(8,128)(2,1)S(1)}, bf16[32,2560]{1,0:T(8,128)(2,1)S(1)}, u32[]{:S(2)}, u32[]{:S(2)}) collective-permute-start(bf16[32,2560]{1,0:T(8,128)(2,1)S(1)} %get-tuple-element.106), channel_id=1, source_target_pairs={{0,96},{32,0},{64,32},{96,64},{128,224},{160,128},{192,160},{224,1... | collective-permute-start | bytes 491528 | tf_op jit(solution)/shard_map/ppermute | solution.py:33
  76.0 2.5 %collective-permute-done.25.refs_5_ = bf16[32,2560]{1,0:T(8,128)(2,1)S(1)} collective-permute-done((bf16[32,2560]{1,0:T(8,128)(2,1)S(1)}, bf16[32,2560]{1,0:T(8,128)(2,1)S(1)}, u32[]{:S(2)}, u32[]{:S(2)}) %collective-permute-start.25) | collective-permute-done | bytes 163872 | tf_op jit(solution)/shard_map/ppermute | solution.py:33
  79.7 1.5 collective-permute-done.20.refs_3_
  81.2 3.7 %collective-permute-done.27.refs_7_ = bf16[32,2560]{1,0:T(8,128)(2,1)S(1)} collective-permute-done((bf16[32,2560]{1,0:T(8,128)(2,1)S(1)}, bf16[32,2560]{1,0:T(8,128)(2,1)S(1)}, u32[]{:S(2)}, u32[]{:S(2)}) %collective-permute-start.27) | collective-permute-done | bytes 163872 | tf_op jit(solution)/shard_map/ppermute | solution.py:33
  85.8 11.1 %all-to-all-start.1 = ((bf16[32,40,128]{2,1,0:T(8,128)(2,1)}), bf16[32,40,128]{2,1,0:T(8,128)(2,1)S(1)}, u32[]{:S(2)}, u32[]{:S(2)}) async-start(bf16[32,40,128]{2,1,0:T(8,128)(2,1)} %bitcast.5), calls=%async_computation.1 | async-start | bytes 655360 | tf_op jit(solution)/shard_map/all_to_all | solution.py:494
  97.0 6.1 %weight_grads.1 = (bf16[2,1280,512]{2,1,0:T(8,128)(2,1)}, bf16[2,512,1280]{2,1,0:T(8,128)(2,1)}) custom-call(bf16[256,2560]{1,0:T(8,128)(2,1)} %get-tuple-element.136.ins_ref, bf16[256,2560]{1,0:T(8,128)(2,1)} %get-tuple-element.137.cots_ref, bf16[256,1024]{1,0:T(8,128)(2,1)} %get-tuple-element.138.act_ref, bf16[256,1024]{1,0:T(8,128)(2,1)} %get-tuple-element.139.pre_ref), custom_call_target="tpu_custom_call" | custom-call | flops 1342177280 | bytes 10485760 | tf_op jit(solution)/shard_map/weight_grads/pallas_call | solution.py:340
  103.1 8.6 %all-to-all-done.1 = bf16[32,40,128]{2,1,0:T(8,128)(2,1)S(1)} async-done(((bf16[32,40,128]{2,1,0:T(8,128)(2,1)}), bf16[32,40,128]{2,1,0:T(8,128)(2,1)S(1)}, u32[]{:S(2)}, u32[]{:S(2)}) %all-to-all-start.1) | async-done | bytes 327712 | tf_op jit(solution)/shard_map/all_to_all | solution.py:494
  114.9 1.3 collective-permute-start.30
  116.3 1.4 collective-permute-done.31
  117.8 1.9 %collective-permute-done.30 = bf16[32,1280]{1,0:T(8,128)(2,1)S(1)} collective-permute-done((bf16[32,1280]{1,0:T(8,128)(2,1)S(1)}, bf16[32,1280]{1,0:T(8,128)(2,1)S(1)}, u32[]{:S(2)}, u32[]{:S(2)}) %collective-permute-start.30) | collective-permute-done | bytes 81952 | tf_op jit(solution)/shard_map/ppermute | solution.py:377
  120.7 2.7 %collective-permute-start.34 = (bf16[32,1280]{1,0:T(8,128)(2,1)S(1)}, bf16[32,1280]{1,0:T(8,128)(2,1)S(1)}, u32[]{:S(2)}, u32[]{:S(2)}) collective-permute-start(bf16[32,1280]{1,0:T(8,128)(2,1)S(1)} %add_convert_fusion.10), channel_id=1, source_target_pairs={{0,24},{1,97},{2,26},{3,99},{4,28},{5,101},{6,30},{7,103},{8,0},{9... | collective-permute-start | bytes 245768 | tf_op jit(solution)/shard_map/ppermute | solution.py:377
  124.4 1.2 collective-permute-done.34
  125.7 2.6 %collective-permute-done.33 = bf16[32,1280]{1,0:T(8,128)(2,1)S(1)} collective-permute-done((bf16[32,1280]{1,0:T(8,128)(2,1)S(1)}, bf16[32,1280]{1,0:T(8,128)(2,1)S(1)}, u32[]{:S(2)}, u32[]{:S(2)}) %collective-permute-start.33) | collective-permute-done | bytes 81952 | tf_op jit(solution)/shard_map/ppermute | solution.py:377
  129.5 1.2 fusion
  130.7 1.5 %collective-permute-done.35 = bf16[32,1280]{1,0:T(8,128)(2,1)S(1)} collective-permute-done((bf16[32,1280]{1,0:T(8,128)(2,1)S(1)}, bf16[32,1280]{1,0:T(8,128)(2,1)S(1)}, u32[]{:S(2)}, u32[]{:S(2)}) %collective-permute-start.35) | collective-permute-done | bytes 81952 | tf_op jit(solution)/shard_map/ppermute | solution.py:33
  132.3 4.5 %collective-permute-done.36 = bf16[32,1280]{1,0:T(8,128)(2,1)S(1)} collective-permute-done((bf16[32,1280]{1,0:T(8,128)(2,1)S(1)}, bf16[32,1280]{1,0:T(8,128)(2,1)S(1)}, u32[]{:S(2)}, u32[]{:S(2)}) %collective-permute-start.36) | collective-permute-done | bytes 81952 | tf_op jit(solution)/shard_map/ppermute | solution.py:392
  136.9 1.6 %collective-permute-start.37 = (bf16[32,1280]{1,0:T(8,128)(2,1)S(1)}, bf16[32,1280]{1,0:T(8,128)(2,1)S(1)}, u32[]{:S(2)}, u32[]{:S(2)}) collective-permute-start(bf16[32,1280]{1,0:T(8,128)(2,1)S(1)} %add_convert_fusion.7), channel_id=1, source_target_pairs={{0,130},{1,131},{8,138},{9,139},{16,146},{17,147},{24,154},{25,155... | collective-permute-start | bytes 245768 | tf_op jit(solution)/shard_map/ppermute | solution.py:392
  138.4 3.6 %collective-permute-done.37 = bf16[32,1280]{1,0:T(8,128)(2,1)S(1)} collective-permute-done((bf16[32,1280]{1,0:T(8,128)(2,1)S(1)}, bf16[32,1280]{1,0:T(8,128)(2,1)S(1)}, u32[]{:S(2)}, u32[]{:S(2)}) %collective-permute-start.37) | collective-permute-done | bytes 81952 | tf_op jit(solution)/shard_map/ppermute | solution.py:392
  142.1 6.9 %collective-permute-start.38 = (bf16[32,1280]{1,0:T(8,128)(2,1)S(1)}, bf16[32,1280]{1,0:T(8,128)(2,1)S(1)}, u32[]{:S(2)}, u32[]{:S(2)}) collective-permute-start(bf16[32,1280]{1,0:T(8,128)(2,1)S(1)} %add_convert_fusion.6), channel_id=1, source_target_pairs={{0,1},{1,0},{2,3},{3,2},{4,5},{5,4},{6,7},{7,6},{8,9},{9,8},{10,11... | collective-permute-start | bytes 245768 | tf_op jit(solution)/shard_map/ppermute | solution.py:47
  (81 shorter events, 24.7 us)
Async XLA Ops:
  30.8 6.2 %collective-permute-start = (bf16[32,2560]{1,0:T(8,128)(2,1)S(1)}, bf16[32,2560]{1,0:T(8,128)(2,1)S(1)}, u32[]{:S(2)}, u32[]{:S(2)}) collective-permute-start(bf16[32,2560]{1,0:T(8,128)(2,1)S(1)} %get-tuple-element.79.refs_0_), channel_id=1, source_target_pairs={{0,96},{32,0},{64,32},{96,64},{128,224},{160,128},{192,160},{224,1... | collective-permute-start | bytes 491528 | tf_op jit(solution)/shard_map/ppermute | solution.py:33
  33.3 6.2 %collective-permute-start.1 = (bf16[32,2560]{1,0:T(8,128)(2,1)S(1)}, bf16[32,2560]{1,0:T(8,128)(2,1)S(1)}, u32[]{:S(2)}, u32[]{:S(2)}) collective-permute-start(bf16[32,2560]{1,0:T(8,128)(2,1)S(1)} %get-tuple-element.79.refs_0_), channel_id=1, source_target_pairs={{0,32},{32,64},{64,96},{96,0},{128,160},{160,192},{192,224},{224,1... | collective-permute-start | bytes 491528 | tf_op jit(solution)/shard_map/ppermute | solution.py:33
  33.3 6.2 %collective-permute-start.2 = (bf16[32,2560]{1,0:T(8,128)(2,1)S(1)}, bf16[32,2560]{1,0:T(8,128)(2,1)S(1)}, u32[]{:S(2)}, u32[]{:S(2)}) collective-permute-start(bf16[32,2560]{1,0:T(8,128)(2,1)S(1)} %get-tuple-element.79.refs_0_), channel_id=1, source_target_pairs={{0,128},{32,160},{64,192},{96,224},{128,0},{160,32},{192,64},{224,... | collective-permute-start | bytes 491528 | tf_op jit(solution)/shard_map/ppermute | solution.py:33
  34.3 6.8 %collective-permute-start.10 = (bf16[32,2560]{1,0:T(8,128)(2,1)S(1)}, bf16[32,2560]{1,0:T(8,128)(2,1)S(1)}, u32[]{:S(2)}, u32[]{:S(2)}) collective-permute-start(bf16[32,2560]{1,0:T(8,128)(2,1)S(1)} %get-tuple-element.94.refs_0_), channel_id=1, source_target_pairs={{0,96},{32,0},{64,32},{96,64},{128,224},{160,128},{192,160},{224,1... | collective-permute-start | bytes 491528 | tf_op jit(solution)/shard_map/ppermute | solution.py:33
  36.9 5.4 %collective-permute-start.11 = (bf16[32,2560]{1,0:T(8,128)(2,1)S(1)}, bf16[32,2560]{1,0:T(8,128)(2,1)S(1)}, u32[]{:S(2)}, u32[]{:S(2)}) collective-permute-start(bf16[32,2560]{1,0:T(8,128)(2,1)S(1)} %get-tuple-element.94.refs_0_), channel_id=1, source_target_pairs={{0,32},{32,64},{64,96},{96,0},{128,160},{160,192},{192,224},{224,1... | collective-permute-start | bytes 491528 | tf_op jit(solution)/shard_map/ppermute | solution.py:33
  37.0 5.4 %collective-permute-start.12 = (bf16[32,2560]{1,0:T(8,128)(2,1)S(1)}, bf16[32,2560]{1,0:T(8,128)(2,1)S(1)}, u32[]{:S(2)}, u32[]{:S(2)}) collective-permute-start(bf16[32,2560]{1,0:T(8,128)(2,1)S(1)} %get-tuple-element.94.refs_0_), channel_id=1, source_target_pairs={{0,128},{32,160},{64,192},{96,224},{128,0},{160,32},{192,64},{224,... | collective-permute-start | bytes 491528 | tf_op jit(solution)/shard_map/ppermute | solution.py:33
  39.5 5.0 %collective-permute-start.3 = (bf16[32,2560]{1,0:T(8,128)(2,1)S(1)}, bf16[32,2560]{1,0:T(8,128)(2,1)S(1)}, u32[]{:S(2)}, u32[]{:S(2)}) collective-permute-start(bf16[32,2560]{1,0:T(8,128)(2,1)S(1)} %collective-permute-done.refs_1_), channel_id=1, source_target_pairs={{0,96},{32,0},{64,32},{96,64},{128,224},{160,128},{192,160},{224,1... | collective-permute-start | bytes 491528 | tf_op jit(solution)/shard_map/ppermute | solution.py:33
  41.0 5.4 %collective-permute-start.4 = (bf16[32,2560]{1,0:T(8,128)(2,1)S(1)}, bf16[32,2560]{1,0:T(8,128)(2,1)S(1)}, u32[]{:S(2)}, u32[]{:S(2)}) collective-permute-start(bf16[32,2560]{1,0:T(8,128)(2,1)S(1)} %collective-permute-done.2.refs_4_), channel_id=1, source_target_pairs={{0,32},{32,64},{64,96},{96,0},{128,160},{160,192},{192,224},{224,1... | collective-permute-start | bytes 491528 | tf_op jit(solution)/shard_map/ppermute | solution.py:33
  41.0 5.4 %collective-permute-start.5 = (bf16[32,2560]{1,0:T(8,128)(2,1)S(1)}, bf16[32,2560]{1,0:T(8,128)(2,1)S(1)}, u32[]{:S(2)}, u32[]{:S(2)}) collective-permute-start(bf16[32,2560]{1,0:T(8,128)(2,1)S(1)} %collective-permute-done.refs_1_), channel_id=1, source_target_pairs={{0,128},{32,160},{64,192},{96,224},{128,0},{160,32},{192,64},{224,... | collective-permute-start | bytes 491528 | tf_op jit(solution)/shard_map/ppermute | solution.py:33
  42.3 5.8 %collective-permute-start.13 = (bf16[32,2560]{1,0:T(8,128)(2,1)S(1)}, bf16[32,2560]{1,0:T(8,128)(2,1)S(1)}, u32[]{:S(2)}, u32[]{:S(2)}) collective-permute-start(bf16[32,2560]{1,0:T(8,128)(2,1)S(1)} %collective-permute-done.10.refs_1_), channel_id=1, source_target_pairs={{0,96},{32,0},{64,32},{96,64},{128,224},{160,128},{192,160},{224,1... | collective-permute-start | bytes 491528 | tf_op jit(solution)/shard_map/ppermute | solution.py:33
  44.5 6.0 %collective-permute-start.14 = (bf16[32,2560]{1,0:T(8,128)(2,1)S(1)}, bf16[32,2560]{1,0:T(8,128)(2,1)S(1)}, u32[]{:S(2)}, u32[]{:S(2)}) collective-permute-start(bf16[32,2560]{1,0:T(8,128)(2,1)S(1)} %collective-permute-done.12.refs_4_), channel_id=1, source_target_pairs={{0,32},{32,64},{64,96},{96,0},{128,160},{160,192},{192,224},{224,1... | collective-permute-start | bytes 491528 | tf_op jit(solution)/shard_map/ppermute | solution.py:33
  44.5 6.0 %collective-permute-start.15 = (bf16[32,2560]{1,0:T(8,128)(2,1)S(1)}, bf16[32,2560]{1,0:T(8,128)(2,1)S(1)}, u32[]{:S(2)}, u32[]{:S(2)}) collective-permute-start(bf16[32,2560]{1,0:T(8,128)(2,1)S(1)} %collective-permute-done.10.refs_1_), channel_id=1, source_target_pairs={{0,128},{32,160},{64,192},{96,224},{128,0},{160,32},{192,64},{224,... | collective-permute-start | bytes 491528 | tf_op jit(solution)/shard_map/ppermute | solution.py:33
  46.4 5.2 %collective-permute-start.6 = (bf16[32,2560]{1,0:T(8,128)(2,1)S(1)}, bf16[32,2560]{1,0:T(8,128)(2,1)S(1)}, u32[]{:S(2)}, u32[]{:S(2)}) collective-permute-start(bf16[32,2560]{1,0:T(8,128)(2,1)S(1)} %collective-permute-done.5.refs_5_), channel_id=1, source_target_pairs={{0,96},{32,0},{64,32},{96,64},{128,224},{160,128},{192,160},{224,1... | collective-permute-start | bytes 491528 | tf_op jit(solution)/shard_map/ppermute | solution.py:33
  50.5 10.0 %collective-permute-start.16 = (bf16[32,2560]{1,0:T(8,128)(2,1)S(1)}, bf16[32,2560]{1,0:T(8,128)(2,1)S(1)}, u32[]{:S(2)}, u32[]{:S(2)}) collective-permute-start(bf16[32,2560]{1,0:T(8,128)(2,1)S(1)} %collective-permute-done.14.refs_7_), channel_id=1, source_target_pairs={{0,32},{32,64},{64,96},{96,0},{128,160},{160,192},{192,224},{224,1... | collective-permute-start | bytes 491528 | tf_op jit(solution)/shard_map/ppermute | solution.py:33
  56.6 10.1 %collective-permute-start.7 = (bf16[32,2560]{1,0:T(8,128)(2,1)S(1)}, bf16[32,2560]{1,0:T(8,128)(2,1)S(1)}, u32[]{:S(2)}, u32[]{:S(2)}) collective-permute-start(bf16[32,2560]{1,0:T(8,128)(2,1)S(1)} %get-tuple-element.86), channel_id=1, source_target_pairs={{0,32},{32,64},{64,96},{96,0},{128,160},{160,192},{192,224},{224,1... | collective-permute-start | bytes 491528 | tf_op jit(solution)/shard_map/ppermute | solution.py:33
  57.5 10.1 %collective-permute-start.8 = (bf16[32,2560]{1,0:T(8,128)(2,1)S(1)}, bf16[32,2560]{1,0:T(8,128)(2,1)S(1)}, u32[]{:S(2)}, u32[]{:S(2)}) collective-permute-start(bf16[32,2560]{1,0:T(8,128)(2,1)S(1)} %get-tuple-element.87), channel_id=1, source_target_pairs={{0,96},{32,0},{64,32},{96,64},{128,224},{160,128},{192,160},{224,1... | collective-permute-start | bytes 491528 | tf_op jit(solution)/shard_map/ppermute | solution.py:33
  59.9 7.7 %collective-permute-start.9 = (bf16[32,2560]{1,0:T(8,128)(2,1)S(1)}, bf16[32,2560]{1,0:T(8,128)(2,1)S(1)}, u32[]{:S(2)}, u32[]{:S(2)}) collective-permute-start(bf16[32,2560]{1,0:T(8,128)(2,1)S(1)} %get-tuple-element.88), channel_id=1, source_target_pairs={{0,128},{32,160},{64,192},{96,224},{128,0},{160,32},{192,64},{224,... | collective-permute-start | bytes 491528 | tf_op jit(solution)/shard_map/ppermute | solution.py:33
  64.0 6.5 %collective-permute-start.21 = (bf16[32,2560]{1,0:T(8,128)(2,1)S(1)}, bf16[32,2560]{1,0:T(8,128)(2,1)S(1)}, u32[]{:S(2)}, u32[]{:S(2)}) collective-permute-start(bf16[32,2560]{1,0:T(8,128)(2,1)S(1)} %get-tuple-element.114), channel_id=1, source_target_pairs={{0,32},{32,64},{64,96},{96,0},{128,160},{160,192},{192,224},{224,1... | collective-permute-start | bytes 491528 | tf_op jit(solution)/shard_map/ppermute | solution.py:33
  64.0 7.1 %collective-permute-start.22 = (bf16[32,2560]{1,0:T(8,128)(2,1)S(1)}, bf16[32,2560]{1,0:T(8,128)(2,1)S(1)}, u32[]{:S(2)}, u32[]{:S(2)}) collective-permute-start(bf16[32,2560]{1,0:T(8,128)(2,1)S(1)} %get-tuple-element.115), channel_id=1, source_target_pairs={{0,96},{32,0},{64,32},{96,64},{128,224},{160,128},{192,160},{224,1... | collective-permute-start | bytes 491528 | tf_op jit(solution)/shard_map/ppermute | solution.py:33
  67.7 5.5 %collective-permute-start.17 = (bf16[32,2560]{1,0:T(8,128)(2,1)S(1)}, bf16[32,2560]{1,0:T(8,128)(2,1)S(1)}, u32[]{:S(2)}, u32[]{:S(2)}) collective-permute-start(bf16[32,2560]{1,0:T(8,128)(2,1)S(1)} %add_convert_fusion.5), channel_id=1, source_target_pairs={{0,32},{32,64},{64,96},{96,0},{128,160},{160,192},{192,224},{224,1... | collective-permute-start | bytes 491528 | tf_op jit(solution)/shard_map/ppermute | solution.py:33
  67.8 6.3 %collective-permute-start.18 = (bf16[32,2560]{1,0:T(8,128)(2,1)S(1)}, bf16[32,2560]{1,0:T(8,128)(2,1)S(1)}, u32[]{:S(2)}, u32[]{:S(2)}) collective-permute-start(bf16[32,2560]{1,0:T(8,128)(2,1)S(1)} %get-tuple-element.106), channel_id=1, source_target_pairs={{0,96},{32,0},{64,32},{96,64},{128,224},{160,128},{192,160},{224,1... | collective-permute-start | bytes 491528 | tf_op jit(solution)/shard_map/ppermute | solution.py:33
  72.3 6.1 %collective-permute-start.25 = (bf16[32,2560]{1,0:T(8,128)(2,1)S(1)}, bf16[32,2560]{1,0:T(8,128)(2,1)S(1)}, u32[]{:S(2)}, u32[]{:S(2)}) collective-permute-start(bf16[32,2560]{1,0:T(8,128)(2,1)S(1)} %get-tuple-element.125), channel_id=1, source_target_pairs={{0,32},{32,64},{64,96},{96,0},{128,160},{160,192},{192,224},{224,1... | collective-permute-start | bytes 491528 | tf_op jit(solution)/shard_map/ppermute | solution.py:33
  73.1 6.0 %collective-permute-start.26 = (bf16[32,2560]{1,0:T(8,128)(2,1)S(1)}, bf16[32,2560]{1,0:T(8,128)(2,1)S(1)}, u32[]{:S(2)}, u32[]{:S(2)}) collective-permute-start(bf16[32,2560]{1,0:T(8,128)(2,1)S(1)} %add_convert_fusion.1), channel_id=1, source_target_pairs={{0,128},{32,160},{64,192},{96,224},{128,0},{160,32},{192,64},{224,... | collective-permute-start | bytes 491528 | tf_op jit(solution)/shard_map/ppermute | solution.py:33
  75.1 6.1 %collective-permute-start.20 = (bf16[32,2560]{1,0:T(8,128)(2,1)S(1)}, bf16[32,2560]{1,0:T(8,128)(2,1)S(1)}, u32[]{:S(2)}, u32[]{:S(2)}) collective-permute-start(bf16[32,2560]{1,0:T(8,128)(2,1)S(1)} %add_convert_fusion.3), channel_id=1, source_target_pairs={{0,32},{32,64},{64,96},{96,0},{128,160},{160,192},{192,224},{224,1... | collective-permute-start | bytes 491528 | tf_op jit(solution)/shard_map/ppermute | solution.py:33
  79.2 5.7 %collective-permute-start.27 = (bf16[32,2560]{1,0:T(8,128)(2,1)S(1)}, bf16[32,2560]{1,0:T(8,128)(2,1)S(1)}, u32[]{:S(2)}, u32[]{:S(2)}) collective-permute-start(bf16[32,2560]{1,0:T(8,128)(2,1)S(1)} %add_convert_fusion), channel_id=1, source_target_pairs={{0,96},{32,0},{64,32},{96,64},{128,224},{160,128},{192,160},{224,1... | collective-permute-start | bytes 491528 | tf_op jit(solution)/shard_map/ppermute | solution.py:33
  85.8 25.9 %all-to-all-start.1 = ((bf16[32,40,128]{2,1,0:T(8,128)(2,1)}), bf16[32,40,128]{2,1,0:T(8,128)(2,1)S(1)}, u32[]{:S(2)}, u32[]{:S(2)}) async-start(bf16[32,40,128]{2,1,0:T(8,128)(2,1)} %bitcast.5), calls=%async_computation.1 | async-start | bytes 655360 | tf_op jit(solution)/shard_map/all_to_all | solution.py:494
  114.9 4.8 %collective-permute-start.30 = (bf16[32,1280]{1,0:T(8,128)(2,1)S(1)}, bf16[32,1280]{1,0:T(8,128)(2,1)S(1)}, u32[]{:S(2)}, u32[]{:S(2)}) collective-permute-start(bf16[32,1280]{1,0:T(8,128)(2,1)S(1)} %add_convert_fusion.11), channel_id=1, source_target_pairs={{0,64},{1,17},{2,66},{3,19},{4,68},{5,21},{6,70},{7,23},{8,72},{9,... | collective-permute-start | bytes 245768 | tf_op jit(solution)/shard_map/ppermute | solution.py:377
  120.7 4.9 %collective-permute-start.34 = (bf16[32,1280]{1,0:T(8,128)(2,1)S(1)}, bf16[32,1280]{1,0:T(8,128)(2,1)S(1)}, u32[]{:S(2)}, u32[]{:S(2)}) collective-permute-start(bf16[32,1280]{1,0:T(8,128)(2,1)S(1)} %add_convert_fusion.10), channel_id=1, source_target_pairs={{0,24},{1,97},{2,26},{3,99},{4,28},{5,101},{6,30},{7,103},{8,0},{9... | collective-permute-start | bytes 245768 | tf_op jit(solution)/shard_map/ppermute | solution.py:377
  123.4 4.9 %collective-permute-start.33 = (bf16[32,1280]{1,0:T(8,128)(2,1)S(1)}, bf16[32,1280]{1,0:T(8,128)(2,1)S(1)}, u32[]{:S(2)}, u32[]{:S(2)}) collective-permute-start(bf16[32,1280]{1,0:T(8,128)(2,1)S(1)} %add_convert_fusion.10), channel_id=1, source_target_pairs={{0,16},{1,65},{2,18},{3,67},{4,20},{5,69},{6,22},{7,71},{8,24},{9,... | collective-permute-start | bytes 245768 | tf_op jit(solution)/shard_map/ppermute | solution.py:377
  123.4 5.4 %collective-permute-start.32 = (bf16[32,1280]{1,0:T(8,128)(2,1)S(1)}, bf16[32,1280]{1,0:T(8,128)(2,1)S(1)}, u32[]{:S(2)}, u32[]{:S(2)}) collective-permute-start(bf16[32,1280]{1,0:T(8,128)(2,1)S(1)} %add_convert_fusion.10), channel_id=1, source_target_pairs={{0,8},{1,33},{2,10},{3,35},{4,12},{5,37},{6,14},{7,39},{8,16},{9,4... | collective-permute-start | bytes 245768 | tf_op jit(solution)/shard_map/ppermute | solution.py:377
  136.9 5.2 %collective-permute-start.37 = (bf16[32,1280]{1,0:T(8,128)(2,1)S(1)}, bf16[32,1280]{1,0:T(8,128)(2,1)S(1)}, u32[]{:S(2)}, u32[]{:S(2)}) collective-permute-start(bf16[32,1280]{1,0:T(8,128)(2,1)S(1)} %add_convert_fusion.7), channel_id=1, source_target_pairs={{0,130},{1,131},{8,138},{9,139},{16,146},{17,147},{24,154},{25,155... | collective-permute-start | bytes 245768 | tf_op jit(solution)/shard_map/ppermute | solution.py:392
  142.1 7.8 %collective-permute-start.38 = (bf16[32,1280]{1,0:T(8,128)(2,1)S(1)}, bf16[32,1280]{1,0:T(8,128)(2,1)S(1)}, u32[]{:S(2)}, u32[]{:S(2)}) collective-permute-start(bf16[32,1280]{1,0:T(8,128)(2,1)S(1)} %add_convert_fusion.6), channel_id=1, source_target_pairs={{0,1},{1,0},{2,3},{3,2},{4,5},{5,4},{6,7},{7,6},{8,9},{9,8},{10,11... | collective-permute-start | bytes 245768 | tf_op jit(solution)/shard_map/ppermute | solution.py:47
  (12 other events, 86.8 us)

commit v10 on v9

--- a/solution.py
+++ b/solution.py
@@ -468,12 +468,14 @@
     parts_a, slope, rows_a, act = expert_step(
         forward_kernel, "expert_forward", blocks_a, [], 1, weight_in, weight_out, hidden, 1
     )
-    first_a = scatter_first(parts_a)
+    sent_a = batch_send(parts_a[5], 0, 1), batch_send(parts_a[6], 1, 0)
     parts_b, rows_b, pre = expert_step(
         backward_kernel, "expert_backward", blocks_b, [slope], 0, weight_out, weight_in, hidden, 0
     )
     first_b = scatter_first(parts_b)
-    first_a, parts_a, pre = together(first_a, parts_a, pre)
+    parts_a, pre = together(parts_a, pre)
+    first_a = sent_a[0], batch_send(parts_a[7], 0, 3), sent_a[1]
+    first_a, parts_a = together(first_a, parts_a)
     second_a = scatter_second(parts_a, first_a, 0)
     first_b, parts_b = together(first_b, parts_b)
     second_b = scatter_second(parts_b, first_b, 1)

time: 151 us -> 152 us (level)
  waiting for transfers between devices: 45.6 us -> 47.3 us
  transfers between devices with their start and end apart: 40 -> 40, of which waited for: 24 -> 25; matrix products, arithmetic and copies ran while one was open for 1% -> 1% of each run, Pallas kernels for 10% -> 10%
where the time goes in v10:
time: 152 us
  starting transfers between devices  54.2 us (36%)
  waiting for transfers between devices  47.3 us (31%)
  blocking collectives  27.3 us (18%)
  Pallas kernels  19.2 us (13%)
  matrix products  1.55 us (1%)
    ppermute x29, starting transfers between devices, batch_send(): return lax.ppermute(value, 'batch', pairs)  28.1 us
    all_to_all x1, blocking collectives, body(): lax.all_to_all(rows.reshape(groups, 2 * each * tiles, LANES), 'expert', s...  27.3 us
    ppermute x29, waiting for transfers between devices, batch_send(): return lax.ppermute(value, 'batch', pairs)  19.7 us
    all_to_all x1, starting transfers between devices, body(): lax.all_to_all(packed.reshape(groups, 2 * each * tiles, LANES), 'expert',...  11 us
    ppermute x6, waiting for transfers between devices, crossed_send(): return lax.ppermute(value, ('batch', 'expert'), pairs)  8.7 us
    all_to_all x1, waiting for transfers between devices, body(): lax.all_to_all(packed.reshape(groups, 2 * each * tiles, LANES), 'expert',...  8.58 us
    ppermute x2, waiting for transfers between devices, depth_swap(): return lax.ppermute(value, ('batch', 'expert'), pairs)  8.56 us
    pallas_call x2, Pallas kernels, expert_step(): local_kernel(functools.partial(kernel, count, each), [jax.ShapeDtypeStruc...  8.52 us
  transfers between devices with their start and end apart: 40, of which 25 were waited for; matrix products, arithmetic and copies ran while one was open for 1% of the time, Pallas kernels for 10%

profile of v10, /device:TPU:1, one launch (start us, length us, event | category | flops | bytes accessed | tf_op | source)
XLA Modules:
  0.0 151.7 jit_solution(3053430660390425281)
XLA Ops:
  0.6 2.6 %front.1 = (bf16[1280,128]{1,0:T(8,128)(2,1)S(1)}, f32[64,256]{1,0:T(8,128)S(1)}, f32[64,256]{1,0:T(8,128)S(1)}) custom-call(bf16[256,1280]{1,0:T(8,128)(2,1)} %bitcast.13, bf16[256,1280]{1,0:T(8,128)(2,1)} %bitcast.15, bf16[64,1280]{1,0:T(8,128)(2,1)} %bitcast.20), custom_call_target="tpu_custom_call" | custom-call | flops 125829120 | bytes 1638400 | tf_op jit(solution)/shard_map/front/pallas_call | solution.py:425
  3.3 27.3 %all_to_all.10 = bf16[32,40,128]{2,1,0:T(8,128)(2,1)S(1)} all-to-all(bf16[32,40,128]{2,1,0:T(8,128)(2,1)S(1)} %bitcast.19), channel_id=1, replica_groups=mesh['batch'=8,'expert'=32] {'expert'}, dimensions={0} | all-to-all | bytes 655360 | tf_op jit(solution)/shard_map/all_to_all | solution.py:442
  30.8 2.6 %collective-permute-start = (bf16[32,2560]{1,0:T(8,128)(2,1)S(1)}, bf16[32,2560]{1,0:T(8,128)(2,1)S(1)}, u32[]{:S(2)}, u32[]{:S(2)}) collective-permute-start(bf16[32,2560]{1,0:T(8,128)(2,1)S(1)} %get-tuple-element.85.refs_0_), channel_id=1, source_target_pairs={{0,96},{32,0},{64,32},{96,64},{128,224},{160,128},{192,160},{224,1... | collective-permute-start | bytes 491528 | tf_op jit(solution)/shard_map/ppermute | solution.py:33
  34.3 2.7 %collective-permute-start.8 = (bf16[32,2560]{1,0:T(8,128)(2,1)S(1)}, bf16[32,2560]{1,0:T(8,128)(2,1)S(1)}, u32[]{:S(2)}, u32[]{:S(2)}) collective-permute-start(bf16[32,2560]{1,0:T(8,128)(2,1)S(1)} %get-tuple-element.100.refs_0_), channel_id=1, source_target_pairs={{0,96},{32,0},{64,32},{96,64},{128,224},{160,128},{192,160},{224,1... | collective-permute-start | bytes 491528 | tf_op jit(solution)/shard_map/ppermute | solution.py:33
  37.6 1.9 %collective-permute-done.1.refs_3_ = bf16[32,2560]{1,0:T(8,128)(2,1)S(1)} collective-permute-done((bf16[32,2560]{1,0:T(8,128)(2,1)S(1)}, bf16[32,2560]{1,0:T(8,128)(2,1)S(1)}, u32[]{:S(2)}, u32[]{:S(2)}) %collective-permute-start.1) | collective-permute-done | bytes 163872 | tf_op jit(solution)/shard_map/ppermute | solution.py:33
  39.5 1.5 collective-permute-start.3
  42.3 2.2 %collective-permute-start.11 = (bf16[32,2560]{1,0:T(8,128)(2,1)S(1)}, bf16[32,2560]{1,0:T(8,128)(2,1)S(1)}, u32[]{:S(2)}, u32[]{:S(2)}) collective-permute-start(bf16[32,2560]{1,0:T(8,128)(2,1)S(1)} %collective-permute-done.8.refs_1_), channel_id=1, source_target_pairs={{0,96},{32,0},{64,32},{96,64},{128,224},{160,128},{192,160},{224,1... | collective-permute-start | bytes 491528 | tf_op jit(solution)/shard_map/ppermute | solution.py:33
  46.4 1.8 %collective-permute-start.6 = (bf16[32,2560]{1,0:T(8,128)(2,1)S(1)}, bf16[32,2560]{1,0:T(8,128)(2,1)S(1)}, u32[]{:S(2)}, u32[]{:S(2)}) collective-permute-start(bf16[32,2560]{1,0:T(8,128)(2,1)S(1)} %collective-permute-done.5.refs_5_), channel_id=1, source_target_pairs={{0,96},{32,0},{64,32},{96,64},{128,224},{160,128},{192,160},{224,1... | collective-permute-start | bytes 491528 | tf_op jit(solution)/shard_map/ppermute | solution.py:33
  48.2 2.3 %collective-permute-done.12.refs_7_ = bf16[32,2560]{1,0:T(8,128)(2,1)S(1)} collective-permute-done((bf16[32,2560]{1,0:T(8,128)(2,1)S(1)}, bf16[32,2560]{1,0:T(8,128)(2,1)S(1)}, u32[]{:S(2)}, u32[]{:S(2)}) %collective-permute-start.12) | collective-permute-done | bytes 163872 | tf_op jit(solution)/shard_map/ppermute | solution.py:33
  51.6 5.1 %expert_forward.1 = (bf16[32,2560]{1,0:T(8,128)(2,1)S(1)}, bf16[32,2560]{1,0:T(8,128)(2,1)S(1)}, bf16[32,2560]{1,0:T(8,128)(2,1)S(1)}, bf16[32,2560]{1,0:T(8,128...) custom-call(bf16[32,2560]{1,0:T(8,128)(2,1)S(1)} %get-tuple-element., ...), custom_call_target="tpu_custom_call" | custom-call | flops 1342177280 | bytes 7864320 | tf_op jit(solution)/shard_map/expert_forward/pallas_call | solution.py:307
  57.5 3.5 %expert_backward.1 = (bf16[32,2560]{1,0:T(8,128)(2,1)S(1)}, bf16[32,2560]{1,0:T(8,128)(2,1)S(1)}, bf16[32,2560]{1,0:T(8,128)(2,1)S(1)}, bf16[32,2560]{1,0:T(8,12...) custom-call(bf16[32,2560]{1,0:T(8,128)(2,1)S(1)} %get-tuple-element., ...), custom_call_target="tpu_custom_call" | custom-call | flops 1342177280 | bytes 7864320 | tf_op jit(solution)/shard_map/expert_backward/pallas_call | solution.py:307
  61.0 2.4 %collective-permute-start.15 = (bf16[32,2560]{1,0:T(8,128)(2,1)S(1)}, bf16[32,2560]{1,0:T(8,128)(2,1)S(1)}, u32[]{:S(2)}, u32[]{:S(2)}) collective-permute-start(bf16[32,2560]{1,0:T(8,128)(2,1)S(1)} %get-tuple-element.109), channel_id=1, source_target_pairs={{0,96},{32,0},{64,32},{96,64},{128,224},{160,128},{192,160},{224,1... | collective-permute-start | bytes 491528 | tf_op jit(solution)/shard_map/ppermute | solution.py:33
  64.0 2.7 %collective-permute-start.22 = (bf16[32,2560]{1,0:T(8,128)(2,1)S(1)}, bf16[32,2560]{1,0:T(8,128)(2,1)S(1)}, u32[]{:S(2)}, u32[]{:S(2)}) collective-permute-start(bf16[32,2560]{1,0:T(8,128)(2,1)S(1)} %get-tuple-element.127), channel_id=1, source_target_pairs={{0,96},{32,0},{64,32},{96,64},{128,224},{160,128},{192,160},{224,1... | collective-permute-start | bytes 491528 | tf_op jit(solution)/shard_map/ppermute | solution.py:33
  68.0 2.7 %collective-permute-start.18 = (bf16[32,2560]{1,0:T(8,128)(2,1)S(1)}, bf16[32,2560]{1,0:T(8,128)(2,1)S(1)}, u32[]{:S(2)}, u32[]{:S(2)}) collective-permute-start(bf16[32,2560]{1,0:T(8,128)(2,1)S(1)} %get-tuple-element.118), channel_id=1, source_target_pairs={{0,96},{32,0},{64,32},{96,64},{128,224},{160,128},{192,160},{224,1... | collective-permute-start | bytes 491528 | tf_op jit(solution)/shard_map/ppermute | solution.py:33
  71.4 1.6 %collective-permute-start.24 = (bf16[32,2560]{1,0:T(8,128)(2,1)S(1)}, bf16[32,2560]{1,0:T(8,128)(2,1)S(1)}, u32[]{:S(2)}, u32[]{:S(2)}) collective-permute-start(bf16[32,2560]{1,0:T(8,128)(2,1)S(1)} %add_convert_fusion.2), channel_id=1, source_target_pairs={{0,96},{32,0},{64,32},{96,64},{128,224},{160,128},{192,160},{224,1... | collective-permute-start | bytes 491528 | tf_op jit(solution)/shard_map/ppermute | solution.py:33
  74.1 1.2 collective-permute-done.19.refs_2_
  76.6 3.1 %collective-permute-done.25.refs_5_ = bf16[32,2560]{1,0:T(8,128)(2,1)S(1)} collective-permute-done((bf16[32,2560]{1,0:T(8,128)(2,1)S(1)}, bf16[32,2560]{1,0:T(8,128)(2,1)S(1)}, u32[]{:S(2)}, u32[]{:S(2)}) %collective-permute-start.25) | collective-permute-done | bytes 163872 | tf_op jit(solution)/shard_map/ppermute | solution.py:33
  80.5 1.5 collective-permute-done.20.refs_3_
  81.9 3.4 %collective-permute-done.27.refs_7_ = bf16[32,2560]{1,0:T(8,128)(2,1)S(1)} collective-permute-done((bf16[32,2560]{1,0:T(8,128)(2,1)S(1)}, bf16[32,2560]{1,0:T(8,128)(2,1)S(1)}, u32[]{:S(2)}, u32[]{:S(2)}) %collective-permute-start.27) | collective-permute-done | bytes 163872 | tf_op jit(solution)/shard_map/ppermute | solution.py:33
  86.2 11.0 %all-to-all-start.1 = ((bf16[32,40,128]{2,1,0:T(8,128)(2,1)}), bf16[32,40,128]{2,1,0:T(8,128)(2,1)S(1)}, u32[]{:S(2)}, u32[]{:S(2)}) async-start(bf16[32,40,128]{2,1,0:T(8,128)(2,1)} %bitcast.5), calls=%async_computation.1 | async-start | bytes 655360 | tf_op jit(solution)/shard_map/all_to_all | solution.py:496
  97.3 6.1 %weight_grads.1 = (bf16[2,1280,512]{2,1,0:T(8,128)(2,1)}, bf16[2,512,1280]{2,1,0:T(8,128)(2,1)}) custom-call(bf16[256,2560]{1,0:T(8,128)(2,1)} %get-tuple-element.148.ins_ref, bf16[256,2560]{1,0:T(8,128)(2,1)} %get-tuple-element.149.cots_ref, bf16[256,1024]{1,0:T(8,128)(2,1)} %get-tuple-element.150.act_ref, bf16[256,1024]{1,0:T(8,128)(2,1)} %get-tuple-element.151.pre_ref), custom_call_target="tpu_custom_call" | custom-call | flops 1342177280 | bytes 10485760 | tf_op jit(solution)/shard_map/weight_grads/pallas_call | solution.py:340
  103.4 8.6 %all-to-all-done.1 = bf16[32,40,128]{2,1,0:T(8,128)(2,1)S(1)} async-done(((bf16[32,40,128]{2,1,0:T(8,128)(2,1)}), bf16[32,40,128]{2,1,0:T(8,128)(2,1)S(1)}, u32[]{:S(2)}, u32[]{:S(2)}) %all-to-all-start.1) | async-done | bytes 327712 | tf_op jit(solution)/shard_map/all_to_all | solution.py:496
  115.3 1.2 collective-permute-start.30
  116.6 1.4 collective-permute-done.31
  118.1 2.0 %collective-permute-done.30 = bf16[32,1280]{1,0:T(8,128)(2,1)S(1)} collective-permute-done((bf16[32,1280]{1,0:T(8,128)(2,1)S(1)}, bf16[32,1280]{1,0:T(8,128)(2,1)S(1)}, u32[]{:S(2)}, u32[]{:S(2)}) %collective-permute-start.30) | collective-permute-done | bytes 81952 | tf_op jit(solution)/shard_map/ppermute | solution.py:377
  121.0 2.8 %collective-permute-start.34 = (bf16[32,1280]{1,0:T(8,128)(2,1)S(1)}, bf16[32,1280]{1,0:T(8,128)(2,1)S(1)}, u32[]{:S(2)}, u32[]{:S(2)}) collective-permute-start(bf16[32,1280]{1,0:T(8,128)(2,1)S(1)} %add_convert_fusion.10), channel_id=1, source_target_pairs={{0,24},{1,97},{2,26},{3,99},{4,28},{5,101},{6,30},{7,103},{8,0},{9... | collective-permute-start | bytes 245768 | tf_op jit(solution)/shard_map/ppermute | solution.py:377
  124.8 1.2 collective-permute-done.34
  126.1 2.6 %collective-permute-done.33 = bf16[32,1280]{1,0:T(8,128)(2,1)S(1)} collective-permute-done((bf16[32,1280]{1,0:T(8,128)(2,1)S(1)}, bf16[32,1280]{1,0:T(8,128)(2,1)S(1)}, u32[]{:S(2)}, u32[]{:S(2)}) %collective-permute-start.33) | collective-permute-done | bytes 81952 | tf_op jit(solution)/shard_map/ppermute | solution.py:377
  131.0 1.6 %collective-permute-done.35 = bf16[32,1280]{1,0:T(8,128)(2,1)S(1)} collective-permute-done((bf16[32,1280]{1,0:T(8,128)(2,1)S(1)}, bf16[32,1280]{1,0:T(8,128)(2,1)S(1)}, u32[]{:S(2)}, u32[]{:S(2)}) %collective-permute-start.35) | collective-permute-done | bytes 81952 | tf_op jit(solution)/shard_map/ppermute | solution.py:33
  132.7 4.5 %collective-permute-done.36 = bf16[32,1280]{1,0:T(8,128)(2,1)S(1)} collective-permute-done((bf16[32,1280]{1,0:T(8,128)(2,1)S(1)}, bf16[32,1280]{1,0:T(8,128)(2,1)S(1)}, u32[]{:S(2)}, u32[]{:S(2)}) %collective-permute-start.36) | collective-permute-done | bytes 81952 | tf_op jit(solution)/shard_map/ppermute | solution.py:392
  138.4 4.1 %collective-permute-done.37 = bf16[32,1280]{1,0:T(8,128)(2,1)S(1)} collective-permute-done((bf16[32,1280]{1,0:T(8,128)(2,1)S(1)}, bf16[32,1280]{1,0:T(8,128)(2,1)S(1)}, u32[]{:S(2)}, u32[]{:S(2)}) %collective-permute-start.37) | collective-permute-done | bytes 81952 | tf_op jit(solution)/shard_map/ppermute | solution.py:392
  142.5 7.6 %collective-permute-start.38 = (bf16[32,1280]{1,0:T(8,128)(2,1)S(1)}, bf16[32,1280]{1,0:T(8,128)(2,1)S(1)}, u32[]{:S(2)}, u32[]{:S(2)}) collective-permute-start(bf16[32,1280]{1,0:T(8,128)(2,1)S(1)} %add_convert_fusion.6), channel_id=1, source_target_pairs={{0,1},{1,0},{2,3},{3,2},{4,5},{5,4},{6,7},{7,6},{8,9},{9,8},{10,11... | collective-permute-start | bytes 245768 | tf_op jit(solution)/shard_map/ppermute | solution.py:47
  (81 shorter events, 24.1 us)
Async XLA Ops:
  30.8 6.2 %collective-permute-start = (bf16[32,2560]{1,0:T(8,128)(2,1)S(1)}, bf16[32,2560]{1,0:T(8,128)(2,1)S(1)}, u32[]{:S(2)}, u32[]{:S(2)}) collective-permute-start(bf16[32,2560]{1,0:T(8,128)(2,1)S(1)} %get-tuple-element.85.refs_0_), channel_id=1, source_target_pairs={{0,96},{32,0},{64,32},{96,64},{128,224},{160,128},{192,160},{224,1... | collective-permute-start | bytes 491528 | tf_op jit(solution)/shard_map/ppermute | solution.py:33
  33.3 6.2 %collective-permute-start.1 = (bf16[32,2560]{1,0:T(8,128)(2,1)S(1)}, bf16[32,2560]{1,0:T(8,128)(2,1)S(1)}, u32[]{:S(2)}, u32[]{:S(2)}) collective-permute-start(bf16[32,2560]{1,0:T(8,128)(2,1)S(1)} %get-tuple-element.85.refs_0_), channel_id=1, source_target_pairs={{0,32},{32,64},{64,96},{96,0},{128,160},{160,192},{192,224},{224,1... | collective-permute-start | bytes 491528 | tf_op jit(solution)/shard_map/ppermute | solution.py:33
  33.3 6.2 %collective-permute-start.2 = (bf16[32,2560]{1,0:T(8,128)(2,1)S(1)}, bf16[32,2560]{1,0:T(8,128)(2,1)S(1)}, u32[]{:S(2)}, u32[]{:S(2)}) collective-permute-start(bf16[32,2560]{1,0:T(8,128)(2,1)S(1)} %get-tuple-element.85.refs_0_), channel_id=1, source_target_pairs={{0,128},{32,160},{64,192},{96,224},{128,0},{160,32},{192,64},{224,... | collective-permute-start | bytes 491528 | tf_op jit(solution)/shard_map/ppermute | solution.py:33
  34.3 6.8 %collective-permute-start.8 = (bf16[32,2560]{1,0:T(8,128)(2,1)S(1)}, bf16[32,2560]{1,0:T(8,128)(2,1)S(1)}, u32[]{:S(2)}, u32[]{:S(2)}) collective-permute-start(bf16[32,2560]{1,0:T(8,128)(2,1)S(1)} %get-tuple-element.100.refs_0_), channel_id=1, source_target_pairs={{0,96},{32,0},{64,32},{96,64},{128,224},{160,128},{192,160},{224,1... | collective-permute-start | bytes 491528 | tf_op jit(solution)/shard_map/ppermute | solution.py:33
  36.9 5.4 %collective-permute-start.9 = (bf16[32,2560]{1,0:T(8,128)(2,1)S(1)}, bf16[32,2560]{1,0:T(8,128)(2,1)S(1)}, u32[]{:S(2)}, u32[]{:S(2)}) collective-permute-start(bf16[32,2560]{1,0:T(8,128)(2,1)S(1)} %get-tuple-element.100.refs_0_), channel_id=1, source_target_pairs={{0,32},{32,64},{64,96},{96,0},{128,160},{160,192},{192,224},{224,1... | collective-permute-start | bytes 491528 | tf_op jit(solution)/shard_map/ppermute | solution.py:33
  37.0 5.4 %collective-permute-start.10 = (bf16[32,2560]{1,0:T(8,128)(2,1)S(1)}, bf16[32,2560]{1,0:T(8,128)(2,1)S(1)}, u32[]{:S(2)}, u32[]{:S(2)}) collective-permute-start(bf16[32,2560]{1,0:T(8,128)(2,1)S(1)} %get-tuple-element.100.refs_0_), channel_id=1, source_target_pairs={{0,128},{32,160},{64,192},{96,224},{128,0},{160,32},{192,64},{224,... | collective-permute-start | bytes 491528 | tf_op jit(solution)/shard_map/ppermute | solution.py:33
  39.5 5.0 %collective-permute-start.3 = (bf16[32,2560]{1,0:T(8,128)(2,1)S(1)}, bf16[32,2560]{1,0:T(8,128)(2,1)S(1)}, u32[]{:S(2)}, u32[]{:S(2)}) collective-permute-start(bf16[32,2560]{1,0:T(8,128)(2,1)S(1)} %collective-permute-done.refs_1_), channel_id=1, source_target_pairs={{0,96},{32,0},{64,32},{96,64},{128,224},{160,128},{192,160},{224,1... | collective-permute-start | bytes 491528 | tf_op jit(solution)/shard_map/ppermute | solution.py:33
  41.0 5.4 %collective-permute-start.4 = (bf16[32,2560]{1,0:T(8,128)(2,1)S(1)}, bf16[32,2560]{1,0:T(8,128)(2,1)S(1)}, u32[]{:S(2)}, u32[]{:S(2)}) collective-permute-start(bf16[32,2560]{1,0:T(8,128)(2,1)S(1)} %collective-permute-done.2.refs_4_), channel_id=1, source_target_pairs={{0,32},{32,64},{64,96},{96,0},{128,160},{160,192},{192,224},{224,1... | collective-permute-start | bytes 491528 | tf_op jit(solution)/shard_map/ppermute | solution.py:33
  41.0 5.4 %collective-permute-start.5 = (bf16[32,2560]{1,0:T(8,128)(2,1)S(1)}, bf16[32,2560]{1,0:T(8,128)(2,1)S(1)}, u32[]{:S(2)}, u32[]{:S(2)}) collective-permute-start(bf16[32,2560]{1,0:T(8,128)(2,1)S(1)} %collective-permute-done.refs_1_), channel_id=1, source_target_pairs={{0,128},{32,160},{64,192},{96,224},{128,0},{160,32},{192,64},{224,... | collective-permute-start | bytes 491528 | tf_op jit(solution)/shard_map/ppermute | solution.py:33
  42.3 5.8 %collective-permute-start.11 = (bf16[32,2560]{1,0:T(8,128)(2,1)S(1)}, bf16[32,2560]{1,0:T(8,128)(2,1)S(1)}, u32[]{:S(2)}, u32[]{:S(2)}) collective-permute-start(bf16[32,2560]{1,0:T(8,128)(2,1)S(1)} %collective-permute-done.8.refs_1_), channel_id=1, source_target_pairs={{0,96},{32,0},{64,32},{96,64},{128,224},{160,128},{192,160},{224,1... | collective-permute-start | bytes 491528 | tf_op jit(solution)/shard_map/ppermute | solution.py:33
  44.5 6.0 %collective-permute-start.12 = (bf16[32,2560]{1,0:T(8,128)(2,1)S(1)}, bf16[32,2560]{1,0:T(8,128)(2,1)S(1)}, u32[]{:S(2)}, u32[]{:S(2)}) collective-permute-start(bf16[32,2560]{1,0:T(8,128)(2,1)S(1)} %collective-permute-done.10.refs_4_), channel_id=1, source_target_pairs={{0,32},{32,64},{64,96},{96,0},{128,160},{160,192},{192,224},{224,1... | collective-permute-start | bytes 491528 | tf_op jit(solution)/shard_map/ppermute | solution.py:33
  44.5 6.0 %collective-permute-start.13 = (bf16[32,2560]{1,0:T(8,128)(2,1)S(1)}, bf16[32,2560]{1,0:T(8,128)(2,1)S(1)}, u32[]{:S(2)}, u32[]{:S(2)}) collective-permute-start(bf16[32,2560]{1,0:T(8,128)(2,1)S(1)} %collective-permute-done.8.refs_1_), channel_id=1, source_target_pairs={{0,128},{32,160},{64,192},{96,224},{128,0},{160,32},{192,64},{224,... | collective-permute-start | bytes 491528 | tf_op jit(solution)/shard_map/ppermute | solution.py:33
  46.4 5.2 %collective-permute-start.6 = (bf16[32,2560]{1,0:T(8,128)(2,1)S(1)}, bf16[32,2560]{1,0:T(8,128)(2,1)S(1)}, u32[]{:S(2)}, u32[]{:S(2)}) collective-permute-start(bf16[32,2560]{1,0:T(8,128)(2,1)S(1)} %collective-permute-done.5.refs_5_), channel_id=1, source_target_pairs={{0,96},{32,0},{64,32},{96,64},{128,224},{160,128},{192,160},{224,1... | collective-permute-start | bytes 491528 | tf_op jit(solution)/shard_map/ppermute | solution.py:33
  50.5 7.0 %collective-permute-start.14 = (bf16[32,2560]{1,0:T(8,128)(2,1)S(1)}, bf16[32,2560]{1,0:T(8,128)(2,1)S(1)}, u32[]{:S(2)}, u32[]{:S(2)}) collective-permute-start(bf16[32,2560]{1,0:T(8,128)(2,1)S(1)} %collective-permute-done.12.refs_7_), channel_id=1, source_target_pairs={{0,32},{32,64},{64,96},{96,0},{128,160},{160,192},{192,224},{224,1... | collective-permute-start | bytes 491528 | tf_op jit(solution)/shard_map/ppermute | solution.py:33
  56.6 10.0 %collective-permute-start.7 = (bf16[32,2560]{1,0:T(8,128)(2,1)S(1)}, bf16[32,2560]{1,0:T(8,128)(2,1)S(1)}, u32[]{:S(2)}, u32[]{:S(2)}) collective-permute-start(bf16[32,2560]{1,0:T(8,128)(2,1)S(1)} %get-tuple-element.92), channel_id=1, source_target_pairs={{0,32},{32,64},{64,96},{96,0},{128,160},{160,192},{192,224},{224,1... | collective-permute-start | bytes 491528 | tf_op jit(solution)/shard_map/ppermute | solution.py:33
  61.0 6.6 %collective-permute-start.15 = (bf16[32,2560]{1,0:T(8,128)(2,1)S(1)}, bf16[32,2560]{1,0:T(8,128)(2,1)S(1)}, u32[]{:S(2)}, u32[]{:S(2)}) collective-permute-start(bf16[32,2560]{1,0:T(8,128)(2,1)S(1)} %get-tuple-element.109), channel_id=1, source_target_pairs={{0,96},{32,0},{64,32},{96,64},{128,224},{160,128},{192,160},{224,1... | collective-permute-start | bytes 491528 | tf_op jit(solution)/shard_map/ppermute | solution.py:33
  64.0 6.8 %collective-permute-start.21 = (bf16[32,2560]{1,0:T(8,128)(2,1)S(1)}, bf16[32,2560]{1,0:T(8,128)(2,1)S(1)}, u32[]{:S(2)}, u32[]{:S(2)}) collective-permute-start(bf16[32,2560]{1,0:T(8,128)(2,1)S(1)} %get-tuple-element.126), channel_id=1, source_target_pairs={{0,32},{32,64},{64,96},{96,0},{128,160},{160,192},{192,224},{224,1... | collective-permute-start | bytes 491528 | tf_op jit(solution)/shard_map/ppermute | solution.py:33
  64.0 7.1 %collective-permute-start.22 = (bf16[32,2560]{1,0:T(8,128)(2,1)S(1)}, bf16[32,2560]{1,0:T(8,128)(2,1)S(1)}, u32[]{:S(2)}, u32[]{:S(2)}) collective-permute-start(bf16[32,2560]{1,0:T(8,128)(2,1)S(1)} %get-tuple-element.127), channel_id=1, source_target_pairs={{0,96},{32,0},{64,32},{96,64},{128,224},{160,128},{192,160},{224,1... | collective-permute-start | bytes 491528 | tf_op jit(solution)/shard_map/ppermute | solution.py:33
  67.9 5.9 %collective-permute-start.17 = (bf16[32,2560]{1,0:T(8,128)(2,1)S(1)}, bf16[32,2560]{1,0:T(8,128)(2,1)S(1)}, u32[]{:S(2)}, u32[]{:S(2)}) collective-permute-start(bf16[32,2560]{1,0:T(8,128)(2,1)S(1)} %add_convert_fusion.5), channel_id=1, source_target_pairs={{0,32},{32,64},{64,96},{96,0},{128,160},{160,192},{192,224},{224,1... | collective-permute-start | bytes 491528 | tf_op jit(solution)/shard_map/ppermute | solution.py:33
  68.0 6.1 %collective-permute-start.18 = (bf16[32,2560]{1,0:T(8,128)(2,1)S(1)}, bf16[32,2560]{1,0:T(8,128)(2,1)S(1)}, u32[]{:S(2)}, u32[]{:S(2)}) collective-permute-start(bf16[32,2560]{1,0:T(8,128)(2,1)S(1)} %get-tuple-element.118), channel_id=1, source_target_pairs={{0,96},{32,0},{64,32},{96,64},{128,224},{160,128},{192,160},{224,1... | collective-permute-start | bytes 491528 | tf_op jit(solution)/shard_map/ppermute | solution.py:33
  71.4 5.1 %collective-permute-start.24 = (bf16[32,2560]{1,0:T(8,128)(2,1)S(1)}, bf16[32,2560]{1,0:T(8,128)(2,1)S(1)}, u32[]{:S(2)}, u32[]{:S(2)}) collective-permute-start(bf16[32,2560]{1,0:T(8,128)(2,1)S(1)} %add_convert_fusion.2), channel_id=1, source_target_pairs={{0,96},{32,0},{64,32},{96,64},{128,224},{160,128},{192,160},{224,1... | collective-permute-start | bytes 491528 | tf_op jit(solution)/shard_map/ppermute | solution.py:33
  73.0 6.6 %collective-permute-start.25 = (bf16[32,2560]{1,0:T(8,128)(2,1)S(1)}, bf16[32,2560]{1,0:T(8,128)(2,1)S(1)}, u32[]{:S(2)}, u32[]{:S(2)}) collective-permute-start(bf16[32,2560]{1,0:T(8,128)(2,1)S(1)} %get-tuple-element.137), channel_id=1, source_target_pairs={{0,32},{32,64},{64,96},{96,0},{128,160},{160,192},{192,224},{224,1... | collective-permute-start | bytes 491528 | tf_op jit(solution)/shard_map/ppermute | solution.py:33
  73.8 5.9 %collective-permute-start.26 = (bf16[32,2560]{1,0:T(8,128)(2,1)S(1)}, bf16[32,2560]{1,0:T(8,128)(2,1)S(1)}, u32[]{:S(2)}, u32[]{:S(2)}) collective-permute-start(bf16[32,2560]{1,0:T(8,128)(2,1)S(1)} %add_convert_fusion.1), channel_id=1, source_target_pairs={{0,128},{32,160},{64,192},{96,224},{128,0},{160,32},{192,64},{224,... | collective-permute-start | bytes 491528 | tf_op jit(solution)/shard_map/ppermute | solution.py:33
  75.4 6.6 %collective-permute-start.20 = (bf16[32,2560]{1,0:T(8,128)(2,1)S(1)}, bf16[32,2560]{1,0:T(8,128)(2,1)S(1)}, u32[]{:S(2)}, u32[]{:S(2)}) collective-permute-start(bf16[32,2560]{1,0:T(8,128)(2,1)S(1)} %add_convert_fusion.3), channel_id=1, source_target_pairs={{0,32},{32,64},{64,96},{96,0},{128,160},{160,192},{192,224},{224,1... | collective-permute-start | bytes 491528 | tf_op jit(solution)/shard_map/ppermute | solution.py:33
  79.7 5.6 %collective-permute-start.27 = (bf16[32,2560]{1,0:T(8,128)(2,1)S(1)}, bf16[32,2560]{1,0:T(8,128)(2,1)S(1)}, u32[]{:S(2)}, u32[]{:S(2)}) collective-permute-start(bf16[32,2560]{1,0:T(8,128)(2,1)S(1)} %add_convert_fusion), channel_id=1, source_target_pairs={{0,96},{32,0},{64,32},{96,64},{128,224},{160,128},{192,160},{224,1... | collective-permute-start | bytes 491528 | tf_op jit(solution)/shard_map/ppermute | solution.py:33
  86.2 25.8 %all-to-all-start.1 = ((bf16[32,40,128]{2,1,0:T(8,128)(2,1)}), bf16[32,40,128]{2,1,0:T(8,128)(2,1)S(1)}, u32[]{:S(2)}, u32[]{:S(2)}) async-start(bf16[32,40,128]{2,1,0:T(8,128)(2,1)} %bitcast.5), calls=%async_computation.1 | async-start | bytes 655360 | tf_op jit(solution)/shard_map/all_to_all | solution.py:496
  115.3 4.8 %collective-permute-start.30 = (bf16[32,1280]{1,0:T(8,128)(2,1)S(1)}, bf16[32,1280]{1,0:T(8,128)(2,1)S(1)}, u32[]{:S(2)}, u32[]{:S(2)}) collective-permute-start(bf16[32,1280]{1,0:T(8,128)(2,1)S(1)} %add_convert_fusion.11), channel_id=1, source_target_pairs={{0,64},{1,17},{2,66},{3,19},{4,68},{5,21},{6,70},{7,23},{8,72},{9,... | collective-permute-start | bytes 245768 | tf_op jit(solution)/shard_map/ppermute | solution.py:377
  121.0 5.0 %collective-permute-start.34 = (bf16[32,1280]{1,0:T(8,128)(2,1)S(1)}, bf16[32,1280]{1,0:T(8,128)(2,1)S(1)}, u32[]{:S(2)}, u32[]{:S(2)}) collective-permute-start(bf16[32,1280]{1,0:T(8,128)(2,1)S(1)} %add_convert_fusion.10), channel_id=1, source_target_pairs={{0,24},{1,97},{2,26},{3,99},{4,28},{5,101},{6,30},{7,103},{8,0},{9... | collective-permute-start | bytes 245768 | tf_op jit(solution)/shard_map/ppermute | solution.py:377
  123.8 4.9 %collective-permute-start.33 = (bf16[32,1280]{1,0:T(8,128)(2,1)S(1)}, bf16[32,1280]{1,0:T(8,128)(2,1)S(1)}, u32[]{:S(2)}, u32[]{:S(2)}) collective-permute-start(bf16[32,1280]{1,0:T(8,128)(2,1)S(1)} %add_convert_fusion.10), channel_id=1, source_target_pairs={{0,16},{1,65},{2,18},{3,67},{4,20},{5,69},{6,22},{7,71},{8,24},{9,... | collective-permute-start | bytes 245768 | tf_op jit(solution)/shard_map/ppermute | solution.py:377
  123.8 5.4 %collective-permute-start.32 = (bf16[32,1280]{1,0:T(8,128)(2,1)S(1)}, bf16[32,1280]{1,0:T(8,128)(2,1)S(1)}, u32[]{:S(2)}, u32[]{:S(2)}) collective-permute-start(bf16[32,1280]{1,0:T(8,128)(2,1)S(1)} %add_convert_fusion.10), channel_id=1, source_target_pairs={{0,8},{1,33},{2,10},{3,35},{4,12},{5,37},{6,14},{7,39},{8,16},{9,4... | collective-permute-start | bytes 245768 | tf_op jit(solution)/shard_map/ppermute | solution.py:377
  137.3 5.2 %collective-permute-start.37 = (bf16[32,1280]{1,0:T(8,128)(2,1)S(1)}, bf16[32,1280]{1,0:T(8,128)(2,1)S(1)}, u32[]{:S(2)}, u32[]{:S(2)}) collective-permute-start(bf16[32,1280]{1,0:T(8,128)(2,1)S(1)} %add_convert_fusion.7), channel_id=1, source_target_pairs={{0,130},{1,131},{8,138},{9,139},{16,146},{17,147},{24,154},{25,155... | collective-permute-start | bytes 245768 | tf_op jit(solution)/shard_map/ppermute | solution.py:392
  142.5 8.5 %collective-permute-start.38 = (bf16[32,1280]{1,0:T(8,128)(2,1)S(1)}, bf16[32,1280]{1,0:T(8,128)(2,1)S(1)}, u32[]{:S(2)}, u32[]{:S(2)}) collective-permute-start(bf16[32,1280]{1,0:T(8,128)(2,1)S(1)} %add_convert_fusion.6), channel_id=1, source_target_pairs={{0,1},{1,0},{2,3},{3,2},{4,5},{5,4},{6,7},{7,6},{8,9},{9,8},{10,11... | collective-permute-start | bytes 245768 | tf_op jit(solution)/shard_map/ppermute | solution.py:47
  (12 other events, 83.7 us)

commit v11 on v9

--- a/solution.py
+++ b/solution.py
@@ -99,13 +99,14 @@
 LANES = 128
 
 
-PIECES = 4
+PIECES = 8
 
 
 def start_loads(source, target, sems):
-    rows = source.shape[0] // PIECES
+    pieces = min(PIECES, source.shape[0] // 16)
+    rows = source.shape[0] // pieces
     copies = []
-    for i in range(PIECES):
+    for i in range(pieces):
         part = pl.ds(i * rows, rows)
         copies.append(pltpu.make_async_copy(source.at[part], target.at[part], sems.at[i]))
         copies[-1].start()
@@ -141,7 +142,7 @@
     return lax.dot_general(a, b, (((1,), (1,)), ((), ())), preferred_element_type=F32)
 
 
-PIECES = 4
+PIECES = 8
 
 
 def tn(a, b):

time: 151 us -> 153 us (1.013)
  no operation moved by 1% of the time
where the time goes in v11:
time: 153 us; the launch traced here: 152 us
  starting transfers between devices  55.3 us (36%)
  waiting for transfers between devices  45.8 us (30%)
  blocking collectives  27.3 us (18%)
  Pallas kernels  20.3 us (13%)
  matrix products  1.54 us (1%)
    ppermute x29, starting transfers between devices, batch_send(): return lax.ppermute(value, 'batch', pairs)  28.9 us
    all_to_all x1, blocking collectives, body(): lax.all_to_all(rows.reshape(groups, 2 * each * tiles, LANES), 'expert', s...  27.3 us
    ppermute x29, waiting for transfers between devices, batch_send(): return lax.ppermute(value, 'batch', pairs)  18.5 us
    all_to_all x1, starting transfers between devices, body(): lax.all_to_all(packed.reshape(groups, 2 * each * tiles, LANES), 'expert',...  11.2 us
    pallas_call x2, Pallas kernels, expert_step(): local_kernel(functools.partial(kernel, count, each), [jax.ShapeDtypeStruc...  9.47 us
    ppermute x6, waiting for transfers between devices, crossed_send(): return lax.ppermute(value, ('batch', 'expert'), pairs)  8.69 us
    all_to_all x1, waiting for transfers between devices, body(): lax.all_to_all(packed.reshape(groups, 2 * each * tiles, LANES), 'expert',...  8.44 us
    ppermute x2, waiting for transfers between devices, depth_swap(): return lax.ppermute(value, ('batch', 'expert'), pairs)  8.31 us
  transfers between devices with their start and end apart: 40, of which 24 were waited for; matrix products, arithmetic and copies ran while one was open for 1% of the time, Pallas kernels for 10%

profile of v11, /device:TPU:1, one launch (start us, length us, event | category | flops | bytes accessed | tf_op | source)
XLA Modules:
  0.0 152.3 jit_solution(17986249083789527950)
XLA Ops:
  0.6 2.7 %front.1 = (bf16[1280,128]{1,0:T(8,128)(2,1)S(1)}, f32[64,256]{1,0:T(8,128)S(1)}, f32[64,256]{1,0:T(8,128)S(1)}) custom-call(bf16[256,1280]{1,0:T(8,128)(2,1)} %bitcast.13, bf16[256,1280]{1,0:T(8,128)(2,1)} %bitcast.15, bf16[64,1280]{1,0:T(8,128)(2,1)} %bitcast.20), custom_call_target="tpu_custom_call" | custom-call | flops 125829120 | bytes 1638400 | tf_op jit(solution)/shard_map/front/pallas_call | solution.py:426
  3.4 27.3 %all_to_all.10 = bf16[32,40,128]{2,1,0:T(8,128)(2,1)S(1)} all-to-all(bf16[32,40,128]{2,1,0:T(8,128)(2,1)S(1)} %bitcast.19), channel_id=1, replica_groups=mesh['batch'=8,'expert'=32] {'expert'}, dimensions={0} | all-to-all | bytes 655360 | tf_op jit(solution)/shard_map/all_to_all | solution.py:443
  30.9 2.6 %collective-permute-start = (bf16[32,2560]{1,0:T(8,128)(2,1)S(1)}, bf16[32,2560]{1,0:T(8,128)(2,1)S(1)}, u32[]{:S(2)}, u32[]{:S(2)}) collective-permute-start(bf16[32,2560]{1,0:T(8,128)(2,1)S(1)} %get-tuple-element.79.refs_0_), channel_id=1, source_target_pairs={{0,96},{32,0},{64,32},{96,64},{128,224},{160,128},{192,160},{224,1... | collective-permute-start | bytes 491528 | tf_op jit(solution)/shard_map/ppermute | solution.py:33
  34.4 2.7 %collective-permute-start.10 = (bf16[32,2560]{1,0:T(8,128)(2,1)S(1)}, bf16[32,2560]{1,0:T(8,128)(2,1)S(1)}, u32[]{:S(2)}, u32[]{:S(2)}) collective-permute-start(bf16[32,2560]{1,0:T(8,128)(2,1)S(1)} %get-tuple-element.94.refs_0_), channel_id=1, source_target_pairs={{0,96},{32,0},{64,32},{96,64},{128,224},{160,128},{192,160},{224,1... | collective-permute-start | bytes 491528 | tf_op jit(solution)/shard_map/ppermute | solution.py:33
  37.7 1.9 %collective-permute-done.1.refs_3_ = bf16[32,2560]{1,0:T(8,128)(2,1)S(1)} collective-permute-done((bf16[32,2560]{1,0:T(8,128)(2,1)S(1)}, bf16[32,2560]{1,0:T(8,128)(2,1)S(1)}, u32[]{:S(2)}, u32[]{:S(2)}) %collective-permute-start.1) | collective-permute-done | bytes 163872 | tf_op jit(solution)/shard_map/ppermute | solution.py:33
  39.6 1.5 collective-permute-start.3
  42.4 2.2 %collective-permute-start.13 = (bf16[32,2560]{1,0:T(8,128)(2,1)S(1)}, bf16[32,2560]{1,0:T(8,128)(2,1)S(1)}, u32[]{:S(2)}, u32[]{:S(2)}) collective-permute-start(bf16[32,2560]{1,0:T(8,128)(2,1)S(1)} %collective-permute-done.10.refs_1_), channel_id=1, source_target_pairs={{0,96},{32,0},{64,32},{96,64},{128,224},{160,128},{192,160},{224,1... | collective-permute-start | bytes 491528 | tf_op jit(solution)/shard_map/ppermute | solution.py:33
  46.5 1.8 %collective-permute-start.6 = (bf16[32,2560]{1,0:T(8,128)(2,1)S(1)}, bf16[32,2560]{1,0:T(8,128)(2,1)S(1)}, u32[]{:S(2)}, u32[]{:S(2)}) collective-permute-start(bf16[32,2560]{1,0:T(8,128)(2,1)S(1)} %collective-permute-done.5.refs_5_), channel_id=1, source_target_pairs={{0,96},{32,0},{64,32},{96,64},{128,224},{160,128},{192,160},{224,1... | collective-permute-start | bytes 491528 | tf_op jit(solution)/shard_map/ppermute | solution.py:33
  48.3 2.3 %collective-permute-done.14.refs_7_ = bf16[32,2560]{1,0:T(8,128)(2,1)S(1)} collective-permute-done((bf16[32,2560]{1,0:T(8,128)(2,1)S(1)}, bf16[32,2560]{1,0:T(8,128)(2,1)S(1)}, u32[]{:S(2)}, u32[]{:S(2)}) %collective-permute-start.14) | collective-permute-done | bytes 163872 | tf_op jit(solution)/shard_map/ppermute | solution.py:33
  51.7 5.4 %expert_forward.1 = (bf16[32,2560]{1,0:T(8,128)(2,1)S(1)}, bf16[32,2560]{1,0:T(8,128)(2,1)S(1)}, bf16[32,2560]{1,0:T(8,128)(2,1)S(1)}, bf16[32,2560]{1,0:T(8,128...) custom-call(bf16[32,2560]{1,0:T(8,128)(2,1)S(1)} %get-tuple-element., ...), custom_call_target="tpu_custom_call" | custom-call | flops 1342177280 | bytes 7864320 | tf_op jit(solution)/shard_map/expert_forward/pallas_call | solution.py:308
  57.9 2.4 %collective-permute-start.8 = (bf16[32,2560]{1,0:T(8,128)(2,1)S(1)}, bf16[32,2560]{1,0:T(8,128)(2,1)S(1)}, u32[]{:S(2)}, u32[]{:S(2)}) collective-permute-start(bf16[32,2560]{1,0:T(8,128)(2,1)S(1)} %get-tuple-element.87), channel_id=1, source_target_pairs={{0,96},{32,0},{64,32},{96,64},{128,224},{160,128},{192,160},{224,1... | collective-permute-start | bytes 491528 | tf_op jit(solution)/shard_map/ppermute | solution.py:33
  60.9 4.1 %expert_backward.1 = (bf16[32,2560]{1,0:T(8,128)(2,1)S(1)}, bf16[32,2560]{1,0:T(8,128)(2,1)S(1)}, bf16[32,2560]{1,0:T(8,128)(2,1)S(1)}, bf16[32,2560]{1,0:T(8,12...) custom-call(bf16[32,2560]{1,0:T(8,128)(2,1)S(1)} %get-tuple-element., ...), custom_call_target="tpu_custom_call" | custom-call | flops 1342177280 | bytes 7864320 | tf_op jit(solution)/shard_map/expert_backward/pallas_call | solution.py:308
  65.1 2.7 %collective-permute-start.22 = (bf16[32,2560]{1,0:T(8,128)(2,1)S(1)}, bf16[32,2560]{1,0:T(8,128)(2,1)S(1)}, u32[]{:S(2)}, u32[]{:S(2)}) collective-permute-start(bf16[32,2560]{1,0:T(8,128)(2,1)S(1)} %get-tuple-element.115), channel_id=1, source_target_pairs={{0,96},{32,0},{64,32},{96,64},{128,224},{160,128},{192,160},{224,1... | collective-permute-start | bytes 491528 | tf_op jit(solution)/shard_map/ppermute | solution.py:33
  68.8 2.7 %collective-permute-start.18 = (bf16[32,2560]{1,0:T(8,128)(2,1)S(1)}, bf16[32,2560]{1,0:T(8,128)(2,1)S(1)}, u32[]{:S(2)}, u32[]{:S(2)}) collective-permute-start(bf16[32,2560]{1,0:T(8,128)(2,1)S(1)} %get-tuple-element.106), channel_id=1, source_target_pairs={{0,96},{32,0},{64,32},{96,64},{128,224},{160,128},{192,160},{224,1... | collective-permute-start | bytes 491528 | tf_op jit(solution)/shard_map/ppermute | solution.py:33
  77.0 2.3 %collective-permute-done.25.refs_5_ = bf16[32,2560]{1,0:T(8,128)(2,1)S(1)} collective-permute-done((bf16[32,2560]{1,0:T(8,128)(2,1)S(1)}, bf16[32,2560]{1,0:T(8,128)(2,1)S(1)}, u32[]{:S(2)}, u32[]{:S(2)}) %collective-permute-start.25) | collective-permute-done | bytes 163872 | tf_op jit(solution)/shard_map/ppermute | solution.py:33
  80.8 1.3 collective-permute-done.20.refs_3_
  82.2 3.8 %collective-permute-done.27.refs_7_ = bf16[32,2560]{1,0:T(8,128)(2,1)S(1)} collective-permute-done((bf16[32,2560]{1,0:T(8,128)(2,1)S(1)}, bf16[32,2560]{1,0:T(8,128)(2,1)S(1)}, u32[]{:S(2)}, u32[]{:S(2)}) %collective-permute-start.27) | collective-permute-done | bytes 163872 | tf_op jit(solution)/shard_map/ppermute | solution.py:33
  86.8 11.2 %all-to-all-start.1 = ((bf16[32,40,128]{2,1,0:T(8,128)(2,1)}), bf16[32,40,128]{2,1,0:T(8,128)(2,1)S(1)}, u32[]{:S(2)}, u32[]{:S(2)}) async-start(bf16[32,40,128]{2,1,0:T(8,128)(2,1)} %bitcast.5), calls=%async_computation.1 | async-start | bytes 655360 | tf_op jit(solution)/shard_map/all_to_all | solution.py:495
  98.1 6.1 %weight_grads.1 = (bf16[2,1280,512]{2,1,0:T(8,128)(2,1)}, bf16[2,512,1280]{2,1,0:T(8,128)(2,1)}) custom-call(bf16[256,2560]{1,0:T(8,128)(2,1)} %get-tuple-element.136.ins_ref, bf16[256,2560]{1,0:T(8,128)(2,1)} %get-tuple-element.137.cots_ref, bf16[256,1024]{1,0:T(8,128)(2,1)} %get-tuple-element.138.act_ref, bf16[256,1024]{1,0:T(8,128)(2,1)} %get-tuple-element.139.pre_ref), custom_call_target="tpu_custom_call" | custom-call | flops 1342177280 | bytes 10485760 | tf_op jit(solution)/shard_map/weight_grads/pallas_call | solution.py:341
  104.2 8.4 %all-to-all-done.1 = bf16[32,40,128]{2,1,0:T(8,128)(2,1)S(1)} async-done(((bf16[32,40,128]{2,1,0:T(8,128)(2,1)}), bf16[32,40,128]{2,1,0:T(8,128)(2,1)S(1)}, u32[]{:S(2)}, u32[]{:S(2)}) %all-to-all-start.1) | async-done | bytes 327712 | tf_op jit(solution)/shard_map/all_to_all | solution.py:495
  115.9 1.2 collective-permute-start.30
  117.3 1.4 collective-permute-done.31
  118.7 2.0 %collective-permute-done.30 = bf16[32,1280]{1,0:T(8,128)(2,1)S(1)} collective-permute-done((bf16[32,1280]{1,0:T(8,128)(2,1)S(1)}, bf16[32,1280]{1,0:T(8,128)(2,1)S(1)}, u32[]{:S(2)}, u32[]{:S(2)}) %collective-permute-start.30) | collective-permute-done | bytes 81952 | tf_op jit(solution)/shard_map/ppermute | solution.py:378
  121.7 3.2 %collective-permute-start.34 = (bf16[32,1280]{1,0:T(8,128)(2,1)S(1)}, bf16[32,1280]{1,0:T(8,128)(2,1)S(1)}, u32[]{:S(2)}, u32[]{:S(2)}) collective-permute-start(bf16[32,1280]{1,0:T(8,128)(2,1)S(1)} %add_convert_fusion.10), channel_id=1, source_target_pairs={{0,24},{1,97},{2,26},{3,99},{4,28},{5,101},{6,30},{7,103},{8,0},{9... | collective-permute-start | bytes 245768 | tf_op jit(solution)/shard_map/ppermute | solution.py:378
  125.9 1.2 collective-permute-done.34
  127.1 2.6 %collective-permute-done.33 = bf16[32,1280]{1,0:T(8,128)(2,1)S(1)} collective-permute-done((bf16[32,1280]{1,0:T(8,128)(2,1)S(1)}, bf16[32,1280]{1,0:T(8,128)(2,1)S(1)}, u32[]{:S(2)}, u32[]{:S(2)}) %collective-permute-start.33) | collective-permute-done | bytes 81952 | tf_op jit(solution)/shard_map/ppermute | solution.py:378
  131.0 1.2 fusion
  132.2 1.5 collective-permute-done.35
  133.8 4.5 %collective-permute-done.36 = bf16[32,1280]{1,0:T(8,128)(2,1)S(1)} collective-permute-done((bf16[32,1280]{1,0:T(8,128)(2,1)S(1)}, bf16[32,1280]{1,0:T(8,128)(2,1)S(1)}, u32[]{:S(2)}, u32[]{:S(2)}) %collective-permute-start.36) | collective-permute-done | bytes 81952 | tf_op jit(solution)/shard_map/ppermute | solution.py:393
  138.3 1.4 collective-permute-start.37
  139.7 3.8 %collective-permute-done.37 = bf16[32,1280]{1,0:T(8,128)(2,1)S(1)} collective-permute-done((bf16[32,1280]{1,0:T(8,128)(2,1)S(1)}, bf16[32,1280]{1,0:T(8,128)(2,1)S(1)}, u32[]{:S(2)}, u32[]{:S(2)}) %collective-permute-start.37) | collective-permute-done | bytes 81952 | tf_op jit(solution)/shard_map/ppermute | solution.py:393
  143.5 7.1 %collective-permute-start.38 = (bf16[32,1280]{1,0:T(8,128)(2,1)S(1)}, bf16[32,1280]{1,0:T(8,128)(2,1)S(1)}, u32[]{:S(2)}, u32[]{:S(2)}) collective-permute-start(bf16[32,1280]{1,0:T(8,128)(2,1)S(1)} %add_convert_fusion.6), channel_id=1, source_target_pairs={{0,1},{1,0},{2,3},{3,2},{4,5},{5,4},{6,7},{7,6},{8,9},{9,8},{10,11... | collective-permute-start | bytes 245768 | tf_op jit(solution)/shard_map/ppermute | solution.py:47
  (81 shorter events, 24.9 us)
Async XLA Ops:
  30.9 6.2 %collective-permute-start = (bf16[32,2560]{1,0:T(8,128)(2,1)S(1)}, bf16[32,2560]{1,0:T(8,128)(2,1)S(1)}, u32[]{:S(2)}, u32[]{:S(2)}) collective-permute-start(bf16[32,2560]{1,0:T(8,128)(2,1)S(1)} %get-tuple-element.79.refs_0_), channel_id=1, source_target_pairs={{0,96},{32,0},{64,32},{96,64},{128,224},{160,128},{192,160},{224,1... | collective-permute-start | bytes 491528 | tf_op jit(solution)/shard_map/ppermute | solution.py:33
  33.4 6.2 %collective-permute-start.1 = (bf16[32,2560]{1,0:T(8,128)(2,1)S(1)}, bf16[32,2560]{1,0:T(8,128)(2,1)S(1)}, u32[]{:S(2)}, u32[]{:S(2)}) collective-permute-start(bf16[32,2560]{1,0:T(8,128)(2,1)S(1)} %get-tuple-element.79.refs_0_), channel_id=1, source_target_pairs={{0,32},{32,64},{64,96},{96,0},{128,160},{160,192},{192,224},{224,1... | collective-permute-start | bytes 491528 | tf_op jit(solution)/shard_map/ppermute | solution.py:33
  33.4 6.2 %collective-permute-start.2 = (bf16[32,2560]{1,0:T(8,128)(2,1)S(1)}, bf16[32,2560]{1,0:T(8,128)(2,1)S(1)}, u32[]{:S(2)}, u32[]{:S(2)}) collective-permute-start(bf16[32,2560]{1,0:T(8,128)(2,1)S(1)} %get-tuple-element.79.refs_0_), channel_id=1, source_target_pairs={{0,128},{32,160},{64,192},{96,224},{128,0},{160,32},{192,64},{224,... | collective-permute-start | bytes 491528 | tf_op jit(solution)/shard_map/ppermute | solution.py:33
  34.4 6.8 %collective-permute-start.10 = (bf16[32,2560]{1,0:T(8,128)(2,1)S(1)}, bf16[32,2560]{1,0:T(8,128)(2,1)S(1)}, u32[]{:S(2)}, u32[]{:S(2)}) collective-permute-start(bf16[32,2560]{1,0:T(8,128)(2,1)S(1)} %get-tuple-element.94.refs_0_), channel_id=1, source_target_pairs={{0,96},{32,0},{64,32},{96,64},{128,224},{160,128},{192,160},{224,1... | collective-permute-start | bytes 491528 | tf_op jit(solution)/shard_map/ppermute | solution.py:33
  37.0 5.4 %collective-permute-start.11 = (bf16[32,2560]{1,0:T(8,128)(2,1)S(1)}, bf16[32,2560]{1,0:T(8,128)(2,1)S(1)}, u32[]{:S(2)}, u32[]{:S(2)}) collective-permute-start(bf16[32,2560]{1,0:T(8,128)(2,1)S(1)} %get-tuple-element.94.refs_0_), channel_id=1, source_target_pairs={{0,32},{32,64},{64,96},{96,0},{128,160},{160,192},{192,224},{224,1... | collective-permute-start | bytes 491528 | tf_op jit(solution)/shard_map/ppermute | solution.py:33
  37.1 5.4 %collective-permute-start.12 = (bf16[32,2560]{1,0:T(8,128)(2,1)S(1)}, bf16[32,2560]{1,0:T(8,128)(2,1)S(1)}, u32[]{:S(2)}, u32[]{:S(2)}) collective-permute-start(bf16[32,2560]{1,0:T(8,128)(2,1)S(1)} %get-tuple-element.94.refs_0_), channel_id=1, source_target_pairs={{0,128},{32,160},{64,192},{96,224},{128,0},{160,32},{192,64},{224,... | collective-permute-start | bytes 491528 | tf_op jit(solution)/shard_map/ppermute | solution.py:33
  39.6 5.0 %collective-permute-start.3 = (bf16[32,2560]{1,0:T(8,128)(2,1)S(1)}, bf16[32,2560]{1,0:T(8,128)(2,1)S(1)}, u32[]{:S(2)}, u32[]{:S(2)}) collective-permute-start(bf16[32,2560]{1,0:T(8,128)(2,1)S(1)} %collective-permute-done.refs_1_), channel_id=1, source_target_pairs={{0,96},{32,0},{64,32},{96,64},{128,224},{160,128},{192,160},{224,1... | collective-permute-start | bytes 491528 | tf_op jit(solution)/shard_map/ppermute | solution.py:33
  41.1 5.4 %collective-permute-start.4 = (bf16[32,2560]{1,0:T(8,128)(2,1)S(1)}, bf16[32,2560]{1,0:T(8,128)(2,1)S(1)}, u32[]{:S(2)}, u32[]{:S(2)}) collective-permute-start(bf16[32,2560]{1,0:T(8,128)(2,1)S(1)} %collective-permute-done.2.refs_4_), channel_id=1, source_target_pairs={{0,32},{32,64},{64,96},{96,0},{128,160},{160,192},{192,224},{224,1... | collective-permute-start | bytes 491528 | tf_op jit(solution)/shard_map/ppermute | solution.py:33
  41.1 5.4 %collective-permute-start.5 = (bf16[32,2560]{1,0:T(8,128)(2,1)S(1)}, bf16[32,2560]{1,0:T(8,128)(2,1)S(1)}, u32[]{:S(2)}, u32[]{:S(2)}) collective-permute-start(bf16[32,2560]{1,0:T(8,128)(2,1)S(1)} %collective-permute-done.refs_1_), channel_id=1, source_target_pairs={{0,128},{32,160},{64,192},{96,224},{128,0},{160,32},{192,64},{224,... | collective-permute-start | bytes 491528 | tf_op jit(solution)/shard_map/ppermute | solution.py:33
  42.4 5.8 %collective-permute-start.13 = (bf16[32,2560]{1,0:T(8,128)(2,1)S(1)}, bf16[32,2560]{1,0:T(8,128)(2,1)S(1)}, u32[]{:S(2)}, u32[]{:S(2)}) collective-permute-start(bf16[32,2560]{1,0:T(8,128)(2,1)S(1)} %collective-permute-done.10.refs_1_), channel_id=1, source_target_pairs={{0,96},{32,0},{64,32},{96,64},{128,224},{160,128},{192,160},{224,1... | collective-permute-start | bytes 491528 | tf_op jit(solution)/shard_map/ppermute | solution.py:33
  44.6 6.0 %collective-permute-start.14 = (bf16[32,2560]{1,0:T(8,128)(2,1)S(1)}, bf16[32,2560]{1,0:T(8,128)(2,1)S(1)}, u32[]{:S(2)}, u32[]{:S(2)}) collective-permute-start(bf16[32,2560]{1,0:T(8,128)(2,1)S(1)} %collective-permute-done.12.refs_4_), channel_id=1, source_target_pairs={{0,32},{32,64},{64,96},{96,0},{128,160},{160,192},{192,224},{224,1... | collective-permute-start | bytes 491528 | tf_op jit(solution)/shard_map/ppermute | solution.py:33
  44.6 6.0 %collective-permute-start.15 = (bf16[32,2560]{1,0:T(8,128)(2,1)S(1)}, bf16[32,2560]{1,0:T(8,128)(2,1)S(1)}, u32[]{:S(2)}, u32[]{:S(2)}) collective-permute-start(bf16[32,2560]{1,0:T(8,128)(2,1)S(1)} %collective-permute-done.10.refs_1_), channel_id=1, source_target_pairs={{0,128},{32,160},{64,192},{96,224},{128,0},{160,32},{192,64},{224,... | collective-permute-start | bytes 491528 | tf_op jit(solution)/shard_map/ppermute | solution.py:33
  46.5 5.2 %collective-permute-start.6 = (bf16[32,2560]{1,0:T(8,128)(2,1)S(1)}, bf16[32,2560]{1,0:T(8,128)(2,1)S(1)}, u32[]{:S(2)}, u32[]{:S(2)}) collective-permute-start(bf16[32,2560]{1,0:T(8,128)(2,1)S(1)} %collective-permute-done.5.refs_5_), channel_id=1, source_target_pairs={{0,96},{32,0},{64,32},{96,64},{128,224},{160,128},{192,160},{224,1... | collective-permute-start | bytes 491528 | tf_op jit(solution)/shard_map/ppermute | solution.py:33
  50.6 10.3 %collective-permute-start.16 = (bf16[32,2560]{1,0:T(8,128)(2,1)S(1)}, bf16[32,2560]{1,0:T(8,128)(2,1)S(1)}, u32[]{:S(2)}, u32[]{:S(2)}) collective-permute-start(bf16[32,2560]{1,0:T(8,128)(2,1)S(1)} %collective-permute-done.14.refs_7_), channel_id=1, source_target_pairs={{0,32},{32,64},{64,96},{96,0},{128,160},{160,192},{192,224},{224,1... | collective-permute-start | bytes 491528 | tf_op jit(solution)/shard_map/ppermute | solution.py:33
  57.1 10.7 %collective-permute-start.7 = (bf16[32,2560]{1,0:T(8,128)(2,1)S(1)}, bf16[32,2560]{1,0:T(8,128)(2,1)S(1)}, u32[]{:S(2)}, u32[]{:S(2)}) collective-permute-start(bf16[32,2560]{1,0:T(8,128)(2,1)S(1)} %get-tuple-element.86), channel_id=1, source_target_pairs={{0,32},{32,64},{64,96},{96,0},{128,160},{160,192},{192,224},{224,1... | collective-permute-start | bytes 491528 | tf_op jit(solution)/shard_map/ppermute | solution.py:33
  57.9 10.7 %collective-permute-start.8 = (bf16[32,2560]{1,0:T(8,128)(2,1)S(1)}, bf16[32,2560]{1,0:T(8,128)(2,1)S(1)}, u32[]{:S(2)}, u32[]{:S(2)}) collective-permute-start(bf16[32,2560]{1,0:T(8,128)(2,1)S(1)} %get-tuple-element.87), channel_id=1, source_target_pairs={{0,96},{32,0},{64,32},{96,64},{128,224},{160,128},{192,160},{224,1... | collective-permute-start | bytes 491528 | tf_op jit(solution)/shard_map/ppermute | solution.py:33
  60.3 8.3 %collective-permute-start.9 = (bf16[32,2560]{1,0:T(8,128)(2,1)S(1)}, bf16[32,2560]{1,0:T(8,128)(2,1)S(1)}, u32[]{:S(2)}, u32[]{:S(2)}) collective-permute-start(bf16[32,2560]{1,0:T(8,128)(2,1)S(1)} %get-tuple-element.88), channel_id=1, source_target_pairs={{0,128},{32,160},{64,192},{96,224},{128,0},{160,32},{192,64},{224,... | collective-permute-start | bytes 491528 | tf_op jit(solution)/shard_map/ppermute | solution.py:33
  65.0 6.5 %collective-permute-start.21 = (bf16[32,2560]{1,0:T(8,128)(2,1)S(1)}, bf16[32,2560]{1,0:T(8,128)(2,1)S(1)}, u32[]{:S(2)}, u32[]{:S(2)}) collective-permute-start(bf16[32,2560]{1,0:T(8,128)(2,1)S(1)} %get-tuple-element.114), channel_id=1, source_target_pairs={{0,32},{32,64},{64,96},{96,0},{128,160},{160,192},{192,224},{224,1... | collective-permute-start | bytes 491528 | tf_op jit(solution)/shard_map/ppermute | solution.py:33
  65.1 7.1 %collective-permute-start.22 = (bf16[32,2560]{1,0:T(8,128)(2,1)S(1)}, bf16[32,2560]{1,0:T(8,128)(2,1)S(1)}, u32[]{:S(2)}, u32[]{:S(2)}) collective-permute-start(bf16[32,2560]{1,0:T(8,128)(2,1)S(1)} %get-tuple-element.115), channel_id=1, source_target_pairs={{0,96},{32,0},{64,32},{96,64},{128,224},{160,128},{192,160},{224,1... | collective-permute-start | bytes 491528 | tf_op jit(solution)/shard_map/ppermute | solution.py:33
  68.7 5.5 %collective-permute-start.17 = (bf16[32,2560]{1,0:T(8,128)(2,1)S(1)}, bf16[32,2560]{1,0:T(8,128)(2,1)S(1)}, u32[]{:S(2)}, u32[]{:S(2)}) collective-permute-start(bf16[32,2560]{1,0:T(8,128)(2,1)S(1)} %add_convert_fusion.5), channel_id=1, source_target_pairs={{0,32},{32,64},{64,96},{96,0},{128,160},{160,192},{192,224},{224,1... | collective-permute-start | bytes 491528 | tf_op jit(solution)/shard_map/ppermute | solution.py:33
  68.8 6.3 %collective-permute-start.18 = (bf16[32,2560]{1,0:T(8,128)(2,1)S(1)}, bf16[32,2560]{1,0:T(8,128)(2,1)S(1)}, u32[]{:S(2)}, u32[]{:S(2)}) collective-permute-start(bf16[32,2560]{1,0:T(8,128)(2,1)S(1)} %get-tuple-element.106), channel_id=1, source_target_pairs={{0,96},{32,0},{64,32},{96,64},{128,224},{160,128},{192,160},{224,1... | collective-permute-start | bytes 491528 | tf_op jit(solution)/shard_map/ppermute | solution.py:33
  73.3 6.1 %collective-permute-start.25 = (bf16[32,2560]{1,0:T(8,128)(2,1)S(1)}, bf16[32,2560]{1,0:T(8,128)(2,1)S(1)}, u32[]{:S(2)}, u32[]{:S(2)}) collective-permute-start(bf16[32,2560]{1,0:T(8,128)(2,1)S(1)} %get-tuple-element.125), channel_id=1, source_target_pairs={{0,32},{32,64},{64,96},{96,0},{128,160},{160,192},{192,224},{224,1... | collective-permute-start | bytes 491528 | tf_op jit(solution)/shard_map/ppermute | solution.py:33
  74.2 6.0 %collective-permute-start.26 = (bf16[32,2560]{1,0:T(8,128)(2,1)S(1)}, bf16[32,2560]{1,0:T(8,128)(2,1)S(1)}, u32[]{:S(2)}, u32[]{:S(2)}) collective-permute-start(bf16[32,2560]{1,0:T(8,128)(2,1)S(1)} %add_convert_fusion.1), channel_id=1, source_target_pairs={{0,128},{32,160},{64,192},{96,224},{128,0},{160,32},{192,64},{224,... | collective-permute-start | bytes 491528 | tf_op jit(solution)/shard_map/ppermute | solution.py:33
  76.2 6.0 %collective-permute-start.20 = (bf16[32,2560]{1,0:T(8,128)(2,1)S(1)}, bf16[32,2560]{1,0:T(8,128)(2,1)S(1)}, u32[]{:S(2)}, u32[]{:S(2)}) collective-permute-start(bf16[32,2560]{1,0:T(8,128)(2,1)S(1)} %add_convert_fusion.3), channel_id=1, source_target_pairs={{0,32},{32,64},{64,96},{96,0},{128,160},{160,192},{192,224},{224,1... | collective-permute-start | bytes 491528 | tf_op jit(solution)/shard_map/ppermute | solution.py:33
  80.2 5.7 %collective-permute-start.27 = (bf16[32,2560]{1,0:T(8,128)(2,1)S(1)}, bf16[32,2560]{1,0:T(8,128)(2,1)S(1)}, u32[]{:S(2)}, u32[]{:S(2)}) collective-permute-start(bf16[32,2560]{1,0:T(8,128)(2,1)S(1)} %add_convert_fusion), channel_id=1, source_target_pairs={{0,96},{32,0},{64,32},{96,64},{128,224},{160,128},{192,160},{224,1... | collective-permute-start | bytes 491528 | tf_op jit(solution)/shard_map/ppermute | solution.py:33
  86.8 25.8 %all-to-all-start.1 = ((bf16[32,40,128]{2,1,0:T(8,128)(2,1)}), bf16[32,40,128]{2,1,0:T(8,128)(2,1)S(1)}, u32[]{:S(2)}, u32[]{:S(2)}) async-start(bf16[32,40,128]{2,1,0:T(8,128)(2,1)} %bitcast.5), calls=%async_computation.1 | async-start | bytes 655360 | tf_op jit(solution)/shard_map/all_to_all | solution.py:495
  115.9 4.8 %collective-permute-start.30 = (bf16[32,1280]{1,0:T(8,128)(2,1)S(1)}, bf16[32,1280]{1,0:T(8,128)(2,1)S(1)}, u32[]{:S(2)}, u32[]{:S(2)}) collective-permute-start(bf16[32,1280]{1,0:T(8,128)(2,1)S(1)} %add_convert_fusion.11), channel_id=1, source_target_pairs={{0,64},{1,17},{2,66},{3,19},{4,68},{5,21},{6,70},{7,23},{8,72},{9,... | collective-permute-start | bytes 245768 | tf_op jit(solution)/shard_map/ppermute | solution.py:378
  121.7 5.4 %collective-permute-start.34 = (bf16[32,1280]{1,0:T(8,128)(2,1)S(1)}, bf16[32,1280]{1,0:T(8,128)(2,1)S(1)}, u32[]{:S(2)}, u32[]{:S(2)}) collective-permute-start(bf16[32,1280]{1,0:T(8,128)(2,1)S(1)} %add_convert_fusion.10), channel_id=1, source_target_pairs={{0,24},{1,97},{2,26},{3,99},{4,28},{5,101},{6,30},{7,103},{8,0},{9... | collective-permute-start | bytes 245768 | tf_op jit(solution)/shard_map/ppermute | solution.py:378
  124.9 4.9 %collective-permute-start.33 = (bf16[32,1280]{1,0:T(8,128)(2,1)S(1)}, bf16[32,1280]{1,0:T(8,128)(2,1)S(1)}, u32[]{:S(2)}, u32[]{:S(2)}) collective-permute-start(bf16[32,1280]{1,0:T(8,128)(2,1)S(1)} %add_convert_fusion.10), channel_id=1, source_target_pairs={{0,16},{1,65},{2,18},{3,67},{4,20},{5,69},{6,22},{7,71},{8,24},{9,... | collective-permute-start | bytes 245768 | tf_op jit(solution)/shard_map/ppermute | solution.py:378
  124.9 5.4 %collective-permute-start.32 = (bf16[32,1280]{1,0:T(8,128)(2,1)S(1)}, bf16[32,1280]{1,0:T(8,128)(2,1)S(1)}, u32[]{:S(2)}, u32[]{:S(2)}) collective-permute-start(bf16[32,1280]{1,0:T(8,128)(2,1)S(1)} %add_convert_fusion.10), channel_id=1, source_target_pairs={{0,8},{1,33},{2,10},{3,35},{4,12},{5,37},{6,14},{7,39},{8,16},{9,4... | collective-permute-start | bytes 245768 | tf_op jit(solution)/shard_map/ppermute | solution.py:378
  138.3 5.2 %collective-permute-start.37 = (bf16[32,1280]{1,0:T(8,128)(2,1)S(1)}, bf16[32,1280]{1,0:T(8,128)(2,1)S(1)}, u32[]{:S(2)}, u32[]{:S(2)}) collective-permute-start(bf16[32,1280]{1,0:T(8,128)(2,1)S(1)} %add_convert_fusion.7), channel_id=1, source_target_pairs={{0,130},{1,131},{8,138},{9,139},{16,146},{17,147},{24,154},{25,155... | collective-permute-start | bytes 245768 | tf_op jit(solution)/shard_map/ppermute | solution.py:393
  143.5 8.0 %collective-permute-start.38 = (bf16[32,1280]{1,0:T(8,128)(2,1)S(1)}, bf16[32,1280]{1,0:T(8,128)(2,1)S(1)}, u32[]{:S(2)}, u32[]{:S(2)}) collective-permute-start(bf16[32,1280]{1,0:T(8,128)(2,1)S(1)} %add_convert_fusion.6), channel_id=1, source_target_pairs={{0,1},{1,0},{2,3},{3,2},{4,5},{5,4},{6,7},{7,6},{8,9},{9,8},{10,11... | collective-permute-start | bytes 245768 | tf_op jit(solution)/shard_map/ppermute | solution.py:47
  (12 other events, 87.3 us)
